TPU v7x, 32 devices: a whole 2x2x4 slice. The times are simulated.
32 devices in a mesh: dp: 8 (over z, y), tensor: 4 (over x, core).
Axes of the slice: x: 2, y: 2, z: 4, core: 2. Of those that a mesh axis runs over, the one named last changes fastest.
Arguments:
- tokens: bfloat16 [8, 16, 16, 1152], P('dp'), may hold values from -6 to 6
- lengths: int32 [8], P('dp'), may hold values from 8 to 16
- timesteps: int32 [8], P('dp'), may hold values from 0 to 999
- labels: int32 [8], P('dp'), may hold values from 0 to 100
- class_table: bfloat16 [101, 1152], P(None, 'tensor'), may hold values from -6 to 6
- ada_weight: bfloat16 [1152, 6912], P(None, 'tensor'), may hold values from -0.1875 to 0.1875
- ada_bias: bfloat16 [6912], P('tensor'), may hold values from -3 to 3
- qkv_weight: bfloat16 [1152, 3456], P(None, 'tensor'), may hold values from -0.1875 to 0.1875
- qv_bias: bfloat16 [2304], P('tensor'), may hold values from -3 to 3
- out_weight: bfloat16 [1152, 1152], P(None, 'tensor'), may hold values from -0.375 to 0.375
- proj_bias: bfloat16 [1152], replicated, may hold values from -3 to 3
- up_weight: bfloat16 [1152, 4608], P(None, 'tensor'), may hold values from -0.1875 to 0.1875
- fc1_bias: bfloat16 [4608], P('tensor'), may hold values from -3 to 3
- down_weight: bfloat16 [1152, 4608], P(None, 'tensor'), may hold values from -0.09375 to 0.09375
- fc2_bias: bfloat16 [1152], replicated, may hold values from -3 to 3
- cotangent: bfloat16 [8, 16, 16, 1152], P('dp'), may hold values from -6 to 6
Outputs:
- result: bfloat16 [8, 16, 16, 1152], P('dp')
- tokens_grad: bfloat16 [8, 16, 16, 1152], P('dp')
- qkv_weight_grad: float32 [1152, 3456], P('dp', 'tensor')
- out_weight_grad: float32 [1152, 1152], P('dp', 'tensor')
- up_weight_grad: float32 [1152, 4608], P('dp', 'tensor')
- down_weight_grad: float32 [1152, 4608], P('dp', 'tensor')
- ada_weight_grad: float32 [1152, 6912], P('dp', 'tensor')
- class_table_grad: float32 [101, 1152], P(None, 'tensor')
- qv_bias_grad: float32 [2304], P('tensor')
- proj_bias_grad: float32 [1152], replicated
- fc1_bias_grad: float32 [4608], P('tensor')
- fc2_bias_grad: float32 [1152], replicated
- ada_bias_grad: float32 [6912], P('tensor')
Inputs may be any that keep to these rules, and one draw needn't show every extreme that they name: Frames of clip c at positions below lengths[c] hold data, the others of the 16 slots are padding.
All inputs are finite; a program needn't handle non-finite values.
Results may differ from a plain program's by a relative error of at most 0.019.
Values may be sent and summed in bfloat16 or wider, within the bound.
No kernel may reach another device: no remote copies, remote signals or barrier semaphores. Data moves between devices by JAX's collectives and lax.ppermute only.
A program may use at most 128 MiB of HBM per device.

v0:
```python
import math

import jax
import jax.numpy as jnp
from jax import lax
from jax.sharding import PartitionSpec as P

HEAD_DIM = 72


def time_embedding(times, width):
    half = width // 2
    freqs = jnp.exp(-math.log(10000.0) * jnp.arange(half, dtype=jnp.float32) / half)
    angles = times.astype(jnp.float32)[:, None] * freqs[None, :]
    return jnp.concatenate([jnp.cos(angles), jnp.sin(angles)], axis=1)


def layer_norm(value):
    center = value - jnp.mean(value, axis=-1, keepdims=True)
    spread = jnp.mean(center * center, axis=-1, keepdims=True)
    return center * lax.rsqrt(spread + 1e-06)


def modulate(value, shift, scale):
    return layer_norm(value) * (1.0 + scale) + shift


def gelu_tanh(value):
    return jax.nn.gelu(value, approximate=True)


def product(left, right):
    return jnp.dot(left, right, preferred_element_type=jnp.float32)


def product_trans(left, right):
    return lax.dot_general(
        left, right, (((1,), (1,)), ((), ())), preferred_element_type=jnp.float32
    )


def product_rows(left, right):
    return lax.dot_general(
        left, right, (((0,), (0,)), ((), ())), preferred_element_type=jnp.float32
    )


def shards(
    tokens,
    lengths,
    timesteps,
    labels,
    class_table,
    ada_weight,
    ada_bias,
    qkv_weight,
    qv_bias,
    out_weight,
    proj_bias,
    up_weight,
    fc1_bias,
    down_weight,
    fc2_bias,
    cotangent,
):
    clips, patches, frames, width = tokens.shape
    seqs = clips * patches
    rows = seqs * frames
    heads = out_weight.shape[1] // HEAD_DIM
    factor = HEAD_DIM ** (-0.5)
    columns = class_table.shape[1]
    ada_cols = ada_weight.shape[1]
    tensor_rank = lax.axis_index("tensor")
    onehot = labels[:, None] == jnp.arange(class_table.shape[0], dtype=jnp.int32)[None, :]
    picked = product(onehot.astype(jnp.bfloat16), class_table).astype(jnp.bfloat16)
    embedded = lax.all_gather(picked, "tensor", axis=1, tiled=True)
    cond = time_embedding(timesteps, width) + embedded.astype(jnp.float32)
    act_cond = jax.nn.silu(cond).astype(jnp.bfloat16)
    mod_part = product(act_cond, ada_weight) + ada_bias.astype(jnp.float32)
    modulation = lax.all_gather(mod_part, "tensor", axis=1, tiled=True)
    mods = modulation.reshape(clips, 6, width)[:, :, None, None, :]
    valid = jnp.arange(frames, dtype=jnp.int32)[None, :] < lengths[:, None]
    keep = valid[:, None, :, None]
    key_valid = jnp.broadcast_to(valid[:, None, :], (clips, patches, frames)).reshape(
        seqs, 1, 1, frames
    )
    inputs = tokens.astype(jnp.float32)
    normed_one, norm_one_back = jax.vjp(modulate, inputs, mods[:, 0], mods[:, 1])
    normed1 = normed_one.astype(jnp.bfloat16).reshape(rows, width)
    qkv = product(normed1, qkv_weight).reshape(seqs, frames, heads, 3, HEAD_DIM)
    biases = qv_bias.astype(jnp.float32).reshape(heads, 2, HEAD_DIM)
    query = (qkv[:, :, :, 0] + biases[:, 0]).astype(jnp.bfloat16)
    key = qkv[:, :, :, 1].astype(jnp.bfloat16)
    value = (qkv[:, :, :, 2] + biases[:, 1]).astype(jnp.bfloat16)
    scores = jnp.einsum("sqhe,skhe->shqk", query, key, preferred_element_type=jnp.float32) * factor
    scores = jnp.where(key_valid, scores, -1e30)
    highest = jnp.max(scores, axis=-1, keepdims=True)
    raised = jnp.exp(scores - highest)
    totals = jnp.sum(raised, axis=-1, keepdims=True)
    probs = raised / totals
    log_total = highest + jnp.log(totals)
    attended = jnp.einsum(
        "shqk,skhe->sqhe", probs.astype(jnp.bfloat16), value, preferred_element_type=jnp.float32
    )
    attended = attended.astype(jnp.bfloat16).reshape(rows, heads * HEAD_DIM)
    attn_part = product_trans(attended, out_weight)
    branch_one = lax.psum(attn_part, "tensor") + proj_bias.astype(jnp.float32)
    branch_one = branch_one.reshape(tokens.shape)
    middle = inputs + mods[:, 2] * branch_one
    normed_two, norm_two_back = jax.vjp(modulate, middle, mods[:, 3], mods[:, 4])
    normed2 = normed_two.astype(jnp.bfloat16).reshape(rows, width)
    hidden_pre = product(normed2, up_weight) + fc1_bias.astype(jnp.float32)
    activated, gelu_back = jax.vjp(gelu_tanh, hidden_pre)
    act_low = activated.astype(jnp.bfloat16)
    mlp_part = product_trans(act_low, down_weight)
    branch_two = lax.psum(mlp_part, "tensor") + fc2_bias.astype(jnp.float32)
    branch_two = branch_two.reshape(tokens.shape)
    final = middle + mods[:, 5] * branch_two
    result = jnp.where(keep, final, inputs).astype(jnp.bfloat16)
    upstream = cotangent.astype(jnp.float32)
    final_grad = jnp.where(keep, upstream, 0.0)
    branch_two_grad = (mods[:, 5] * final_grad).astype(jnp.bfloat16).reshape(rows, width)
    down_grad = product_rows(branch_two_grad, act_low)
    fc2_grad = jnp.sum(branch_two_grad.astype(jnp.float32), axis=0)
    act_grad = product(branch_two_grad, down_weight)
    (pre_grad,) = gelu_back(act_grad)
    pre_low = pre_grad.astype(jnp.bfloat16)
    up_grad = product_rows(normed2, pre_low)
    fc1_grad = jnp.sum(pre_low.astype(jnp.float32), axis=0)
    mlp_back = product_trans(pre_low, up_weight)
    gate_two_grad = jnp.sum(final_grad * branch_two, axis=(1, 2))
    normed2_grad = lax.psum(mlp_back, "tensor").reshape(tokens.shape)
    middle_ln_grad, shift_two_full, scale_two_full = norm_two_back(normed2_grad)
    shift_two_grad = shift_two_full.reshape(clips, width)
    scale_two_grad = scale_two_full.reshape(clips, width)
    middle_grad = final_grad + middle_ln_grad
    gate_one_grad = jnp.sum(middle_grad * branch_one, axis=(1, 2))
    branch_one_grad = (mods[:, 2] * middle_grad).astype(jnp.bfloat16).reshape(rows, width)
    out_grad = product_rows(branch_one_grad, attended)
    proj_grad = jnp.sum(branch_one_grad.astype(jnp.float32), axis=0)
    attended_grad = product(branch_one_grad, out_weight).astype(jnp.bfloat16)
    attended_grad = attended_grad.reshape(seqs, frames, heads, HEAD_DIM)
    again = jnp.einsum("sqhe,skhe->shqk", query, key, preferred_element_type=jnp.float32) * factor
    again = jnp.where(key_valid, again, -1e30)
    probs_again = jnp.exp(again - log_total)
    value_grad = jnp.einsum(
        "shqk,sqhe->skhe",
        probs_again.astype(jnp.bfloat16),
        attended_grad,
        preferred_element_type=jnp.float32,
    ).astype(jnp.bfloat16)
    probs_grad = jnp.einsum(
        "sqhe,skhe->shqk", attended_grad, value, preferred_element_type=jnp.float32
    )
    scores_grad = probs_again * (
        probs_grad - jnp.sum(probs_again * probs_grad, axis=-1, keepdims=True)
    )
    scores_low = scores_grad.astype(jnp.bfloat16)
    query_grad = (
        jnp.einsum("shqk,skhe->sqhe", scores_low, key, preferred_element_type=jnp.float32) * factor
    ).astype(jnp.bfloat16)
    key_grad = (
        jnp.einsum("shqk,sqhe->skhe", scores_low, query, preferred_element_type=jnp.float32)
        * factor
    ).astype(jnp.bfloat16)
    stacked = jnp.stack([query_grad, key_grad, value_grad], axis=3).reshape(
        rows, heads * 3 * HEAD_DIM
    )
    qkv_grad = product_rows(normed1, stacked)
    bias_query = jnp.sum(query_grad.astype(jnp.float32), axis=(0, 1))
    bias_value = jnp.sum(value_grad.astype(jnp.float32), axis=(0, 1))
    qv_grad = jnp.stack([bias_query, bias_value], axis=1).reshape(heads * 2 * HEAD_DIM)
    attn_back = product_trans(stacked, qkv_weight)
    normed1_grad = lax.psum(attn_back, "tensor").reshape(tokens.shape)
    input_ln_grad, shift_one_grad, scale_one_grad = norm_one_back(normed1_grad)
    tokens_grad = (middle_grad + input_ln_grad + jnp.where(keep, 0.0, upstream)).astype(
        jnp.bfloat16
    )
    mod_grad = jnp.stack(
        [
            shift_one_grad.reshape(clips, width),
            scale_one_grad.reshape(clips, width),
            gate_one_grad,
            shift_two_grad,
            scale_two_grad,
            gate_two_grad,
        ],
        axis=1,
    )
    mod_low = mod_grad.reshape(clips, 6 * width).astype(jnp.bfloat16)
    mod_cols = lax.dynamic_slice_in_dim(mod_low, tensor_rank * ada_cols, ada_cols, 1)
    ada_grad = product_rows(act_cond, mod_cols)
    ada_bias_grad = jnp.sum(mod_cols.astype(jnp.float32), axis=0)
    cond_part = product_trans(mod_cols, ada_weight)
    act_cond_grad = lax.psum_scatter(cond_part, "tensor", scatter_dimension=1, tiled=True)
    cond_cols = lax.dynamic_slice_in_dim(cond, tensor_rank * columns, columns, 1)
    silu_value, silu_back = jax.vjp(jax.nn.silu, cond_cols)
    (cond_grad,) = silu_back(act_cond_grad)
    table_grad = lax.dot_general(
        onehot.astype(jnp.float32),
        cond_grad,
        (((0,), (0,)), ((), ())),
        precision=lax.Precision.HIGHEST,
        preferred_element_type=jnp.float32,
    )
    qkv_grad, out_grad, up_grad, down_grad, ada_grad = (
        lax.psum_scatter(qkv_grad, "dp", scatter_dimension=0, tiled=True),
        lax.psum_scatter(out_grad, "dp", scatter_dimension=0, tiled=True),
        lax.psum_scatter(up_grad, "dp", scatter_dimension=0, tiled=True),
        lax.psum_scatter(down_grad, "dp", scatter_dimension=0, tiled=True),
        lax.psum_scatter(ada_grad, "dp", scatter_dimension=0, tiled=True),
    )
    table_grad, qv_grad, proj_grad, fc1_grad, fc2_grad, ada_bias_grad = lax.psum(
        (table_grad, qv_grad, proj_grad, fc1_grad, fc2_grad, ada_bias_grad), "dp"
    )
    return (
        result,
        tokens_grad,
        qkv_grad,
        out_grad,
        up_grad,
        down_grad,
        ada_grad,
        table_grad,
        qv_grad,
        proj_grad,
        fc1_grad,
        fc2_grad,
        ada_bias_grad,
    )


def solution(mesh):
    placed = (
        P("dp", None, None, None),
        P("dp"),
        P("dp"),
        P("dp"),
        P(None, "tensor"),
        P(None, "tensor"),
        P("tensor"),
        P(None, "tensor"),
        P("tensor"),
        P(None, "tensor"),
        P(),
        P(None, "tensor"),
        P("tensor"),
        P(None, "tensor"),
        P(),
        P("dp", None, None, None),
    )
    return jax.shard_map(
        shards,
        mesh=mesh,
        in_specs=placed,
        out_specs=(
            P("dp", None, None, None),
            P("dp", None, None, None),
            P("dp", "tensor"),
            P("dp", "tensor"),
            P("dp", "tensor"),
            P("dp", "tensor"),
            P("dp", "tensor"),
            P(None, "tensor"),
            P("tensor"),
            P(),
            P("tensor"),
            P(),
            P("tensor"),
        ),
        check_vma=False,
    )
```

profile of v0, /device:TPU:0, one launch (start us, length us, event | category | flops | bytes accessed | tf_op | source)
XLA Modules:
  0.0 855.8 jit_solution(1607597603194945001)
XLA Ops:
  9.4 1.2 dynamic-slice
  11.9 0.8 reshape.442
  12.7 1.0 convolution_reduce_fusion.1
  14.0 8.3 all-reduce
  22.5 1.2 convert_reduce_fusion
  23.7 1.3 fusion.26
  25.1 0.7 convert_reduce_fusion.6
  25.8 3.4 convolution_reduce_fusion
  29.3 10.3 %all-reduce.1 = f32[6912]{0:T(1024)S(1)} all-reduce(f32[6912]{0:T(1024)S(1)} %add_dynamic-update-slice_fusion), channel_id=3, replica_groups=mesh['dp'=8,'tensor'=4] {'tensor'}, use_global_device_ids=true, to_apply=%add.1 | all-reduce | flops 6912 | bytes 55296
  39.6 0.7 slice_reduce_fusion.1
  40.6 3.0 fusion.31
  44.9 0.8 copy.41
  45.7 1.2 reshape.422
  46.9 2.6 fusion.82
  49.6 0.6 convert_element_type.150
  50.2 1.3 convert_element_type.152
  51.5 1.9 convert_reduce_fusion.1
  53.4 0.9 copy-done.24
  54.3 4.0 fusion.83
  58.3 29.1 %all-reduce.9.cloned.1.call-done = f32[256,1152]{1,0:T(8,128)} async-done(((f32[256,1152]{1,0:T(8,128)}), f32[256,1152]{1,0:T(8,128)}) %all-reduce.9.cloned.1.call-update) | async-done | bytes 1179664 | tf_op jit(solution)/shard_map/psum | solution.py:107
  87.4 1.3 broadcast_add_fusion.1
  89.3 0.7 copy-done.38
  90.7 3.2 convert_reduce_fusion.2
  93.8 0.8 copy-done.28
  94.6 2.1 fusion.84
  97.0 1.0 copy-done.26
  98.0 4.0 fusion.75
  102.1 32.4 %all-reduce.11.cloned.1.call-done = f32[256,1152]{1,0:T(8,128)} async-done(((f32[256,1152]{1,0:T(8,128)}), f32[256,1152]{1,0:T(8,128)}) %all-reduce.11.cloned.1.call-update) | async-done | bytes 1179664 | tf_op jit(solution)/shard_map/psum | solution.py:132
  134.5 1.6 multiply_reduce_fusion.2
  137.2 1.6 convert_reduce_fusion.3
  138.8 0.8 copy-done.11
  140.1 0.8 copy.42
  140.9 1.1 reshape.429
  142.0 1.3 convert_reduce_fusion.4
  143.3 1.6 multiply_reduce_fusion.4
  145.9 1.7 copy.46
  147.6 3.5 reshape.430
  151.0 3.6 fusion.85
  154.7 0.6 copy-done.54
  155.4 55.4 %all-reduce.15.cloned.1.call-done = (f32[256,1152]{1,0:T(8,128)}, f32[256,1152]{1,0:T(8,128)}) async-done(((f32[256,1152]{1,0:T(8,128)}, f32[256,1152]{1,0:T(8,128)}), (f32[256,1152]{1,0:T(8,128)}, f32[256,1152]{1,0:T(8,128)})) %all-reduce.15.cloned.1.call-update) | async-done | bytes 2359312 | tf_op jit(solution)/shard_map/psum | solution.py:116
  210.8 2.9 fusion.16
  216.4 1.7 multiply_reduce_fusion.1
  218.1 4.7 convolution_bitcast_fusion
  223.0 22.2 %reduce-scatter.19.cloned.1.call-done = f32[288,1]{1,0:T(8,128)} async-done(((f32[1152,1]{1,0:T(8,128)}), f32[288,1]{1,0:T(8,128)}) %reduce-scatter.19.cloned.1.call-update) | async-done | bytes 1168
  245.2 1.0 copy.51
  246.2 0.8 fusion.67
  247.0 0.8 broadcast_multiply_fusion.1
  247.9 1.7 fusion.87
  249.9 0.8 copy-done.17
  250.8 2.8 fusion.86
  253.6 1.0 copy-done.25
  255.0 3.4 fusion.74
  258.5 1.0 copy-done.22
  259.7 3.3 fusion.88
  263.1 0.6 copy-done.45
  263.8 3.8 broadcast_multiply_fusion
  268.3 38.2 %all-reduce.2 = (f32[576]{0:T(1024)}, f32[1152]{0:T(1024)}, f32[1152]{0:T(1024)}, f32[1152]{0:T(1024)}, f32[1728]{0:T(1024)}) all-reduce(f32[576]{0:T(1024)S(1)} %reshape.440, f32[1152]{0:T(1024)S(1)} %get-tuple-element.34, f32[1152]{0:T(1024)S(1)} %copy-done.52, ...), channel_id=1, replica_groups=mesh['dp'=8,'tensor'=4] {'dp'}, use_global_device_ids=true, to_apply=%region_30.31 | all-reduce | flops 5760 | bytes 42624 | tf_op jit(solution)/shard_map/psum | solution.py:213
  306.5 12.5 %all-reduce.13.cloned.1.call-done = f32[101,288]{0,1:T(8,128)} async-done(((f32[101,288]{0,1:T(8,128)}), f32[101,288]{0,1:T(8,128)}) %all-reduce.13.cloned.1.call-update) | async-done | bytes 116368 | tf_op jit(solution)/shard_map/psum | solution.py:213
  318.9 69.4 %reduce-scatter.11.cloned.1.call-done = f32[144,288]{1,0:T(8,128)} async-done(((f32[1152,288]{1,0:T(8,128)}), f32[144,288]{1,0:T(8,128)}) %reduce-scatter.11.cloned.1.call-update) | async-done | bytes 165904 | tf_op jit(solution)/shard_map/reduce_scatter | solution.py:208
  388.3 90.7 %reduce-scatter.9.cloned.1.call-done = f32[144,864]{1,0:T(8,128)} async-done(((f32[1152,864]{1,0:T(8,128)}), f32[144,864]{1,0:T(8,128)}) %reduce-scatter.9.cloned.1.call-update) | async-done | bytes 497680 | tf_op jit(solution)/shard_map/reduce_scatter | solution.py:207
  479.0 108.6 %reduce-scatter.15.cloned.1.call-done = f32[144,1152]{1,0:T(8,128)} async-done(((f32[1152,1152]{1,0:T(8,128)}), f32[144,1152]{1,0:T(8,128)}) %reduce-scatter.15.cloned.1.call-update) | async-done | bytes 663568 | tf_op jit(solution)/shard_map/reduce_scatter | solution.py:210
  587.6 108.2 %reduce-scatter.13.cloned.1.call-done = f32[144,1152]{1,0:T(8,128)} async-done(((f32[1152,1152]{1,0:T(8,128)}), f32[144,1152]{1,0:T(8,128)}) %reduce-scatter.13.cloned.1.call-update) | async-done | bytes 663568 | tf_op jit(solution)/shard_map/reduce_scatter | solution.py:209
  695.8 151.6 %reduce-scatter.17.cloned.1.call-done = f32[144,1728]{1,0:T(8,128)} async-done(((f32[1152,1728]{1,0:T(8,128)}), f32[144,1728]{1,0:T(8,128)}) %reduce-scatter.17.cloned.1.call-update) | async-done | bytes 995344 | tf_op jit(solution)/shard_map/reduce_scatter | solution.py:211
  847.3 1.6 copy.71
  (174 shorter events, 11.1 us)
Async XLA Ops:
  7.2 83.1 %copy-start = (bf16[1152,1152]{1,0:T(8,128)(2,1)S(1)}, bf16[1152,1152]{1,0:T(8,128)(2,1)}, u32[]{:S(2)}) copy-start(bf16[1152,1152]{1,0:T(8,128)(2,1)} %param.27) | copy-start | bytes 7962628
  7.2 80.2 %all-reduce.9.cloned.1.call-start = ((), (), s32[]{:S(2)}) async-start(), calls=%async_computation.6 | async-start | bytes 2359296 | tf_op jit(solution)/shard_map/psum | solution.py:107
  9.3 34.3 %copy-start.46 = (pred[16]{0:T(512)(128)(4,1)}, pred[16]{0:T(512)(128)(4,1)S(1)}, u32[]{:S(2)}) copy-start(pred[16]{0:T(512)(128)(4,1)S(1)} %iota_compare_fusion) | copy-start | bytes 52
  12.7 30.9 %copy-start.43 = (f32[4,1,72]{2,1,0:T(1,128)}, f32[4,1,72]{2,1,0:T(1,128)S(1)}, u32[]{:S(2)}) copy-start(f32[4,1,72]{2,1,0:T(1,128)S(1)} %get-tuple-element.47) | copy-start | bytes 3460
  12.7 31.4 %copy-start.49 = (f32[4,1,72]{2,1,0:T(1,128)}, f32[4,1,72]{2,1,0:T(1,128)S(1)}, u32[]{:S(2)}) copy-start(f32[4,1,72]{2,1,0:T(1,128)S(1)} %get-tuple-element.46) | copy-start | bytes 3460
  25.0 4.1 copy-start.36
  25.8 3.4 copy-start.42
  25.8 3.4 copy-start.55
  25.8 14.5 %copy-start.6 = (bf16[1,16,16,1152]{3,2,1,0:T(8,128)(2,1)S(1)}, bf16[1,16,16,1152]{3,2,1,0:T(8,128)(2,1)}, u32[]{:S(2)}) copy-start(bf16[1,16,16,1152]{3,2,1,0:T(8,128)(2,1)} %param.16) | copy-start | bytes 1769476
  40.3 11.2 %copy-start.30 = (f32[1152]{0:T(1024)}, f32[1152]{0:T(1024)S(1)}, u32[]{:S(2)}) copy-start(f32[1152]{0:T(1024)S(1)} %get-tuple-element.17) | copy-start | bytes 13828
  40.6 3.0 copy-start.16
  43.6 1.2 copy-start.18
  43.9 1.0 copy-start.7
  46.9 2.7 copy-start.53
  46.9 4.6 copy-start.47
  49.5 84.9 %all-reduce.11.cloned.1.call-start = ((), (), s32[]{:S(2)}) async-start(), calls=%async_computation.7 | async-start | bytes 2359296 | tf_op jit(solution)/shard_map/psum | solution.py:132
  53.4 0.9 copy-start.24
  54.3 33.1 %copy-start.34 = (f32[1152]{0:T(1024)S(1)}, f32[1152]{0:T(1024)}, u32[]{:S(2)}) copy-start(f32[1152]{0:T(1024)} %convert_element_type.150) | copy-start | bytes 13828
  58.3 30.4 %copy-start.32 = (f32[1152]{0:T(1024)S(1)}, f32[1152]{0:T(1024)}, u32[]{:S(2)}) copy-start(f32[1152]{0:T(1024)} %get-tuple-element.22) | copy-start | bytes 13828
  89.0 1.3 copy-start.2
  89.0 1.0 copy-start.40
  89.2 0.7 copy-start.38
  89.2 1.0 copy-start.51
  89.3 1.4 copy-start.56
  90.2 3.6 copy-start.21
  93.8 0.8 copy-start.28
  96.8 1.3 copy-start.26
  96.8 114.0 %all-reduce.15.cloned.1.call-start = ((), (), s32[]{:S(2)}) async-start(), calls=%async_computation.15 | async-start | bytes 4718592 | tf_op jit(solution)/shard_map/psum | solution.py:116
  98.0 36.4 %copy-start.3 = (f32[1,16,16,1152]{3,2,1,0:T(8,128)S(1)}, f32[1,16,16,1152]{3,2,1,0:T(8,128)}, u32[]{:S(2)}) copy-start(f32[1,16,16,1152]{3,2,1,0:T(8,128)} %copy-done.2) | copy-start | bytes 3538948
  134.5 1.6 copy-start.39
  134.5 1.7 copy-start.5
  136.1 1.1 copy-start.9
  136.2 1.1 copy-start.33
  136.2 1.0 copy-start.48
  137.2 2.5 copy-start.23
  138.8 0.8 copy-start.11
  140.1 3.2 copy-start.50
  143.3 1.7 copy-start.8
  143.3 1.9 copy-start.19
  143.3 1.9 copy-start.44
  154.7 90.6 %reduce-scatter.19.cloned.1.call-start = ((), (), s32[]{:S(2)}) async-start(), calls=%async_computation.14 | async-start | bytes 737280
  210.8 2.9 copy-start.4
  213.7 0.7 copy-start.37
  213.8 1.3 copy-start.15
  214.5 1.2 copy-start.10
  214.5 1.5 copy-start.13
  214.5 1.9 copy-start.14
  214.5 1.9 copy-start.31
  214.5 1.9 copy-start.35
  222.9 25.0 %copy-start.12 = (bf16[1,16,16,1152]{3,2,1,0:T(8,128)(2,1)S(1)}, bf16[1,16,16,1152]{3,2,1,0:T(8,128)(2,1)}, u32[]{:S(2)}) copy-start(bf16[1,16,16,1152]{3,2,1,0:T(8,128)(2,1)} %copy-done.11) | copy-start | bytes 1769476
  222.9 96.0 %all-reduce.13.cloned.1.call-start = ((), (), s32[]{:S(2)}) async-start(), calls=%async_computation.13 | async-start | bytes 294912 | tf_op jit(solution)/shard_map/psum | solution.py:213
  247.8 140.5 %reduce-scatter.11.cloned.1.call-start = ((), (), s32[]{:S(2)}) async-start(), calls=%async_computation.9 | async-start | bytes 1990656 | tf_op jit(solution)/shard_map/reduce_scatter | solution.py:208
  249.6 1.1 copy-start.17
  249.6 1.2 copy-start.20
  249.6 229.4 %reduce-scatter.9.cloned.1.call-start = ((), (), s32[]{:S(2)}) async-start(), calls=%async_computation.8 | async-start | bytes 4644864 | tf_op jit(solution)/shard_map/reduce_scatter | solution.py:207
  253.6 1.1 copy-start.25
  253.6 1.5 copy-start.27
  253.6 334.0 %reduce-scatter.15.cloned.1.call-start = ((), (), s32[]{:S(2)}) async-start(), calls=%async_computation.11 | async-start | bytes 5971968 | tf_op jit(solution)/shard_map/reduce_scatter | solution.py:210
  258.5 1.1 copy-start.22
  258.5 1.2 copy-start.29
  258.5 437.3 %reduce-scatter.13.cloned.1.call-start = ((), (), s32[]{:S(2)}) async-start(), calls=%async_computation.10 | async-start | bytes 5971968 | tf_op jit(solution)/shard_map/reduce_scatter | solution.py:209
  263.0 584.3 %reduce-scatter.17.cloned.1.call-start = ((), (), s32[]{:S(2)}) async-start(), calls=%async_computation.12 | async-start | bytes 9289728 | tf_op jit(solution)/shard_map/reduce_scatter | solution.py:211
  267.6 0.7 copy-start.52
  267.6 581.3 %copy-start.1 = (bf16[1152,1152]{1,0:T(8,128)(2,1)S(1)}, bf16[1152,1152]{1,0:T(8,128)(2,1)}, u32[]{:S(2)}) copy-start(bf16[1152,1152]{1,0:T(8,128)(2,1)} %param.27) | copy-start | bytes 7962628
  (3 other events, 2.1 us)
Sparse Core Ops, SparseCore 0:
  49.7 37.6 all-reduce.8
  96.9 37.5 all-reduce.10
  154.8 55.9 all-reduce.14
  223.0 22.1 reduce-scatter.18
  249.0 69.9 all-reduce.12
  323.2 65.0 reduce-scatter.10
  392.4 86.5 reduce-scatter.8
  483.6 103.9 reduce-scatter.14
  591.8 103.9 reduce-scatter.12
  700.3 146.9 reduce-scatter.16
where the time goes:
time: 857 us; the launch traced here: 856 us
  waiting for transfers between devices  680 us (79%)
  blocking collectives  56.8 us (7%)
  matrix products  47.2 us (6%)
  local copies, waits for them, and re-layouts  26.9 us (3%)
  other arithmetic  25.7 us (3%)
  between operations  18.3 us (2%)
    reduce_scatter x1, waiting for transfers between devices, shards(): lax.psum_scatter(ada_grad, 'dp', scatter_dimension=0, tiled=True)  152 us
    reduce_scatter x1, waiting for transfers between devices, shards(): lax.psum_scatter(down_grad, 'dp', scatter_dimension=0, tiled=True)  109 us
    reduce_scatter x1, waiting for transfers between devices, shards(): lax.psum_scatter(up_grad, 'dp', scatter_dimension=0, tiled=True)  108 us
    reduce_scatter x1, waiting for transfers between devices, shards(): lax.psum_scatter(qkv_grad, 'dp', scatter_dimension=0, tiled=True)  90.7 us
    reduce_scatter x1, waiting for transfers between devices, shards(): lax.psum_scatter(out_grad, 'dp', scatter_dimension=0, tiled=True)  69.4 us
    psum x1, waiting for transfers between devices, shards(): branch_two = lax.psum(mlp_part, 'tensor') + fc2_bias.astype(jnp.float32)  55.4 us
    psum x1, blocking collectives, shards(): lax.psum((table_grad, qv_grad, proj_grad, fc1_grad, fc2_grad, ada_bias_gr...  38.2 us
    psum x1, waiting for transfers between devices, shards(): normed2_grad = lax.psum(mlp_back, 'tensor').reshape(tokens.shape)  32.4 us
  transfers between devices with their start and end apart: 10, of which 10 were waited for; matrix products, arithmetic and copies ran while one was open for 3% of the time, Pallas kernels for 0%

commit v1 on v0

v1 whole, which is shorter than its diff:
```python
import math

import jax
import jax.numpy as jnp
from jax import lax
from jax.sharding import PartitionSpec as P

HEAD_DIM = 72
BF = jnp.bfloat16
F32 = jnp.float32


def dot(left, right):
    return jnp.dot(left, right, preferred_element_type=F32)


def dot_trans(left, right):
    return lax.dot_general(left, right, (((1,), (1,)), ((), ())), preferred_element_type=F32)


def dot_rows(left, right):
    return lax.dot_general(left, right, (((0,), (0,)), ((), ())), preferred_element_type=F32)


def swap(value, axis, bit):
    size = lax.axis_size(axis)
    return lax.ppermute(value, axis, [(i, i ^ (1 << bit)) for i in range(size)])


def gather_bits(value, axis):
    rank = lax.axis_index(axis)
    for bit in range((lax.axis_size(axis) - 1).bit_length()):
        other = swap(value, axis, bit)
        mine_high = (rank >> bit) & 1
        value = jnp.where(
            mine_high == 0,
            jnp.concatenate([value, other], axis=0),
            jnp.concatenate([other, value], axis=0),
        )
    return value


def layer_norm(value):
    center = value - jnp.mean(value, axis=-1, keepdims=True)
    spread = jnp.mean(center * center, axis=-1, keepdims=True)
    inv = lax.rsqrt(spread + 1e-06)
    return center * inv, inv


def layer_norm_back(grad, scale, normed, inv):
    g = grad * (1.0 + scale)
    back = (
        g
        - jnp.mean(g, axis=-1, keepdims=True)
        - normed * jnp.mean(g * normed, axis=-1, keepdims=True)
    ) * inv
    return back, jnp.sum(grad, axis=0), jnp.sum(grad * normed, axis=0)


def gelu_pair(value):
    k = math.sqrt(2.0 / math.pi)
    square = value * value
    t = jnp.tanh(k * (value + 0.044715 * value * square))
    act = 0.5 * value * (1.0 + t)
    slope = 0.5 * (1.0 + t) + 0.5 * value * (1.0 - t * t) * k * (1.0 + 3 * 0.044715 * square)
    return act, slope


def shards(
    tokens,
    lengths,
    timesteps,
    labels,
    class_table,
    ada_weight,
    ada_bias,
    qkv_weight,
    qv_bias,
    out_weight,
    proj_bias,
    up_weight,
    fc1_bias,
    down_weight,
    fc2_bias,
    cotangent,
):
    clips, patches, frames, width = tokens.shape
    assert clips == 1
    rows = patches * frames
    half = rows // 2
    heads = out_weight.shape[1] // HEAD_DIM
    factor = HEAD_DIM ** (-0.5)
    columns = class_table.shape[1]
    ada_cols = ada_weight.shape[1]
    t_rank = lax.axis_index("tensor")
    d_rank = lax.axis_index("dp")
    n_dp = lax.axis_size("dp")
    core = t_rank & 1

    pair = lambda w: (w, swap(w, "tensor", 0))
    qkv_ws = pair(qkv_weight)
    qv_bs = pair(qv_bias.reshape(1, -1))
    out_ws = pair(out_weight)
    up_ws = pair(up_weight)
    fc1_bs = pair(fc1_bias.reshape(1, -1))
    down_ws = pair(down_weight)

    picked = lax.dynamic_slice_in_dim(class_table, labels[0], 1, 0)
    half_width = width // 2
    freqs = jnp.exp(-math.log(10000.0) * jnp.arange(half_width, dtype=F32) / half_width)
    angles = timesteps.astype(F32)[:, None] * freqs[None, :]
    clock = jnp.concatenate([jnp.cos(angles), jnp.sin(angles)], axis=1)
    embedded = gather_bits(picked.reshape(1, columns), "tensor").reshape(1, width)
    cond = clock + embedded.astype(F32)
    act_cond = jax.nn.silu(cond).astype(BF)
    mod_part = dot(act_cond, ada_weight) + ada_bias.astype(F32)
    mods = gather_bits(mod_part, "tensor").reshape(6, width)
    known = jnp.concatenate([cond, labels.astype(F32).reshape(1, 1)], axis=1)
    known = gather_bits(known, "dp")

    my_half = lambda v: lax.dynamic_slice_in_dim(v.reshape(rows, width), core * half, half, 0)
    inputs = my_half(tokens).astype(F32)
    upstream = my_half(cotangent).astype(F32)
    length = lengths[0]
    keep = (lax.broadcasted_iota(jnp.int32, (half, 1), 0) % frames) < length
    row_id = lax.broadcasted_iota(jnp.int32, (half, half), 0)
    col_id = lax.broadcasted_iota(jnp.int32, (half, half), 1)
    seen = ((row_id // frames) == (col_id // frames)) & ((col_id % frames) < length)

    norm1, inv1 = layer_norm(inputs)
    normed1 = (norm1 * (1.0 + mods[1:2]) + mods[0:1]).astype(BF)
    saved, attended, part1 = [], [], 0.0
    for w, b, o in zip(qkv_ws, qv_bs, out_ws):
        qkv = dot(normed1, w).reshape(half, heads, 3, HEAD_DIM)
        bias = b.astype(F32).reshape(heads, 2, HEAD_DIM)
        query = (qkv[:, :, 0] + bias[:, 0]).astype(BF)
        key = qkv[:, :, 1].astype(BF)
        value = (qkv[:, :, 2] + bias[:, 1]).astype(BF)
        scores = jnp.einsum("qhe,khe->hqk", query, key, preferred_element_type=F32) * factor
        scores = jnp.where(seen[None], scores, -1e30)
        raised = jnp.exp(scores - jnp.max(scores, axis=-1, keepdims=True))
        probs = raised / jnp.sum(raised, axis=-1, keepdims=True)
        att = jnp.einsum("hqk,khe->qhe", probs.astype(BF), value, preferred_element_type=F32)
        att = att.astype(BF).reshape(half, heads * HEAD_DIM)
        saved.append((query, key, value, probs))
        attended.append(att)
        part1 = part1 + dot_trans(att, o)
    part1 = part1.astype(BF)
    part1_other = swap(part1, "tensor", 1)

    final_grad = jnp.where(keep, upstream, 0.0)
    branch2_grad = (mods[5:6] * final_grad).astype(BF)
    act_grads = [dot(branch2_grad, w) for w in down_ws]

    branch1 = part1.astype(F32) + part1_other.astype(F32) + proj_bias.astype(F32)
    mid = inputs + mods[2:3] * branch1
    norm2, inv2 = layer_norm(mid)
    normed2 = (norm2 * (1.0 + mods[4:5]) + mods[3:4]).astype(BF)
    act_low, pre_low = [], []
    part2, part3 = 0.0, 0.0
    for u, b, w, g in zip(up_ws, fc1_bs, down_ws, act_grads):
        pre = dot(normed2, u) + b.astype(F32)
        act, slope = gelu_pair(pre)
        act_low.append(act.astype(BF))
        pre_low.append((g * slope).astype(BF))
        part3 = part3 + dot_trans(pre_low[-1], u)
        part2 = part2 + dot_trans(act_low[-1], w)
    part3 = part3.astype(BF)
    part3_other = swap(part3, "tensor", 1)
    part2 = part2.astype(BF)
    part2_other = swap(part2, "tensor", 1)

    both = lambda v: jnp.concatenate([v, swap(v, "tensor", 0)], axis=0)
    mine = lambda two: jnp.concatenate([two[0], swap(two[1], "tensor", 0)], axis=0)

    def scatter(grad):
        cols = grad.shape[1]
        grad = grad.reshape(n_dp, width // n_dp, cols)
        for bit in range((n_dp - 1).bit_length()):
            my_bit = (d_rank >> bit) & 1
            grad = grad.reshape(grad.shape[0] // 2, 2, width // n_dp, cols)
            send = lax.dynamic_index_in_dim(grad, 1 - my_bit, 1, keepdims=False).astype(BF)
            stay = lax.dynamic_index_in_dim(grad, my_bit, 1, keepdims=False)
            grad = stay + swap(send, "dp", bit).astype(F32)
        return grad.reshape(width // n_dp, cols)

    down_grad = scatter(dot_rows(both(branch2_grad), mine(act_low)))
    pre_mine = mine(pre_low)
    up_grad = scatter(dot_rows(both(normed2), pre_mine))
    fc1_grad = jnp.sum(pre_mine.astype(F32), axis=0, keepdims=True)
    fc2_part = jnp.sum(branch2_grad.astype(F32), axis=0)

    normed2_grad = part3.astype(F32) + part3_other.astype(F32)
    mid_ln_grad, shift2_part, scale2_part = layer_norm_back(normed2_grad, mods[4:5], norm2, inv2)
    mid_grad = final_grad + mid_ln_grad
    gate1_part = jnp.sum(mid_grad * branch1, axis=0)
    branch1_grad = (mods[2:3] * mid_grad).astype(BF)
    proj_part = jnp.sum(branch1_grad.astype(F32), axis=0)
    stacked, part4 = [], 0.0
    for (query, key, value, probs), w, o in zip(saved, qkv_ws, out_ws):
        att_grad = dot(branch1_grad, o).astype(BF).reshape(half, heads, HEAD_DIM)
        value_grad = jnp.einsum(
            "hqk,qhe->khe", probs.astype(BF), att_grad, preferred_element_type=F32
        ).astype(BF)
        probs_grad = jnp.einsum("qhe,khe->hqk", att_grad, value, preferred_element_type=F32)
        scores_grad = probs * (probs_grad - jnp.sum(probs * probs_grad, axis=-1, keepdims=True))
        low = scores_grad.astype(BF)
        query_grad = jnp.einsum("hqk,khe->qhe", low, key, preferred_element_type=F32) * factor
        key_grad = jnp.einsum("hqk,qhe->khe", low, query, preferred_element_type=F32) * factor
        stack = jnp.stack([query_grad.astype(BF), key_grad.astype(BF), value_grad], axis=2)
        stacked.append(stack.reshape(half, heads * 3 * HEAD_DIM))
        part4 = part4 + dot_trans(stacked[-1], w)
    part4 = part4.astype(BF)
    part4_other = swap(part4, "tensor", 1)

    out_grad = scatter(dot_rows(both(branch1_grad), mine(attended)))
    stacked_mine = mine(stacked)
    qkv_grad = scatter(dot_rows(both(normed1), stacked_mine))
    stack_sum = jnp.sum(stacked_mine.astype(F32), axis=0).reshape(heads, 3, HEAD_DIM)
    qv_grad = jnp.stack([stack_sum[:, 0], stack_sum[:, 2]], axis=1).reshape(1, -1)

    branch2 = part2.astype(F32) + part2_other.astype(F32) + fc2_bias.astype(F32)
    gate2_part = jnp.sum(final_grad * branch2, axis=0)
    result = jnp.where(keep, mid + mods[5:6] * branch2, inputs).astype(BF)

    def whole_rows(value):
        other = swap(value, "tensor", 0)
        return jnp.where(
            core == 0,
            jnp.concatenate([value, other], axis=0),
            jnp.concatenate([other, value], axis=0),
        ).reshape(tokens.shape)

    result = whole_rows(result)

    normed1_grad = part4.astype(F32) + part4_other.astype(F32)
    input_ln_grad, shift1_part, scale1_part = layer_norm_back(
        normed1_grad, mods[1:2], norm1, inv1
    )
    tokens_grad = (mid_grad + input_ln_grad + jnp.where(keep, 0.0, upstream)).astype(BF)
    tokens_grad = whole_rows(tokens_grad)

    sums = jnp.stack(
        [
            shift1_part,
            scale1_part,
            gate1_part,
            shift2_part,
            scale2_part,
            gate2_part,
            fc2_part,
            proj_part,
        ]
    )
    sums = sums + swap(sums, "tensor", 0)
    mod_grad = sums[:6].astype(BF).astype(F32).reshape(1, 6 * width)
    mod_cols = lax.dynamic_slice_in_dim(mod_grad, t_rank * ada_cols, ada_cols, 1)
    totals = jnp.concatenate([sums[6:].reshape(1, -1), fc1_grad, qv_grad], axis=1)
    for bit in range((n_dp - 1).bit_length()):
        other = swap(jnp.concatenate([totals, mod_cols.reshape(1, -1)], axis=1), "dp", bit)
        totals = totals + other[:, : totals.shape[1]]
        other = other[:, totals.shape[1] :].reshape(mod_cols.shape)
        mod_cols = jnp.where(
            ((d_rank >> bit) & 1) == 0,
            jnp.concatenate([mod_cols, other], axis=0),
            jnp.concatenate([other, mod_cols], axis=0),
        )
    ada_bias_grad = jnp.sum(mod_cols, axis=0)
    mod_low = mod_cols.astype(BF)
    cond_rows, labels_all = known[:, :width], known[:, width]
    act_rows = lax.dynamic_slice_in_dim(
        jax.nn.silu(cond_rows), d_rank * (width // n_dp), width // n_dp, 1
    ).astype(BF)
    ada_grad = dot_rows(act_rows, mod_low)
    cond_part = dot_trans(mod_low, ada_weight)
    for bit in (1, 0):
        my_bit = (t_rank >> bit) & 1
        two = cond_part.reshape(n_dp, 2, -1)
        stay = lax.dynamic_index_in_dim(two, my_bit, 1, keepdims=False)
        send = lax.dynamic_index_in_dim(two, 1 - my_bit, 1, keepdims=False)
        cond_part = stay + swap(send, "tensor", bit)
    cond_cols = lax.dynamic_slice_in_dim(cond_rows, t_rank * columns, columns, 1)
    gate = jax.nn.sigmoid(cond_cols)
    cond_grad = cond_part * gate * (1.0 + cond_cols * (1.0 - gate))
    classes = jnp.arange(class_table.shape[0], dtype=F32)
    onehot = (labels_all[:, None] == classes[None, :]).astype(F32)
    table_grad = lax.dot_general(
        onehot,
        cond_grad,
        (((0,), (0,)), ((), ())),
        precision=lax.Precision.HIGHEST,
        preferred_element_type=F32,
    )
    ends = [width, 2 * width, 2 * width + fc1_grad.shape[1]]
    fc2_grad, proj_grad, fc1_grad, qv_grad = jnp.split(totals[0], ends)
    return (
        result,
        tokens_grad,
        qkv_grad,
        out_grad,
        up_grad,
        down_grad,
        ada_grad,
        table_grad,
        qv_grad,
        proj_grad,
        fc1_grad,
        fc2_grad,
        ada_bias_grad,
    )


def solution(mesh):
    placed = (
        P("dp", None, None, None),
        P("dp"),
        P("dp"),
        P("dp"),
        P(None, "tensor"),
        P(None, "tensor"),
        P("tensor"),
        P(None, "tensor"),
        P("tensor"),
        P(None, "tensor"),
        P(),
        P(None, "tensor"),
        P("tensor"),
        P(None, "tensor"),
        P(),
        P("dp", None, None, None),
    )
    return jax.shard_map(
        shards,
        mesh=mesh,
        in_specs=placed,
        out_specs=(
            P("dp", None, None, None),
            P("dp", None, None, None),
            P("dp", "tensor"),
            P("dp", "tensor"),
            P("dp", "tensor"),
            P("dp", "tensor"),
            P("dp", "tensor"),
            P(None, "tensor"),
            P("tensor"),
            P(),
            P("tensor"),
            P(),
            P("tensor"),
        ),
        check_vma=False,
    )
```

time: 857 us -> 309 us (0.36)
  waiting for transfers between devices: 680 us -> 144 us
  blocking collectives: 56.8 us -> 0 us
  starting transfers between devices: 0.82 us -> 35.4 us
  matrix products: 47.2 us -> 63 us
  between operations: 18.3 us -> 4.21 us
  other arithmetic: 25.7 us -> 35.8 us
    reduce_scatter x5 -> x0, waiting for transfers between devices: 528 us -> none  [the longest x1 152 us: shards(): lax.psum_scatter(ada_grad, 'dp', scatter_dimension=0, tiled=True)]
    ppermute x0 -> x45, waiting for transfers between devices: none -> 144 us  [swap(): return lax.ppermute(value, axis, [(i, i ^ 1 << bit) for i in range(size)])]
    psum x4 -> x0, waiting for transfers between devices: 129 us -> none  [the longest x1 55.4 us: shards(): branch_two = lax.psum(mlp_part, 'tensor') + fc2_bias.astype(jnp.float32)]
    psum x1 -> x0, blocking collectives: 38.2 us -> none  [shards(): lax.psum((table_grad, qv_grad, proj_grad, fc1_grad, fc2_grad, ada_bias_gr...]
    ppermute x0 -> x45, starting transfers between devices: none -> 35.4 us  [swap(): return lax.ppermute(value, axis, [(i, i ^ 1 << bit) for i in range(size)])]
    unnamed x11 -> x0, waiting for transfers between devices: 22.4 us -> none
    dot_general x20 -> x36, matrix products: 42.5 us -> 63 us  [the longest x9 18.6 us: dot(): return jnp.dot(left, right, preferred_element_type=F32)]
    unnamed x2 -> x0, blocking collectives: 18.6 us -> none
  transfers between devices with their start and end apart: 10 -> 45, of which waited for: 10 -> 20; matrix products, arithmetic and copies ran while one was open for 3% -> 38% of each run, Pallas kernels for 0% -> 0%
where the time goes in v1:
time: 309 us; the launch traced here: 308 us
  waiting for transfers between devices  144 us (47%)
  matrix products  63 us (20%)
  other arithmetic  35.8 us (12%)
  starting transfers between devices  35.4 us (11%)
  local copies, waits for them, and re-layouts  25.1 us (8%)
  between operations  4.21 us (1%)
    ppermute x45, waiting for transfers between devices, swap(): return lax.ppermute(value, axis, [(i, i ^ 1 << bit) for i in range(size)])  144 us
    ppermute x45, starting transfers between devices, swap(): return lax.ppermute(value, axis, [(i, i ^ 1 << bit) for i in range(size)])  35.4 us
    dot_general x9, matrix products, dot(): return jnp.dot(left, right, preferred_element_type=F32)  18.6 us
    dot_general x9, matrix products, dot_trans(): lax.dot_general(left, right, (((1,), (1,)), ((), ())), preferred_element_...  16.9 us
    dot_general x5, matrix products, dot_rows(): lax.dot_general(left, right, (((0,), (0,)), ((), ())), preferred_element_...  11.6 us
    add x8, other arithmetic, scatter(): grad = stay + swap(send, 'dp', bit).astype(F32)  6.44 us
    convert_element_type x12, local copies, waits for them, and re-layouts, scatter(): lax.dynamic_index_in_dim(grad, 1 - my_bit, 1, keepdims=False).astype(BF)  6.38 us
  transfers between devices with their start and end apart: 45, of which 20 were waited for; matrix products, arithmetic and copies ran while one was open for 38% of the time, Pallas kernels for 0%

profile of v1, /device:TPU:0, one launch (start us, length us, event | category | flops | bytes accessed | tf_op | source)
XLA Modules:
  0.0 307.7 jit_solution(14390877236669197939)
XLA Ops:
  10.4 1.3 convert_element_type.357
  11.7 1.3 convert_element_type.365
  13.4 3.0 collective-permute-start.1
  18.2 3.4 %convolution_reduce_fusion = f32[1728]{0:T(1024)S(1)} fusion(bf16[1152,1]{0,1:T(2,128)(2,1)S(1)} %reshape.582, bf16[1152,1728]{0,1:T(8,128)(2,1)} %param.21), kind=kOutput, calls=%fused_computation.57 | convolution fusion | flops 3981312 | bytes 3990528 | tf_op jit(solution)/shard_map/dot_general | solution.py:14
  21.8 2.1 collective-permute-start.36
  26.7 2.1 collective-permute-start.37
  28.8 1.6 collective-permute-done.37
  30.4 1.9 collective-permute-start.3
  34.2 3.0 collective-permute-start.38
  40.5 1.6 fusion.156
  44.0 1.3 convolution_convert_fusion.5
  46.5 2.3 fusion.158
  52.0 1.9 convolution_convert_fusion.4
  54.5 1.6 fusion.2
  56.2 1.6 collective-permute-start.7
  59.8 5.4 %collective-permute-done.7 = bf16[128,1152]{1,0:T(8,128)(2,1)S(1)} collective-permute-done((bf16[128,1152]{1,0:T(8,128)(2,1)S(1)}, bf16[128,1152]{1,0:T(8,128)(2,1)S(1)}, u32[]{:S(2)}, u32[]{:S(2)}) %collective-permute-start.7) | collective-permute-done | bytes 294944 | tf_op jit(solution)/shard_map/ppermute | solution.py:27
  66.8 1.8 multiply_convert_fusion.2
  71.7 3.2 %multiply_convert_fusion.1 = (bf16[128,1152]{1,0:T(8,128)(2,1)}, f32[128,1152]{1,0:T(8,128)S(1)}) fusion(f32[1152]{0:T(1024)S(1)} %copy-done.72, bf16[128,1152]{1,0:T(8,128)(2,1)} %add_convert_fusion, bf16[1152,1152]{1,0:T(8,128)(2,1)} %collective-permute-done.8), kind=kOutput, calls=%fused_computation.129 | convolution fusion | flops 341213184 | bytes 3838464 | tf_op jit(solution)/shard_map/dot_general | solution.py:14
  74.9 2.5 fusion.5
  77.4 2.8 fusion.6
  80.2 1.6 collective-permute-start.13
  81.7 3.5 %fusion.3 = bf16[128,1152]{1,0:T(8,128)(2,1)} fusion(f32[128,1152]{1,0:T(8,128)S(1)} %fusion.159, bf16[128,1152]{1,0:T(8,128)(2,1)} %get-tuple-element.60, bf16[1152,1152]{1,0:T(8,128)(2,1)} %collective-permute-done.10), kind=kOutput, calls=%fused_computation.15 | convolution fusion | flops 340033536 | bytes 3833856 | tf_op jit(solution)/shard_map/dot_general | solution.py:18
  85.3 4.1 %collective-permute-done.13 = bf16[128,1152]{1,0:T(8,128)(2,1)S(1)} collective-permute-done((bf16[128,1152]{1,0:T(8,128)(2,1)S(1)}, bf16[128,1152]{1,0:T(8,128)(2,1)S(1)}, u32[]{:S(2)}, u32[]{:S(2)}) %collective-permute-start.13) | collective-permute-done | bytes 294944 | tf_op jit(solution)/shard_map/ppermute | solution.py:27
  89.8 1.8 convert_reduce_fusion.3
  91.6 1.5 convolution_convert_fusion
  95.7 2.0 fusion.21
  97.7 1.5 convolution_convert_fusion.1
  99.2 1.4 multiply_reduce_fusion.5
  100.7 1.7 fusion.25
  103.3 2.0 fusion.20
  108.5 1.5 collective-permute-start.11
  110.0 2.0 fusion.63
  114.2 2.6 fusion.7
  117.5 2.0 fusion.59
  123.9 1.5 collective-permute-start.33
  125.4 3.9 %fusion.51 = f32[1152,864]{1,0:T(8,128)} fusion(bf16[128,1152]{1,0:T(8,128)(2,1)} %collective-permute-done.16, bf16[128,1152]{1,0:T(8,128)(2,1)} %fusion.39, bf16[128,864]{0,1:T(8,128)(2,1)S(1)} %collective-permute-done.17, bf16[128,864]{0,1:T(8,128)(2,1)S(1)} %bitcast.254), kind=kOutput, calls=%fused_computation.100 | convolution fusion | flops 511672320 | bytes 5013504 | tf_op jit(solution)/shard_map/dot_general | solution.py:22
  129.7 2.7 collective-permute-done.14
  132.4 1.5 collective-permute-start.28
  134.4 2.4 fusion.49
  139.1 2.7 fusion.26
  141.8 42.1 %collective-permute-done.40 = f32[1,5760]{1,0:T(1,128)S(1)} collective-permute-done((f32[1,5760]{1,0:T(1,128)S(1)}, f32[1,5760]{1,0:T(1,128)S(1)}, u32[]{:S(2)}, u32[]{:S(2)}) %collective-permute-start.40) | collective-permute-done | bytes 23072 | tf_op jit(solution)/shard_map/ppermute | solution.py:27
  183.9 1.5 collective-permute-start.18
  185.8 1.6 collective-permute-start.41
  187.4 1.5 fusion.55
  191.8 3.4 %collective-permute-done.42 = f32[1,10944]{1,0:T(1,128)S(1)} collective-permute-done((f32[1,10944]{1,0:T(1,128)S(1)}, f32[1,10944]{1,0:T(1,128)S(1)}, u32[]{:S(2)}, u32[]{:S(2)}) %collective-permute-start.42) | collective-permute-done | bytes 43808 | tf_op jit(solution)/shard_map/ppermute | solution.py:27
  196.1 2.8 fusion.143
  199.1 1.5 collective-permute-start.43
  200.6 2.1 fusion.131
  205.4 1.4 reshape.572
  207.8 1.3 slice_reduce_fusion.10
  210.2 1.8 fusion.117
  212.0 5.5 %collective-permute-done.23 = bf16[4,144,288]{2,1,0:T(8,128)(2,1)} collective-permute-done((bf16[4,144,288]{2,1,0:T(8,128)(2,1)}, bf16[4,144,288]{2,1,0:T(8,128)(2,1)}, u32[]{:S(2)}, u32[]{:S(2)}) %collective-permute-start.23) | collective-permute-done | bytes 331808 | tf_op jit(solution)/shard_map/ppermute | solution.py:27
  218.6 1.7 collective-permute-start.24
  221.2 5.3 %collective-permute-done.24 = bf16[2,144,288]{2,1,0:T(8,128)(2,1)S(1)} collective-permute-done((bf16[2,144,288]{2,1,0:T(8,128)(2,1)S(1)}, bf16[2,144,288]{2,1,0:T(8,128)(2,1)S(1)}, u32[]{:S(2)}, u32[]{:S(2)}) %collective-permute-start.24) | collective-permute-done | bytes 165920 | tf_op jit(solution)/shard_map/ppermute | solution.py:27
  227.9 6.7 %collective-permute-done.25 = bf16[1,144,288]{2,1,0:T(8,128)(2,1)S(1)} collective-permute-done((bf16[1,144,288]{2,1,0:T(8,128)(2,1)S(1)}, bf16[1,144,288]{2,1,0:T(8,128)(2,1)S(1)}, u32[]{:S(2)}, u32[]{:S(2)}) %collective-permute-start.25) | collective-permute-done | bytes 82976 | tf_op jit(solution)/shard_map/ppermute | solution.py:27
  235.4 1.5 bitcast_add_fusion.2
  237.1 1.7 bitcast_add_fusion
  238.9 2.0 collective-permute-start.34
  240.9 1.6 bitcast_add_fusion.1
  242.5 12.0 %collective-permute-done.19 = bf16[2,144,864]{2,1,0:T(8,128)(2,1)S(1)} collective-permute-done((bf16[2,144,864]{2,1,0:T(8,128)(2,1)S(1)}, bf16[2,144,864]{2,1,0:T(8,128)(2,1)S(1)}, u32[]{:S(2)}, u32[]{:S(2)}) %collective-permute-start.19) | collective-permute-done | bytes 497696 | tf_op jit(solution)/shard_map/ppermute | solution.py:27
  254.9 14.1 %collective-permute-done.20 = bf16[1,144,864]{2,1,0:T(8,128)(2,1)S(1)} collective-permute-done((bf16[1,144,864]{2,1,0:T(8,128)(2,1)S(1)}, bf16[1,144,864]{2,1,0:T(8,128)(2,1)S(1)}, u32[]{:S(2)}, u32[]{:S(2)}) %collective-permute-start.20) | collective-permute-done | bytes 248864 | tf_op jit(solution)/shard_map/ppermute | solution.py:27
  269.9 5.2 %collective-permute-done.34 = bf16[2,144,1152]{2,1,0:T(8,128)(2,1)S(1)} collective-permute-done((bf16[2,144,1152]{2,1,0:T(8,128)(2,1)S(1)}, bf16[2,144,1152]{2,1,0:T(8,128)(2,1)S(1)}, u32[]{:S(2)}, u32[]{:S(2)}) %collective-permute-start.34) | collective-permute-done | bytes 663584 | tf_op jit(solution)/shard_map/ppermute | solution.py:27
  275.3 15.4 %collective-permute-done.29 = bf16[2,144,1152]{2,1,0:T(8,128)(2,1)S(1)} collective-permute-done((bf16[2,144,1152]{2,1,0:T(8,128)(2,1)S(1)}, bf16[2,144,1152]{2,1,0:T(8,128)(2,1)S(1)}, u32[]{:S(2)}, u32[]{:S(2)}) %collective-permute-start.29) | collective-permute-done | bytes 663584 | tf_op jit(solution)/shard_map/ppermute | solution.py:27
  292.3 14.5 %collective-permute-done.30 = bf16[1,144,1152]{2,1,0:T(8,128)(2,1)S(1)} collective-permute-done((bf16[1,144,1152]{2,1,0:T(8,128)(2,1)S(1)}, bf16[1,144,1152]{2,1,0:T(8,128)(2,1)S(1)}, u32[]{:S(2)}, u32[]{:S(2)}) %collective-permute-start.30) | collective-permute-done | bytes 331808 | tf_op jit(solution)/shard_map/ppermute | solution.py:27
  (383 shorter events, 65.4 us)
Async XLA Ops:
  1.7 11.4 %collective-permute-start = (bf16[1,288]{1,0:T(2,128)(2,1)S(1)}, bf16[1,288]{1,0:T(2,128)(2,1)S(1)}, u32[]{:S(2)}, u32[]{:S(2)}) collective-permute-start(bf16[1,288]{1,0:T(2,128)(2,1)S(1)} %copy.155), channel_id=1, source_target_pairs={{0,1},{1,0},{2,3},{3,2},{4,5},{5,4},{6,7},{7,6},{8,9},{9,8},{10,11... | collective-permute-start | bytes 1736 | tf_op jit(solution)/shard_map/ppermute | solution.py:27
  2.2 44.3 %collective-permute-start.4 = (bf16[1152,864]{0,1:T(8,128)(2,1)}, bf16[1152,864]{0,1:T(8,128)(2,1)}, u32[]{:S(2)}, u32[]{:S(2)}) collective-permute-start(bf16[1152,864]{0,1:T(8,128)(2,1)} %param.23), channel_id=1, source_target_pairs={{0,1},{1,0},{2,3},{3,2},{4,5},{5,4},{6,7},{7,6},{8,9},{9,8},{10,11... | collective-permute-start | bytes 5971976 | tf_op jit(solution)/shard_map/ppermute | solution.py:27
  3.0 10.4 %collective-permute-start.5 = (bf16[1,576]{1,0:T(2,128)(2,1)S(1)}, bf16[1,576]{1,0:T(2,128)(2,1)S(1)}, u32[]{:S(2)}, u32[]{:S(2)}) collective-permute-start(bf16[1,576]{1,0:T(2,128)(2,1)S(1)} %reshape.545), channel_id=1, source_target_pairs={{0,1},{1,0},{2,3},{3,2},{4,5},{5,4},{6,7},{7,6},{8,9},{9,8},{10,11... | collective-permute-start | bytes 3464 | tf_op jit(solution)/shard_map/ppermute | solution.py:27
  3.4 50.5 %collective-permute-start.6 = (bf16[1152,288]{0,1:T(8,128)(2,1)}, bf16[1152,288]{0,1:T(8,128)(2,1)}, u32[]{:S(2)}, u32[]{:S(2)}) collective-permute-start(bf16[1152,288]{0,1:T(8,128)(2,1)} %param.25), channel_id=1, source_target_pairs={{0,1},{1,0},{2,3},{3,2},{4,5},{5,4},{6,7},{7,6},{8,9},{9,8},{10,11... | collective-permute-start | bytes 1990664 | tf_op jit(solution)/shard_map/ppermute | solution.py:27
  3.5 67.8 %collective-permute-start.8 = (bf16[1152,1152]{1,0:T(8,128)(2,1)}, bf16[1152,1152]{1,0:T(8,128)(2,1)}, u32[]{:S(2)}, u32[]{:S(2)}) collective-permute-start(bf16[1152,1152]{1,0:T(8,128)(2,1)} %param.27), channel_id=1, source_target_pairs={{0,1},{1,0},{2,3},{3,2},{4,5},{5,4},{6,7},{7,6},{8,9},{9,8},{10,11... | collective-permute-start | bytes 7962632 | tf_op jit(solution)/shard_map/ppermute | solution.py:27
  8.5 31.0 %copy-start.73 = (f32[128]{0:T(128)}, f32[128]{0:T(128)S(1)}, u32[]{:S(2)}) copy-start(f32[128]{0:T(128)S(1)} %broadcast_multiply_fusion.5) | copy-start | bytes 1540
  9.7 29.8 %copy-start.78 = (f32[128]{0:T(128)}, f32[128]{0:T(128)S(1)}, u32[]{:S(2)}) copy-start(f32[128]{0:T(128)S(1)} %add_rsqrt_fusion.1) | copy-start | bytes 1540
  10.4 31.8 %copy-start.59 = (f32[4,1,72]{2,1,0:T(1,128)}, f32[4,1,72]{2,1,0:T(1,128)S(1)}, u32[]{:S(2)}) copy-start(f32[4,1,72]{2,1,0:T(1,128)S(1)} %get-tuple-element.52) | copy-start | bytes 3460
  10.4 33.6 %copy-start.82 = (f32[4,1,72]{2,1,0:T(1,128)}, f32[4,1,72]{2,1,0:T(1,128)S(1)}, u32[]{:S(2)}) copy-start(f32[4,1,72]{2,1,0:T(1,128)S(1)} %get-tuple-element.53) | copy-start | bytes 3460
  11.7 26.3 %copy-start.75 = (pred[128]{0:T(512)(128)(4,1)}, pred[128]{0:T(512)(128)(4,1)S(1)}, u32[]{:S(2)}) copy-start(pred[128]{0:T(512)(128)(4,1)S(1)} %select_compare_fusion.2) | copy-start | bytes 388
  13.2 8.6 %collective-permute-start.9 = (bf16[1,1152]{1,0:T(2,128)(2,1)S(1)}, bf16[1,1152]{1,0:T(2,128)(2,1)S(1)}, u32[]{:S(2)}, u32[]{:S(2)}) collective-permute-start(bf16[1,1152]{1,0:T(2,128)(2,1)S(1)} %reshape.549), channel_id=1, source_target_pairs={{0,1},{1,0},{2,3},{3,2},{4,5},{5,4},{6,7},{7,6},{8,9},{9,8},{10,11... | collective-permute-start | bytes 6920 | tf_op jit(solution)/shard_map/ppermute | solution.py:27
  13.4 4.5 %collective-permute-start.1 = (bf16[2,288]{1,0:T(2,128)(2,1)S(1)}, bf16[2,288]{1,0:T(2,128)(2,1)S(1)}, u32[]{:S(2)}, u32[]{:S(2)}) collective-permute-start(bf16[2,288]{1,0:T(2,128)(2,1)S(1)} %broadcast_select_fusion), channel_id=1, source_target_pairs={{0,2},{1,3},{2,0},{3,1},{4,6},{5,7},{6,4},{7,5},{8,10},{9,11},{10,... | collective-permute-start | bytes 3464 | tf_op jit(solution)/shard_map/ppermute | solution.py:27
  17.9 57.0 %collective-permute-start.10 = (bf16[1152,1152]{1,0:T(8,128)(2,1)}, bf16[1152,1152]{1,0:T(8,128)(2,1)}, u32[]{:S(2)}, u32[]{:S(2)}) collective-permute-start(bf16[1152,1152]{1,0:T(8,128)(2,1)} %param.29), channel_id=1, source_target_pairs={{0,1},{1,0},{2,3},{3,2},{4,5},{5,4},{6,7},{7,6},{8,9},{9,8},{10,11... | collective-permute-start | bytes 7962632 | tf_op jit(solution)/shard_map/ppermute | solution.py:27
  18.2 19.8 %copy-start.18 = (bf16[1,16,16,1152]{3,2,1,0:T(8,128)(2,1)S(1)}, bf16[1,16,16,1152]{3,2,1,0:T(8,128)(2,1)}, u32[]{:S(2)}) copy-start(bf16[1,16,16,1152]{3,2,1,0:T(8,128)(2,1)} %param.31) | copy-start | bytes 1769476
  18.2 21.3 %copy-start.6 = (bf16[1,16,16,1152]{3,2,1,0:T(8,128)(2,1)S(1)}, bf16[1,16,16,1152]{3,2,1,0:T(8,128)(2,1)}, u32[]{:S(2)}) copy-start(bf16[1,16,16,1152]{3,2,1,0:T(8,128)(2,1)} %param.16) | copy-start | bytes 1769476
  18.2 22.2 %copy-start.5 = (bf16[1152,864]{0,1:T(8,128)(2,1)S(1)}, bf16[1152,864]{0,1:T(8,128)(2,1)}, u32[]{:S(2)}) copy-start(bf16[1152,864]{0,1:T(8,128)(2,1)} %param.23) | copy-start | bytes 5971972
  21.8 3.7 %collective-permute-start.36 = (f32[1,1153]{1,0:T(1,128)S(1)}, f32[1,1153]{1,0:T(1,128)S(1)}, u32[]{:S(2)}, u32[]{:S(2)}) collective-permute-start(f32[1,1153]{1,0:T(1,128)S(1)} %pad_maximum_fusion.8), channel_id=1, source_target_pairs={{0,4},{4,0},{8,12},{12,8},{16,20},{20,16},{24,28},{28,24},{1,5},{5... | collective-permute-start | bytes 13844 | tf_op jit(solution)/shard_map/ppermute | solution.py:27
  25.5 1.2 collective-permute-start.2
  26.7 3.7 %collective-permute-start.37 = (f32[2,1153]{1,0:T(2,128)S(1)}, f32[2,1153]{1,0:T(2,128)S(1)}, u32[]{:S(2)}, u32[]{:S(2)}) collective-permute-start(f32[2,1153]{1,0:T(2,128)S(1)} %maximum_select_fusion.9), channel_id=1, source_target_pairs={{0,8},{4,12},{8,0},{12,4},{16,24},{20,28},{24,16},{28,20},{1,9},{5... | collective-permute-start | bytes 27680 | tf_op jit(solution)/shard_map/ppermute | solution.py:27
  30.4 3.7 %collective-permute-start.3 = (f32[2,1728]{1,0:T(2,128)S(1)}, f32[2,1728]{1,0:T(2,128)S(1)}, u32[]{:S(2)}, u32[]{:S(2)}) collective-permute-start(f32[2,1728]{1,0:T(2,128)S(1)} %maximum_select_fusion.7), channel_id=1, source_target_pairs={{0,2},{1,3},{2,0},{3,1},{4,6},{5,7},{6,4},{7,5},{8,10},{9,11},{10,... | collective-permute-start | bytes 41480 | tf_op jit(solution)/shard_map/ppermute | solution.py:27
  34.2 22.0 %collective-permute-start.38 = (f32[4,1153]{1,0:T(4,128)}, f32[4,1153]{1,0:T(4,128)}, u32[]{:S(2)}, u32[]{:S(2)}) collective-permute-start(f32[4,1153]{1,0:T(4,128)} %maximum_select_fusion.6), channel_id=1, source_target_pairs={{0,16},{4,20},{8,24},{12,28},{16,0},{20,4},{24,8},{28,12},{1,17},{... | collective-permute-start | bytes 55352 | tf_op jit(solution)/shard_map/ppermute | solution.py:27
  46.5 76.8 %collective-permute-start.16 = (bf16[128,1152]{1,0:T(8,128)(2,1)}, bf16[128,1152]{1,0:T(8,128)(2,1)}, u32[]{:S(2)}, u32[]{:S(2)}) collective-permute-start(bf16[128,1152]{1,0:T(8,128)(2,1)} %fusion.39), channel_id=1, source_target_pairs={{0,1},{1,0},{2,3},{3,2},{4,5},{5,4},{6,7},{7,6},{8,9},{9,8},{10,11... | collective-permute-start | bytes 884744 | tf_op jit(solution)/shard_map/ppermute | solution.py:27
  49.7 15.5 %copy-start.49 = (f32[1152]{0:T(1024)S(1)}, f32[1152]{0:T(1024)}, u32[]{:S(2)}) copy-start(f32[1152]{0:T(1024)} %get-tuple-element.26) | copy-start | bytes 13828
  49.7 15.5 %copy-start.50 = (f32[1152]{0:T(1024)S(1)}, f32[1152]{0:T(1024)}, u32[]{:S(2)}) copy-start(f32[1152]{0:T(1024)} %convert_element_type.357) | copy-start | bytes 13828
  53.9 54.0 %collective-permute-start.31 = (bf16[128,1152]{1,0:T(8,128)(2,1)}, bf16[128,1152]{1,0:T(8,128)(2,1)}, u32[]{:S(2)}, u32[]{:S(2)}) collective-permute-start(bf16[128,1152]{1,0:T(8,128)(2,1)} %get-tuple-element.34), channel_id=1, source_target_pairs={{0,1},{1,0},{2,3},{3,2},{4,5},{5,4},{6,7},{7,6},{8,9},{9,8},{10,11... | collective-permute-start | bytes 884744 | tf_op jit(solution)/shard_map/ppermute | solution.py:27
  54.5 12.3 %copy-start.10 = (bf16[1152,1152]{1,0:T(8,128)(2,1)S(1)}, bf16[1152,1152]{1,0:T(8,128)(2,1)}, u32[]{:S(2)}) copy-start(bf16[1152,1152]{1,0:T(8,128)(2,1)} %param.27) | copy-start | bytes 7962628
  54.5 12.3 %copy-start.71 = (f32[1152]{0:T(1024)S(1)}, f32[1152]{0:T(1024)}, u32[]{:S(2)}) copy-start(f32[1152]{0:T(1024)} %convert_element_type.359) | copy-start | bytes 13828
  56.2 9.0 %collective-permute-start.7 = (bf16[128,1152]{1,0:T(8,128)(2,1)S(1)}, bf16[128,1152]{1,0:T(8,128)(2,1)S(1)}, u32[]{:S(2)}, u32[]{:S(2)}) collective-permute-start(bf16[128,1152]{1,0:T(8,128)(2,1)S(1)} %fusion.2), channel_id=1, source_target_pairs={{0,2},{1,3},{2,0},{3,1},{4,6},{5,7},{6,4},{7,5},{8,10},{9,11},{10,... | collective-permute-start | bytes 884744 | tf_op jit(solution)/shard_map/ppermute | solution.py:27
  65.2 120.6 %collective-permute-start.22 = (bf16[128,288]{0,1:T(8,128)(2,1)}, bf16[128,288]{0,1:T(8,128)(2,1)}, u32[]{:S(2)}, u32[]{:S(2)}) collective-permute-start(bf16[128,288]{0,1:T(8,128)(2,1)} %bitcast.276), channel_id=1, source_target_pairs={{0,1},{1,0},{2,3},{3,2},{4,5},{5,4},{6,7},{7,6},{8,9},{9,8},{10,11... | collective-permute-start | bytes 221192 | tf_op jit(solution)/shard_map/ppermute | solution.py:27
  71.3 45.6 %collective-permute-start.26 = (bf16[128,1152]{1,0:T(8,128)(2,1)}, bf16[128,1152]{1,0:T(8,128)(2,1)}, u32[]{:S(2)}, u32[]{:S(2)}) collective-permute-start(bf16[128,1152]{1,0:T(8,128)(2,1)} %add_convert_fusion), channel_id=1, source_target_pairs={{0,1},{1,0},{2,3},{3,2},{4,5},{5,4},{6,7},{7,6},{8,9},{9,8},{10,11... | collective-permute-start | bytes 884744 | tf_op jit(solution)/shard_map/ppermute | solution.py:27
  80.2 9.2 %collective-permute-start.13 = (bf16[128,1152]{1,0:T(8,128)(2,1)S(1)}, bf16[128,1152]{1,0:T(8,128)(2,1)S(1)}, u32[]{:S(2)}, u32[]{:S(2)}) collective-permute-start(bf16[128,1152]{1,0:T(8,128)(2,1)S(1)} %fusion.6), channel_id=1, source_target_pairs={{0,2},{1,3},{2,0},{3,1},{4,6},{5,7},{6,4},{7,5},{8,10},{9,11},{10,... | collective-permute-start | bytes 884744 | tf_op jit(solution)/shard_map/ppermute | solution.py:27
  89.4 19.1 %collective-permute-start.32 = (bf16[128,1152]{1,0:T(8,128)(2,1)}, bf16[128,1152]{1,0:T(8,128)(2,1)}, u32[]{:S(2)}, u32[]{:S(2)}) collective-permute-start(bf16[128,1152]{1,0:T(8,128)(2,1)} %get-tuple-element.60), channel_id=1, source_target_pairs={{0,1},{1,0},{2,3},{3,2},{4,5},{5,4},{6,7},{7,6},{8,9},{9,8},{10,11... | collective-permute-start | bytes 884744 | tf_op jit(solution)/shard_map/ppermute | solution.py:27
  107.9 9.1 %collective-permute-start.27 = (bf16[128,1152]{1,0:T(8,128)(2,1)S(1)}, bf16[128,1152]{1,0:T(8,128)(2,1)S(1)}, u32[]{:S(2)}, u32[]{:S(2)}) collective-permute-start(bf16[128,1152]{1,0:T(8,128)(2,1)S(1)} %copy-done.40), channel_id=1, source_target_pairs={{0,1},{1,0},{2,3},{3,2},{4,5},{5,4},{6,7},{7,6},{8,9},{9,8},{10,11... | collective-permute-start | bytes 884744 | tf_op jit(solution)/shard_map/ppermute | solution.py:27
  108.5 25.9 %collective-permute-start.11 = (bf16[128,1152]{1,0:T(8,128)(2,1)}, bf16[128,1152]{1,0:T(8,128)(2,1)}, u32[]{:S(2)}, u32[]{:S(2)}) collective-permute-start(bf16[128,1152]{1,0:T(8,128)(2,1)} %fusion.3), channel_id=1, source_target_pairs={{0,2},{1,3},{2,0},{3,1},{4,6},{5,7},{6,4},{7,5},{8,10},{9,11},{10,... | collective-permute-start | bytes 884744 | tf_op jit(solution)/shard_map/ppermute | solution.py:27
  116.9 7.0 %collective-permute-start.17 = (bf16[128,864]{0,1:T(8,128)(2,1)S(1)}, bf16[128,864]{0,1:T(8,128)(2,1)S(1)}, u32[]{:S(2)}, u32[]{:S(2)}) collective-permute-start(bf16[128,864]{0,1:T(8,128)(2,1)S(1)} %bitcast.268), channel_id=1, source_target_pairs={{0,1},{1,0},{2,3},{3,2},{4,5},{5,4},{6,7},{7,6},{8,9},{9,8},{10,11... | collective-permute-start | bytes 663560 | tf_op jit(solution)/shard_map/ppermute | solution.py:27
  117.0 70.4 %collective-permute-start.21 = (bf16[128,1152]{1,0:T(8,128)(2,1)S(1)}, bf16[128,1152]{1,0:T(8,128)(2,1)}, u32[]{:S(2)}, u32[]{:S(2)}) collective-permute-start(bf16[128,1152]{1,0:T(8,128)(2,1)S(1)} %get-tuple-element.31), channel_id=1, source_target_pairs={{0,1},{1,0},{2,3},{3,2},{4,5},{5,4},{6,7},{7,6},{8,9},{9,8},{10,11... | collective-permute-start | bytes 884744 | tf_op jit(solution)/shard_map/ppermute | solution.py:27
  123.3 9.1 %collective-permute-start.14 = (bf16[128,1152]{1,0:T(8,128)(2,1)S(1)}, bf16[128,1152]{1,0:T(8,128)(2,1)S(1)}, u32[]{:S(2)}, u32[]{:S(2)}) collective-permute-start(bf16[128,1152]{1,0:T(8,128)(2,1)S(1)} %fusion.7), channel_id=1, source_target_pairs={{0,2},{1,3},{2,0},{3,1},{4,6},{5,7},{6,4},{7,5},{8,10},{9,11},{10,... | collective-permute-start | bytes 884744 | tf_op jit(solution)/shard_map/ppermute | solution.py:27
  123.9 113.2 %collective-permute-start.33 = (bf16[4,144,1152]{2,1,0:T(8,128)(2,1)}, bf16[4,144,1152]{2,1,0:T(8,128)(2,1)}, u32[]{:S(2)}, u32[]{:S(2)}) collective-permute-start(bf16[4,144,1152]{2,1,0:T(8,128)(2,1)} %fusion.9), channel_id=1, source_target_pairs={{0,4},{4,0},{8,12},{12,8},{16,20},{20,16},{24,28},{28,24},{1,5},{5... | collective-permute-start | bytes 3981320 | tf_op jit(solution)/shard_map/ppermute | solution.py:27
  132.4 108.5 %collective-permute-start.28 = (bf16[4,144,1152]{2,1,0:T(8,128)(2,1)}, bf16[4,144,1152]{2,1,0:T(8,128)(2,1)}, u32[]{:S(2)}, u32[]{:S(2)}) collective-permute-start(bf16[4,144,1152]{2,1,0:T(8,128)(2,1)} %fusion.8), channel_id=1, source_target_pairs={{0,4},{4,0},{8,12},{12,8},{16,20},{20,16},{24,28},{28,24},{1,5},{5... | collective-permute-start | bytes 3981320 | tf_op jit(solution)/shard_map/ppermute | solution.py:27
  136.8 50.6 %copy-start.38 = (bf16[4,72,128]{2,1,0:T(8,128)(2,1)S(1)}, bf16[4,72,128]{2,1,0:T(8,128)(2,1)}, u32[]{:S(2)}) copy-start(bf16[4,72,128]{2,1,0:T(8,128)(2,1)} %copy-done.37) | copy-start | bytes 221188
  137.0 1.3 collective-permute-start.39
  138.5 45.4 %collective-permute-start.40 = (f32[1,5760]{1,0:T(1,128)S(1)}, f32[1,5760]{1,0:T(1,128)S(1)}, u32[]{:S(2)}, u32[]{:S(2)}) collective-permute-start(f32[1,5760]{1,0:T(1,128)S(1)} %concatenate.162), channel_id=1, source_target_pairs={{0,4},{4,0},{8,12},{12,8},{16,20},{20,16},{24,28},{28,24},{1,5},{5... | collective-permute-start | bytes 69128 | tf_op jit(solution)/shard_map/ppermute | solution.py:27
  183.9 51.5 %collective-permute-start.18 = (bf16[4,144,864]{2,1,0:T(8,128)(2,1)}, bf16[4,144,864]{2,1,0:T(8,128)(2,1)}, u32[]{:S(2)}, u32[]{:S(2)}) collective-permute-start(bf16[4,144,864]{2,1,0:T(8,128)(2,1)} %fusion.26), channel_id=1, source_target_pairs={{0,4},{4,0},{8,12},{12,8},{16,20},{20,16},{24,28},{28,24},{1,5},{5... | collective-permute-start | bytes 2985992 | tf_op jit(solution)/shard_map/ppermute | solution.py:27
  185.8 4.0 %collective-permute-start.41 = (f32[1,7488]{1,0:T(1,128)S(1)}, f32[1,7488]{1,0:T(1,128)S(1)}, u32[]{:S(2)}, u32[]{:S(2)}) collective-permute-start(f32[1,7488]{1,0:T(1,128)S(1)} %pad_maximum_fusion.7), channel_id=1, source_target_pairs={{0,8},{4,12},{8,0},{12,4},{16,24},{20,28},{24,16},{28,20},{1,9},{5... | collective-permute-start | bytes 89864 | tf_op jit(solution)/shard_map/ppermute | solution.py:27
  190.2 5.0 %collective-permute-start.42 = (f32[1,10944]{1,0:T(1,128)S(1)}, f32[1,10944]{1,0:T(1,128)S(1)}, u32[]{:S(2)}, u32[]{:S(2)}) collective-permute-start(f32[1,10944]{1,0:T(1,128)S(1)} %pad_maximum_fusion.6), channel_id=1, source_target_pairs={{0,16},{4,20},{8,24},{12,28},{16,0},{20,4},{24,8},{28,12},{1,17},{... | collective-permute-start | bytes 131336 | tf_op jit(solution)/shard_map/ppermute | solution.py:27
  191.4 26.0 %collective-permute-start.23 = (bf16[4,144,288]{2,1,0:T(8,128)(2,1)}, bf16[4,144,288]{2,1,0:T(8,128)(2,1)}, u32[]{:S(2)}, u32[]{:S(2)}) collective-permute-start(bf16[4,144,288]{2,1,0:T(8,128)(2,1)} %fusion.77), channel_id=1, source_target_pairs={{0,4},{4,0},{8,12},{12,8},{16,20},{20,16},{24,28},{28,24},{1,5},{5... | collective-permute-start | bytes 995336 | tf_op jit(solution)/shard_map/ppermute | solution.py:27
  196.1 13.6 %copy-start.26 = (bf16[128,1152]{1,0:T(8,128)(2,1)S(1)}, bf16[128,1152]{1,0:T(8,128)(2,1)}, u32[]{:S(2)}) copy-start(bf16[128,1152]{1,0:T(8,128)(2,1)} %get-tuple-element.39) | copy-start | bytes 884740
  196.1 14.1 %copy-start.81 = (f32[8]{0:T(128)S(1)}, f32[8]{0:T(128)}, u32[]{:S(2)}) copy-start(f32[8]{0:T(128)} %slice_reduce_fusion.9) | copy-start | bytes 100
  196.1 21.4 %copy-start.25 = (bf16[128,1152]{1,0:T(8,128)(2,1)S(1)}, bf16[128,1152]{1,0:T(8,128)(2,1)}, u32[]{:S(2)}) copy-start(bf16[128,1152]{1,0:T(8,128)(2,1)} %get-tuple-element.38) | copy-start | bytes 884740
  199.1 5.7 %collective-permute-start.43 = (f32[8,576]{1,0:T(8,128)S(1)}, f32[8,576]{1,0:T(8,128)S(1)}, u32[]{:S(2)}, u32[]{:S(2)}) collective-permute-start(f32[8,576]{1,0:T(8,128)S(1)} %bitcast.282), channel_id=1, source_target_pairs={{0,2},{1,3},{2,0},{3,1},{4,6},{5,7},{6,4},{7,5},{8,10},{9,11},{10,... | collective-permute-start | bytes 55304 | tf_op jit(solution)/shard_map/ppermute | solution.py:27
  202.7 34.4 %slice-start = ((s8[5308416]{0:T(1024)(128)(4,1)}), s8[1114112]{0:T(1024)(128)(4,1)S(1)}, s32[]{:S(2)}) async-start(s8[5308416]{0:T(1024)(128)(4,1)} %bitcast.230), calls=%async_computation | async-start | bytes 2228224
  207.7 2.0 collective-permute-start.44
  209.7 8.9 %collective-permute-start.15 = (bf16[128,1152]{1,0:T(8,128)(2,1)S(1)}, bf16[128,1152]{1,0:T(8,128)(2,1)S(1)}, u32[]{:S(2)}, u32[]{:S(2)}) collective-permute-start(bf16[128,1152]{1,0:T(8,128)(2,1)S(1)} %copy-done.26), channel_id=1, source_target_pairs={{0,1},{1,0},{2,3},{3,2},{4,5},{5,4},{6,7},{7,6},{8,9},{9,8},{10,11... | collective-permute-start | bytes 884744 | tf_op jit(solution)/shard_map/ppermute | solution.py:27
  217.5 9.5 %collective-permute-start.12 = (bf16[128,1152]{1,0:T(8,128)(2,1)S(1)}, bf16[128,1152]{1,0:T(8,128)(2,1)S(1)}, u32[]{:S(2)}, u32[]{:S(2)}) collective-permute-start(bf16[128,1152]{1,0:T(8,128)(2,1)S(1)} %copy-done.25), channel_id=1, source_target_pairs={{0,1},{1,0},{2,3},{3,2},{4,5},{5,4},{6,7},{7,6},{8,9},{9,8},{10,11... | collective-permute-start | bytes 884744 | tf_op jit(solution)/shard_map/ppermute | solution.py:27
  218.6 16.8 %copy-start.4 = (f32[1152,864]{1,0:T(8,128)S(1)}, f32[1152,864]{1,0:T(8,128)}, u32[]{:S(2)}) copy-start(f32[1152,864]{1,0:T(8,128)} %fusion.51) | copy-start | bytes 11943940
  218.6 7.9 %collective-permute-start.24 = (bf16[2,144,288]{2,1,0:T(8,128)(2,1)S(1)}, bf16[2,144,288]{2,1,0:T(8,128)(2,1)S(1)}, u32[]{:S(2)}, u32[]{:S(2)}) collective-permute-start(bf16[2,144,288]{2,1,0:T(8,128)(2,1)S(1)} %fusion.78), channel_id=1, source_target_pairs={{0,8},{4,12},{8,0},{12,4},{16,24},{20,28},{24,16},{28,20},{1,9},{5... | collective-permute-start | bytes 497672 | tf_op jit(solution)/shard_map/ppermute | solution.py:27
  226.6 8.0 %collective-permute-start.25 = (bf16[1,144,288]{2,1,0:T(8,128)(2,1)S(1)}, bf16[1,144,288]{2,1,0:T(8,128)(2,1)S(1)}, u32[]{:S(2)}, u32[]{:S(2)}) collective-permute-start(bf16[1,144,288]{2,1,0:T(8,128)(2,1)S(1)} %dynamic-slice_convert_fusion.9), channel_id=1, source_target_pairs={{0,16},{4,20},{8,24},{12,28},{16,0},{20,4},{24,8},{28,12},{1,17},{... | collective-permute-start | bytes 248840 | tf_op jit(solution)/shard_map/ppermute | solution.py:27
  237.0 17.5 %collective-permute-start.19 = (bf16[2,144,864]{2,1,0:T(8,128)(2,1)S(1)}, bf16[2,144,864]{2,1,0:T(8,128)(2,1)S(1)}, u32[]{:S(2)}, u32[]{:S(2)}) collective-permute-start(bf16[2,144,864]{2,1,0:T(8,128)(2,1)S(1)} %fusion.74), channel_id=1, source_target_pairs={{0,8},{4,12},{8,0},{12,4},{16,24},{20,28},{24,16},{28,20},{1,9},{5... | collective-permute-start | bytes 1493000 | tf_op jit(solution)/shard_map/ppermute | solution.py:27
  238.9 36.1 %collective-permute-start.34 = (bf16[2,144,1152]{2,1,0:T(8,128)(2,1)S(1)}, bf16[2,144,1152]{2,1,0:T(8,128)(2,1)S(1)}, u32[]{:S(2)}, u32[]{:S(2)}) collective-permute-start(bf16[2,144,1152]{2,1,0:T(8,128)(2,1)S(1)} %fusion.37), channel_id=1, source_target_pairs={{0,8},{4,12},{8,0},{12,4},{16,24},{20,28},{24,16},{28,20},{1,9},{5... | collective-permute-start | bytes 1990664 | tf_op jit(solution)/shard_map/ppermute | solution.py:27
  254.7 14.3 %collective-permute-start.20 = (bf16[1,144,864]{2,1,0:T(8,128)(2,1)S(1)}, bf16[1,144,864]{2,1,0:T(8,128)(2,1)S(1)}, u32[]{:S(2)}, u32[]{:S(2)}) collective-permute-start(bf16[1,144,864]{2,1,0:T(8,128)(2,1)S(1)} %dynamic-slice_convert_fusion.7), channel_id=1, source_target_pairs={{0,16},{4,20},{8,24},{12,28},{16,0},{20,4},{24,8},{28,12},{1,17},{... | collective-permute-start | bytes 746504 | tf_op jit(solution)/shard_map/ppermute | solution.py:27
  254.8 35.9 %collective-permute-start.29 = (bf16[2,144,1152]{2,1,0:T(8,128)(2,1)S(1)}, bf16[2,144,1152]{2,1,0:T(8,128)(2,1)S(1)}, u32[]{:S(2)}, u32[]{:S(2)}) collective-permute-start(bf16[2,144,1152]{2,1,0:T(8,128)(2,1)S(1)} %fusion.36), channel_id=1, source_target_pairs={{0,8},{4,12},{8,0},{12,4},{16,24},{20,28},{24,16},{28,20},{1,9},{5... | collective-permute-start | bytes 1990664 | tf_op jit(solution)/shard_map/ppermute | solution.py:27
  275.3 16.1 %collective-permute-start.35 = (bf16[1,144,1152]{2,1,0:T(8,128)(2,1)S(1)}, bf16[1,144,1152]{2,1,0:T(8,128)(2,1)S(1)}, u32[]{:S(2)}, u32[]{:S(2)}) collective-permute-start(bf16[1,144,1152]{2,1,0:T(8,128)(2,1)S(1)} %dynamic-slice_convert_fusion.5), channel_id=1, source_target_pairs={{0,16},{4,20},{8,24},{12,28},{16,0},{20,4},{24,8},{28,12},{1,17},{... | collective-permute-start | bytes 995336 | tf_op jit(solution)/shard_map/ppermute | solution.py:27
  290.8 16.9 %copy-start.1 = (bf16[101,288]{0,1:T(8,128)(2,1)S(1)}, bf16[101,288]{0,1:T(8,128)(2,1)}, u32[]{:S(2)}) copy-start(bf16[101,288]{0,1:T(8,128)(2,1)} %param.20) | copy-start | bytes 174532
  291.0 15.8 %collective-permute-start.30 = (bf16[1,144,1152]{2,1,0:T(8,128)(2,1)S(1)}, bf16[1,144,1152]{2,1,0:T(8,128)(2,1)S(1)}, u32[]{:S(2)}, u32[]{:S(2)}) collective-permute-start(bf16[1,144,1152]{2,1,0:T(8,128)(2,1)S(1)} %dynamic-slice_convert_fusion.6), channel_id=1, source_target_pairs={{0,16},{4,20},{8,24},{12,28},{16,0},{20,4},{24,8},{28,12},{1,17},{... | collective-permute-start | bytes 995336 | tf_op jit(solution)/shard_map/ppermute | solution.py:27
  (69 other events, 300.6 us)

commit v2 on v0

v2 whole, which is shorter than its diff:
```python
import math

import jax
import jax.numpy as jnp
from jax import lax
from jax.experimental import pallas as pl
from jax.experimental.pallas import tpu as pltpu
from jax.sharding import PartitionSpec as P

HEAD_DIM = 72
BF = jnp.bfloat16
F32 = jnp.float32


def dot(left, right):
    return jnp.dot(left, right, preferred_element_type=F32)


def dot_trans(left, right):
    return lax.dot_general(left, right, (((1,), (1,)), ((), ())), preferred_element_type=F32)


def dot_rows(left, right):
    return lax.dot_general(left, right, (((0,), (0,)), ((), ())), preferred_element_type=F32)


def swap(value, axis, flip):
    size = lax.axis_size(axis)
    return lax.ppermute(value, axis, [(i, i ^ flip) for i in range(size)])


def call(body, name, us, outs, args, scratch=(), limit=24, after=(), anywhere=()):
    specs = [
        pl.BlockSpec(
            memory_space=pltpu.SMEM
            if a.dtype == jnp.int32
            else (pl.ANY if i in anywhere else pltpu.VMEM)
        )
        for i, a in enumerate(args)
    ]
    specs += [pl.BlockSpec(memory_space=pl.ANY)] * len(after)
    n_args, n_after = len(args), len(after)
    return pl.pallas_call(
        lambda *refs: body(*refs[:n_args], *refs[n_args + n_after :]),
        out_shape=[jax.ShapeDtypeStruct(s, d) for s, d in outs],
        in_specs=specs,
        out_specs=[pl.BlockSpec(memory_space=pltpu.VMEM)] * len(outs),
        scratch_shapes=list(scratch),
        compiler_params=pltpu.CompilerParams(vmem_limit_bytes=limit << 20),
        cost_estimate=pl.CostEstimate(
            flops=int(us * 1.1e7), bytes_accessed=1024, transcendentals=0
        ),
        name=name,
    )(*args, *after)


def behind(value, *others):
    return lax.optimization_barrier((value, *others))[0]


def pad_lanes(width):
    return -(-width // 128) * 128


def standardize(value):
    center = value - jnp.mean(value, axis=-1, keepdims=True)
    spread = jnp.mean(center * center, axis=-1, keepdims=True)
    inv = lax.rsqrt(spread + 1e-06)
    return center * inv, inv


def standardize_back(grad, scale, normed, inv):
    g = grad * (1.0 + scale)
    return (
        g
        - jnp.mean(g, axis=-1, keepdims=True)
        - normed * jnp.mean(g * normed, axis=-1, keepdims=True)
    ) * inv


def gelu_pair(value):
    k = math.sqrt(2.0 / math.pi)
    square = value * value
    t = jnp.tanh(k * (value + 0.044715 * value * square))
    act = 0.5 * value * (1.0 + t)
    slope = 0.5 * (1.0 + t) + 0.5 * value * (1.0 - t * t) * k * (1.0 + 3 * 0.044715 * square)
    return act, slope


def column_sum(value):
    return jnp.sum(value, axis=0, keepdims=True)


def my_rows(ref):
    half = ref.shape[0] // 2
    start = pl.multiple_of((lax.axis_index("tensor") & 1) * half, half)
    return ref[pl.ds(start, half), :].astype(F32)


def kept_rows(length_ref, half, frames):
    frame = lax.broadcasted_iota(jnp.int32, (half, 1), 0) % frames
    return frame < length_ref[0]


def split_chunks(value, n_dp, bit):
    r = value.shape[1] // n_dp
    low, high = (
        jnp.concatenate(
            [value[:, i * r : i * r + r] for i in range(n_dp) if (i >> bit) & 1 == side], axis=1
        )
        for side in range(2)
    )
    mine_low = ((lax.axis_index("dp") >> bit) & 1) == 0
    return jnp.where(mine_low, low, high), jnp.where(mine_low, high, low)


def start_kernel(tokens, weight, normed, inv, weight_out, sem):
    copy = pltpu.make_async_copy(weight, weight_out, sem)
    copy.start()
    normed[...], inv[...] = standardize(my_rows(tokens))
    copy.wait()


def modulation_kernel(e0, e1, e2, e3, clock, weight, bias, cond_out, part, rows):
    rank = lax.axis_index("tensor")
    for flip, piece in enumerate((e0, e1, e2, e3)):
        rows[pl.ds(rank ^ flip, 1), :] = piece[...].astype(F32)
    cond = clock[...] + jnp.concatenate([rows[i : i + 1, :] for i in range(4)], axis=1)
    cond_out[...] = cond
    act = (cond / (1.0 + jnp.exp(-cond))).astype(BF)
    act = jnp.broadcast_to(act, (16, act.shape[1]))
    part[...] = dot_trans(act, weight[...])[0:1, :] + bias[...].astype(F32)


def attention_kernel(
    frames, length, normed, m0, m1, m2, m3, qkv_a, qkv_b, bias_a, bias_b, out_a, out_b,
    part, mods, normed_low, saved_a, saved_b, probs_out, att_a, att_b, rows,
):
    rank = lax.axis_index("tensor")
    width = normed.shape[1]
    for flip, piece in enumerate((m0, m1, m2, m3)):
        rows[pl.ds(rank ^ flip, 1), :] = piece[...]
    cols = rows.shape[1]
    extra = cols - width
    for side in range(2):
        a, b = rows[2 * side : 2 * side + 1, :], rows[2 * side + 1 : 2 * side + 2, :]
        mods[3 * side : 3 * side + 1, :] = a[:, :width]
        mods[3 * side + 1 : 3 * side + 2, :] = jnp.concatenate([a[:, width:], b[:, :extra]], axis=1)
        mods[3 * side + 2 : 3 * side + 3, :] = b[:, extra:]
    mods[6:8, :] = jnp.zeros((2, width), F32)
    low = (normed[...] * (1.0 + mods[1:2, :]) + mods[0:1, :]).astype(BF)
    normed_low[...] = low
    half = low.shape[0]
    row_id = lax.broadcasted_iota(jnp.int32, (half, half), 0)
    col_id = lax.broadcasted_iota(jnp.int32, (half, half), 1)
    seen = ((row_id // frames) == (col_id // frames)) & ((col_id % frames) < length[0])
    factor = HEAD_DIM ** (-0.5)
    heads = out_a.shape[0] // HEAD_DIM
    total = None
    blocks = ((qkv_a, bias_a, out_a, saved_a, att_a), (qkv_b, bias_b, out_b, saved_b, att_b))
    for block, (w, b, o, saved, att_ref) in enumerate(blocks):
        qkv = dot_trans(low, w[...]) + b[...].astype(F32)
        saved[...] = qkv.astype(BF)
        for h in range(heads):
            base = h * 3 * HEAD_DIM
            q, k, v = (
                qkv[:, base + j * HEAD_DIM : base + (j + 1) * HEAD_DIM].astype(BF)
                for j in range(3)
            )
            scores = jnp.where(seen, dot_trans(q, k) * factor, -1e30)
            raised = jnp.exp(scores - jnp.max(scores, axis=-1, keepdims=True))
            probs = raised / jnp.sum(raised, axis=-1, keepdims=True)
            probs_out[block * heads + h] = probs
            att_ref[:, h * HEAD_DIM : (h + 1) * HEAD_DIM] = dot(probs.astype(BF), v).astype(BF)
        term = dot(att_ref[...], o[...])
        total = term if total is None else total + term
    part[...] = total.astype(BF)


def early_back_kernel(
    frames, n_dp, length, mods, cotangent, down_a, down_b, normed_low, att_a, att_b,
    grad_a, grad_b, pack_far, pack_core, chunks_far, chunks_core, fc2_sum,
):
    upstream = my_rows(cotangent)
    half, width = upstream.shape
    keep = kept_rows(length, half, frames)
    low32 = (mods[5:6, :] * jnp.where(keep, upstream, 0.0)).astype(BF).astype(F32)
    low = low32.astype(BF)
    grad_a[...] = dot(low, down_a[...])
    grad_b[...] = dot(low, down_b[...])
    fc2_sum[...] = column_sum(low32)
    n_att = att_a.shape[1]
    part = width // 2
    mine, other = split_chunks(normed_low[...].astype(F32), n_dp, 0)
    pack_far[:, 0:n_att] = att_a[...]
    pack_far[:, n_att : 2 * n_att] = att_b[...]
    at = pad_lanes(2 * n_att)
    pack_far[:, at : at + part] = other.astype(BF)
    pack_core[:, 0:n_att] = att_b[...]
    at = pad_lanes(n_att)
    pack_core[:, at : at + part] = mine.astype(BF)
    mine, other = split_chunks(low32, n_dp, 2)
    chunks_far[:, 0:part] = other.astype(BF)
    chunks_core[:, 0:part] = mine.astype(BF)


def mlp_kernel(
    n_dp, tokens, part1, part1_other, proj_bias, mods, up_a, up_b, fc1_a, fc1_b, grad_a, grad_b,
    chunks_far, part3, pack_act, pack_pre, chunks_core, branch_out, normed_out, inv_out,
):
    branch = part1[...].astype(F32) + part1_other[...].astype(F32) + proj_bias[...].astype(F32)
    branch_out[...] = branch
    mid = my_rows(tokens) + mods[2:3, :] * branch
    normed, inv = standardize(mid)
    normed_out[...] = normed
    inv_out[...] = inv
    low32 = normed * (1.0 + mods[4:5, :]) + mods[3:4, :]
    low = low32.astype(BF)
    total = None
    cols = up_a.shape[1]
    for block, (u, b, g) in enumerate(((up_a, fc1_a, grad_a), (up_b, fc1_b, grad_b))):
        act, slope = gelu_pair(dot(low, u[...]) + b[...].astype(F32))
        pack_act[:, block * cols : (block + 1) * cols] = act.astype(BF)
        pre = (g[...] * slope).astype(BF)
        pack_pre[:, block * cols : (block + 1) * cols] = pre
        term = dot_trans(pre, u[...])
        total = term if total is None else total + term
    part3[...] = total.astype(BF)
    mine, other = split_chunks(low32, n_dp, 0)
    part = mine.shape[1]
    pack_pre[:, 2 * cols : 2 * cols + part] = other.astype(BF)
    chunks_core[:, 0:part] = mine.astype(BF)
    pack_act[:, 2 * cols :] = chunks_far[...]


def mlp_tail_kernel(
    pack_act, pack_pre, down_a, down_b, chunks_act, chunks_pre, part2, core_act, core_pre, sums
):
    cols = down_a.shape[1]
    part2[...] = (
        dot_trans(pack_act[:, 0:cols], down_a[...]) + dot_trans(pack_act[:, cols : 2 * cols], down_b[...])
    ).astype(BF)
    core_act[:, 0:cols] = pack_act[:, cols : 2 * cols]
    core_act[:, cols:] = chunks_act[...]
    core_pre[:, 0:cols] = pack_pre[:, cols : 2 * cols]
    core_pre[:, cols:] = chunks_pre[...]
    sums[0:1, :] = column_sum(pack_pre[:, 0:cols].astype(F32))
    sums[1:2, :] = column_sum(pack_pre[:, cols : 2 * cols].astype(F32))


def attention_back_kernel(
    frames, length, part3, part3_other, mods, normed, inv, branch, cotangent,
    out_a, out_b, qkv_a, qkv_b, saved_a, saved_b, probs_in,
    part4, mid_grad_out, low_out, stacked, sums,
):
    upstream = my_rows(cotangent)
    half, width = upstream.shape
    keep = kept_rows(length, half, frames)
    grad = part3[...].astype(F32) + part3_other[...].astype(F32)
    norm = normed[...]
    mid_grad = jnp.where(keep, upstream, 0.0) + standardize_back(grad, mods[4:5, :], norm, inv[...])
    mid_grad_out[...] = mid_grad
    low = (mods[2:3, :] * mid_grad).astype(BF)
    low_out[...] = low
    sums[0:1, :] = column_sum(grad)
    sums[1:2, :] = column_sum(grad * norm)
    sums[2:3, :] = column_sum(mid_grad * branch[...])
    sums[3:4, :] = column_sum(low.astype(F32))
    factor = HEAD_DIM ** (-0.5)
    heads = out_a.shape[0] // HEAD_DIM
    cols = heads * 3 * HEAD_DIM
    wide = pad_lanes(cols)
    total = None
    for block, (w, o, saved) in enumerate(((qkv_a, out_a, saved_a), (qkv_b, out_b, saved_b))):
        att_grad = dot_trans(low, o[...])
        qkv = saved[...].astype(F32)
        for h in range(heads):
            base = h * 3 * HEAD_DIM
            q, k, v = (
                qkv[:, base + j * HEAD_DIM : base + (j + 1) * HEAD_DIM].astype(BF)
                for j in range(3)
            )
            ag = att_grad[:, h * HEAD_DIM : (h + 1) * HEAD_DIM].astype(BF)
            probs = probs_in[block * heads + h]
            value_grad = dot_rows(probs.astype(BF), ag)
            probs_grad = dot_trans(ag, v)
            inner = jnp.sum(probs * probs_grad, axis=-1, keepdims=True)
            scores_low = (probs * (probs_grad - inner)).astype(BF)
            query_grad = dot(scores_low, k) * factor
            key_grad = dot_rows(scores_low, q) * factor
            at = block * wide + base
            for j, piece in enumerate((query_grad, key_grad, value_grad)):
                stacked[:, at + j * HEAD_DIM : at + (j + 1) * HEAD_DIM] = piece.astype(BF)
        mine = stacked[:, block * wide : block * wide + cols]
        sums[4 + block : 5 + block, 0:cols] = column_sum(mine.astype(F32))
        term = dot(mine, w[...])
        total = term if total is None else total + term
    part4[...] = total.astype(BF)


def pack_back_kernel(n_dp, low, stacked, pack_far, pack_core):
    mine, other = split_chunks(low[...].astype(F32), n_dp, 0)
    part, cols = mine.shape[1], stacked.shape[1]
    pack_far[:, 0:cols] = stacked[...]
    pack_far[:, cols : cols + part] = other.astype(BF)
    pack_core[:, 0 : cols // 2] = stacked[:, cols // 2 :]
    pack_core[:, cols // 2 : cols // 2 + part] = mine.astype(BF)


def output_kernel(
    frames, length, tokens, part2, part2_other, fc2_bias, mods, branch1, cotangent, result, gate_sum
):
    inputs, upstream = my_rows(tokens), my_rows(cotangent)
    keep = kept_rows(length, inputs.shape[0], frames)
    branch = part2[...].astype(F32) + part2_other[...].astype(F32) + fc2_bias[...].astype(F32)
    mid = inputs + mods[2:3, :] * branch1[...]
    result[...] = jnp.where(keep, mid + mods[5:6, :] * branch, inputs).astype(BF)
    gate_sum[...] = column_sum(jnp.where(keep, upstream, 0.0) * branch)


def input_back_kernel(
    frames, length, part4, part4_other, mods, normed, inv, mid_grad, cotangent,
    back_sums, gate2_sum, fc2_sum, pre_sums, tokens_grad, sums,
):
    upstream = my_rows(cotangent)
    keep = kept_rows(length, upstream.shape[0], frames)
    grad = part4[...].astype(F32) + part4_other[...].astype(F32)
    norm = normed[...]
    back = standardize_back(grad, mods[1:2, :], norm, inv[...])
    tokens_grad[...] = (mid_grad[...] + back + jnp.where(keep, 0.0, upstream)).astype(BF)
    sums[0:1, :] = column_sum(grad)
    sums[1:2, :] = column_sum(grad * norm)
    sums[2:3, :] = back_sums[2:3, :]
    sums[3:5, :] = back_sums[0:2, :]
    sums[5:6, :] = gate2_sum[...]
    sums[6:7, :] = fc2_sum[...]
    sums[7:8, :] = back_sums[3:4, :]
    sums[8:10, :] = pre_sums[0:2, :]
    sums[10:12, :] = back_sums[4:6, :]
    sums[12:16, :] = jnp.zeros((4, sums.shape[1]), F32)


def vector_kernel(layout, label, mine, other, cond, vector):
    rank = lax.axis_index("tensor")
    width = mine.shape[1]
    both = mine[...] + other[...]
    upper = rank >= 2
    pick = lambda i: jnp.where(upper, both[3 + i : 4 + i, :], both[i : i + 1, :])
    cols = layout["mod"][1]
    extra = cols - width
    shift, scale, gate = pick(0), pick(1), pick(2)
    even = jnp.concatenate([shift, scale[:, :extra]], axis=1)
    odd = jnp.concatenate([scale[:, extra:], gate], axis=1)
    vector[...] = jnp.zeros(vector.shape, F32)

    def put(name, value):
        at, size = layout[name]
        vector[:, at : at + size] = value

    put("mod", jnp.where((rank & 1) == 0, even, odd).astype(BF).astype(F32))
    put("fc2", both[6:7, :])
    put("proj", both[7:8, :])
    put("fc1", (mine[8:9, :] + other[9:10, :])[:, : layout["fc1"][1]])
    put("stack", (mine[10:11, :] + other[11:12, :])[:, : layout["stack"][1]])
    put("cond", cond[...])
    put("label", jnp.full((1, 128), label[0], jnp.int32).astype(F32))


def gathered_kernel(layout, n_dp, rows_out, blocks, weight, *refs):
    sources, refs = refs[:blocks], refs[blocks:]
    ada_grad, totals, c0, c1, c23, cond_cols, labels, table = refs
    rank, place = lax.axis_index("tensor"), lax.axis_index("dp")
    slot = 0
    for source in sources:
        for i in range(source.shape[0]):
            table[pl.ds(place ^ slot, 1), :] = source[i : i + 1, :]
            slot += 1

    def get(name):
        at, size = layout[name]
        return table[:, at : at + size]

    totals[...] = column_sum(table[...])
    mod = get("mod").astype(BF)
    cond = get("cond")
    act = cond / (1.0 + jnp.exp(-cond))
    width = act.shape[1]
    mine = pltpu.roll(act, (width - place * rows_out) % width, 1)[:, :rows_out].astype(BF)
    ada_grad[...] = dot_rows(mine, mod)
    columns = c0.shape[1]
    cond_part = dot(mod, weight[...])
    wide = pad_lanes(columns)
    outs = (c0, c1, c23.at[:, 0:columns], c23.at[:, wide : wide + columns])
    for flip, out in enumerate(outs):
        out[...] = pltpu.roll(cond_part, (width - (rank ^ flip) * columns) % width, 1)[:, :columns]
    cond_cols[...] = pltpu.roll(cond, (width - rank * columns) % width, 1)[:, :columns]
    labels[...] = get("label")


def table_kernel(c0, c1, c2, c3, cond_cols, labels, out):
    cond = cond_cols[...]
    columns = cond.shape[1]
    wide = pad_lanes(columns)
    gate = 1.0 / (1.0 + jnp.exp(-cond))
    grad = c0[...] + c1[...] + c2[:, :columns] + c3[:, wide : wide + columns]
    grad = grad * gate * (1.0 + cond * (1.0 - gate))
    classes = lax.broadcasted_iota(jnp.int32, (cond.shape[0], out.shape[1]), 1).astype(F32)
    onehot = jnp.where(labels[:, : out.shape[1]] == classes, 1.0, 0.0)
    out[...] = lax.dot_general(
        grad,
        onehot,
        (((0,), (0,)), ((), ())),
        precision=lax.Precision.HIGHEST,
        preferred_element_type=F32,
    )


def forward_kernel(spans, *refs):
    for (at, size, chunks), source, out in zip(spans, refs[: len(spans)], refs[len(spans) :]):
        out[:, 0:size] = source[:, at : at + size]
        out[:, size:] = source[:, chunks : chunks + out.shape[1] - size]


def weight_kernel(n_dp, split_bit, products, *refs):
    n_sets = 1 + max(max(p[0][0], p[1][0]) for p in products)
    sets = [refs[5 * i : 5 * i + 5] for i in range(n_sets)]
    outs, lefts = refs[5 * n_sets : -len(products)], refs[-len(products) :]
    half = sets[0][0].shape[0]
    part = lefts[0].shape[0]
    r = part // (n_dp // 2)
    at = 0
    for left, product in zip(lefts, products):
        (l_set, l_far, l_core), (r_set, r_far, r_core), cols = product
        own, core, core_in, far, far_core = sets[l_set]
        rows = (
            core[:, l_core : l_core + part],
            core_in[:, l_core : l_core + part],
            far[:, l_far : l_far + part],
            far_core[:, l_core : l_core + part],
        )
        for i, value in enumerate(rows):
            left[:, i * half : (i + 1) * half] = value.astype(F32).T.astype(BF)
        own, core, core_in, far, far_core = sets[r_set]
        right = jnp.concatenate(
            [
                own[:, r_far : r_far + cols],
                core_in[:, r_core : r_core + cols],
                far[:, r_far : r_far + cols],
                far_core[:, r_core : r_core + cols],
            ],
            axis=0,
        )
        if split_bit is None:
            outs[0][:, at : at + cols] = dot(left[...], right)
        else:
            stay, send = outs
            mine = (lax.axis_index("dp") >> split_bit) & 1
            for k in range(n_dp // 4):
                for out, side in ((stay, mine), (send, 1 - mine)):
                    start = pl.multiple_of((2 * k + side) * r, r)
                    out[k, :, at : at + cols] = dot(left[pl.ds(start, r), :], right).astype(out.dtype)
        at += cols


def halve_kernel(bit, stay, other, out_stay, out_send):
    mine = (lax.axis_index("dp") >> bit) & 1
    out_stay[...] = stay[mine] + other[mine].astype(F32)
    out_send[...] = (stay[1 - mine] + other[1 - mine].astype(F32)).astype(BF)


def add_kernel(widths, stay, other, *outs):
    total = stay[...] + other[...].astype(F32)
    at = 0
    for out, cols in zip(outs, widths):
        out[...] = total[:, at : at + cols]
        at += cols


def join_kernel(mine, other, mine2, other2, out, out2):
    half = mine.shape[0]
    core = lax.axis_index("tensor") & 1
    for part, side in (((mine, mine2), core), ((other, other2), 1 - core)):
        for source, target in zip(part, (out, out2)):
            target[pl.ds(pl.multiple_of(side * half, half), half), :] = source[...]


def shards(
    tokens,
    lengths,
    timesteps,
    labels,
    class_table,
    ada_weight,
    ada_bias,
    qkv_weight,
    qv_bias,
    out_weight,
    proj_bias,
    up_weight,
    fc1_bias,
    down_weight,
    fc2_bias,
    cotangent,
):
    clips, patches, frames, width = tokens.shape
    assert clips == 1 and lax.axis_size("tensor") == 4
    rows = patches * frames
    half = rows // 2
    n_att = out_weight.shape[1]
    heads = n_att // HEAD_DIM
    n_qkv = qkv_weight.shape[1]
    hidden = up_weight.shape[1]
    columns = class_table.shape[1]
    ada_cols = ada_weight.shape[1]
    n_classes = class_table.shape[0]
    t_rank = lax.axis_index("tensor")
    d_rank = lax.axis_index("dp")
    n_dp = lax.axis_size("dp")
    chunk = width // n_dp
    part = width // 2
    wide = pad_lanes(part)

    tokens2 = tokens.reshape(rows, width)
    cot2 = cotangent.reshape(rows, width)
    proj_row = proj_bias.reshape(1, width)
    fc2_row = fc2_bias.reshape(1, width)

    def gather_tensor(own, *others):
        across = behind(swap(own, "tensor", 2), *others)
        return [own, swap(own, "tensor", 1), across, swap(across, "tensor", 1)]

    picked = lax.dynamic_slice_in_dim(class_table, labels[0], 1, 0)
    pieces = gather_tensor(picked)
    normed1, inv1, ada_rows = call(
        start_kernel,
        "start",
        1.0,
        [((half, width), F32), ((half, 1), F32), ((ada_cols, width), BF)],
        [tokens2, ada_weight.T],
        [pltpu.SemaphoreType.DMA],
        anywhere=(1,),
    )

    def pair(weight, *others):
        return weight, swap(behind(weight, *others), "tensor", 1)

    two = qv_bias.reshape(heads, 2, HEAD_DIM)
    bias_row = jnp.stack([two[:, 0], jnp.zeros_like(two[:, 0]), two[:, 1]], axis=1)
    qkv_ws = pair(qkv_weight.T, pieces[3])
    bias_ws = pair(bias_row.reshape(1, n_qkv))
    fc1_ws = pair(fc1_bias.reshape(1, hidden))
    out_ws = pair(out_weight.T, pieces[3])

    half_width = width // 2
    freqs = jnp.exp(-math.log(10000.0) * jnp.arange(half_width, dtype=F32) / half_width)
    angles = timesteps.astype(F32)[:, None] * freqs[None, :]
    clock = jnp.concatenate([jnp.cos(angles), jnp.sin(angles)], axis=1)
    cond, mod_part = call(
        modulation_kernel,
        "modulation",
        1.0,
        [((1, width), F32), ((1, ada_cols), F32)],
        [*pieces, clock, ada_rows, ada_bias.reshape(1, ada_cols)],
        [pltpu.VMEM((8, columns), F32)],
    )
    mod_pieces = gather_tensor(mod_part, qkv_ws[1], out_ws[1], bias_ws[1], fc1_ws[1])
    up_ws = pair(up_weight, *mod_pieces)
    down_ws = pair(down_weight, *mod_pieces)

    part1, mods, low1, saved_a, saved_b, probs, att_a, att_b = call(
        lambda *refs: attention_kernel(frames, *refs),
        "attention",
        4.0,
        [
            ((half, width), BF),
            ((8, width), F32),
            ((half, width), BF),
            ((half, n_qkv), BF),
            ((half, n_qkv), BF),
            ((2 * heads, half, half), F32),
            ((half, n_att), BF),
            ((half, n_att), BF),
        ],
        [lengths, normed1, *mod_pieces, *qkv_ws, *bias_ws, *out_ws],
        [pltpu.VMEM((8, ada_cols), F32)],
    )
    part1_other = swap(part1, "tensor", 2)

    att_far, att_core = pad_lanes(2 * n_att), pad_lanes(n_att)
    grad_a, grad_b, *pack1, chunks_far, chunks_act, fc2_sum = call(
        lambda *refs: early_back_kernel(frames, n_dp, *refs),
        "early_back",
        2.0,
        [
            ((half, hidden), F32),
            ((half, hidden), F32),
            ((half, att_far + wide), BF),
            ((half, att_core + wide), BF),
            ((half, wide), BF),
            ((half, wide), BF),
            ((1, width), F32),
        ],
        [lengths, mods, cot2, *down_ws, low1, att_a, att_b],
    )

    part3, pack_act, pack_pre, chunks_pre, branch1, normed2, inv2 = call(
        lambda *refs: mlp_kernel(n_dp, *refs),
        "mlp",
        3.0,
        [
            ((half, width), BF),
            ((half, 2 * hidden + wide), BF),
            ((half, 2 * hidden + wide), BF),
            ((half, wide), BF),
            ((half, width), F32),
            ((half, width), F32),
            ((half, 1), F32),
        ],
        [
            tokens2, part1, part1_other, proj_row, mods, *up_ws, *fc1_ws, grad_a, grad_b,
            chunks_far,
        ],
    )
    part3_other = swap(part3, "tensor", 2)

    part2, core_act, core_pre, pre_sums = call(
        mlp_tail_kernel,
        "mlp_tail",
        2.0,
        [
            ((half, width), BF),
            ((half, hidden + wide), BF),
            ((half, hidden + wide), BF),
            ((2, hidden), F32),
        ],
        [pack_act, pack_pre, *down_ws, chunks_act, chunks_pre],
    )
    part2_other = swap(part2, "tensor", 2)

    def cross(pack, bit):
        own, core = pack
        return [own, core, swap(core, "tensor", 1), swap(own, "dp", 1 << bit)]

    def forward(name, sets, spans, after):
        outs = call(
            lambda *refs: forward_kernel(spans, *refs),
            name,
            0.5,
            [((half, at_size + wide), BF) for _, at_size, _ in spans],
            [s[3] for s in sets],
            after=after,
        )
        for one, out in zip(sets, outs):
            one.append(swap(out, "tensor", 1))
        return outs

    set1 = cross(pack1, 0)
    set_act = cross((pack_act, core_act), 2)
    set_pre = cross((pack_pre, core_pre), 0)
    part4, mid_grad, low_back, stacked, back_sums = call(
        lambda *refs: attention_back_kernel(frames, *refs),
        "attention_back",
        5.0,
        [
            ((half, width), BF),
            ((half, width), F32),
            ((half, width), BF),
            ((half, 2 * pad_lanes(n_qkv)), BF),
            ((8, width), F32),
        ],
        [
            lengths, part3, part3_other, mods, normed2, inv2, branch1, cot2,
            *out_ws, *qkv_ws, saved_a, saved_b, probs,
        ],
    )
    part4_other = swap(part4, "tensor", 2)
    s_wide = pad_lanes(n_qkv)
    second = forward("forward1", [set1], [(n_att, pad_lanes(n_att), att_far)], [part4])
    second += forward(
        "forward2", [set_act, set_pre], [(hidden, hidden, 2 * hidden)] * 2, [part4]
    )

    result, gate2_sum = call(
        lambda *refs: output_kernel(frames, *refs),
        "output",
        1.0,
        [((half, width), BF), ((1, width), F32)],
        [lengths, tokens2, part2, part2_other, fc2_row, mods, branch1, cot2],
    )

    result_other = swap(result, "tensor", 1)

    tokens_grad, sums = call(
        lambda *refs: input_back_kernel(frames, *refs),
        "input_back",
        1.0,
        [((half, width), BF), ((16, width), F32)],
        [
            lengths, part4, part4_other, mods, normed1, inv1, mid_grad, cot2,
            back_sums, gate2_sum, fc2_sum, pre_sums,
        ],
        after=second,
    )
    sums_other = swap(sums, "tensor", 1)
    tokens_grad_other = swap(tokens_grad, "tensor", 1)

    layout, at = {}, 0
    for name, size in (
        ("mod", ada_cols), ("fc2", width), ("proj", width), ("fc1", hidden), ("stack", n_qkv),
        ("cond", width), ("label", 128),
    ):
        layout[name] = (at, size)
        at += pad_lanes(size)
    (vector,) = call(
        lambda *refs: vector_kernel(layout, *refs),
        "vector",
        0.5,
        [((1, at), F32)],
        [labels, sums, sums_other, cond],
    )
    pack3 = call(
        lambda *refs: pack_back_kernel(n_dp, *refs),
        "pack_back",
        0.5,
        [((half, 2 * s_wide + wide), BF), ((half, s_wide + wide), BF)],
        [low_back, stacked],
        after=[vector],
    )

    set3 = cross(pack3, 0)

    vector = jnp.concatenate([vector, swap(vector, "dp", 1)], axis=0)
    if n_dp == 8:
        sources = [vector] + [swap(vector, "dp", flip) for flip in (2, 4, 6)]
    else:
        flip = 2
        while flip < n_dp:
            vector = jnp.concatenate([vector, swap(vector, "dp", flip)], axis=0)
            flip *= 2
        sources = [vector]
    def first_grads(name, us, bit, products, sets, after):
        cols = sum(p[2] for p in products)
        args = [a for s in sets for a in s]
        scratch = [pltpu.VMEM((part, 4 * half), BF)] * len(products)
        if n_dp != 8:
            return call(
                lambda *refs: weight_kernel(n_dp, None, products, *refs),
                name, us, [((part, cols), F32)], args, scratch,
            ) * 2
        second = 0 if bit else 1
        assert n_dp == 8
        return call(
            lambda *refs: weight_kernel(n_dp, second, products, *refs),
            name, us, [((2, chunk, cols), F32), ((2, chunk, cols), BF)], args, scratch, after=after,
        )

    def second_grads(name, bit, stay, send, after):
        if n_dp != 8:
            return stay, send
        second = 0 if bit else 1
        return call(
            lambda *refs: halve_kernel(1 if bit == 2 else 2, *refs),
            name,
            0.5,
            [((chunk, stay.shape[2]), F32), ((chunk, stay.shape[2]), BF)],
            [stay, swap(send, "dp", 1 << second)],
            after=after,
        )

    def last_grads(name, bit, widths, stay, send, after):
        if n_dp != 8:
            grad = stay.reshape(n_dp // 2, chunk, -1)
            for b in range((n_dp - 1).bit_length()):
                if b != bit:
                    my_bit = (d_rank >> b) & 1
                    grad = grad.reshape(grad.shape[0] // 2, 2, chunk, grad.shape[2])
                    send = lax.dynamic_index_in_dim(grad, 1 - my_bit, 1, keepdims=False).astype(BF)
                    stay = lax.dynamic_index_in_dim(grad, my_bit, 1, keepdims=False)
                    grad = stay + swap(send, "dp", 1 << b).astype(F32)
            ends = [sum(widths[:i]) for i in range(1, len(widths))]
            return jnp.split(grad[0] if grad.ndim == 3 else grad, ends, axis=1)
        return call(
            lambda *refs: add_kernel(widths, *refs),
            name,
            0.5,
            [((chunk, w), F32) for w in widths],
            [stay, swap(send, "dp", 2 if bit == 2 else 4)],
            after=after,
        )

    mlp_spec = [((0, 2 * hidden, hidden), (0, 0, 0), hidden)]
    down_stay, down_send = first_grads("down_grad", 2.0, 2, mlp_spec, [set_act], sources[:1])
    up_stay, up_send = first_grads("up_grad", 2.0, 0, mlp_spec, [set_pre], sources[:1])
    ada_grad, totals, c0, c1, c23, cond_cols, labels_all = call(
        lambda *refs: gathered_kernel(layout, n_dp, chunk, len(sources), *refs),
        "gathered",
        2.0,
        [((chunk, ada_cols), F32), ((1, at), F32)]
        + [((n_dp, columns), F32)] * 2
        + [((n_dp, 2 * pad_lanes(columns)), F32), ((n_dp, columns), F32), ((n_dp, 128), F32)],
        [ada_rows, *sources],
        [pltpu.VMEM((n_dp, at), F32)],
        after=[down_stay, up_stay],
    )
    c23 = swap(c23, "tensor", 2)
    forward("forward3", [set3], [(s_wide, s_wide, 2 * s_wide)], [c1])
    qkv_stay, qkv_send = first_grads(
        "qkv_grad",
        2.0,
        0,
        [
            ((0, att_far, att_core), (1, 0, 0), n_qkv),
            ((1, 2 * s_wide, s_wide), (0, 0, 0), n_att),
        ],
        [set1, set3],
        [],
    )
    down_stay, down_send = second_grads("down_halve", 2, down_stay, down_send, [qkv_stay])
    up_stay, up_send = second_grads("up_halve", 0, up_stay, up_send, [down_stay])
    (table_grad,) = call(
        table_kernel,
        "table",
        0.5,
        [((columns, n_classes), F32)],
        [c0, swap(c1, "tensor", 1), c23, swap(c23, "tensor", 1), cond_cols, labels_all],
        after=[up_stay],
    )

    def take(name):
        start, size = layout[name]
        return totals[0, start : start + size]

    qv_grad = take("stack").reshape(heads, 3, HEAD_DIM)
    qv_grad = jnp.stack([qv_grad[:, 0], qv_grad[:, 2]], axis=1).reshape(-1)

    result, tokens_grad = call(
        join_kernel,
        "join",
        0.8,
        [((rows, width), BF)] * 2,
        [result, result_other, tokens_grad, tokens_grad_other],
        after=[up_stay],
    )
    result, tokens_grad = result.reshape(tokens.shape), tokens_grad.reshape(tokens.shape)
    qkv_stay, qkv_send = second_grads("qkv_halve", 0, qkv_stay, qkv_send, [table_grad])
    (down_grad,) = last_grads("down_add", 2, [hidden], down_stay, down_send, [qkv_stay])
    (up_grad,) = last_grads("up_add", 0, [hidden], up_stay, up_send, [down_grad])
    qkv_grad, out_grad = last_grads("qkv_add", 0, [n_qkv, n_att], qkv_stay, qkv_send, [up_grad])
    return (
        result,
        tokens_grad,
        qkv_grad,
        out_grad,
        up_grad,
        down_grad,
        ada_grad,
        table_grad.T,
        qv_grad,
        take("proj"),
        take("fc1"),
        take("fc2"),
        take("mod"),
    )


def solution(mesh):
    placed = (
        P("dp", None, None, None),
        P("dp"),
        P("dp"),
        P("dp"),
        P(None, "tensor"),
        P(None, "tensor"),
        P("tensor"),
        P(None, "tensor"),
        P("tensor"),
        P(None, "tensor"),
        P(),
        P(None, "tensor"),
        P("tensor"),
        P(None, "tensor"),
        P(),
        P("dp", None, None, None),
    )
    return jax.shard_map(
        shards,
        mesh=mesh,
        in_specs=placed,
        out_specs=(
            P("dp", None, None, None),
            P("dp", None, None, None),
            P("dp", "tensor"),
            P("dp", "tensor"),
            P("dp", "tensor"),
            P("dp", "tensor"),
            P("dp", "tensor"),
            P(None, "tensor"),
            P("tensor"),
            P(),
            P("tensor"),
            P(),
            P("tensor"),
        ),
        check_vma=False,
    )
```

time: 857 us -> 169 us (0.20)
  waiting for transfers between devices: 680 us -> 66.1 us
  blocking collectives: 56.8 us -> 0 us
  matrix products: 47.2 us -> 0 us
  Pallas kernels: 0 us -> 42.5 us
  starting transfers between devices: 0.82 us -> 38.1 us
  other arithmetic: 25.7 us -> 0.32 us
  between operations: 18.3 us -> 3.02 us
  local copies, waits for them, and re-layouts: 26.9 us -> 17.9 us
    reduce_scatter x5 -> x0, waiting for transfers between devices: 528 us -> none  [the longest x1 152 us: shards(): lax.psum_scatter(ada_grad, 'dp', scatter_dimension=0, tiled=True)]
    psum x4 -> x0, waiting for transfers between devices: 129 us -> none  [the longest x1 55.4 us: shards(): branch_two = lax.psum(mlp_part, 'tensor') + fc2_bias.astype(jnp.float32)]
    ppermute x0 -> x44, waiting for transfers between devices: none -> 66.1 us  [swap(): return lax.ppermute(value, axis, [(i, i ^ flip) for i in range(size)])]
    pallas_call x0 -> x26, Pallas kernels: none -> 42.5 us  [call(): pl.pallas_call(lambda *refs: body(*refs[:n_args], *refs[n_args + n_after:...]
    dot_general x20 -> x0, matrix products: 42.5 us -> none  [the longest x6 14.9 us: product(): return jnp.dot(left, right, preferred_element_type=jnp.float32)]
    psum x1 -> x0, blocking collectives: 38.2 us -> none  [shards(): lax.psum((table_grad, qv_grad, proj_grad, fc1_grad, fc2_grad, ada_bias_gr...]
    ppermute x0 -> x44, starting transfers between devices: none -> 38.1 us  [swap(): return lax.ppermute(value, axis, [(i, i ^ flip) for i in range(size)])]
    unnamed x11 -> x0, waiting for transfers between devices: 22.4 us -> none
  transfers between devices with their start and end apart: 10 -> 44, of which waited for: 10 -> 17; matrix products, arithmetic and copies ran while one was open for 3% -> 2% of each run, Pallas kernels for 0% -> 22%
where the time goes in v2:
time: 169 us; the launch traced here: 168 us
  waiting for transfers between devices  66.1 us (39%)
  Pallas kernels  42.5 us (25%)
  starting transfers between devices  38.1 us (23%)
  local copies, waits for them, and re-layouts  17.9 us (11%)
  between operations  3.02 us (2%)
    ppermute x44, waiting for transfers between devices, swap(): return lax.ppermute(value, axis, [(i, i ^ flip) for i in range(size)])  66.1 us
    pallas_call x26, Pallas kernels, call(): pl.pallas_call(lambda *refs: body(*refs[:n_args], *refs[n_args + n_after:...  42.5 us
    ppermute x44, starting transfers between devices, swap(): return lax.ppermute(value, axis, [(i, i ^ flip) for i in range(size)])  38.1 us
    unnamed x55, local copies, waits for them, and re-layouts  14.1 us
  transfers between devices with their start and end apart: 44, of which 17 were waited for; matrix products, arithmetic and copies ran while one was open for 2% of the time, Pallas kernels for 22%

profile of v2, /device:TPU:0, one launch (start us, length us, event | category | flops | bytes accessed | tf_op | source)
XLA Modules:
  0.0 168.0 jit_solution(12567911411200247203)
XLA Ops:
  1.7 3.0 %collective-permute-start.1 = (bf16[1,288]{1,0:T(2,128)(2,1)S(1)}, bf16[1,288]{1,0:T(2,128)(2,1)S(1)}, u32[]{:S(2)}, u32[]{:S(2)}) collective-permute-start(bf16[1,288]{1,0:T(2,128)(2,1)S(1)} %copy.31.refs_0_), channel_id=1, source_target_pairs={{0,2},{1,3},{2,0},{3,1},{4,6},{5,7},{6,4},{7,5},{8,10},{9,11},{10,... | collective-permute-start | bytes 1736 | tf_op jit(solution)/shard_map/ppermute | solution.py:29
  4.7 1.6 collective-permute-done.1.refs_2_
  6.2 1.1 collective-permute-done.2.refs_3_
  7.9 0.7 reshape.89.refs_7_
  9.4 0.8 reshape.87
  10.8 1.1 copy-done.7
  11.9 2.1 %copy-done.11 = bf16[1152,1728]{0,1:T(8,128)(2,1)S(1)} copy-done((bf16[1152,1728]{0,1:T(8,128)(2,1)S(1)}, bf16[1152,1728]{0,1:T(8,128)(2,1)}, u32[]{:S(2)}) %copy-start.11) | copy-done | bytes 3981336
  14.7 1.2 modulation.1
  16.0 1.9 %copy-done.1 = bf16[1728,1152]{1,0:T(8,128)(2,1)} copy-done((bf16[1728,1152]{1,0:T(8,128)(2,1)}, bf16[1728,1152]{1,0:T(8,128)(2,1)S(1)}, u32[]{:S(2)}) %copy-start.1) | copy-done | bytes 3981336
  17.9 2.0 %collective-permute-start.4 = (f32[1,1728]{1,0:T(1,128)S(1)}, f32[1,1728]{1,0:T(1,128)S(1)}, u32[]{:S(2)}, u32[]{:S(2)}) collective-permute-start(f32[1,1728]{1,0:T(1,128)S(1)} %get-tuple-element.87.refs_2_), channel_id=1, source_target_pairs={{0,2},{1,3},{2,0},{3,1},{4,6},{5,7},{6,4},{7,5},{8,10},{9,11},{10,... | collective-permute-start | bytes 20744 | tf_op jit(solution)/shard_map/ppermute | solution.py:29
  20.2 1.2 collective-permute-done.7.refs_9_
  23.9 1.5 copy-done.5
  25.5 1.1 copy-done.17
  26.6 5.9 %attention.1 = (bf16[128,1152]{1,0:T(8,128)(2,1)S(1)}, f32[8,1152]{1,0:T(8,128)S(1)}, bf16[128,1152]{1,0:T(8,128)(2,1)S(1)}, bf16[128,864]{1,0:T(8,128)(2,1)S(1)...) custom-call(s32[1]{0:T(128)S(6)} %copy.32.refs_0_, ...), custom_call_target="tpu_custom_call" | custom-call | flops 44000000 | bytes 1024 | tf_op jit(solution)/shard_map/attention/pallas_call | solution.py:43
  32.5 2.0 %collective-permute-start.10 = (bf16[128,1152]{1,0:T(8,128)(2,1)S(1)}, bf16[128,1152]{1,0:T(8,128)(2,1)S(1)}, u32[]{:S(2)}, u32[]{:S(2)}) collective-permute-start(bf16[128,1152]{1,0:T(8,128)(2,1)S(1)} %get-tuple-element.91.refs_1_), channel_id=1, source_target_pairs={{0,2},{1,3},{2,0},{3,1},{4,6},{5,7},{6,4},{7,5},{8,10},{9,11},{10,... | collective-permute-start | bytes 884744 | tf_op jit(solution)/shard_map/ppermute | solution.py:29
  34.6 1.1 early_back.1
  35.7 6.2 %collective-permute-done.10.refs_2_ = bf16[128,1152]{1,0:T(8,128)(2,1)S(1)} collective-permute-done((bf16[128,1152]{1,0:T(8,128)(2,1)S(1)}, bf16[128,1152]{1,0:T(8,128)(2,1)S(1)}, u32[]{:S(2)}, u32[]{:S(2)}) %collective-permute-start.10) | collective-permute-done | bytes 294944 | tf_op jit(solution)/shard_map/ppermute | solution.py:29
  41.9 3.2 %mlp.1 = (bf16[128,1152]{1,0:T(8,128)(2,1)S(1)}, bf16[128,2944]{1,0:T(8,128)(2,1)S(1)}, bf16[128,2944]{1,0:T(8,128)(2,1)S(1)}, bf16[128,640]{1,0:T(8,128)(2,1)S(...) custom-call(bf16[256,1152]{1,0:T(8,128)(2,1)S(1)} %bitcast.22, ...), custom_call_target="tpu_custom_call" | custom-call | flops 33000000 | bytes 1024 | tf_op jit(solution)/shard_map/mlp/pallas_call | solution.py:43
  45.0 2.9 %collective-permute-start.18 = (bf16[128,2944]{1,0:T(8,128)(2,1)S(1)}, bf16[128,2944]{1,0:T(8,128)(2,1)S(1)}, u32[]{:S(2)}, u32[]{:S(2)}) collective-permute-start(bf16[128,2944]{1,0:T(8,128)(2,1)S(1)} %get-tuple-element.101.refs_0_), channel_id=1, source_target_pairs={{0,16},{4,20},{8,24},{12,28},{16,0},{20,4},{24,8},{28,12},{1,17},{... | collective-permute-start | bytes 2261000 | tf_op jit(solution)/shard_map/ppermute | solution.py:29
  47.9 1.5 collective-permute-start.19
  49.5 1.5 collective-permute-start.15
  51.5 1.8 %mlp_tail.1 = (bf16[128,1152]{1,0:T(8,128)(2,1)S(1)}, bf16[128,1792]{1,0:T(8,128)(2,1)S(1)}, bf16[128,1792]{1,0:T(8,128)(2,1)S(1)}, f32[2,1152]{1,0:T(2,128)S(1)}) custom-call(bf16[128,2944]{1,0:T(8,128)(2,1)S(1)} %get-tuple-element.101.refs_0_, bf16[128,2944]{1,0:T(8,128)(2,1)S(1)} %get-tuple-element.102.refs_1_.refs_0_, bf16[1152,1152]{1,0:T(8,128)(2,1)S(1)} %copy-done.3, ...), custom_call_target="tpu_custom_call" | custom-call | flops 22000000 | bytes 1024 | tf_op jit(solution)/shard_map/mlp_tail/pallas_call | solution.py:43
  53.8 5.6 %collective-permute-done.15.refs_2_ = bf16[128,1152]{1,0:T(8,128)(2,1)S(1)} collective-permute-done((bf16[128,1152]{1,0:T(8,128)(2,1)S(1)}, bf16[128,1152]{1,0:T(8,128)(2,1)S(1)}, u32[]{:S(2)}, u32[]{:S(2)}) %collective-permute-start.15) | collective-permute-done | bytes 294944 | tf_op jit(solution)/shard_map/ppermute | solution.py:29
  59.4 5.8 %attention_back.1 = (bf16[128,1152]{1,0:T(8,128)(2,1)S(1)}, f32[128,1152]{1,0:T(8,128)S(1)}, bf16[128,1152]{1,0:T(8,128)(2,1)S(1)}, bf16[128,1792]{1,0:T(8,128)(2,1)S(1)}, f32[8,1152]{1,0:T(8,128)S(1)}) custom-call(s32[1]{0:T(128)S(6)} %copy.32.refs_0_, bf16[128,1152]{1,0:T(8,128)(2,1)S(1)} %get-tuple-element.108.refs_1_, ...), custom_call_target="tpu_custom_call" | custom-call | flops 55000000 | bytes 1024 | tf_op jit(solution)/shard_map/attention_back/pallas_call | solution.py:43
  65.3 1.6 collective-permute-start.16
  67.4 5.4 %collective-permute-done.17.refs_0_.refs_3_ = bf16[128,1280]{1,0:T(8,128)(2,1)S(1)} collective-permute-done((bf16[128,1280]{1,0:T(8,128)(2,1)S(1)}, bf16[128,1280]{1,0:T(8,128)(2,1)S(1)}, u32[]{:S(2)}, u32[]{:S(2)}) %collective-permute-start.17) | collective-permute-done | bytes 327712 | tf_op jit(solution)/shard_map/ppermute | solution.py:29
  72.9 7.6 %collective-permute-done.18.refs_0_.refs_3_ = bf16[128,2944]{1,0:T(8,128)(2,1)S(1)} collective-permute-done((bf16[128,2944]{1,0:T(8,128)(2,1)S(1)}, bf16[128,2944]{1,0:T(8,128)(2,1)S(1)}, u32[]{:S(2)}, u32[]{:S(2)}) %collective-permute-start.18) | collective-permute-done | bytes 753696 | tf_op jit(solution)/shard_map/ppermute | solution.py:29
  80.6 1.3 input_back.1
  81.9 1.3 collective-permute-done.23.refs_2_
  83.2 1.6 collective-permute-start.24
  86.0 1.1 collective-permute-done.24
  87.2 1.5 collective-permute-start.32
  88.8 0.7 collective-permute-start.33
  89.5 3.4 %collective-permute-start.34 = (f32[2,7424]{1,0:T(2,128)S(1)}, f32[2,7424]{1,0:T(2,128)S(1)}, u32[]{:S(2)}, u32[]{:S(2)}) collective-permute-start(f32[2,7424]{1,0:T(2,128)S(1)} %pad_maximum_fusion.refs_5_.refs_1_), channel_id=1, source_target_pairs={{0,16},{4,20},{8,24},{12,28},{16,0},{20,4},{24,8},{28,12},{1,17},{... | collective-permute-start | bytes 178184 | tf_op jit(solution)/shard_map/ppermute | solution.py:29
  93.2 1.9 %down_grad.1 = (f32[2,144,1152]{2,1,0:T(8,128)S(1)}, bf16[2,144,1152]{2,1,0:T(8,128)(2,1)}) custom-call(bf16[128,2944]{1,0:T(8,128)(2,1)S(1)} %get-tuple-element.101.refs_0_, bf16[128,1792]{1,0:T(8,128)(2,1)S(1)} %get-tuple-element.130.refs_1_, bf16[128,1792]{1,0:T(8,128)(2,1)S(1)} %collective-permute-done.26.refs_2_, ...), custom_call_target="tpu_custom_call" | custom-call | flops 22000000 | bytes 1024 | tf_op jit(solution)/shard_map/down_grad/pallas_call | solution.py:43
  95.1 1.9 %up_grad.1 = (f32[2,144,1152]{2,1,0:T(8,128)S(1)}, bf16[2,144,1152]{2,1,0:T(8,128)(2,1)}) custom-call(bf16[128,2944]{1,0:T(8,128)(2,1)S(1)} %get-tuple-element.102.refs_1_.refs_0_, bf16[128,1792]{1,0:T(8,128)(2,1)S(1)} %get-tuple-element.125.refs_1_, bf16[128,1792]{1,0:T(8,128)(2,1)S(1)} %collective-permute-done.21.refs_2_, ...), custom_call_target="tpu_custom_call" | custom-call | flops 22000000 | bytes 1024 | tf_op jit(solution)/shard_map/up_grad/pallas_call | solution.py:43
  97.1 1.8 %collective-permute-done.35.refs_4_ = f32[2,7424]{1,0:T(2,128)S(1)} collective-permute-done((f32[2,7424]{1,0:T(2,128)S(1)}, f32[2,7424]{1,0:T(2,128)S(1)}, u32[]{:S(2)}, u32[]{:S(2)}) %collective-permute-start.35) | collective-permute-done | bytes 59424 | tf_op jit(solution)/shard_map/ppermute | solution.py:29
  98.9 1.9 %gathered.1 = (f32[144,1728]{1,0:T(8,128)}, f32[1,7424]{1,0:T(1,128)S(1)}, f32[8,288]{1,0:T(8,128)S(1)}, f32[8,288]{1,0:T(8,128)S(1)}, f32[8,768]{1,0:T(8,128)S(...) custom-call(bf16[1728,1152]{1,0:T(8,128)(2,1)S(1)} %copy-done.2, f32[2,7424]{1,0:T(2,128)S(1)} %pad_maximum_fusion.refs_5_.refs_1_, ...), custom_call_target="tpu_custom_call" | custom-call | flops 22000000 | bytes 1024 | tf_op jit(solution)/shard_map/gathered/pallas_call | solution.py:43
  100.8 1.4 collective-permute-done.32.refs_0_.refs_8_
  102.8 1.5 collective-permute-start.28
  105.0 2.2 %qkv_grad.1 = (f32[2,144,1152]{2,1,0:T(8,128)S(1)}, bf16[2,144,1152]{2,1,0:T(8,128)(2,1)}) custom-call(bf16[128,1280]{1,0:T(8,128)(2,1)S(1)} %get-tuple-element.121.refs_0_, bf16[128,1024]{1,0:T(8,128)(2,1)S(1)} %get-tuple-element.133.refs_1_, bf16[128,1024]{1,0:T(8,128)(2,1)S(1)} %collective-permute-done.29.refs_2_, ...), custom_call_target="tpu_custom_call" | custom-call | flops 22000000 | bytes 1024 | tf_op jit(solution)/shard_map/qkv_grad/pallas_call | solution.py:43
  107.2 1.4 collective-permute-start.37
  108.6 1.5 collective-permute-start.39
  110.2 2.2 %collective-permute-done.39.refs_2_ = f32[8,768]{1,0:T(8,128)S(1)} collective-permute-done((f32[8,768]{1,0:T(8,128)S(1)}, f32[8,768]{1,0:T(8,128)S(1)}, u32[]{:S(2)}, u32[]{:S(2)}) %collective-permute-start.39) | collective-permute-done | bytes 24608 | tf_op jit(solution)/shard_map/ppermute | solution.py:29
  112.4 7.9 %collective-permute-done.28.refs_1_ = bf16[2,144,1152]{2,1,0:T(8,128)(2,1)S(1)} collective-permute-done((bf16[2,144,1152]{2,1,0:T(8,128)(2,1)}, bf16[2,144,1152]{2,1,0:T(8,128)(2,1)S(1)}, u32[]{:S(2)}, u32[]{:S(2)}) %collective-permute-start.28) | collective-permute-done | bytes 663584 | tf_op jit(solution)/shard_map/ppermute | solution.py:29
  120.3 0.8 copy-done.19
  121.1 1.1 copy-done.20
  122.2 0.8 down_halve.1
  123.6 1.9 %up_halve.1 = (f32[144,1152]{1,0:T(8,128)S(1)}, bf16[144,1152]{1,0:T(8,128)(2,1)}) custom-call(f32[2,144,1152]{2,1,0:T(8,128)S(1)} %copy-done.10, bf16[2,144,1152]{2,1,0:T(8,128)(2,1)} %collective-permute-done.25.refs_1_, f32[144,1152]{1,0:T(8,128)S(1)} %get-tuple-element.140.refs_2_.refs_0_), custom_call_target="tpu_custom_call" | custom-call | flops 5500000 | bytes 1024 | tf_op jit(solution)/shard_map/up_halve/pallas_call | solution.py:43
  125.5 0.7 collective-permute-start.43
  126.2 3.4 %collective-permute-start.42 = (bf16[144,1152]{1,0:T(8,128)(2,1)}, bf16[144,1152]{1,0:T(8,128)(2,1)}, u32[]{:S(2)}, u32[]{:S(2)}) collective-permute-start(bf16[144,1152]{1,0:T(8,128)(2,1)} %get-tuple-element.151), channel_id=1, source_target_pairs={{0,16},{4,20},{8,24},{12,28},{16,0},{20,4},{24,8},{28,12},{1,17},{... | collective-permute-start | bytes 995336 | tf_op jit(solution)/shard_map/ppermute | solution.py:29
  129.5 1.0 table.1.refs_2_
  130.5 13.2 %collective-permute-done.37.refs_1_ = bf16[2,144,1152]{2,1,0:T(8,128)(2,1)} collective-permute-done((bf16[2,144,1152]{2,1,0:T(8,128)(2,1)}, bf16[2,144,1152]{2,1,0:T(8,128)(2,1)}, u32[]{:S(2)}, u32[]{:S(2)}) %collective-permute-start.37) | collective-permute-done | bytes 663584 | tf_op jit(solution)/shard_map/ppermute | solution.py:29
  143.7 0.9 copy-done.21
  144.6 2.0 %qkv_halve.1 = (f32[144,1152]{1,0:T(8,128)S(1)}, bf16[144,1152]{1,0:T(8,128)(2,1)}) custom-call(f32[2,144,1152]{2,1,0:T(8,128)S(1)} %get-tuple-element.139.refs_2_.refs_0_, bf16[2,144,1152]{2,1,0:T(8,128)(2,1)} %collective-permute-done.37.refs_1_, f32[288,101]{1,0:T(8,128)S(1)} %copy-done.21), custom_call_target="tpu_custom_call" | custom-call | flops 5500000 | bytes 1024 | tf_op jit(solution)/shard_map/qkv_halve/pallas_call | solution.py:43
  146.6 1.5 collective-permute-start.41
  150.1 1.0 copy-done.23
  151.0 2.2 %join.1 = (bf16[256,1152]{1,0:T(8,128)(2,1)}, bf16[256,1152]{1,0:T(8,128)(2,1)}) custom-call(bf16[128,1152]{1,0:T(8,128)(2,1)S(1)} %copy-done.23, bf16[128,1152]{1,0:T(8,128)(2,1)} %collective-permute-done.14.refs_1_, bf16[128,1152]{1,0:T(8,128)(2,1)} %get-tuple-element.124.refs_2_, bf16[128,1152]{1,0:T(8,128)(2,1)} %collective-permute-done.20.refs_3_, ...), custom_call_target="tpu_custom_call" | custom-call | flops 8800000 | bytes 1024 | tf_op jit(solution)/shard_map/join/pallas_call | solution.py:43
  153.3 1.9 %down_add.1.refs_2_ = f32[144,1152]{1,0:T(8,128)} custom-call(f32[144,1152]{1,0:T(8,128)S(1)} %get-tuple-element.140.refs_2_.refs_0_, bf16[144,1152]{1,0:T(8,128)(2,1)} %collective-permute-done.43.refs_1_, f32[144,1152]{1,0:T(8,128)S(1)} %get-tuple-element.149.refs_2_.refs_0_), custom_call_target="tpu_custom_call" | custom-call | flops 5500000 | bytes 1024 | tf_op jit(solution)/shard_map/down_add/pallas_call | solution.py:43
  155.2 1.1 copy-done.15
  156.3 1.9 %up_add.1.refs_2_ = f32[144,1152]{1,0:T(8,128)} custom-call(f32[144,1152]{1,0:T(8,128)S(1)} %get-tuple-element.141.refs_4_.refs_6_.refs_0_, bf16[144,1152]{1,0:T(8,128)(2,1)} %collective-permute-done.42.refs_1_, f32[144,1152]{1,0:T(8,128)S(1)} %copy-done.15), custom_call_target="tpu_custom_call" | custom-call | flops 5500000 | bytes 1024 | tf_op jit(solution)/shard_map/up_add/pallas_call | solution.py:43
  158.2 7.8 %collective-permute-done.41.refs_1_ = bf16[144,1152]{1,0:T(8,128)(2,1)S(1)} collective-permute-done((bf16[144,1152]{1,0:T(8,128)(2,1)}, bf16[144,1152]{1,0:T(8,128)(2,1)S(1)}, u32[]{:S(2)}, u32[]{:S(2)}) %collective-permute-start.41) | collective-permute-done | bytes 331808 | tf_op jit(solution)/shard_map/ppermute | solution.py:29
  165.9 1.1 copy-done.12
  167.0 1.0 qkv_add.1
  (125 shorter events, 12.1 us)
Async XLA Ops:
  0.7 13.9 %copy-start.26 = (bf16[1728]{0:T(1024)(128)(2,1)S(1)}, bf16[1728]{0:T(1024)(128)(2,1)}, u32[]{:S(2)}) copy-start(bf16[1728]{0:T(1024)(128)(2,1)} %param.22) | copy-start | bytes 10372
  1.7 4.5 %collective-permute-start.1 = (bf16[1,288]{1,0:T(2,128)(2,1)S(1)}, bf16[1,288]{1,0:T(2,128)(2,1)S(1)}, u32[]{:S(2)}, u32[]{:S(2)}) collective-permute-start(bf16[1,288]{1,0:T(2,128)(2,1)S(1)} %copy.31.refs_0_), channel_id=1, source_target_pairs={{0,2},{1,3},{2,0},{3,1},{4,6},{5,7},{6,4},{7,5},{8,10},{9,11},{10,... | collective-permute-start | bytes 1736 | tf_op jit(solution)/shard_map/ppermute | solution.py:29
  6.2 1.2 collective-permute-start.2
  7.4 14.1 %collective-permute-start.5 = (bf16[864,1152]{1,0:T(8,128)(2,1)}, bf16[864,1152]{1,0:T(8,128)(2,1)}, u32[]{:S(2)}, u32[]{:S(2)}) collective-permute-start(bf16[864,1152]{1,0:T(8,128)(2,1)} %bitcast.18), channel_id=1, source_target_pairs={{0,1},{1,0},{2,3},{3,2},{4,5},{5,4},{6,7},{7,6},{8,9},{9,8},{10,11... | collective-permute-start | bytes 5971976 | tf_op jit(solution)/shard_map/ppermute | solution.py:29
  7.6 7.2 %collective-permute-start = (bf16[1,288]{1,0:T(2,128)(2,1)S(1)}, bf16[1,288]{1,0:T(2,128)(2,1)S(1)}, u32[]{:S(2)}, u32[]{:S(2)}) collective-permute-start(bf16[1,288]{1,0:T(2,128)(2,1)S(1)} %copy.31.refs_0_), channel_id=1, source_target_pairs={{0,1},{1,0},{2,3},{3,2},{4,5},{5,4},{6,7},{7,6},{8,9},{9,8},{10,11... | collective-permute-start | bytes 1736 | tf_op jit(solution)/shard_map/ppermute | solution.py:29
  8.6 12.9 %collective-permute-start.8 = (bf16[1,1152]{1,0:T(2,128)(2,1)S(1)}, bf16[1,1152]{1,0:T(2,128)(2,1)S(1)}, u32[]{:S(2)}, u32[]{:S(2)}) collective-permute-start(bf16[1,1152]{1,0:T(2,128)(2,1)S(1)} %reshape.89.refs_7_), channel_id=1, source_target_pairs={{0,1},{1,0},{2,3},{3,2},{4,5},{5,4},{6,7},{7,6},{8,9},{9,8},{10,11... | collective-permute-start | bytes 6920 | tf_op jit(solution)/shard_map/ppermute | solution.py:29
  10.3 11.2 %collective-permute-start.6 = (bf16[288,1152]{1,0:T(8,128)(2,1)}, bf16[288,1152]{1,0:T(8,128)(2,1)}, u32[]{:S(2)}, u32[]{:S(2)}) collective-permute-start(bf16[288,1152]{1,0:T(8,128)(2,1)} %bitcast.25), channel_id=1, source_target_pairs={{0,1},{1,0},{2,3},{3,2},{4,5},{5,4},{6,7},{7,6},{8,9},{9,8},{10,11... | collective-permute-start | bytes 1990664 | tf_op jit(solution)/shard_map/ppermute | solution.py:29
  11.9 2.1 %copy-start.11 = (bf16[1152,1728]{0,1:T(8,128)(2,1)S(1)}, bf16[1152,1728]{0,1:T(8,128)(2,1)}, u32[]{:S(2)}) copy-start(bf16[1152,1728]{0,1:T(8,128)(2,1)} %param.21) | copy-start | bytes 11943940
  14.6 1.3 copy-start.16
  14.6 8.1 %copy-start.3 = (bf16[1152,1152]{1,0:T(8,128)(2,1)S(1)}, bf16[1152,1152]{1,0:T(8,128)(2,1)}, u32[]{:S(2)}) copy-start(bf16[1152,1152]{1,0:T(8,128)(2,1)} %refs_2_.1) | copy-start | bytes 7962628
  14.6 9.3 %copy-start.14 = (bf16[1152,288]{0,1:T(8,128)(2,1)S(1)}, bf16[1152,288]{0,1:T(8,128)(2,1)}, u32[]{:S(2)}) copy-start(bf16[1152,288]{0,1:T(8,128)(2,1)} %param.25) | copy-start | bytes 1990660
  16.0 1.9 %copy-start.1 = (bf16[1728,1152]{1,0:T(8,128)(2,1)}, bf16[1728,1152]{1,0:T(8,128)(2,1)S(1)}, u32[]{:S(2)}) copy-start(bf16[1728,1152]{1,0:T(8,128)(2,1)S(1)} %get-tuple-element.86.refs_5_.refs_0_) | copy-start | bytes 11943940
  17.9 3.6 %collective-permute-start.4 = (f32[1,1728]{1,0:T(1,128)S(1)}, f32[1,1728]{1,0:T(1,128)S(1)}, u32[]{:S(2)}, u32[]{:S(2)}) collective-permute-start(f32[1,1728]{1,0:T(1,128)S(1)} %get-tuple-element.87.refs_2_), channel_id=1, source_target_pairs={{0,2},{1,3},{2,0},{3,1},{4,6},{5,7},{6,4},{7,5},{8,10},{9,11},{10,... | collective-permute-start | bytes 20744 | tf_op jit(solution)/shard_map/ppermute | solution.py:29
  20.1 1.2 collective-permute-start.7
  21.3 1.2 collective-permute-start.3
  21.5 1.2 collective-permute-start.9
  22.8 11.8 %collective-permute-start.12 = (bf16[1152,1152]{1,0:T(8,128)(2,1)S(1)}, bf16[1152,1152]{1,0:T(8,128)(2,1)S(1)}, u32[]{:S(2)}, u32[]{:S(2)}) collective-permute-start(bf16[1152,1152]{1,0:T(8,128)(2,1)S(1)} %copy-done.3), channel_id=1, source_target_pairs={{0,1},{1,0},{2,3},{3,2},{4,5},{5,4},{6,7},{7,6},{8,9},{9,8},{10,11... | collective-permute-start | bytes 7962632 | tf_op jit(solution)/shard_map/ppermute | solution.py:29
  23.1 18.8 %collective-permute-start.11 = (bf16[1152,1152]{1,0:T(8,128)(2,1)}, bf16[1152,1152]{1,0:T(8,128)(2,1)S(1)}, u32[]{:S(2)}, u32[]{:S(2)}) collective-permute-start(bf16[1152,1152]{1,0:T(8,128)(2,1)} %refs_5_.1), channel_id=1, source_target_pairs={{0,1},{1,0},{2,3},{3,2},{4,5},{5,4},{6,7},{7,6},{8,9},{9,8},{10,11... | collective-permute-start | bytes 7962632 | tf_op jit(solution)/shard_map/ppermute | solution.py:29
  23.9 1.6 copy-start.5
  26.6 8.0 %copy-start.24 = (bf16[1152]{0:T(1024)(128)(2,1)S(1)}, bf16[1152]{0:T(1024)(128)(2,1)}, u32[]{:S(2)}) copy-start(bf16[1152]{0:T(1024)(128)(2,1)} %param.26) | copy-start | bytes 6916
  26.6 8.0 %copy-start.4 = (bf16[1,16,16,1152]{3,2,1,0:T(8,128)(2,1)S(1)}, bf16[1,16,16,1152]{3,2,1,0:T(8,128)(2,1)}, u32[]{:S(2)}) copy-start(bf16[1,16,16,1152]{3,2,1,0:T(8,128)(2,1)} %param.31) | copy-start | bytes 1769476
  32.5 9.4 %collective-permute-start.10 = (bf16[128,1152]{1,0:T(8,128)(2,1)S(1)}, bf16[128,1152]{1,0:T(8,128)(2,1)S(1)}, u32[]{:S(2)}, u32[]{:S(2)}) collective-permute-start(bf16[128,1152]{1,0:T(8,128)(2,1)S(1)} %get-tuple-element.91.refs_1_), channel_id=1, source_target_pairs={{0,2},{1,3},{2,0},{3,1},{4,6},{5,7},{6,4},{7,5},{8,10},{9,11},{10,... | collective-permute-start | bytes 884744 | tf_op jit(solution)/shard_map/ppermute | solution.py:29
  34.5 7.3 %copy-start.8 = (bf16[1,16,16,1152]{3,2,1,0:T(8,128)(2,1)S(1)}, bf16[1,16,16,1152]{3,2,1,0:T(8,128)(2,1)}, u32[]{:S(2)}) copy-start(bf16[1,16,16,1152]{3,2,1,0:T(8,128)(2,1)} %param.16) | copy-start | bytes 1769476
  34.6 7.3 %copy-start.13 = (bf16[1152,1152]{1,0:T(8,128)(2,1)S(1)}, bf16[1152,1152]{1,0:T(8,128)(2,1)}, u32[]{:S(2)}) copy-start(bf16[1152,1152]{1,0:T(8,128)(2,1)} %refs_5_.1) | copy-start | bytes 7962628
  45.0 35.5 %collective-permute-start.18 = (bf16[128,2944]{1,0:T(8,128)(2,1)S(1)}, bf16[128,2944]{1,0:T(8,128)(2,1)S(1)}, u32[]{:S(2)}, u32[]{:S(2)}) collective-permute-start(bf16[128,2944]{1,0:T(8,128)(2,1)S(1)} %get-tuple-element.101.refs_0_), channel_id=1, source_target_pairs={{0,16},{4,20},{8,24},{12,28},{16,0},{20,4},{24,8},{28,12},{1,17},{... | collective-permute-start | bytes 2261000 | tf_op jit(solution)/shard_map/ppermute | solution.py:29
  47.9 32.6 %collective-permute-start.19 = (bf16[128,2944]{1,0:T(8,128)(2,1)S(1)}, bf16[128,2944]{1,0:T(8,128)(2,1)S(1)}, u32[]{:S(2)}, u32[]{:S(2)}) collective-permute-start(bf16[128,2944]{1,0:T(8,128)(2,1)S(1)} %get-tuple-element.102.refs_1_.refs_0_), channel_id=1, source_target_pairs={{0,4},{4,0},{8,12},{12,8},{16,20},{20,16},{24,28},{28,24},{1,5},{5... | collective-permute-start | bytes 2261000 | tf_op jit(solution)/shard_map/ppermute | solution.py:29
  49.5 9.9 %collective-permute-start.15 = (bf16[128,1152]{1,0:T(8,128)(2,1)S(1)}, bf16[128,1152]{1,0:T(8,128)(2,1)S(1)}, u32[]{:S(2)}, u32[]{:S(2)}) collective-permute-start(bf16[128,1152]{1,0:T(8,128)(2,1)S(1)} %get-tuple-element.108.refs_1_), channel_id=1, source_target_pairs={{0,2},{1,3},{2,0},{3,1},{4,6},{5,7},{6,4},{7,5},{8,10},{9,11},{10,... | collective-permute-start | bytes 884744 | tf_op jit(solution)/shard_map/ppermute | solution.py:29
  50.9 21.8 %collective-permute-start.17 = (bf16[128,1280]{1,0:T(8,128)(2,1)S(1)}, bf16[128,1280]{1,0:T(8,128)(2,1)S(1)}, u32[]{:S(2)}, u32[]{:S(2)}) collective-permute-start(bf16[128,1280]{1,0:T(8,128)(2,1)S(1)} %get-tuple-element.121.refs_0_), channel_id=1, source_target_pairs={{0,4},{4,0},{8,12},{12,8},{16,20},{20,16},{24,28},{28,24},{1,5},{5... | collective-permute-start | bytes 983048 | tf_op jit(solution)/shard_map/ppermute | solution.py:29
  51.5 8.0 %copy-start.6 = (bf16[1152,864]{0,1:T(8,128)(2,1)S(1)}, bf16[1152,864]{0,1:T(8,128)(2,1)}, u32[]{:S(2)}) copy-start(bf16[1152,864]{0,1:T(8,128)(2,1)} %param.23) | copy-start | bytes 5971972
  53.2 13.6 %collective-permute-start.13 = (bf16[128,1152]{1,0:T(8,128)(2,1)S(1)}, bf16[128,1152]{1,0:T(8,128)(2,1)S(1)}, u32[]{:S(2)}, u32[]{:S(2)}) collective-permute-start(bf16[128,1152]{1,0:T(8,128)(2,1)S(1)} %get-tuple-element.105.refs_2_), channel_id=1, source_target_pairs={{0,2},{1,3},{2,0},{3,1},{4,6},{5,7},{6,4},{7,5},{8,10},{9,11},{10,... | collective-permute-start | bytes 884744 | tf_op jit(solution)/shard_map/ppermute | solution.py:29
  59.4 7.4 %copy-start.25 = (bf16[1152]{0:T(1024)(128)(2,1)S(1)}, bf16[1152]{0:T(1024)(128)(2,1)}, u32[]{:S(2)}) copy-start(bf16[1152]{0:T(1024)(128)(2,1)} %param.30) | copy-start | bytes 6916
  65.2 15.3 %copy-start.18 = (f32[128,1152]{1,0:T(8,128)S(1)}, f32[128,1152]{1,0:T(8,128)}, u32[]{:S(2)}) copy-start(f32[128,1152]{1,0:T(8,128)} %copy-done.16) | copy-start | bytes 1769476
  65.3 15.3 %collective-permute-start.16 = (bf16[128,1152]{1,0:T(8,128)(2,1)S(1)}, bf16[128,1152]{1,0:T(8,128)(2,1)S(1)}, u32[]{:S(2)}, u32[]{:S(2)}) collective-permute-start(bf16[128,1152]{1,0:T(8,128)(2,1)S(1)} %get-tuple-element.114.refs_1_.refs_2_), channel_id=1, source_target_pairs={{0,2},{1,3},{2,0},{3,1},{4,6},{5,7},{6,4},{7,5},{8,10},{9,11},{10,... | collective-permute-start | bytes 884744 | tf_op jit(solution)/shard_map/ppermute | solution.py:29
  67.3 13.2 %copy-start.22 = (bf16[128,1152]{1,0:T(8,128)(2,1)}, bf16[128,1152]{1,0:T(8,128)(2,1)S(1)}, u32[]{:S(2)}) copy-start(bf16[128,1152]{1,0:T(8,128)(2,1)S(1)} %get-tuple-element.107.refs_0_) | copy-start | bytes 884740
  81.9 1.3 collective-permute-start.23
  83.2 3.9 %collective-permute-start.24 = (f32[1,7424]{1,0:T(1,128)S(1)}, f32[1,7424]{1,0:T(1,128)S(1)}, u32[]{:S(2)}, u32[]{:S(2)}) collective-permute-start(f32[1,7424]{1,0:T(1,128)S(1)} %vector.1.refs_2_), channel_id=1, source_target_pairs={{0,4},{4,0},{8,12},{12,8},{16,20},{20,16},{24,28},{28,24},{1,5},{5... | collective-permute-start | bytes 89096 | tf_op jit(solution)/shard_map/ppermute | solution.py:29
  84.8 4.0 %collective-permute-start.26 = (bf16[128,1792]{1,0:T(8,128)(2,1)S(1)}, bf16[128,1792]{1,0:T(8,128)(2,1)S(1)}, u32[]{:S(2)}, u32[]{:S(2)}) collective-permute-start(bf16[128,1792]{1,0:T(8,128)(2,1)S(1)} %get-tuple-element.130.refs_1_), channel_id=1, source_target_pairs={{0,1},{1,0},{2,3},{3,2},{4,5},{5,4},{6,7},{7,6},{8,9},{9,8},{10,11... | collective-permute-start | bytes 1376264 | tf_op jit(solution)/shard_map/ppermute | solution.py:29
  84.8 4.7 %collective-permute-start.21 = (bf16[128,1792]{1,0:T(8,128)(2,1)S(1)}, bf16[128,1792]{1,0:T(8,128)(2,1)S(1)}, u32[]{:S(2)}, u32[]{:S(2)}) collective-permute-start(bf16[128,1792]{1,0:T(8,128)(2,1)S(1)} %get-tuple-element.125.refs_1_), channel_id=1, source_target_pairs={{0,1},{1,0},{2,3},{3,2},{4,5},{5,4},{6,7},{7,6},{8,9},{9,8},{10,11... | collective-permute-start | bytes 1376264 | tf_op jit(solution)/shard_map/ppermute | solution.py:29
  85.3 7.6 %collective-permute-start.27 = (bf16[128,1792]{1,0:T(8,128)(2,1)S(1)}, bf16[128,1792]{1,0:T(8,128)(2,1)S(1)}, u32[]{:S(2)}, u32[]{:S(2)}) collective-permute-start(bf16[128,1792]{1,0:T(8,128)(2,1)S(1)} %get-tuple-element.122.refs_13_), channel_id=1, source_target_pairs={{0,1},{1,0},{2,3},{3,2},{4,5},{5,4},{6,7},{7,6},{8,9},{9,8},{10,11... | collective-permute-start | bytes 1376264 | tf_op jit(solution)/shard_map/ppermute | solution.py:29
  85.3 9.8 %collective-permute-start.22 = (bf16[128,1792]{1,0:T(8,128)(2,1)S(1)}, bf16[128,1792]{1,0:T(8,128)(2,1)S(1)}, u32[]{:S(2)}, u32[]{:S(2)}) collective-permute-start(bf16[128,1792]{1,0:T(8,128)(2,1)S(1)} %get-tuple-element.123.refs_14_), channel_id=1, source_target_pairs={{0,1},{1,0},{2,3},{3,2},{4,5},{5,4},{6,7},{7,6},{8,9},{9,8},{10,11... | collective-permute-start | bytes 1376264 | tf_op jit(solution)/shard_map/ppermute | solution.py:29
  87.2 14.9 %collective-permute-start.32 = (bf16[128,2432]{1,0:T(8,128)(2,1)S(1)}, bf16[128,2432]{1,0:T(8,128)(2,1)S(1)}, u32[]{:S(2)}, u32[]{:S(2)}) collective-permute-start(bf16[128,2432]{1,0:T(8,128)(2,1)S(1)} %get-tuple-element.136.refs_5_), channel_id=1, source_target_pairs={{0,4},{4,0},{8,12},{12,8},{16,20},{20,16},{24,28},{28,24},{1,5},{5... | collective-permute-start | bytes 1867784 | tf_op jit(solution)/shard_map/ppermute | solution.py:29
  88.7 10.1 %copy-start.2 = (bf16[1728,1152]{1,0:T(8,128)(2,1)S(1)}, bf16[1728,1152]{1,0:T(8,128)(2,1)}, u32[]{:S(2)}) copy-start(bf16[1728,1152]{1,0:T(8,128)(2,1)} %copy-done.1) | copy-start | bytes 11943940
  88.8 8.3 %collective-permute-start.33 = (f32[2,7424]{1,0:T(2,128)S(1)}, f32[2,7424]{1,0:T(2,128)S(1)}, u32[]{:S(2)}, u32[]{:S(2)}) collective-permute-start(f32[2,7424]{1,0:T(2,128)S(1)} %pad_maximum_fusion.refs_5_.refs_1_), channel_id=1, source_target_pairs={{0,8},{4,12},{8,0},{12,4},{16,24},{20,28},{24,16},{28,20},{1,9},{5... | collective-permute-start | bytes 178184 | tf_op jit(solution)/shard_map/ppermute | solution.py:29
  89.5 7.6 %collective-permute-start.34 = (f32[2,7424]{1,0:T(2,128)S(1)}, f32[2,7424]{1,0:T(2,128)S(1)}, u32[]{:S(2)}, u32[]{:S(2)}) collective-permute-start(f32[2,7424]{1,0:T(2,128)S(1)} %pad_maximum_fusion.refs_5_.refs_1_), channel_id=1, source_target_pairs={{0,16},{4,20},{8,24},{12,28},{16,0},{20,4},{24,8},{28,12},{1,17},{... | collective-permute-start | bytes 178184 | tf_op jit(solution)/shard_map/ppermute | solution.py:29
  92.9 6.0 %collective-permute-start.35 = (f32[2,7424]{1,0:T(2,128)S(1)}, f32[2,7424]{1,0:T(2,128)S(1)}, u32[]{:S(2)}, u32[]{:S(2)}) collective-permute-start(f32[2,7424]{1,0:T(2,128)S(1)} %pad_maximum_fusion.refs_5_.refs_1_), channel_id=1, source_target_pairs={{0,24},{4,28},{8,16},{12,20},{16,8},{20,12},{24,0},{28,4},{1,25},{... | collective-permute-start | bytes 178184 | tf_op jit(solution)/shard_map/ppermute | solution.py:29
  95.1 9.9 %collective-permute-start.31 = (bf16[128,1536]{1,0:T(8,128)(2,1)S(1)}, bf16[128,1536]{1,0:T(8,128)(2,1)S(1)}, u32[]{:S(2)}, u32[]{:S(2)}) collective-permute-start(bf16[128,1536]{1,0:T(8,128)(2,1)S(1)} %get-tuple-element.137.refs_6_), channel_id=1, source_target_pairs={{0,1},{1,0},{2,3},{3,2},{4,5},{5,4},{6,7},{7,6},{8,9},{9,8},{10,11... | collective-permute-start | bytes 1179656 | tf_op jit(solution)/shard_map/ppermute | solution.py:29
  97.1 3.7 %copy-start.9 = (f32[2,144,1152]{2,1,0:T(8,128)}, f32[2,144,1152]{2,1,0:T(8,128)S(1)}, u32[]{:S(2)}) copy-start(f32[2,144,1152]{2,1,0:T(8,128)S(1)} %get-tuple-element.128.refs_6_.refs_0_) | copy-start | bytes 3981316
  102.1 2.9 %collective-permute-start.36 = (bf16[128,1536]{1,0:T(8,128)(2,1)S(1)}, bf16[128,1536]{1,0:T(8,128)(2,1)S(1)}, u32[]{:S(2)}, u32[]{:S(2)}) collective-permute-start(bf16[128,1536]{1,0:T(8,128)(2,1)S(1)} %forward3.1), channel_id=1, source_target_pairs={{0,1},{1,0},{2,3},{3,2},{4,5},{5,4},{6,7},{7,6},{8,9},{9,8},{10,11... | collective-permute-start | bytes 1179656 | tf_op jit(solution)/shard_map/ppermute | solution.py:29
  102.2 2.1 %collective-permute-start.29 = (bf16[128,1024]{1,0:T(8,128)(2,1)S(1)}, bf16[128,1024]{1,0:T(8,128)(2,1)S(1)}, u32[]{:S(2)}, u32[]{:S(2)}) collective-permute-start(bf16[128,1024]{1,0:T(8,128)(2,1)S(1)} %get-tuple-element.133.refs_1_), channel_id=1, source_target_pairs={{0,1},{1,0},{2,3},{3,2},{4,5},{5,4},{6,7},{7,6},{8,9},{9,8},{10,11... | collective-permute-start | bytes 786440 | tf_op jit(solution)/shard_map/ppermute | solution.py:29
  102.7 2.3 %collective-permute-start.30 = (bf16[128,1024]{1,0:T(8,128)(2,1)S(1)}, bf16[128,1024]{1,0:T(8,128)(2,1)S(1)}, u32[]{:S(2)}, u32[]{:S(2)}) collective-permute-start(bf16[128,1024]{1,0:T(8,128)(2,1)S(1)} %forward1.1.refs_12_), channel_id=1, source_target_pairs={{0,1},{1,0},{2,3},{3,2},{4,5},{5,4},{6,7},{7,6},{8,9},{9,8},{10,11... | collective-permute-start | bytes 786440 | tf_op jit(solution)/shard_map/ppermute | solution.py:29
  102.8 17.5 %collective-permute-start.28 = (bf16[2,144,1152]{2,1,0:T(8,128)(2,1)}, bf16[2,144,1152]{2,1,0:T(8,128)(2,1)S(1)}, u32[]{:S(2)}, u32[]{:S(2)}) collective-permute-start(bf16[2,144,1152]{2,1,0:T(8,128)(2,1)} %get-tuple-element.132), channel_id=1, source_target_pairs={{0,4},{4,0},{8,12},{12,8},{16,20},{20,16},{24,28},{28,24},{1,5},{5... | collective-permute-start | bytes 1990664 | tf_op jit(solution)/shard_map/ppermute | solution.py:29
  104.3 18.7 %collective-permute-start.25 = (bf16[2,144,1152]{2,1,0:T(8,128)(2,1)}, bf16[2,144,1152]{2,1,0:T(8,128)(2,1)}, u32[]{:S(2)}, u32[]{:S(2)}) collective-permute-start(bf16[2,144,1152]{2,1,0:T(8,128)(2,1)} %get-tuple-element.129), channel_id=1, source_target_pairs={{0,8},{4,12},{8,0},{12,4},{16,24},{20,28},{24,16},{28,20},{1,9},{5... | collective-permute-start | bytes 1990664 | tf_op jit(solution)/shard_map/ppermute | solution.py:29
  107.2 36.5 %collective-permute-start.37 = (bf16[2,144,1152]{2,1,0:T(8,128)(2,1)}, bf16[2,144,1152]{2,1,0:T(8,128)(2,1)}, u32[]{:S(2)}, u32[]{:S(2)}) collective-permute-start(bf16[2,144,1152]{2,1,0:T(8,128)(2,1)} %get-tuple-element.144), channel_id=1, source_target_pairs={{0,8},{4,12},{8,0},{12,4},{16,24},{20,28},{24,16},{28,20},{1,9},{5... | collective-permute-start | bytes 1990664 | tf_op jit(solution)/shard_map/ppermute | solution.py:29
  108.6 16.9 %collective-permute-start.38 = (f32[8,288]{1,0:T(8,128)S(1)}, f32[8,288]{1,0:T(8,128)S(1)}, u32[]{:S(2)}, u32[]{:S(2)}) collective-permute-start(f32[8,288]{1,0:T(8,128)S(1)} %get-tuple-element.138.refs_1_), channel_id=1, source_target_pairs={{0,1},{1,0},{2,3},{3,2},{4,5},{5,4},{6,7},{7,6},{8,9},{9,8},{10,11... | collective-permute-start | bytes 27656 | tf_op jit(solution)/shard_map/ppermute | solution.py:29
  108.6 3.8 %collective-permute-start.39 = (f32[8,768]{1,0:T(8,128)S(1)}, f32[8,768]{1,0:T(8,128)S(1)}, u32[]{:S(2)}, u32[]{:S(2)}) collective-permute-start(f32[8,768]{1,0:T(8,128)S(1)} %get-tuple-element.146), channel_id=1, source_target_pairs={{0,2},{1,3},{2,0},{3,1},{4,6},{5,7},{6,4},{7,5},{8,10},{9,11},{10,... | collective-permute-start | bytes 73736 | tf_op jit(solution)/shard_map/ppermute | solution.py:29
  110.2 13.4 %copy-start.10 = (f32[2,144,1152]{2,1,0:T(8,128)S(1)}, f32[2,144,1152]{2,1,0:T(8,128)}, u32[]{:S(2)}) copy-start(f32[2,144,1152]{2,1,0:T(8,128)} %copy-done.9) | copy-start | bytes 3981316
  112.4 13.8 %collective-permute-start.40 = (f32[8,768]{1,0:T(8,128)S(1)}, f32[8,768]{1,0:T(8,128)S(1)}, u32[]{:S(2)}, u32[]{:S(2)}) collective-permute-start(f32[8,768]{1,0:T(8,128)S(1)} %collective-permute-done.39.refs_2_), channel_id=1, source_target_pairs={{0,1},{1,0},{2,3},{3,2},{4,5},{5,4},{6,7},{7,6},{8,9},{9,8},{10,11... | collective-permute-start | bytes 73736 | tf_op jit(solution)/shard_map/ppermute | solution.py:29
  121.1 29.0 %collective-permute-start.14 = (bf16[128,1152]{1,0:T(8,128)(2,1)}, bf16[128,1152]{1,0:T(8,128)(2,1)}, u32[]{:S(2)}, u32[]{:S(2)}) collective-permute-start(bf16[128,1152]{1,0:T(8,128)(2,1)} %copy-done.22), channel_id=1, source_target_pairs={{0,1},{1,0},{2,3},{3,2},{4,5},{5,4},{6,7},{7,6},{8,9},{9,8},{10,11... | collective-permute-start | bytes 884744 | tf_op jit(solution)/shard_map/ppermute | solution.py:29
  121.1 1.1 copy-start.20
  123.0 27.0 %collective-permute-start.20 = (bf16[128,1152]{1,0:T(8,128)(2,1)}, bf16[128,1152]{1,0:T(8,128)(2,1)}, u32[]{:S(2)}, u32[]{:S(2)}) collective-permute-start(bf16[128,1152]{1,0:T(8,128)(2,1)} %get-tuple-element.124.refs_2_), channel_id=1, source_target_pairs={{0,1},{1,0},{2,3},{3,2},{4,5},{5,4},{6,7},{7,6},{8,9},{9,8},{10,11... | collective-permute-start | bytes 884744 | tf_op jit(solution)/shard_map/ppermute | solution.py:29
  125.5 27.8 %collective-permute-start.43 = (bf16[144,1152]{1,0:T(8,128)(2,1)}, bf16[144,1152]{1,0:T(8,128)(2,1)}, u32[]{:S(2)}, u32[]{:S(2)}) collective-permute-start(bf16[144,1152]{1,0:T(8,128)(2,1)} %get-tuple-element.152), channel_id=1, source_target_pairs={{0,8},{4,12},{8,0},{12,4},{16,24},{20,28},{24,16},{28,20},{1,9},{5... | collective-permute-start | bytes 995336 | tf_op jit(solution)/shard_map/ppermute | solution.py:29
  126.2 29.0 %collective-permute-start.42 = (bf16[144,1152]{1,0:T(8,128)(2,1)}, bf16[144,1152]{1,0:T(8,128)(2,1)}, u32[]{:S(2)}, u32[]{:S(2)}) collective-permute-start(bf16[144,1152]{1,0:T(8,128)(2,1)} %get-tuple-element.151), channel_id=1, source_target_pairs={{0,16},{4,20},{8,24},{12,28},{16,0},{20,4},{24,8},{28,12},{1,17},{... | collective-permute-start | bytes 995336 | tf_op jit(solution)/shard_map/ppermute | solution.py:29
  146.6 19.3 %collective-permute-start.41 = (bf16[144,1152]{1,0:T(8,128)(2,1)}, bf16[144,1152]{1,0:T(8,128)(2,1)S(1)}, u32[]{:S(2)}, u32[]{:S(2)}) collective-permute-start(bf16[144,1152]{1,0:T(8,128)(2,1)} %get-tuple-element.150), channel_id=1, source_target_pairs={{0,16},{4,20},{8,24},{12,28},{16,0},{20,4},{24,8},{28,12},{1,17},{... | collective-permute-start | bytes 995336 | tf_op jit(solution)/shard_map/ppermute | solution.py:29
  155.2 1.1 copy-start.15
  (7 other events, 6.8 us)

commit v3 on v2

v3 whole, which is shorter than its diff:
```python
import math

import jax
import jax.numpy as jnp
import numpy as np
from jax import lax
from jax.experimental import pallas as pl
from jax.experimental.pallas import tpu as pltpu
from jax.sharding import PartitionSpec as P

HEAD_DIM = 72
BF = jnp.bfloat16
F32 = jnp.float32


def dot(left, right):
    return jnp.dot(left, right, preferred_element_type=F32)


def dot_trans(left, right):
    return lax.dot_general(left, right, (((1,), (1,)), ((), ())), preferred_element_type=F32)


def dot_rows(left, right):
    return lax.dot_general(left, right, (((0,), (0,)), ((), ())), preferred_element_type=F32)


def swap(value, axis, flip):
    size = lax.axis_size(axis)
    return lax.ppermute(value, axis, [(i, i ^ flip) for i in range(size)])


def call(order, body, name, us, outs, args, scratch=(), also=(), limit=24, free=False):
    specs = [
        pl.BlockSpec(
            memory_space=pltpu.SMEM if a.dtype == jnp.int32 else pltpu.VMEM
        )
        for a in args
    ]
    marks = [*(order[:1] if free else order), *also]
    specs += [pl.BlockSpec(memory_space=pl.ANY)] * len(marks)
    n_args, n_outs = len(args), len(outs)
    first_out = n_args + len(marks)

    def whole(*refs):
        body(*refs[:n_args], *refs[first_out : first_out + n_outs], *refs[first_out + n_outs + 1 :])
        refs[first_out + n_outs][...] = jnp.zeros((8, 128), F32)

    *results, mark = pl.pallas_call(
        whole,
        out_shape=[jax.ShapeDtypeStruct(s, d) for s, d in [*outs, ((8, 128), F32)]],
        in_specs=specs,
        out_specs=[pl.BlockSpec(memory_space=pltpu.VMEM)] * (n_outs + 1),
        scratch_shapes=list(scratch),
        compiler_params=pltpu.CompilerParams(vmem_limit_bytes=limit << 20),
        cost_estimate=pl.CostEstimate(
            flops=int(us * 1.1e9), bytes_accessed=1024, transcendentals=0
        ),
        name=name,
    )(*args, *marks)
    if not free:
        order.clear()
    order.append(mark)
    return results


def behind(value, *others):
    return lax.optimization_barrier((value, *others))[0]


def pad_lanes(width):
    return -(-width // 128) * 128


def standardize(value):
    center = value - jnp.mean(value, axis=-1, keepdims=True)
    spread = jnp.mean(center * center, axis=-1, keepdims=True)
    inv = lax.rsqrt(spread + 1e-06)
    return center * inv, inv


def standardize_back(grad, scale, normed, inv):
    g = grad * (1.0 + scale)
    return (
        g
        - jnp.mean(g, axis=-1, keepdims=True)
        - normed * jnp.mean(g * normed, axis=-1, keepdims=True)
    ) * inv


def gelu_pair(value):
    k = math.sqrt(2.0 / math.pi)
    square = value * value
    t = jnp.tanh(k * (value + 0.044715 * value * square))
    act = 0.5 * value * (1.0 + t)
    slope = 0.5 * (1.0 + t) + 0.5 * value * (1.0 - t * t) * k * (1.0 + 3 * 0.044715 * square)
    return act, slope


def row_part(ref, spots, name):
    at, size = spots[name]
    return ref[:, at : at + size].astype(F32)


def column_sum(value):
    return jnp.sum(value, axis=0, keepdims=True)


def kept_rows(length_ref, half, frames):
    frame = lax.broadcasted_iota(jnp.int32, (half, 1), 0) % frames
    return frame < length_ref[0]


def split_chunks(value, n_dp, bit):
    r = value.shape[1] // n_dp
    low, high = (
        jnp.concatenate(
            [value[:, i * r : i * r + r] for i in range(n_dp) if (i >> bit) & 1 == side], axis=1
        )
        for side in range(2)
    )
    mine_low = ((lax.axis_index("dp") >> bit) & 1) == 0
    return jnp.where(mine_low, low, high), jnp.where(mine_low, high, low)


def clock_kernel(spots, times, row, clock):
    freqs = row_part(row, spots, "freqs")
    angles = jnp.full(freqs.shape, times[0], jnp.int32).astype(F32) * freqs
    clock[...] = jnp.concatenate([jnp.cos(angles), jnp.sin(angles)], axis=1)


def start_kernel(tokens, cotangent, normed, inv, tok_half, cot_half):
    half = tok_half.shape[0]
    rows = pl.ds(pl.multiple_of((lax.axis_index("tensor") & 1) * half, half), half)
    tok_half[...] = tokens[rows, :]
    cot_half[...] = cotangent[rows, :]
    normed[...], inv[...] = standardize(tok_half[...].astype(F32))


def modulation_kernel(spots, e0, e1, e2, e3, clock, weight, bias, cond_out, part, rows):
    rank = lax.axis_index("tensor")
    for flip, piece in enumerate((e0, e1, e2, e3)):
        rows[pl.ds(rank ^ flip, 1), :] = piece[...].astype(F32)
    cond = clock[...] + jnp.concatenate([rows[i : i + 1, :] for i in range(4)], axis=1)
    cond_out[...] = cond
    act = (cond / (1.0 + jnp.exp(-cond))).astype(BF)
    act = jnp.broadcast_to(act, (16, act.shape[1]))
    part[...] = dot_trans(act, weight[...])[0:1, :] + row_part(bias, spots, "ada")


def attention_kernel(
    frames, spots, length, normed, m0, m1, m2, m3, qkv_a, qkv_b, bias_a, bias_b, out_a, out_b,
    part, mods, normed_low, saved_a, saved_b, probs_out, att_a, att_b, rows,
):
    rank = lax.axis_index("tensor")
    width = normed.shape[1]
    for flip, piece in enumerate((m0, m1, m2, m3)):
        rows[pl.ds(rank ^ flip, 1), :] = piece[...]
    cols = rows.shape[1]
    extra = cols - width
    for side in range(2):
        a, b = rows[2 * side : 2 * side + 1, :], rows[2 * side + 1 : 2 * side + 2, :]
        mods[3 * side : 3 * side + 1, :] = a[:, :width]
        mods[3 * side + 1 : 3 * side + 2, :] = jnp.concatenate([a[:, width:], b[:, :extra]], axis=1)
        mods[3 * side + 2 : 3 * side + 3, :] = b[:, extra:]
    mods[6:8, :] = jnp.zeros((2, width), F32)
    low = (normed[...] * (1.0 + mods[1:2, :]) + mods[0:1, :]).astype(BF)
    normed_low[...] = low
    half = low.shape[0]
    row_id = lax.broadcasted_iota(jnp.int32, (half, half), 0)
    col_id = lax.broadcasted_iota(jnp.int32, (half, half), 1)
    seen = ((row_id // frames) == (col_id // frames)) & ((col_id % frames) < length[0])
    factor = HEAD_DIM ** (-0.5)
    heads = out_a.shape[0] // HEAD_DIM
    total = None
    blocks = ((qkv_a, bias_a, out_a, saved_a, att_a), (qkv_b, bias_b, out_b, saved_b, att_b))
    for block, (w, b, o, saved, att_ref) in enumerate(blocks):
        qv = row_part(b, spots, "qv")
        zero = jnp.zeros((1, HEAD_DIM), F32)
        pieces = [
            piece
            for h in range(heads)
            for piece in (
                qv[:, 2 * h * HEAD_DIM : (2 * h + 1) * HEAD_DIM],
                zero,
                qv[:, (2 * h + 1) * HEAD_DIM : (2 * h + 2) * HEAD_DIM],
            )
        ]
        qkv = dot_trans(low, w[...]) + jnp.concatenate(pieces, axis=1)
        saved[...] = qkv.astype(BF)
        for h in range(heads):
            base = h * 3 * HEAD_DIM
            q, k, v = (
                qkv[:, base + j * HEAD_DIM : base + (j + 1) * HEAD_DIM].astype(BF)
                for j in range(3)
            )
            scores = jnp.where(seen, dot_trans(q, k) * factor, -1e30)
            raised = jnp.exp(scores - jnp.max(scores, axis=-1, keepdims=True))
            probs = raised / jnp.sum(raised, axis=-1, keepdims=True)
            probs_out[block * heads + h] = probs
            att_ref[:, h * HEAD_DIM : (h + 1) * HEAD_DIM] = dot(probs.astype(BF), v).astype(BF)
        term = dot(att_ref[...], o[...])
        total = term if total is None else total + term
    part[...] = total.astype(BF)


def early_back_kernel(
    frames, n_dp, length, mods, cotangent, down_a, down_b, normed_low, att_a, att_b,
    grad_a, grad_b, pack_far, own_chunks, chunks_far, chunks_core, fc2_sum,
):
    upstream = cotangent[...].astype(F32)
    half, width = upstream.shape
    keep = kept_rows(length, half, frames)
    low32 = (mods[5:6, :] * jnp.where(keep, upstream, 0.0)).astype(BF).astype(F32)
    low = low32.astype(BF)
    grad_a[...] = dot(low, down_a[...])
    grad_b[...] = dot(low, down_b[...])
    fc2_sum[...] = column_sum(low32)
    n_att = att_a.shape[1]
    part = width // 2
    mine, other = split_chunks(normed_low[...].astype(F32), n_dp, 1)
    pack_far[:, 0:n_att] = att_a[...]
    pack_far[:, n_att : 2 * n_att] = att_b[...]
    at = pad_lanes(2 * n_att)
    pack_far[:, at : at + part] = other.astype(BF)
    own_chunks[:, 0:part] = mine.astype(BF)
    mine, other = split_chunks(low32, n_dp, 2)
    chunks_far[:, 0:part] = other.astype(BF)
    chunks_core[:, 0:part] = mine.astype(BF)


def mlp_kernel(
    n_dp, spots, tokens, part1, part1_other, mods, up_a, up_b, fc1_a, fc1_b, grad_a, grad_b,
    chunks_far, part3, pack_act, pack_pre, chunks_core, branch_out, normed_out, inv_out,
):
    branch = part1[...].astype(F32) + part1_other[...].astype(F32) + row_part(fc1_a, spots, "proj")
    branch_out[...] = branch
    mid = tokens[...].astype(F32) + mods[2:3, :] * branch
    normed, inv = standardize(mid)
    normed_out[...] = normed
    inv_out[...] = inv
    low32 = normed * (1.0 + mods[4:5, :]) + mods[3:4, :]
    low = low32.astype(BF)
    total = None
    cols = up_a.shape[1]
    for block, (u, b, g) in enumerate(((up_a, fc1_a, grad_a), (up_b, fc1_b, grad_b))):
        act, slope = gelu_pair(dot(low, u[...]) + row_part(b, spots, "fc1"))
        pack_act[:, block * cols : (block + 1) * cols] = act.astype(BF)
        pre = (g[...] * slope).astype(BF)
        pack_pre[:, block * cols : (block + 1) * cols] = pre
        term = dot_trans(pre, u[...])
        total = term if total is None else total + term
    part3[...] = total.astype(BF)
    mine, other = split_chunks(low32, n_dp, 0)
    part = mine.shape[1]
    pack_pre[:, 2 * cols : 2 * cols + part] = other.astype(BF)
    chunks_core[:, 0:part] = mine.astype(BF)
    pack_act[:, 2 * cols :] = chunks_far[...]


def mlp_tail_kernel(
    spans, pack_act, pack_pre, down_a, down_b, chunks_act, chunks_pre, far1, pack1, chunks1,
    part2, core, sums,
):
    cols = down_a.shape[1]
    part2[...] = (
        dot_trans(pack_act[:, 0:cols], down_a[...]) + dot_trans(pack_act[:, cols : 2 * cols], down_b[...])
    ).astype(BF)
    forward_kernel([spans], pack_act, pack_pre, chunks_act, chunks_pre, far1, pack1, chunks1, core)
    sums[0:1, :] = column_sum(pack_pre[:, 0:cols].astype(F32))
    sums[1:2, :] = column_sum(pack_pre[:, cols : 2 * cols].astype(F32))


def attention_back_kernel(
    frames, length, part3, part3_other, mods, normed, inv, branch, cotangent,
    out_a, out_b, qkv_a, qkv_b, saved_a, saved_b, probs_in,
    part4, mid_grad_out, low_out, stacked, sums,
):
    upstream = cotangent[...].astype(F32)
    half, width = upstream.shape
    keep = kept_rows(length, half, frames)
    grad = part3[...].astype(F32) + part3_other[...].astype(F32)
    norm = normed[...]
    mid_grad = jnp.where(keep, upstream, 0.0) + standardize_back(grad, mods[4:5, :], norm, inv[...])
    mid_grad_out[...] = mid_grad
    low = (mods[2:3, :] * mid_grad).astype(BF)
    low_out[...] = low
    sums[0:1, :] = column_sum(grad)
    sums[1:2, :] = column_sum(grad * norm)
    sums[2:3, :] = column_sum(mid_grad * branch[...])
    sums[3:4, :] = column_sum(low.astype(F32))
    factor = HEAD_DIM ** (-0.5)
    heads = out_a.shape[0] // HEAD_DIM
    cols = heads * 3 * HEAD_DIM
    wide = pad_lanes(cols)
    total = None
    for block, (w, o, saved) in enumerate(((qkv_a, out_a, saved_a), (qkv_b, out_b, saved_b))):
        att_grad = dot_trans(low, o[...])
        qkv = saved[...].astype(F32)
        for h in range(heads):
            base = h * 3 * HEAD_DIM
            q, k, v = (
                qkv[:, base + j * HEAD_DIM : base + (j + 1) * HEAD_DIM].astype(BF)
                for j in range(3)
            )
            ag = att_grad[:, h * HEAD_DIM : (h + 1) * HEAD_DIM].astype(BF)
            probs = probs_in[block * heads + h]
            value_grad = dot_rows(probs.astype(BF), ag)
            probs_grad = dot_trans(ag, v)
            inner = jnp.sum(probs * probs_grad, axis=-1, keepdims=True)
            scores_low = (probs * (probs_grad - inner)).astype(BF)
            query_grad = dot(scores_low, k) * factor
            key_grad = dot_rows(scores_low, q) * factor
            at = block * wide + base
            for j, piece in enumerate((query_grad, key_grad, value_grad)):
                stacked[:, at + j * HEAD_DIM : at + (j + 1) * HEAD_DIM] = piece.astype(BF)
        mine = stacked[:, block * wide : block * wide + cols]
        sums[4 + block : 5 + block, 0:cols] = column_sum(mine.astype(F32))
        term = dot(mine, w[...])
        total = term if total is None else total + term
    part4[...] = total.astype(BF)


def pack_back_kernel(n_dp, low, stacked, pack_far, own_chunks):
    mine, other = split_chunks(low[...].astype(F32), n_dp, 1)
    part, cols = mine.shape[1], stacked.shape[1]
    pack_far[:, 0:cols] = stacked[...]
    pack_far[:, cols : cols + part] = other.astype(BF)
    own_chunks[:, 0:part] = mine.astype(BF)


def output_kernel(
    frames, spots, length, tokens, part2, part2_other, bias, mods, branch1, cotangent,
    result, gate_sum,
):
    inputs, upstream = tokens[...].astype(F32), cotangent[...].astype(F32)
    keep = kept_rows(length, inputs.shape[0], frames)
    branch = part2[...].astype(F32) + part2_other[...].astype(F32) + row_part(bias, spots, "fc2")
    mid = inputs + mods[2:3, :] * branch1[...]
    result[...] = jnp.where(keep, mid + mods[5:6, :] * branch, inputs).astype(BF)
    gate_sum[...] = column_sum(jnp.where(keep, upstream, 0.0) * branch)


def input_back_kernel(
    frames, length, part4, part4_other, mods, normed, inv, mid_grad, cotangent,
    back_sums, gate2_sum, fc2_sum, pre_sums, result, both, sums,
):
    upstream = cotangent[...].astype(F32)
    keep = kept_rows(length, upstream.shape[0], frames)
    grad = part4[...].astype(F32) + part4_other[...].astype(F32)
    norm = normed[...]
    back = standardize_back(grad, mods[1:2, :], norm, inv[...])
    width = norm.shape[1]
    both[:, :width] = result[...]
    both[:, width:] = (mid_grad[...] + back + jnp.where(keep, 0.0, upstream)).astype(BF)
    sums[0:1, :] = column_sum(grad)
    sums[1:2, :] = column_sum(grad * norm)
    sums[2:3, :] = back_sums[2:3, :]
    sums[3:5, :] = back_sums[0:2, :]
    sums[5:6, :] = gate2_sum[...]
    sums[6:7, :] = fc2_sum[...]
    sums[7:8, :] = back_sums[3:4, :]
    sums[8:10, :] = pre_sums[0:2, :]
    sums[10:12, :] = back_sums[4:6, :]
    sums[12:16, :] = jnp.zeros((4, sums.shape[1]), F32)


def vector_kernel(layout, label, mine, other, cond, vector):
    rank = lax.axis_index("tensor")
    width = mine.shape[1]
    both = mine[...] + other[...]
    upper = rank >= 2
    pick = lambda i: jnp.where(upper, both[3 + i : 4 + i, :], both[i : i + 1, :])
    cols = layout["mod"][1]
    extra = cols - width
    shift, scale, gate = pick(0), pick(1), pick(2)
    even = jnp.concatenate([shift, scale[:, :extra]], axis=1)
    odd = jnp.concatenate([scale[:, extra:], gate], axis=1)
    vector[...] = jnp.zeros(vector.shape, F32)

    def put(name, value):
        at, size = layout[name]
        vector[:, at : at + size] = value

    put("mod", jnp.where((rank & 1) == 0, even, odd).astype(BF).astype(F32))
    put("fc2", both[6:7, :])
    put("proj", both[7:8, :])
    put("fc1", (mine[8:9, :] + other[9:10, :])[:, : layout["fc1"][1]])
    put("stack", (mine[10:11, :] + other[11:12, :])[:, : layout["stack"][1]])
    put("cond", cond[...])
    put("label", jnp.full((1, 128), label[0], jnp.int32).astype(F32))


def gathered_kernel(layout, n_dp, rows_out, weight, source, *refs):
    ada_grad, ada_bias, qv, proj, fc1, fc2, stay, send, cond_cols, labels, table = refs
    rank, place = lax.axis_index("tensor"), lax.axis_index("dp")
    for i in range(n_dp):
        table[pl.ds(place ^ i, 1), :] = source[i : i + 1, :]

    def get(name):
        at, size = layout[name]
        return table[:, at : at + size]

    sums = lambda name: column_sum(get(name))
    for name, out in (("mod", ada_bias), ("proj", proj), ("fc1", fc1), ("fc2", fc2)):
        out[...] = sums(name).reshape(out.shape)
    stack = sums("stack")
    pieces = [
        stack[:, i * HEAD_DIM : (i + 1) * HEAD_DIM]
        for i in range(stack.shape[1] // HEAD_DIM)
        if i % 3 != 1
    ]
    qv[...] = jnp.concatenate(pieces, axis=1).reshape(qv.shape)
    mod = get("mod").astype(BF)
    cond = get("cond")
    act = cond / (1.0 + jnp.exp(-cond))
    width = act.shape[1]
    mine = pltpu.roll(act, (width - place * rows_out) % width, 1)[:, :rows_out].astype(BF)
    ada_grad[...] = dot_rows(mine, mod)
    columns = cond_cols.shape[1]
    cond_part = dot(mod, weight[...])
    wide = pad_lanes(columns)
    for flip in range(4):
        out, at = (stay, send)[flip & 1], (flip >> 1) * wide
        piece = pltpu.roll(cond_part, (width - (rank ^ flip) * columns) % width, 1)[:, :columns]
        out[:, at : at + columns] = piece
    cond_cols[...] = pltpu.roll(cond, (width - rank * columns) % width, 1)[:, :columns]
    labels[...] = get("label")


def middle_kernel(stay, other, mine, send):
    columns = mine.shape[1]
    wide = pad_lanes(columns)
    mine[...] = stay[:, 0:columns] + other[:, 0:columns]
    send[...] = stay[:, wide : wide + columns] + other[:, wide : wide + columns]


def table_kernel(mine, other, cond_cols, labels, out):
    cond = cond_cols[...]
    gate = 1.0 / (1.0 + jnp.exp(-cond))
    grad = (mine[...] + other[...]) * gate * (1.0 + cond * (1.0 - gate))
    classes = lax.broadcasted_iota(jnp.int32, (cond.shape[0], out.shape[1]), 1).astype(F32)
    onehot = jnp.where(labels[:, : out.shape[1]] == classes, 1.0, 0.0)
    out[...] = lax.dot_general(
        grad,
        onehot,
        (((0,), (0,)), ((), ())),
        precision=lax.Precision.HIGHEST,
        preferred_element_type=F32,
    )


def forward_kernel(spans, *refs):
    for parts, out in zip(spans, refs[-len(spans) :]):
        at = 0
        for i, start, size in parts:
            out[:, at : at + size] = refs[i][:, start : start + size]
            at += size


def weight_kernel(n_dp, split_bit, products, n_in, *refs):
    outs, lefts = refs[n_in : -len(products)], refs[-len(products) :]
    half = refs[0].shape[0]
    part = lefts[0].shape[0]
    r = part // (n_dp // 2)
    at = 0
    for left, (left_rows, right_rows, cols) in zip(lefts, products):
        for i, (j, start) in enumerate(left_rows):
            value = refs[j][:, start : start + part]
            left[:, i * half : (i + 1) * half] = value.astype(F32).T.astype(BF)
        right = [refs[j][:, start : start + cols] for j, start in right_rows]
        right = jnp.concatenate(right, axis=0)
        if split_bit is None:
            outs[0][:, at : at + cols] = dot(left[...], right)
        else:
            stay, send = outs
            mine = (lax.axis_index("dp") >> split_bit) & 1
            for k in range(n_dp // 4):
                for out, side in ((stay, mine), (send, 1 - mine)):
                    start = pl.multiple_of((2 * k + side) * r, r)
                    out[k, :, at : at + cols] = dot(left[pl.ds(start, r), :], right).astype(out.dtype)
        at += cols


def halve_kernel(bit, stay, other, out_stay, out_send):
    mine = (lax.axis_index("dp") >> bit) & 1
    out_stay[...] = stay[mine] + other[mine].astype(F32)
    out_send[...] = (stay[1 - mine] + other[1 - mine].astype(F32)).astype(BF)


def add_kernel(widths, stay, other, *outs):
    total = stay[...] + other[...].astype(F32)
    at = 0
    for out, cols in zip(outs, widths):
        out[...] = total[:, at : at + cols]
        at += cols


def join_kernel(mine, other, *outs):
    half, width = mine.shape[0], outs[0].shape[1]
    core = lax.axis_index("tensor") & 1
    for source, side in ((mine, core), (other, 1 - core)):
        rows = pl.ds(pl.multiple_of(side * half, half), half)
        for i, out in enumerate(outs):
            out[rows, :] = source[:, i * width : (i + 1) * width]


def stack_kernel(mine, other, out):
    n = mine.shape[0]
    out[0:n, :] = mine[...]
    out[n : 2 * n, :] = other[...]


def shards(
    tokens,
    lengths,
    timesteps,
    labels,
    class_table,
    ada_weight,
    ada_bias,
    qkv_weight,
    qv_bias,
    out_weight,
    proj_bias,
    up_weight,
    fc1_bias,
    down_weight,
    fc2_bias,
    cotangent,
):
    clips, patches, frames, width = tokens.shape
    assert clips == 1 and lax.axis_size("tensor") == 4
    rows = patches * frames
    half = rows // 2
    n_att = out_weight.shape[1]
    heads = n_att // HEAD_DIM
    n_qkv = qkv_weight.shape[1]
    hidden = up_weight.shape[1]
    columns = class_table.shape[1]
    ada_cols = ada_weight.shape[1]
    n_classes = class_table.shape[0]
    t_rank = lax.axis_index("tensor")
    d_rank = lax.axis_index("dp")
    n_dp = lax.axis_size("dp")
    order = []
    chunk = width // n_dp
    part = width // 2
    wide = pad_lanes(part)

    tokens2 = tokens.reshape(rows, width)
    cot2 = cotangent.reshape(rows, width)
    half_width = width // 2
    freqs = np.exp(-math.log(10000.0) * np.arange(half_width) / half_width)
    small = (
        ("ada", ada_bias), ("qv", qv_bias), ("fc1", fc1_bias), ("proj", proj_bias),
        ("fc2", fc2_bias), ("freqs", jnp.asarray(freqs, F32)),
    )
    spots, n_row = {}, 0
    for name, v in small:
        spots[name] = (n_row, v.shape[0])
        n_row += pad_lanes(v.shape[0])
    bias_row = sum(
        jnp.pad(v.astype(F32), (spots[name][0], n_row - spots[name][0] - v.shape[0]))
        for name, v in small
    ).reshape(1, n_row)

    def gather_tensor(own, *others):
        across = behind(swap(own, "tensor", 2), *others)
        return [own, swap(own, "tensor", 1), across, swap(across, "tensor", 1)]

    def pair(weight, *others):
        return weight, swap(behind(weight, *others), "tensor", 1)

    picked = lax.dynamic_slice_in_dim(class_table, labels[0], 1, 0)
    (clock,) = call(
        order,
        lambda *refs: clock_kernel(spots, *refs),
        "clock",
        5.0,
        [((1, width), F32)],
        [timesteps, bias_row],
    )
    pieces = gather_tensor(picked, clock, bias_row)
    bias_ws = pair(bias_row)
    cond, mod_part = call(
        order,
        lambda *refs: modulation_kernel(spots, *refs),
        "modulation",
        1.0,
        [((1, width), F32), ((1, ada_cols), F32)],
        [*pieces, clock, ada_weight.T, bias_row],
        [pltpu.VMEM((8, columns), F32)],
    )
    normed1, inv1, tok, cot = call(
        order,
        start_kernel,
        "start",
        1.0,
        [((half, width), F32), ((half, 1), F32), ((half, width), BF), ((half, width), BF)],
        [tokens2, cot2],
    )
    qkv_ws = pair(qkv_weight.T, pieces[1], pieces[3])
    out_ws = pair(out_weight.T, pieces[1], pieces[3])
    mod_pieces = gather_tensor(mod_part, bias_ws[1], qkv_ws[1], out_ws[1], normed1)
    up_ws = pair(up_weight, *mod_pieces)
    down_ws = pair(down_weight, *mod_pieces)

    part1, mods, low1, saved_a, saved_b, probs, att_a, att_b = call(
        order,
        lambda *refs: attention_kernel(frames, spots, *refs),
        "attention",
        4.0,
        [
            ((half, width), BF),
            ((8, width), F32),
            ((half, width), BF),
            ((half, n_qkv), BF),
            ((half, n_qkv), BF),
            ((2 * heads, half, half), F32),
            ((half, n_att), BF),
            ((half, n_att), BF),
        ],
        [lengths, normed1, *mod_pieces, *qkv_ws, *bias_ws, *out_ws],
        [pltpu.VMEM((8, ada_cols), F32)],
    )
    part1_other = swap(part1, "tensor", 2)

    att_far, att_core = pad_lanes(2 * n_att), pad_lanes(n_att)
    grad_a, grad_b, pack1, chunks1, chunks_far, chunks_act, fc2_sum = call(
        order,
        lambda *refs: early_back_kernel(frames, n_dp, *refs),
        "early_back",
        2.0,
        [
            ((half, hidden), F32),
            ((half, hidden), F32),
            ((half, att_far + wide), BF),
            ((half, wide), BF),
            ((half, wide), BF),
            ((half, wide), BF),
            ((1, width), F32),
        ],
        [lengths, mods, cot, *down_ws, low1, att_a, att_b],
    )

    part3, pack_act, pack_pre, chunks_pre, branch1, normed2, inv2 = call(
        order,
        lambda *refs: mlp_kernel(n_dp, spots, *refs),
        "mlp",
        3.0,
        [
            ((half, width), BF),
            ((half, 2 * hidden + wide), BF),
            ((half, 2 * hidden + wide), BF),
            ((half, wide), BF),
            ((half, width), F32),
            ((half, width), F32),
            ((half, 1), F32),
        ],
        [
            tok, part1, part1_other, mods, *up_ws, *bias_ws, grad_a, grad_b,
            chunks_far,
        ],
    )
    part3_other = swap(part3, "tensor", 2)

    def forward(name, spans, sources, also=()):
        outs = [((half, sum(size for _, _, size in parts)), BF) for parts in spans]
        outs = call(
            order, lambda *refs: forward_kernel(spans, *refs), name, 0.02, outs, sources, also=also
        )
        return [swap(out, "tensor", 1) for out in outs]

    def first_grads(name, bit, products, args):
        cols = sum(p[2] for p in products)
        scratch = [pltpu.VMEM((part, 4 * half), BF)] * len(products)
        split, outs = None, [((part, cols), F32)]
        if n_dp == 8:
            split = 0 if bit else 1
            outs = [((2, chunk, cols), F32), ((2, chunk, cols), BF)]
        outs = call(
            order,
            lambda *refs: weight_kernel(n_dp, split, products, len(args), *refs),
            name,
            0.02,
            outs,
            args,
            scratch,
        )
        return outs[0], swap(outs[1], "dp", 1 << split) if n_dp == 8 else None

    def second_grads(name, bit, stay, other):
        if n_dp != 8:
            return stay, other
        last = 1 if bit == 2 else 2
        shape = (chunk, stay.shape[2])
        stay, send = call(
            order, lambda *refs: halve_kernel(last, *refs), name, 0.02, [(shape, F32), (shape, BF)], [stay, other]
        )
        return stay, swap(send, "dp", 1 << last)

    def last_grads(name, bit, widths, stay, other):
        if n_dp == 8:
            return call(
                order,
                lambda *refs: add_kernel(widths, *refs),
                name,
                0.02,
                [((chunk, w), F32) for w in widths],
                [stay, other],
            )
        grad = stay.reshape(n_dp // 2, chunk, -1)
        for b in range((n_dp - 1).bit_length()):
            if b != bit:
                my_bit = (d_rank >> b) & 1
                grad = grad.reshape(grad.shape[0] // 2, 2, chunk, grad.shape[2])
                send = lax.dynamic_index_in_dim(grad, 1 - my_bit, 1, keepdims=False).astype(BF)
                stay = lax.dynamic_index_in_dim(grad, my_bit, 1, keepdims=False)
                grad = stay + swap(send, "dp", 1 << b).astype(F32)
        return jnp.split(grad[0], [sum(widths[:i]) for i in range(1, len(widths))], axis=1)

    far1 = swap(pack1, "dp", 2)
    n_mix = hidden + wide
    n_mix1 = att_core + wide
    at1 = 2 * n_mix
    core_spans = [
        (0, hidden, hidden), (2, 0, wide), (1, hidden, hidden), (3, 0, wide),
        (4, n_att, att_core), (4, att_far, wide), (5, n_att, att_core), (6, 0, wide),
    ]
    part2, core_mlp, pre_sums = call(
        order,
        lambda *refs: mlp_tail_kernel(core_spans, *refs),
        "mlp_tail",
        2.0,
        [((half, width), BF), ((half, 2 * n_mix + 2 * n_mix1), BF), ((2, hidden), F32)],
        [pack_act, pack_pre, *down_ws, chunks_act, chunks_pre, far1, pack1, chunks1],
    )
    part2_other = swap(part2, "tensor", 2)
    core_mlp = swap(core_mlp, "tensor", 1)
    far_act = swap(behind(pack_act, part2), "dp", 4)
    far_pre = swap(behind(pack_pre, part2), "dp", 1)

    part4, mid_grad, low_back, stacked, back_sums = call(
        order,
        lambda *refs: attention_back_kernel(frames, *refs),
        "attention_back",
        5.0,
        [
            ((half, width), BF),
            ((half, width), F32),
            ((half, width), BF),
            ((half, 2 * pad_lanes(n_qkv)), BF),
            ((8, width), F32),
        ],
        [
            lengths, part3, part3_other, mods, normed2, inv2, branch1, cot,
            *out_ws, *qkv_ws, saved_a, saved_b, probs,
        ],
    )
    part4_other = swap(part4, "tensor", 2)
    s_wide = pad_lanes(n_qkv)
    pack3, chunks3 = call(
        order,
        lambda *refs: pack_back_kernel(n_dp, *refs),
        "pack_back",
        0.02,
        [((half, 2 * s_wide + wide), BF), ((half, wide), BF)],
        [low_back, stacked],
        free=True,
    )
    far3 = swap(pack3, "dp", 2)

    result, gate2_sum = call(
        order,
        lambda *refs: output_kernel(frames, spots, *refs),
        "output",
        0.02,
        [((half, width), BF), ((1, width), F32)],
        [lengths, tok, part2, part2_other, bias_row, mods, branch1, cot],
    )
    both, sums = call(
        order,
        lambda *refs: input_back_kernel(frames, *refs),
        "input_back",
        0.02,
        [((half, 2 * width), BF), ((16, width), F32)],
        [
            lengths, part4, part4_other, mods, normed1, inv1, mid_grad, cot,
            back_sums, gate2_sum, fc2_sum, pre_sums, result,
        ],
    )
    sums_other = swap(sums, "tensor", 1)
    layout, at = {}, 0
    for name, size in (
        ("mod", ada_cols), ("fc2", width), ("proj", width), ("fc1", hidden), ("stack", n_qkv),
        ("cond", width), ("label", 128),
    ):
        layout[name] = (at, size)
        at += pad_lanes(size)
    (vector,) = call(
        order,
        lambda *refs: vector_kernel(layout, *refs),
        "vector",
        0.02,
        [((1, at), F32)],
        [labels, sums, sums_other, cond],
    )

    def stack(name, value, flip):
        n, cols = value.shape
        other = swap(value, "dp", flip)
        return call(order, stack_kernel, name, 0.02, [((2 * n, cols), F32)], [value, other])[0]

    def mlp_grads(name, bit, pack, chunks, far, mixed, at):
        left = ((1, 0), (4, at + hidden), (2, 2 * hidden), (3, hidden))
        right = ((0, 0), (4, at), (2, 0), (3, 0))
        return first_grads(name, bit, [(left, right, hidden)], [pack, chunks, far, mixed, core_mlp])

    vector = stack("stack0", vector, 1)
    mixed_act, mixed_pre = forward(
        "forward_mlp", [[(i, hidden, hidden), (i, 2 * hidden, wide)] for i in range(2)], [far_act, far_pre]
    )
    down_grad = mlp_grads("down_grad", 2, pack_act, chunks_act, far_act, mixed_act, 0)
    up_grad = mlp_grads("up_grad", 0, pack_pre, chunks_pre, far_pre, mixed_pre, n_mix)
    (mixed3,) = forward(
        "forward3",
        [[(0, s_wide, s_wide), (0, 2 * s_wide, wide), (1, s_wide, s_wide), (2, 0, wide)]],
        [far3, pack3, chunks3],
    )
    vector = stack("stack1", vector, 2)
    n_mix3 = s_wide + wide
    left_qkv = ((1, 0), (3, at1 + n_mix1 + att_core), (2, att_far), (3, at1 + att_core))
    right_qkv = ((4, 0), (7, n_mix3), (6, 0), (7, 0))
    left_out = ((5, 0), (7, n_mix3 + s_wide), (6, 2 * s_wide), (7, s_wide))
    right_out = ((0, 0), (3, at1 + n_mix1), (2, 0), (3, at1))
    qkv_grad = first_grads(
        "qkv_grad",
        1,
        [(left_qkv, right_qkv, n_qkv), (left_out, right_out, n_att)],
        [pack1, chunks1, far1, core_mlp, pack3, chunks3, far3, mixed3],
    )
    both_other = swap(behind(both, qkv_grad[0]), "tensor", 1)
    down_grad = second_grads("down_halve", 2, *down_grad)
    up_grad = second_grads("up_halve", 0, *up_grad)
    result, tokens_grad = call(
        order, join_kernel, "join", 0.02, [((rows, width), BF)] * 2, [both, both_other]
    )
    result, tokens_grad = result.reshape(tokens.shape), tokens_grad.reshape(tokens.shape)
    flip = 4
    while flip < n_dp:
        vector = stack("stack%d" % flip, vector, flip)
        flip *= 2
    ada_grad, ada_bias_grad, qv_grad, proj_grad, fc1_grad, fc2_grad, stay, send, cond_cols, labels_all = call(
        order,
        lambda *refs: gathered_kernel(layout, n_dp, chunk, *refs),
        "gathered",
        0.02,
        [((chunk, ada_cols), F32)]
        + [((n,), F32) for n in (ada_cols, qv_bias.shape[0], width, hidden, width)]
        + [((n_dp, 2 * pad_lanes(columns)), F32)] * 2
        + [((n_dp, columns), F32), ((n_dp, 128), F32)],
        [ada_weight.T, vector],
        [pltpu.VMEM((n_dp, at), F32)],
    )
    qkv_grad = second_grads("qkv_halve", 1, *qkv_grad)
    mine, send = call(
        order,
        middle_kernel,
        "middle",
        0.02,
        [((n_dp, columns), F32)] * 2,
        [stay, swap(send, "tensor", 1)],
    )
    (table_grad,) = call(
        order,
        table_kernel,
        "table",
        0.02,
        [((columns, n_classes), F32)],
        [mine, swap(send, "tensor", 2), cond_cols, labels_all],
    )
    (down_grad,) = last_grads("down_add", 2, [hidden], *down_grad)
    (up_grad,) = last_grads("up_add", 0, [hidden], *up_grad)
    qkv_grad, out_grad = last_grads("qkv_add", 1, [n_qkv, n_att], *qkv_grad)
    return (
        result,
        tokens_grad,
        qkv_grad,
        out_grad,
        up_grad,
        down_grad,
        ada_grad,
        table_grad.T,
        qv_grad,
        proj_grad,
        fc1_grad,
        fc2_grad,
        ada_bias_grad,
    )


def solution(mesh):
    placed = (
        P("dp", None, None, None),
        P("dp"),
        P("dp"),
        P("dp"),
        P(None, "tensor"),
        P(None, "tensor"),
        P("tensor"),
        P(None, "tensor"),
        P("tensor"),
        P(None, "tensor"),
        P(),
        P(None, "tensor"),
        P("tensor"),
        P(None, "tensor"),
        P(),
        P("dp", None, None, None),
    )
    return jax.shard_map(
        shards,
        mesh=mesh,
        in_specs=placed,
        out_specs=(
            P("dp", None, None, None),
            P("dp", None, None, None),
            P("dp", "tensor"),
            P("dp", "tensor"),
            P("dp", "tensor"),
            P("dp", "tensor"),
            P("dp", "tensor"),
            P(None, "tensor"),
            P("tensor"),
            P(),
            P("tensor"),
            P(),
            P("tensor"),
        ),
        check_vma=False,
    )
```

time: 169 us -> 133 us (0.79)
  local copies, waits for them, and re-layouts: 17.9 us -> 0.83 us
  Pallas kernels: 42.5 us -> 27.9 us
  starting transfers between devices: 38.1 us -> 34.7 us
    pallas_call x26 -> x30, Pallas kernels: 42.5 us -> 27.9 us  [call(): pl.pallas_call(whole, out_shape=[jax.ShapeDtypeStruct(s, d) for s, d in [...]
    unnamed x55 -> x17, local copies, waits for them, and re-layouts: 14.1 us -> 0.72 us
    ppermute x44 -> x36, starting transfers between devices: 38.1 us -> 34.7 us  [swap(): return lax.ppermute(value, axis, [(i, i ^ flip) for i in range(size)])]
    reshape x7 -> x1, local copies, waits for them, and re-layouts: 2.24 us -> 0.02 us  [shards(): bias_row = sum((jnp.pad(v.astype(F32), (spots[name][0], n_row - spots[nam...]
    ppermute x44 -> x36, waiting for transfers between devices: 66.1 us -> 65.3 us  [swap(): return lax.ppermute(value, axis, [(i, i ^ flip) for i in range(size)])]
  transfers between devices with their start and end apart: 44 -> 36, of which waited for: 17 -> 18; matrix products, arithmetic and copies ran while one was open for 2% -> 1% of each run, Pallas kernels for 22% -> 20%
where the time goes in v3:
time: 133 us; the launch traced here: 132 us
  waiting for transfers between devices  65.3 us (49%)
  starting transfers between devices  34.7 us (26%)
  Pallas kernels  27.9 us (21%)
  between operations  2.92 us (2%)
    ppermute x36, waiting for transfers between devices, swap(): return lax.ppermute(value, axis, [(i, i ^ flip) for i in range(size)])  65.3 us
    ppermute x36, starting transfers between devices, swap(): return lax.ppermute(value, axis, [(i, i ^ flip) for i in range(size)])  34.7 us
    pallas_call x30, Pallas kernels, call(): pl.pallas_call(whole, out_shape=[jax.ShapeDtypeStruct(s, d) for s, d in [...  27.9 us
  transfers between devices with their start and end apart: 36, of which 18 were waited for; matrix products, arithmetic and copies ran while one was open for 1% of the time, Pallas kernels for 20%

profile of v3, /device:TPU:0, one launch (start us, length us, event | category | flops | bytes accessed | tf_op | source)
XLA Modules:
  0.0 132.4 jit_solution(8145108596139091860)
XLA Ops:
  1.3 0.2 copy-done
  1.7 3.0 %collective-permute-start.1 = (bf16[1,288]{1,0:T(2,128)(2,1)S(1)}, bf16[1,288]{1,0:T(2,128)(2,1)S(1)}, u32[]{:S(2)}, u32[]{:S(2)}) collective-permute-start(bf16[1,288]{1,0:T(2,128)(2,1)S(1)} %copy.31.refs_0_), channel_id=1, source_target_pairs={{0,2},{1,3},{2,0},{3,1},{4,6},{5,7},{6,4},{7,5},{8,10},{9,11},{10,... | collective-permute-start | bytes 1736 | tf_op jit(solution)/shard_map/ppermute | solution.py:30
  5.4 0.8 add_add_fusion
  6.3 0.6 collective-permute-start.2
  6.9 0.8 collective-permute-done.2.refs_3_
  7.7 0.5 collective-permute-start.6
  8.4 0.4 collective-permute-start.5
  8.7 0.4 copy-done.1
  9.1 1.2 modulation.1
  10.3 1.1 collective-permute-start.4
  11.5 0.3 start.1
  11.8 2.3 %collective-permute-done.4.refs_4_ = f32[1,1728]{1,0:T(1,128)S(1)} collective-permute-done((f32[1,1728]{1,0:T(1,128)S(1)}, f32[1,1728]{1,0:T(1,128)S(1)}, u32[]{:S(2)}, u32[]{:S(2)}) %collective-permute-start.4) | collective-permute-done | bytes 6944 | tf_op jit(solution)/shard_map/ppermute | solution.py:30
  14.1 1.1 collective-permute-done.8.refs_5_
  15.4 0.3 collective-permute-start.10
  16.4 4.2 %attention.1 = (bf16[128,1152]{1,0:T(8,128)(2,1)S(1)}, f32[8,1152]{1,0:T(8,128)S(1)}, bf16[128,1152]{1,0:T(8,128)(2,1)S(1)}, bf16[128,864]{1,0:T(8,128)(2,1)S(1)...) custom-call(s32[1]{0:T(128)S(6)} %copy.32.refs_0_, ...), custom_call_target="tpu_custom_call" | custom-call | flops 4400000000 | bytes 1024 | tf_op jit(solution)/shard_map/attention/pallas_call | solution.py:49
  20.7 1.1 collective-permute-start.9
  21.8 1.1 early_back.1
  22.8 1.6 %collective-permute-start.13 = (bf16[128,1280]{1,0:T(8,128)(2,1)S(1)}, bf16[128,1280]{1,0:T(8,128)(2,1)S(1)}, u32[]{:S(2)}, u32[]{:S(2)}) collective-permute-start(bf16[128,1280]{1,0:T(8,128)(2,1)S(1)} %get-tuple-element.167.refs_7_.refs_0_), channel_id=1, source_target_pairs={{0,8},{4,12},{8,0},{12,4},{16,24},{20,28},{24,16},{28,20},{1,9},{5... | collective-permute-start | bytes 983048 | tf_op jit(solution)/shard_map/ppermute | solution.py:30
  24.5 5.3 %collective-permute-done.9.refs_2_ = bf16[128,1152]{1,0:T(8,128)(2,1)S(1)} collective-permute-done((bf16[128,1152]{1,0:T(8,128)(2,1)S(1)}, bf16[128,1152]{1,0:T(8,128)(2,1)S(1)}, u32[]{:S(2)}, u32[]{:S(2)}) %collective-permute-start.9) | collective-permute-done | bytes 294944 | tf_op jit(solution)/shard_map/ppermute | solution.py:30
  29.8 3.1 %mlp.1 = (bf16[128,1152]{1,0:T(8,128)(2,1)S(1)}, bf16[128,2944]{1,0:T(8,128)(2,1)S(1)}, bf16[128,2944]{1,0:T(8,128)(2,1)S(1)}, bf16[128,640]{1,0:T(8,128)(2,1)S(...) custom-call(bf16[128,1152]{1,0:T(8,128)(2,1)S(1)} %get-tuple-element.136.re, ...), custom_call_target="tpu_custom_call" | custom-call | flops 3300000000 | bytes 1024 | tf_op jit(solution)/shard_map/mlp/pallas_call | solution.py:49
  32.9 1.1 collective-permute-start.12
  34.0 1.8 %mlp_tail.1 = (bf16[128,1152]{1,0:T(8,128)(2,1)S(1)}, bf16[128,5632]{1,0:T(8,128)(2,1)S(1)}, f32[2,1152]{1,0:T(2,128)S(1)}, f32[8,128]{1,0:T(8,128)S(1)}) custom-call(bf16[128,2944]{1,0:T(8,128)(2,1)S(1)} %get-tuple-element.190.refs_0_, bf16[128,2944]{1,0:T(8,128)(2,1)S(1)} %get-tuple-element.189.refs_1_.refs_0_, bf16[1152,1152]{1,0:T(8,128)(2,1)S(1)} %copy-done.3, ...), custom_call_target="tpu_custom_call" | custom-call | flops 2200000000 | bytes 1024 | tf_op jit(solution)/shard_map/mlp_tail/pallas_call | solution.py:49
  35.9 1.1 collective-permute-start.15
  37.0 1.5 %collective-permute-start.18 = (bf16[128,2944]{1,0:T(8,128)(2,1)S(1)}, bf16[128,2944]{1,0:T(8,128)(2,1)S(1)}, u32[]{:S(2)}, u32[]{:S(2)}) collective-permute-start(bf16[128,2944]{1,0:T(8,128)(2,1)S(1)} %get-tuple-element.189.refs_1_.refs_0_), channel_id=1, source_target_pairs={{0,4},{4,0},{8,12},{12,8},{16,20},{20,16},{24,28},{28,24},{1,5},{5... | collective-permute-start | bytes 2261000 | tf_op jit(solution)/shard_map/ppermute | solution.py:30
  38.5 2.6 %collective-permute-start.19 = (bf16[128,2944]{1,0:T(8,128)(2,1)S(1)}, bf16[128,2944]{1,0:T(8,128)(2,1)S(1)}, u32[]{:S(2)}, u32[]{:S(2)}) collective-permute-start(bf16[128,2944]{1,0:T(8,128)(2,1)S(1)} %get-tuple-element.190.refs_0_), channel_id=1, source_target_pairs={{0,16},{4,20},{8,24},{12,28},{16,0},{20,4},{24,8},{28,12},{1,17},{... | collective-permute-start | bytes 2261000 | tf_op jit(solution)/shard_map/ppermute | solution.py:30
  41.1 1.9 %collective-permute-done.12.refs_2_ = bf16[128,1152]{1,0:T(8,128)(2,1)S(1)} collective-permute-done((bf16[128,1152]{1,0:T(8,128)(2,1)S(1)}, bf16[128,1152]{1,0:T(8,128)(2,1)S(1)}, u32[]{:S(2)}, u32[]{:S(2)}) %collective-permute-start.12) | collective-permute-done | bytes 294944 | tf_op jit(solution)/shard_map/ppermute | solution.py:30
  42.9 4.3 %attention_back.1 = (bf16[128,1152]{1,0:T(8,128)(2,1)S(1)}, f32[128,1152]{1,0:T(8,128)S(1)}, bf16[128,1152]{1,0:T(8,128)(2,1)S(1)}, bf16[128,1792]{1,0:T(8,128)(...) custom-call(s32[1]{0:T(128)S(6)} %copy.32.refs_0_, bf16[128,1152]{1,0:T(8,128)(2,1)S(1)} %get-tuple-element.156.refs_1_, ...), custom_call_target="tpu_custom_call" | custom-call | flops 5500000256 | bytes 1024 | tf_op jit(solution)/shard_map/attention_back/pallas_call | solution.py:49
  47.2 1.1 collective-permute-start.14
  48.5 1.6 %collective-permute-start.17 = (bf16[128,2432]{1,0:T(8,128)(2,1)S(1)}, bf16[128,2432]{1,0:T(8,128)(2,1)S(1)}, u32[]{:S(2)}, u32[]{:S(2)}) collective-permute-start(bf16[128,2432]{1,0:T(8,128)(2,1)S(1)} %get-tuple-element.187.refs_1_.refs_4_), channel_id=1, source_target_pairs={{0,8},{4,12},{8,0},{12,4},{16,24},{20,28},{24,16},{28,20},{1,9},{5... | collective-permute-start | bytes 1867784 | tf_op jit(solution)/shard_map/ppermute | solution.py:30
  50.1 0.3 output.1
  50.4 3.6 %collective-permute-done.14.refs_2_ = bf16[128,1152]{1,0:T(8,128)(2,1)S(1)} collective-permute-done((bf16[128,1152]{1,0:T(8,128)(2,1)S(1)}, bf16[128,1152]{1,0:T(8,128)(2,1)S(1)}, u32[]{:S(2)}, u32[]{:S(2)}) %collective-permute-start.14) | collective-permute-done | bytes 294944 | tf_op jit(solution)/shard_map/ppermute | solution.py:30
  54.0 0.5 input_back.1
  54.6 1.3 collective-permute-done.20.refs_2_
  55.9 1.6 %collective-permute-start.21 = (f32[1,7424]{1,0:T(1,128)S(1)}, f32[1,7424]{1,0:T(1,128)S(1)}, u32[]{:S(2)}, u32[]{:S(2)}) collective-permute-start(f32[1,7424]{1,0:T(1,128)S(1)} %get-tuple-element.194.refs_0_), channel_id=1, source_target_pairs={{0,4},{4,0},{8,12},{12,8},{16,20},{20,16},{24,28},{28,24},{1,5},{5... | collective-permute-start | bytes 89096 | tf_op jit(solution)/shard_map/ppermute | solution.py:30
  57.5 2.4 %collective-permute-done.21.refs_1_ = f32[1,7424]{1,0:T(1,128)S(1)} collective-permute-done((f32[1,7424]{1,0:T(1,128)S(1)}, f32[1,7424]{1,0:T(1,128)S(1)}, u32[]{:S(2)}, u32[]{:S(2)}) %collective-permute-start.21) | collective-permute-done | bytes 29728 | tf_op jit(solution)/shard_map/ppermute | solution.py:30
  59.9 14.4 %collective-permute-done.19.refs_0_.refs_2_ = bf16[128,2944]{1,0:T(8,128)(2,1)S(1)} collective-permute-done((bf16[128,2944]{1,0:T(8,128)(2,1)S(1)}, bf16[128,2944]{1,0:T(8,128)(2,1)S(1)}, u32[]{:S(2)}, u32[]{:S(2)}) %collective-permute-start.19) | collective-permute-done | bytes 753696 | tf_op jit(solution)/shard_map/ppermute | solution.py:30
  74.4 0.5 collective-permute-start.22
  74.9 1.3 collective-permute-done.23.refs_3_
  76.2 1.1 down_grad.1
  77.3 1.1 up_grad.1
  78.5 0.2 collective-permute-start.24
  78.7 0.6 collective-permute-start.25
  79.3 0.5 collective-permute-start.28
  79.8 1.4 %collective-permute-start.27 = (bf16[2,144,1152]{2,1,0:T(8,128)(2,1)S(1)}, bf16[2,144,1152]{2,1,0:T(8,128)(2,1)S(1)}, u32[]{:S(2)}, u32[]{:S(2)}) collective-permute-start(bf16[2,144,1152]{2,1,0:T(8,128)(2,1)S(1)} %get-tuple-element.209), channel_id=1, source_target_pairs={{0,8},{4,12},{8,0},{12,4},{16,24},{20,28},{24,16},{28,20},{1,9},{5... | collective-permute-start | bytes 1990664 | tf_op jit(solution)/shard_map/ppermute | solution.py:30
  81.2 2.2 %collective-permute-done.25.refs_1_ = f32[2,7424]{1,0:T(2,128)S(1)} collective-permute-done((f32[2,7424]{1,0:T(2,128)S(1)}, f32[2,7424]{1,0:T(2,128)S(1)}, u32[]{:S(2)}, u32[]{:S(2)}) %collective-permute-start.25) | collective-permute-done | bytes 59424 | tf_op jit(solution)/shard_map/ppermute | solution.py:30
  83.5 1.4 %qkv_grad.1 = (f32[2,144,1152]{2,1,0:T(8,128)S(1)}, bf16[2,144,1152]{2,1,0:T(8,128)(2,1)S(1)}, f32[8,128]{1,0:T(8,128)S(1)}) custom-call(bf16[128,1280]{1,0:T(8,128)(2,1)S(1)} %get-tuple-element.167.refs_7_.refs_0_, bf16[128,640]{1,0:T(8,128)(2,1)S(1)} %get-tuple-element.168.refs_8_.refs_1_, bf16[128,1280]{1,0:T(8,128)(2,1)S(1)} %collective-permute-done.13.refs_6_.refs_2_, ...), custom_call_target="tpu_custom_call" | custom-call | flops 22000000 | bytes 1024 | tf_op jit(solution)/shard_map/qkv_grad/pallas_call | solution.py:49
  85.0 2.9 %collective-permute-start.30 = (f32[4,7424]{1,0:T(4,128)S(1)}, f32[4,7424]{1,0:T(4,128)S(1)}, u32[]{:S(2)}, u32[]{:S(2)}) collective-permute-start(f32[4,7424]{1,0:T(4,128)S(1)} %get-tuple-element.218.refs_0_), channel_id=1, source_target_pairs={{0,16},{4,20},{8,24},{12,28},{16,0},{20,4},{24,8},{28,12},{1,17},{... | collective-permute-start | bytes 356360 | tf_op jit(solution)/shard_map/ppermute | solution.py:30
  87.9 9.1 %collective-permute-done.28.refs_1_ = bf16[2,144,1152]{2,1,0:T(8,128)(2,1)S(1)} collective-permute-done((bf16[2,144,1152]{2,1,0:T(8,128)(2,1)S(1)}, bf16[2,144,1152]{2,1,0:T(8,128)(2,1)S(1)}, u32[]{:S(2)}, u32[]{:S(2)}) %collective-permute-start.28) | collective-permute-done | bytes 663584 | tf_op jit(solution)/shard_map/ppermute | solution.py:30
  97.2 2.5 %collective-permute-done.27.refs_1_ = bf16[2,144,1152]{2,1,0:T(8,128)(2,1)S(1)} collective-permute-done((bf16[2,144,1152]{2,1,0:T(8,128)(2,1)S(1)}, bf16[2,144,1152]{2,1,0:T(8,128)(2,1)S(1)}, u32[]{:S(2)}, u32[]{:S(2)}) %collective-permute-start.27) | collective-permute-done | bytes 663584 | tf_op jit(solution)/shard_map/ppermute | solution.py:30
  99.8 2.0 %collective-permute-start.32 = (bf16[144,1152]{1,0:T(8,128)(2,1)S(1)}, bf16[144,1152]{1,0:T(8,128)(2,1)S(1)}, u32[]{:S(2)}, u32[]{:S(2)}) collective-permute-start(bf16[144,1152]{1,0:T(8,128)(2,1)S(1)} %get-tuple-element.226), channel_id=1, source_target_pairs={{0,16},{4,20},{8,24},{12,28},{16,0},{20,4},{24,8},{28,12},{1,17},{... | collective-permute-start | bytes 995336 | tf_op jit(solution)/shard_map/ppermute | solution.py:30
  101.9 2.1 %collective-permute-start.33 = (bf16[144,1152]{1,0:T(8,128)(2,1)S(1)}, bf16[144,1152]{1,0:T(8,128)(2,1)S(1)}, u32[]{:S(2)}, u32[]{:S(2)}) collective-permute-start(bf16[144,1152]{1,0:T(8,128)(2,1)S(1)} %get-tuple-element.228), channel_id=1, source_target_pairs={{0,8},{4,12},{8,0},{12,4},{16,24},{20,28},{24,16},{28,20},{1,9},{5... | collective-permute-start | bytes 995336 | tf_op jit(solution)/shard_map/ppermute | solution.py:30
  104.0 1.1 join.1
  105.1 1.6 %gathered.1 = (f32[144,1728]{1,0:T(8,128)}, f32[1728]{0:T(1024)}, f32[576]{0:T(1024)}, f32[1152]{0:T(1024)}, f32[1152]{0:T(1024)}, /*index=5*/f32[1152]{0:T(1024...) custom-call(bf16[1728,1152]{1,0:T(8,128)(2,1)S(1)} %bitcast.13, ...), custom_call_target="tpu_custom_call" | custom-call | flops 22000000 | bytes 1024 | tf_op jit(solution)/shard_map/gathered/pallas_call | solution.py:49
  106.7 3.7 %collective-permute-done.29.refs_1_ = bf16[2,144,1152]{2,1,0:T(8,128)(2,1)S(1)} collective-permute-done((bf16[2,144,1152]{2,1,0:T(8,128)(2,1)S(1)}, bf16[2,144,1152]{2,1,0:T(8,128)(2,1)S(1)}, u32[]{:S(2)}, u32[]{:S(2)}) %collective-permute-start.29) | collective-permute-done | bytes 663584 | tf_op jit(solution)/shard_map/ppermute | solution.py:30
  110.5 3.5 %collective-permute-start.31 = (bf16[144,1152]{1,0:T(8,128)(2,1)S(1)}, bf16[144,1152]{1,0:T(8,128)(2,1)S(1)}, u32[]{:S(2)}, u32[]{:S(2)}) collective-permute-start(bf16[144,1152]{1,0:T(8,128)(2,1)S(1)} %get-tuple-element.224), channel_id=1, source_target_pairs={{0,16},{4,20},{8,24},{12,28},{16,0},{20,4},{24,8},{28,12},{1,17},{... | collective-permute-start | bytes 995336 | tf_op jit(solution)/shard_map/ppermute | solution.py:30
  114.0 1.2 collective-permute-done.34.refs_1_
  115.2 1.0 collective-permute-start.35
  116.3 2.7 %collective-permute-done.35.refs_1_ = f32[8,288]{1,0:T(8,128)S(1)} collective-permute-done((f32[8,288]{1,0:T(8,128)S(1)}, f32[8,288]{1,0:T(8,128)S(1)}, u32[]{:S(2)}, u32[]{:S(2)}) %collective-permute-start.35) | collective-permute-done | bytes 9248 | tf_op jit(solution)/shard_map/ppermute | solution.py:30
  118.9 1.0 table.1
  120.0 0.9 down_add.1
  120.9 4.5 %collective-permute-done.32.refs_1_ = bf16[144,1152]{1,0:T(8,128)(2,1)S(1)} collective-permute-done((bf16[144,1152]{1,0:T(8,128)(2,1)S(1)}, bf16[144,1152]{1,0:T(8,128)(2,1)S(1)}, u32[]{:S(2)}, u32[]{:S(2)}) %collective-permute-start.32) | collective-permute-done | bytes 331808 | tf_op jit(solution)/shard_map/ppermute | solution.py:30
  125.4 0.9 up_add.1
  126.3 5.2 %collective-permute-done.31.refs_1_ = bf16[144,1152]{1,0:T(8,128)(2,1)S(1)} collective-permute-done((bf16[144,1152]{1,0:T(8,128)(2,1)S(1)}, bf16[144,1152]{1,0:T(8,128)(2,1)S(1)}, u32[]{:S(2)}, u32[]{:S(2)}) %collective-permute-start.31) | collective-permute-done | bytes 331808 | tf_op jit(solution)/shard_map/ppermute | solution.py:30
  131.4 1.0 qkv_add.1
  (58 shorter events, 2.1 us)
Async XLA Ops:
  0.6 0.9 copy-start
  1.7 4.6 %collective-permute-start.1 = (bf16[1,288]{1,0:T(2,128)(2,1)S(1)}, bf16[1,288]{1,0:T(2,128)(2,1)S(1)}, u32[]{:S(2)}, u32[]{:S(2)}) collective-permute-start(bf16[1,288]{1,0:T(2,128)(2,1)S(1)} %copy.31.refs_0_), channel_id=1, source_target_pairs={{0,2},{1,3},{2,0},{3,1},{4,6},{5,7},{6,4},{7,5},{8,10},{9,11},{10,... | collective-permute-start | bytes 1736 | tf_op jit(solution)/shard_map/ppermute | solution.py:30
  4.7 2.2 %collective-permute-start = (bf16[1,288]{1,0:T(2,128)(2,1)S(1)}, bf16[1,288]{1,0:T(2,128)(2,1)S(1)}, u32[]{:S(2)}, u32[]{:S(2)}) collective-permute-start(bf16[1,288]{1,0:T(2,128)(2,1)S(1)} %copy.31.refs_0_), channel_id=1, source_target_pairs={{0,1},{1,0},{2,3},{3,2},{4,5},{5,4},{6,7},{7,6},{8,9},{9,8},{10,11... | collective-permute-start | bytes 1736 | tf_op jit(solution)/shard_map/ppermute | solution.py:30
  6.2 1.6 %copy-start.4 = (bf16[1152,864]{0,1:T(8,128)(2,1)S(1)}, bf16[1152,864]{0,1:T(8,128)(2,1)}, u32[]{:S(2)}) copy-start(bf16[1152,864]{0,1:T(8,128)(2,1)} %param.24) | copy-start | bytes 5971972
  6.2 2.1 %copy-start.5 = (bf16[1152,288]{0,1:T(8,128)(2,1)S(1)}, bf16[1152,288]{0,1:T(8,128)(2,1)}, u32[]{:S(2)}) copy-start(bf16[1152,288]{0,1:T(8,128)(2,1)} %param.26) | copy-start | bytes 1990660
  6.2 2.9 %copy-start.1 = (bf16[1152,1728]{0,1:T(8,128)(2,1)S(1)}, bf16[1152,1728]{0,1:T(8,128)(2,1)}, u32[]{:S(2)}) copy-start(bf16[1152,1728]{0,1:T(8,128)(2,1)} %param.22) | copy-start | bytes 11943940
  6.3 1.4 %collective-permute-start.2 = (bf16[1,288]{1,0:T(2,128)(2,1)S(1)}, bf16[1,288]{1,0:T(2,128)(2,1)S(1)}, u32[]{:S(2)}, u32[]{:S(2)}) collective-permute-start(bf16[1,288]{1,0:T(2,128)(2,1)S(1)} %collective-permute-done.1.refs_2_), channel_id=1, source_target_pairs={{0,1},{1,0},{2,3},{3,2},{4,5},{5,4},{6,7},{7,6},{8,9},{9,8},{10,11... | collective-permute-start | bytes 1736 | tf_op jit(solution)/shard_map/ppermute | solution.py:30
  7.7 6.3 %collective-permute-start.6 = (bf16[864,1152]{1,0:T(8,128)(2,1)S(1)}, bf16[864,1152]{1,0:T(8,128)(2,1)S(1)}, u32[]{:S(2)}, u32[]{:S(2)}) collective-permute-start(bf16[864,1152]{1,0:T(8,128)(2,1)S(1)} %bitcast.14), channel_id=1, source_target_pairs={{0,1},{1,0},{2,3},{3,2},{4,5},{5,4},{6,7},{7,6},{8,9},{9,8},{10,11... | collective-permute-start | bytes 5971976 | tf_op jit(solution)/shard_map/ppermute | solution.py:30
  8.2 5.8 %collective-permute-start.7 = (bf16[288,1152]{1,0:T(8,128)(2,1)S(1)}, bf16[288,1152]{1,0:T(8,128)(2,1)S(1)}, u32[]{:S(2)}, u32[]{:S(2)}) collective-permute-start(bf16[288,1152]{1,0:T(8,128)(2,1)S(1)} %bitcast.17), channel_id=1, source_target_pairs={{0,1},{1,0},{2,3},{3,2},{4,5},{5,4},{6,7},{7,6},{8,9},{9,8},{10,11... | collective-permute-start | bytes 1990664 | tf_op jit(solution)/shard_map/ppermute | solution.py:30
  8.4 5.7 %collective-permute-start.5 = (f32[1,6528]{1,0:T(1,128)S(1)}, f32[1,6528]{1,0:T(1,128)S(1)}, u32[]{:S(2)}, u32[]{:S(2)}) collective-permute-start(f32[1,6528]{1,0:T(1,128)S(1)} %reshape.43.refs_1_.refs_6_.refs_8_.refs_4_), channel_id=1, source_target_pairs={{0,1},{1,0},{2,3},{3,2},{4,5},{5,4},{6,7},{7,6},{8,9},{9,8},{10,11... | collective-permute-start | bytes 78344 | tf_op jit(solution)/shard_map/ppermute | solution.py:30
  9.1 2.3 %copy-start.6 = (bf16[1,16,16,1152]{3,2,1,0:T(8,128)(2,1)S(1)}, bf16[1,16,16,1152]{3,2,1,0:T(8,128)(2,1)}, u32[]{:S(2)}) copy-start(bf16[1,16,16,1152]{3,2,1,0:T(8,128)(2,1)} %param.17) | copy-start | bytes 1769476
  9.1 2.3 %copy-start.7 = (bf16[1,16,16,1152]{3,2,1,0:T(8,128)(2,1)S(1)}, bf16[1,16,16,1152]{3,2,1,0:T(8,128)(2,1)}, u32[]{:S(2)}) copy-start(bf16[1,16,16,1152]{3,2,1,0:T(8,128)(2,1)} %param.32) | copy-start | bytes 1769476
  9.1 6.2 %copy-start.3 = (bf16[1152,1152]{1,0:T(8,128)(2,1)S(1)}, bf16[1152,1152]{1,0:T(8,128)(2,1)}, u32[]{:S(2)}) copy-start(bf16[1152,1152]{1,0:T(8,128)(2,1)} %refs_2_.1) | copy-start | bytes 7962628
  10.3 3.7 %collective-permute-start.4 = (f32[1,1728]{1,0:T(1,128)S(1)}, f32[1,1728]{1,0:T(1,128)S(1)}, u32[]{:S(2)}, u32[]{:S(2)}) collective-permute-start(f32[1,1728]{1,0:T(1,128)S(1)} %get-tuple-element.138.refs_2_), channel_id=1, source_target_pairs={{0,2},{1,3},{2,0},{3,1},{4,6},{5,7},{6,4},{7,5},{8,10},{9,11},{10,... | collective-permute-start | bytes 20744 | tf_op jit(solution)/shard_map/ppermute | solution.py:30
  11.4 2.7 %collective-permute-start.3 = (f32[1,1728]{1,0:T(1,128)S(1)}, f32[1,1728]{1,0:T(1,128)S(1)}, u32[]{:S(2)}, u32[]{:S(2)}) collective-permute-start(f32[1,1728]{1,0:T(1,128)S(1)} %get-tuple-element.138.refs_2_), channel_id=1, source_target_pairs={{0,1},{1,0},{2,3},{3,2},{4,5},{5,4},{6,7},{7,6},{8,9},{9,8},{10,11... | collective-permute-start | bytes 20744 | tf_op jit(solution)/shard_map/ppermute | solution.py:30
  11.5 4.0 %copy-start.2 = (bf16[1152,1152]{1,0:T(8,128)(2,1)S(1)}, bf16[1152,1152]{1,0:T(8,128)(2,1)}, u32[]{:S(2)}) copy-start(bf16[1152,1152]{1,0:T(8,128)(2,1)} %refs_4_.1) | copy-start | bytes 7962628
  14.0 1.2 collective-permute-start.8
  15.3 6.5 %collective-permute-start.11 = (bf16[1152,1152]{1,0:T(8,128)(2,1)S(1)}, bf16[1152,1152]{1,0:T(8,128)(2,1)S(1)}, u32[]{:S(2)}, u32[]{:S(2)}) collective-permute-start(bf16[1152,1152]{1,0:T(8,128)(2,1)S(1)} %copy-done.3), channel_id=1, source_target_pairs={{0,1},{1,0},{2,3},{3,2},{4,5},{5,4},{6,7},{7,6},{8,9},{9,8},{10,11... | collective-permute-start | bytes 7962632 | tf_op jit(solution)/shard_map/ppermute | solution.py:30
  15.4 14.4 %collective-permute-start.10 = (bf16[1152,1152]{1,0:T(8,128)(2,1)S(1)}, bf16[1152,1152]{1,0:T(8,128)(2,1)S(1)}, u32[]{:S(2)}, u32[]{:S(2)}) collective-permute-start(bf16[1152,1152]{1,0:T(8,128)(2,1)S(1)} %copy-done.2), channel_id=1, source_target_pairs={{0,1},{1,0},{2,3},{3,2},{4,5},{5,4},{6,7},{7,6},{8,9},{9,8},{10,11... | collective-permute-start | bytes 7962632 | tf_op jit(solution)/shard_map/ppermute | solution.py:30
  20.7 9.2 %collective-permute-start.9 = (bf16[128,1152]{1,0:T(8,128)(2,1)S(1)}, bf16[128,1152]{1,0:T(8,128)(2,1)S(1)}, u32[]{:S(2)}, u32[]{:S(2)}) collective-permute-start(bf16[128,1152]{1,0:T(8,128)(2,1)S(1)} %get-tuple-element.143.refs_1_), channel_id=1, source_target_pairs={{0,2},{1,3},{2,0},{3,1},{4,6},{5,7},{6,4},{7,5},{8,10},{9,11},{10,... | collective-permute-start | bytes 884744 | tf_op jit(solution)/shard_map/ppermute | solution.py:30
  22.8 11.2 %collective-permute-start.13 = (bf16[128,1280]{1,0:T(8,128)(2,1)S(1)}, bf16[128,1280]{1,0:T(8,128)(2,1)S(1)}, u32[]{:S(2)}, u32[]{:S(2)}) collective-permute-start(bf16[128,1280]{1,0:T(8,128)(2,1)S(1)} %get-tuple-element.167.refs_7_.refs_0_), channel_id=1, source_target_pairs={{0,8},{4,12},{8,0},{12,4},{16,24},{20,28},{24,16},{28,20},{1,9},{5... | collective-permute-start | bytes 983048 | tf_op jit(solution)/shard_map/ppermute | solution.py:30
  32.9 10.0 %collective-permute-start.12 = (bf16[128,1152]{1,0:T(8,128)(2,1)S(1)}, bf16[128,1152]{1,0:T(8,128)(2,1)S(1)}, u32[]{:S(2)}, u32[]{:S(2)}) collective-permute-start(bf16[128,1152]{1,0:T(8,128)(2,1)S(1)} %get-tuple-element.156.refs_1_), channel_id=1, source_target_pairs={{0,2},{1,3},{2,0},{3,1},{4,6},{5,7},{6,4},{7,5},{8,10},{9,11},{10,... | collective-permute-start | bytes 884744 | tf_op jit(solution)/shard_map/ppermute | solution.py:30
  35.8 40.4 %collective-permute-start.16 = (bf16[128,5632]{1,0:T(8,128)(2,1)S(1)}, bf16[128,5632]{1,0:T(8,128)(2,1)S(1)}, u32[]{:S(2)}, u32[]{:S(2)}) collective-permute-start(bf16[128,5632]{1,0:T(8,128)(2,1)S(1)} %get-tuple-element.186), channel_id=1, source_target_pairs={{0,1},{1,0},{2,3},{3,2},{4,5},{5,4},{6,7},{7,6},{8,9},{9,8},{10,11... | collective-permute-start | bytes 4325384 | tf_op jit(solution)/shard_map/ppermute | solution.py:30
  35.9 12.6 %collective-permute-start.15 = (bf16[128,1152]{1,0:T(8,128)(2,1)S(1)}, bf16[128,1152]{1,0:T(8,128)(2,1)S(1)}, u32[]{:S(2)}, u32[]{:S(2)}) collective-permute-start(bf16[128,1152]{1,0:T(8,128)(2,1)S(1)} %get-tuple-element.175.refs_2_), channel_id=1, source_target_pairs={{0,2},{1,3},{2,0},{3,1},{4,6},{5,7},{6,4},{7,5},{8,10},{9,11},{10,... | collective-permute-start | bytes 884744 | tf_op jit(solution)/shard_map/ppermute | solution.py:30
  37.0 22.9 %collective-permute-start.18 = (bf16[128,2944]{1,0:T(8,128)(2,1)S(1)}, bf16[128,2944]{1,0:T(8,128)(2,1)S(1)}, u32[]{:S(2)}, u32[]{:S(2)}) collective-permute-start(bf16[128,2944]{1,0:T(8,128)(2,1)S(1)} %get-tuple-element.189.refs_1_.refs_0_), channel_id=1, source_target_pairs={{0,4},{4,0},{8,12},{12,8},{16,20},{20,16},{24,28},{28,24},{1,5},{5... | collective-permute-start | bytes 2261000 | tf_op jit(solution)/shard_map/ppermute | solution.py:30
  38.5 35.8 %collective-permute-start.19 = (bf16[128,2944]{1,0:T(8,128)(2,1)S(1)}, bf16[128,2944]{1,0:T(8,128)(2,1)S(1)}, u32[]{:S(2)}, u32[]{:S(2)}) collective-permute-start(bf16[128,2944]{1,0:T(8,128)(2,1)S(1)} %get-tuple-element.190.refs_0_), channel_id=1, source_target_pairs={{0,16},{4,20},{8,24},{12,28},{16,0},{20,4},{24,8},{28,12},{1,17},{... | collective-permute-start | bytes 2261000 | tf_op jit(solution)/shard_map/ppermute | solution.py:30
  47.2 6.8 %collective-permute-start.14 = (bf16[128,1152]{1,0:T(8,128)(2,1)S(1)}, bf16[128,1152]{1,0:T(8,128)(2,1)S(1)}, u32[]{:S(2)}, u32[]{:S(2)}) collective-permute-start(bf16[128,1152]{1,0:T(8,128)(2,1)S(1)} %get-tuple-element.171.refs_1_), channel_id=1, source_target_pairs={{0,2},{1,3},{2,0},{3,1},{4,6},{5,7},{6,4},{7,5},{8,10},{9,11},{10,... | collective-permute-start | bytes 884744 | tf_op jit(solution)/shard_map/ppermute | solution.py:30
  48.5 29.9 %collective-permute-start.17 = (bf16[128,2432]{1,0:T(8,128)(2,1)S(1)}, bf16[128,2432]{1,0:T(8,128)(2,1)S(1)}, u32[]{:S(2)}, u32[]{:S(2)}) collective-permute-start(bf16[128,2432]{1,0:T(8,128)(2,1)S(1)} %get-tuple-element.187.refs_1_.refs_4_), channel_id=1, source_target_pairs={{0,8},{4,12},{8,0},{12,4},{16,24},{20,28},{24,16},{28,20},{1,9},{5... | collective-permute-start | bytes 1867784 | tf_op jit(solution)/shard_map/ppermute | solution.py:30
  54.5 1.3 %collective-permute-start.20 = (f32[16,1152]{1,0:T(8,128)S(1)}, f32[16,1152]{1,0:T(8,128)S(1)}, u32[]{:S(2)}, u32[]{:S(2)}) collective-permute-start(f32[16,1152]{1,0:T(8,128)S(1)} %get-tuple-element.191.refs_1_), channel_id=1, source_target_pairs={{0,1},{1,0},{2,3},{3,2},{4,5},{5,4},{6,7},{7,6},{8,9},{9,8},{10,11... | collective-permute-start | bytes 221192 | tf_op jit(solution)/shard_map/ppermute | solution.py:30
  55.9 3.9 %collective-permute-start.21 = (f32[1,7424]{1,0:T(1,128)S(1)}, f32[1,7424]{1,0:T(1,128)S(1)}, u32[]{:S(2)}, u32[]{:S(2)}) collective-permute-start(f32[1,7424]{1,0:T(1,128)S(1)} %get-tuple-element.194.refs_0_), channel_id=1, source_target_pairs={{0,4},{4,0},{8,12},{12,8},{16,20},{20,16},{24,28},{28,24},{1,5},{5... | collective-permute-start | bytes 89096 | tf_op jit(solution)/shard_map/ppermute | solution.py:30
  74.3 1.9 %collective-permute-start.23 = (bf16[128,1792]{1,0:T(8,128)(2,1)S(1)}, bf16[128,1792]{1,0:T(8,128)(2,1)S(1)}, u32[]{:S(2)}, u32[]{:S(2)}) collective-permute-start(bf16[128,1792]{1,0:T(8,128)(2,1)S(1)} %get-tuple-element.198), channel_id=1, source_target_pairs={{0,1},{1,0},{2,3},{3,2},{4,5},{5,4},{6,7},{7,6},{8,9},{9,8},{10,11... | collective-permute-start | bytes 1376264 | tf_op jit(solution)/shard_map/ppermute | solution.py:30
  74.4 2.9 %collective-permute-start.22 = (bf16[128,1792]{1,0:T(8,128)(2,1)S(1)}, bf16[128,1792]{1,0:T(8,128)(2,1)S(1)}, u32[]{:S(2)}, u32[]{:S(2)}) collective-permute-start(bf16[128,1792]{1,0:T(8,128)(2,1)S(1)} %get-tuple-element.197), channel_id=1, source_target_pairs={{0,1},{1,0},{2,3},{3,2},{4,5},{5,4},{6,7},{7,6},{8,9},{9,8},{10,11... | collective-permute-start | bytes 1376264 | tf_op jit(solution)/shard_map/ppermute | solution.py:30
  78.5 5.0 %collective-permute-start.24 = (bf16[128,3072]{1,0:T(8,128)(2,1)S(1)}, bf16[128,3072]{1,0:T(8,128)(2,1)S(1)}, u32[]{:S(2)}, u32[]{:S(2)}) collective-permute-start(bf16[128,3072]{1,0:T(8,128)(2,1)S(1)} %get-tuple-element.202), channel_id=1, source_target_pairs={{0,1},{1,0},{2,3},{3,2},{4,5},{5,4},{6,7},{7,6},{8,9},{9,8},{10,11... | collective-permute-start | bytes 2359304 | tf_op jit(solution)/shard_map/ppermute | solution.py:30
  78.7 4.8 %collective-permute-start.25 = (f32[2,7424]{1,0:T(2,128)S(1)}, f32[2,7424]{1,0:T(2,128)S(1)}, u32[]{:S(2)}, u32[]{:S(2)}) collective-permute-start(f32[2,7424]{1,0:T(2,128)S(1)} %get-tuple-element.203.refs_0_), channel_id=1, source_target_pairs={{0,8},{4,12},{8,0},{12,4},{16,24},{20,28},{24,16},{28,20},{1,9},{5... | collective-permute-start | bytes 178184 | tf_op jit(solution)/shard_map/ppermute | solution.py:30
  79.3 17.8 %collective-permute-start.28 = (bf16[2,144,1152]{2,1,0:T(8,128)(2,1)S(1)}, bf16[2,144,1152]{2,1,0:T(8,128)(2,1)S(1)}, u32[]{:S(2)}, u32[]{:S(2)}) collective-permute-start(bf16[2,144,1152]{2,1,0:T(8,128)(2,1)S(1)} %get-tuple-element.211), channel_id=1, source_target_pairs={{0,4},{4,0},{8,12},{12,8},{16,20},{20,16},{24,28},{28,24},{1,5},{5... | collective-permute-start | bytes 1990664 | tf_op jit(solution)/shard_map/ppermute | solution.py:30
  79.8 19.9 %collective-permute-start.27 = (bf16[2,144,1152]{2,1,0:T(8,128)(2,1)S(1)}, bf16[2,144,1152]{2,1,0:T(8,128)(2,1)S(1)}, u32[]{:S(2)}, u32[]{:S(2)}) collective-permute-start(bf16[2,144,1152]{2,1,0:T(8,128)(2,1)S(1)} %get-tuple-element.209), channel_id=1, source_target_pairs={{0,8},{4,12},{8,0},{12,4},{16,24},{20,28},{24,16},{28,20},{1,9},{5... | collective-permute-start | bytes 1990664 | tf_op jit(solution)/shard_map/ppermute | solution.py:30
  84.9 25.5 %collective-permute-start.29 = (bf16[2,144,1152]{2,1,0:T(8,128)(2,1)S(1)}, bf16[2,144,1152]{2,1,0:T(8,128)(2,1)S(1)}, u32[]{:S(2)}, u32[]{:S(2)}) collective-permute-start(bf16[2,144,1152]{2,1,0:T(8,128)(2,1)S(1)} %get-tuple-element.217), channel_id=1, source_target_pairs={{0,4},{4,0},{8,12},{12,8},{16,20},{20,16},{24,28},{28,24},{1,5},{5... | collective-permute-start | bytes 1990664 | tf_op jit(solution)/shard_map/ppermute | solution.py:30
  85.0 19.0 %collective-permute-start.26 = (bf16[128,2304]{1,0:T(8,128)(2,1)S(1)}, bf16[128,2304]{1,0:T(8,128)(2,1)S(1)}, u32[]{:S(2)}, u32[]{:S(2)}) collective-permute-start(bf16[128,2304]{1,0:T(8,128)(2,1)S(1)} %get-tuple-element.207.refs_0_), channel_id=1, source_target_pairs={{0,1},{1,0},{2,3},{3,2},{4,5},{5,4},{6,7},{7,6},{8,9},{9,8},{10,11... | collective-permute-start | bytes 1769480 | tf_op jit(solution)/shard_map/ppermute | solution.py:30
  85.0 20.0 %collective-permute-start.30 = (f32[4,7424]{1,0:T(4,128)S(1)}, f32[4,7424]{1,0:T(4,128)S(1)}, u32[]{:S(2)}, u32[]{:S(2)}) collective-permute-start(f32[4,7424]{1,0:T(4,128)S(1)} %get-tuple-element.218.refs_0_), channel_id=1, source_target_pairs={{0,16},{4,20},{8,24},{12,28},{16,0},{20,4},{24,8},{28,12},{1,17},{... | collective-permute-start | bytes 356360 | tf_op jit(solution)/shard_map/ppermute | solution.py:30
  99.8 25.5 %collective-permute-start.32 = (bf16[144,1152]{1,0:T(8,128)(2,1)S(1)}, bf16[144,1152]{1,0:T(8,128)(2,1)S(1)}, u32[]{:S(2)}, u32[]{:S(2)}) collective-permute-start(bf16[144,1152]{1,0:T(8,128)(2,1)S(1)} %get-tuple-element.226), channel_id=1, source_target_pairs={{0,16},{4,20},{8,24},{12,28},{16,0},{20,4},{24,8},{28,12},{1,17},{... | collective-permute-start | bytes 995336 | tf_op jit(solution)/shard_map/ppermute | solution.py:30
  101.9 18.1 %collective-permute-start.33 = (bf16[144,1152]{1,0:T(8,128)(2,1)S(1)}, bf16[144,1152]{1,0:T(8,128)(2,1)S(1)}, u32[]{:S(2)}, u32[]{:S(2)}) collective-permute-start(bf16[144,1152]{1,0:T(8,128)(2,1)S(1)} %get-tuple-element.228), channel_id=1, source_target_pairs={{0,8},{4,12},{8,0},{12,4},{16,24},{20,28},{24,16},{28,20},{1,9},{5... | collective-permute-start | bytes 995336 | tf_op jit(solution)/shard_map/ppermute | solution.py:30
  110.5 20.9 %collective-permute-start.31 = (bf16[144,1152]{1,0:T(8,128)(2,1)S(1)}, bf16[144,1152]{1,0:T(8,128)(2,1)S(1)}, u32[]{:S(2)}, u32[]{:S(2)}) collective-permute-start(bf16[144,1152]{1,0:T(8,128)(2,1)S(1)} %get-tuple-element.224), channel_id=1, source_target_pairs={{0,16},{4,20},{8,24},{12,28},{16,0},{20,4},{24,8},{28,12},{1,17},{... | collective-permute-start | bytes 995336 | tf_op jit(solution)/shard_map/ppermute | solution.py:30
  114.0 1.2 collective-permute-start.34
  115.2 3.7 %collective-permute-start.35 = (f32[8,288]{1,0:T(8,128)S(1)}, f32[8,288]{1,0:T(8,128)S(1)}, u32[]{:S(2)}, u32[]{:S(2)}) collective-permute-start(f32[8,288]{1,0:T(8,128)S(1)} %get-tuple-element.233), channel_id=1, source_target_pairs={{0,2},{1,3},{2,0},{3,1},{4,6},{5,7},{6,4},{7,5},{8,10},{9,11},{10,... | collective-permute-start | bytes 27656 | tf_op jit(solution)/shard_map/ppermute | solution.py:30

commit v4 on v3

--- a/solution.py
+++ b/solution.py
@@ -89,12 +89,11 @@
 
 
 def gelu_pair(value):
-    k = math.sqrt(2.0 / math.pi)
+    k, c = math.sqrt(2.0 / math.pi), 0.044715
     square = value * value
-    t = jnp.tanh(k * (value + 0.044715 * value * square))
-    act = 0.5 * value * (1.0 + t)
-    slope = 0.5 * (1.0 + t) + 0.5 * value * (1.0 - t * t) * k * (1.0 + 3 * 0.044715 * square)
-    return act, slope
+    h = 0.5 + 0.5 * jnp.tanh(value * (k + (k * c) * square))
+    steep = value * (2.0 * k + (6.0 * k * c) * square)
+    return value * h, h * (1.0 + (1.0 - h) * steep)
 
 
 def row_part(ref, spots, name):
@@ -206,16 +205,16 @@
 
 def early_back_kernel(
     frames, n_dp, length, mods, cotangent, down_a, down_b, normed_low, att_a, att_b,
-    grad_a, grad_b, pack_far, own_chunks, chunks_far, chunks_core, fc2_sum,
+    grad_a, grad_b, low_out, pack_far, own_chunks, fc2_sum, pick,
 ):
     upstream = cotangent[...].astype(F32)
     half, width = upstream.shape
     keep = kept_rows(length, half, frames)
-    low32 = (mods[5:6, :] * jnp.where(keep, upstream, 0.0)).astype(BF).astype(F32)
-    low = low32.astype(BF)
+    low = (mods[5:6, :] * jnp.where(keep, upstream, 0.0)).astype(BF)
+    low_out[...] = low
     grad_a[...] = dot(low, down_a[...])
     grad_b[...] = dot(low, down_b[...])
-    fc2_sum[...] = column_sum(low32)
+    fc2_sum[...] = column_sum(low.astype(F32))
     n_att = att_a.shape[1]
     part = width // 2
     mine, other = split_chunks(normed_low[...].astype(F32), n_dp, 1)
@@ -224,14 +223,21 @@
     at = pad_lanes(2 * n_att)
     pack_far[:, at : at + part] = other.astype(BF)
     own_chunks[:, 0:part] = mine.astype(BF)
-    mine, other = split_chunks(low32, n_dp, 2)
-    chunks_far[:, 0:part] = other.astype(BF)
-    chunks_core[:, 0:part] = mine.astype(BF)
+    r = width // n_dp
+    feature = lax.broadcasted_iota(jnp.int32, pick.shape, 1)
+    column = lax.broadcasted_iota(jnp.int32, pick.shape, 0)
+    target = column + (lax.axis_index("dp") & 5) * r
+    ahead = 0
+    for k in range(1, n_dp // 4):
+        now = ((k & 1) << 1) + ((k >> 1) << 3) - k
+        target = target + jnp.where(column >= k * r, (now - ahead) * r, 0)
+        ahead = now
+    pick[...] = jnp.where(feature == target, 1.0, 0.0).astype(BF)
 
 
 def mlp_kernel(
-    n_dp, spots, tokens, part1, part1_other, mods, up_a, up_b, fc1_a, fc1_b, grad_a, grad_b,
-    chunks_far, part3, pack_act, pack_pre, chunks_core, branch_out, normed_out, inv_out,
+    spots, tokens, part1, part1_other, mods, up_a, up_b, fc1_a, fc1_b, grad_a, grad_b,
+    part3, act_out, pre_out, low_out, branch_out, normed_out, inv_out, sums,
 ):
     branch = part1[...].astype(F32) + part1_other[...].astype(F32) + row_part(fc1_a, spots, "proj")
     branch_out[...] = branch
@@ -239,36 +245,65 @@
     normed, inv = standardize(mid)
     normed_out[...] = normed
     inv_out[...] = inv
-    low32 = normed * (1.0 + mods[4:5, :]) + mods[3:4, :]
-    low = low32.astype(BF)
+    low = (normed * (1.0 + mods[4:5, :]) + mods[3:4, :]).astype(BF)
+    low_out[...] = low
     total = None
     cols = up_a.shape[1]
     for block, (u, b, g) in enumerate(((up_a, fc1_a, grad_a), (up_b, fc1_b, grad_b))):
         act, slope = gelu_pair(dot(low, u[...]) + row_part(b, spots, "fc1"))
-        pack_act[:, block * cols : (block + 1) * cols] = act.astype(BF)
+        act_out[:, block * cols : (block + 1) * cols] = act.astype(BF)
         pre = (g[...] * slope).astype(BF)
-        pack_pre[:, block * cols : (block + 1) * cols] = pre
+        if block == 0:
+            pre_out[...] = pre
+        sums[block : block + 1, :] = column_sum(pre.astype(F32))
         term = dot_trans(pre, u[...])
         total = term if total is None else total + term
     part3[...] = total.astype(BF)
-    mine, other = split_chunks(low32, n_dp, 0)
-    part = mine.shape[1]
-    pack_pre[:, 2 * cols : 2 * cols + part] = other.astype(BF)
-    chunks_core[:, 0:part] = mine.astype(BF)
-    pack_act[:, 2 * cols :] = chunks_far[...]
-
-
-def mlp_tail_kernel(
-    spans, pack_act, pack_pre, down_a, down_b, chunks_act, chunks_pre, far1, pack1, chunks1,
-    part2, core, sums,
-):
+
+
+def mlp_tail_kernel(act, down_a, down_b, part2):
     cols = down_a.shape[1]
     part2[...] = (
-        dot_trans(pack_act[:, 0:cols], down_a[...]) + dot_trans(pack_act[:, cols : 2 * cols], down_b[...])
+        dot_trans(act[:, 0:cols], down_a[...]) + dot_trans(act[:, cols : 2 * cols], down_b[...])
     ).astype(BF)
-    forward_kernel([spans], pack_act, pack_pre, chunks_act, chunks_pre, far1, pack1, chunks1, core)
-    sums[0:1, :] = column_sum(pack_pre[:, 0:cols].astype(F32))
-    sums[1:2, :] = column_sum(pack_pre[:, cols : 2 * cols].astype(F32))
+
+
+def rows_kernel(*refs):
+    half = refs[0].shape[0]
+    for i, source in enumerate(refs[:-1]):
+        refs[-1][i * half : (i + 1) * half, :] = source[...]
+
+
+def remake_kernel(n_dp, spots, own, before, last, n_blocks, span, pick, up, down, bias, *refs):
+    cols = up.shape[1]
+    normed, grads, refs = refs[:n_blocks], refs[n_blocks : 2 * n_blocks], refs[2 * n_blocks :]
+    if span is not None:
+        normed, grads = ([ref.at[span[0] : span[1], :] for ref in v] for v in (normed, grads))
+    down_sum, up_sum = 0.0, 0.0
+    if own:
+        act_own, pre_own, refs = refs[0][:, 0:cols], refs[1][...], refs[2:]
+    if before:
+        down_sum, up_sum, refs = refs[0][...], refs[1][...], refs[2:]
+    joined = lambda parts: parts[0] if len(parts) == 1 else jnp.concatenate(parts, axis=0)
+    n_new, g_new = (joined([ref[...] for ref in v[int(own) :]]) for v in (normed, grads))
+    act, slope = gelu_pair(dot(n_new, up[...]) + row_part(bias, spots, "fc1"))
+    act, pre = act.astype(BF), (dot(g_new, down[...]) * slope).astype(BF)
+    if own:
+        n_new, g_new = joined([normed[0][...], n_new]), joined([grads[0][...], g_new])
+        act, pre = joined([act_own, act]), joined([pre_own, pre])
+    down_sum = down_sum + dot(dot_trans(pick[...], g_new).astype(BF), act)
+    up_sum = up_sum + dot(dot_trans(pick[...], n_new).astype(BF), pre)
+    if last and n_dp == 8:
+        stay, send = refs
+        r = down_sum.shape[0] // 2
+        high = ((lax.axis_index("dp") >> 1) & 1) == 1
+        for i, total in enumerate((down_sum, up_sum)):
+            one, two = total[:r, :], total[r:, :]
+            stay[:, i * cols : (i + 1) * cols] = jnp.where(high, two, one)
+            send[:, i * cols : (i + 1) * cols] = jnp.where(high, one, two).astype(BF)
+    else:
+        refs[0][...] = down_sum
+        refs[1][...] = up_sum
 
 
 def attention_back_kernel(
@@ -391,11 +426,12 @@
     put("label", jnp.full((1, 128), label[0], jnp.int32).astype(F32))
 
 
-def gathered_kernel(layout, n_dp, rows_out, weight, source, *refs):
+def gathered_kernel(layout, n_dp, rows_out, flips, weight, source, *refs):
     ada_grad, ada_bias, qv, proj, fc1, fc2, stay, send, cond_cols, labels, table = refs
     rank, place = lax.axis_index("tensor"), lax.axis_index("dp")
     for i in range(n_dp):
-        table[pl.ds(place ^ i, 1), :] = source[i : i + 1, :]
+        flip = sum(f for k, f in enumerate(flips) if (i >> k) & 1)
+        table[pl.ds(place ^ flip, 1), :] = source[i : i + 1, :]
 
     def get(name):
         at, size = layout[name]
@@ -627,7 +663,7 @@
     part1_other = swap(part1, "tensor", 2)
 
     att_far, att_core = pad_lanes(2 * n_att), pad_lanes(n_att)
-    grad_a, grad_b, pack1, chunks1, chunks_far, chunks_act, fc2_sum = call(
+    grad_a, grad_b, low_grad, pack1, chunks1, fc2_sum, pick = call(
         order,
         lambda *refs: early_back_kernel(frames, n_dp, *refs),
         "early_back",
@@ -635,40 +671,43 @@
         [
             ((half, hidden), F32),
             ((half, hidden), F32),
+            ((half, width), BF),
             ((half, att_far + wide), BF),
             ((half, wide), BF),
-            ((half, wide), BF),
-            ((half, wide), BF),
             ((1, width), F32),
+            ((part // 2, width), BF),
         ],
         [lengths, mods, cot, *down_ws, low1, att_a, att_b],
     )
-
-    part3, pack_act, pack_pre, chunks_pre, branch1, normed2, inv2 = call(
-        order,
-        lambda *refs: mlp_kernel(n_dp, spots, *refs),
+    far1 = swap(pack1, "dp", 2)
+    grad_y = swap(low_grad, "dp", 1)
+    grad_f = swap(low_grad, "dp", 4)
+
+    part3, act, pre_own, low2, branch1, normed2, inv2, pre_sums = call(
+        order,
+        lambda *refs: mlp_kernel(spots, *refs),
         "mlp",
         3.0,
         [
             ((half, width), BF),
-            ((half, 2 * hidden + wide), BF),
-            ((half, 2 * hidden + wide), BF),
-            ((half, wide), BF),
+            ((half, 2 * hidden), BF),
+            ((half, hidden), BF),
+            ((half, width), BF),
             ((half, width), F32),
             ((half, width), F32),
             ((half, 1), F32),
+            ((2, hidden), F32),
         ],
-        [
-            tok, part1, part1_other, mods, *up_ws, *bias_ws, grad_a, grad_b,
-            chunks_far,
-        ],
+        [tok, part1, part1_other, mods, *up_ws, *bias_ws, grad_a, grad_b],
     )
     part3_other = swap(part3, "tensor", 2)
-
-    def forward(name, spans, sources, also=()):
+    rows_y = swap(behind(low2, grad_y), "dp", 1)
+    rows_f = swap(low2, "dp", 4)
+
+    def forward(name, spans, sources, us=0.02):
         outs = [((half, sum(size for _, _, size in parts)), BF) for parts in spans]
         outs = call(
-            order, lambda *refs: forward_kernel(spans, *refs), name, 0.02, outs, sources, also=also
+            order, lambda *refs: forward_kernel(spans, *refs), name, us, outs, sources
         )
         return [swap(out, "tensor", 1) for out in outs]
 
@@ -700,6 +739,16 @@
         )
         return stay, swap(send, "dp", 1 << last)
 
+    def halve_all(grad, done):
+        for b in range((n_dp - 1).bit_length()):
+            if b not in done:
+                my_bit = (d_rank >> b) & 1
+                grad = grad.reshape(grad.shape[0] // 2, 2, chunk, grad.shape[2])
+                send = lax.dynamic_index_in_dim(grad, 1 - my_bit, 1, keepdims=False).astype(BF)
+                stay = lax.dynamic_index_in_dim(grad, my_bit, 1, keepdims=False)
+                grad = stay + swap(send, "dp", 1 << b).astype(F32)
+        return grad[0]
+
     def last_grads(name, bit, widths, stay, other):
         if n_dp == 8:
             return call(
@@ -710,36 +759,20 @@
                 [((chunk, w), F32) for w in widths],
                 [stay, other],
             )
-        grad = stay.reshape(n_dp // 2, chunk, -1)
-        for b in range((n_dp - 1).bit_length()):
-            if b != bit:
-                my_bit = (d_rank >> b) & 1
-                grad = grad.reshape(grad.shape[0] // 2, 2, chunk, grad.shape[2])
-                send = lax.dynamic_index_in_dim(grad, 1 - my_bit, 1, keepdims=False).astype(BF)
-                stay = lax.dynamic_index_in_dim(grad, my_bit, 1, keepdims=False)
-                grad = stay + swap(send, "dp", 1 << b).astype(F32)
-        return jnp.split(grad[0], [sum(widths[:i]) for i in range(1, len(widths))], axis=1)
-
-    far1 = swap(pack1, "dp", 2)
-    n_mix = hidden + wide
-    n_mix1 = att_core + wide
-    at1 = 2 * n_mix
-    core_spans = [
-        (0, hidden, hidden), (2, 0, wide), (1, hidden, hidden), (3, 0, wide),
-        (4, n_att, att_core), (4, att_far, wide), (5, n_att, att_core), (6, 0, wide),
-    ]
-    part2, core_mlp, pre_sums = call(
-        order,
-        lambda *refs: mlp_tail_kernel(core_spans, *refs),
+        grad = halve_all(stay.reshape(n_dp // 2, chunk, -1), [bit])
+        return jnp.split(grad, [sum(widths[:i]) for i in range(1, len(widths))], axis=1)
+
+    (part2,) = call(
+        order,
+        mlp_tail_kernel,
         "mlp_tail",
-        2.0,
-        [((half, width), BF), ((half, 2 * n_mix + 2 * n_mix1), BF), ((2, hidden), F32)],
-        [pack_act, pack_pre, *down_ws, chunks_act, chunks_pre, far1, pack1, chunks1],
+        1.0,
+        [((half, width), BF)],
+        [act, *down_ws],
+        also=[far1, grad_f],
     )
     part2_other = swap(part2, "tensor", 2)
-    core_mlp = swap(core_mlp, "tensor", 1)
-    far_act = swap(behind(pack_act, part2), "dp", 4)
-    far_pre = swap(behind(pack_pre, part2), "dp", 1)
+    grad_yf = swap(grad_f, "dp", 1)
 
     part4, mid_grad, low_back, stacked, back_sums = call(
         order,
@@ -760,6 +793,7 @@
     )
     part4_other = swap(part4, "tensor", 2)
     s_wide = pad_lanes(n_qkv)
+    rows_yf = swap(rows_f, "dp", 1)
     pack3, chunks3 = call(
         order,
         lambda *refs: pack_back_kernel(n_dp, *refs),
@@ -771,11 +805,45 @@
     )
     far3 = swap(pack3, "dp", 2)
 
+    def remake(name, normed, grads, own, before, last, span=None, us=0.02):
+        outs = [((part // 2, hidden), F32)] * 2
+        if last and n_dp == 8:
+            outs = [((chunk, 2 * hidden), F32), ((chunk, 2 * hidden), BF)]
+        return call(
+            order,
+            lambda *refs: remake_kernel(
+                n_dp, spots, bool(own), bool(before), last, len(normed), span, *refs
+            ),
+            name,
+            us,
+            outs,
+            [pick, up_weight, down_weight, bias_row, *normed, *grads, *own, *before],
+            limit=40,
+        )
+
+    sums2 = remake(
+        "remake_near",
+        [low2, rows_y, rows_f],
+        [low_grad, grad_y, grad_f],
+        [act, pre_own],
+        [],
+        False,
+        us=1.0,
+    )
+    (grads_core,) = call(
+        order,
+        rows_kernel,
+        "rows_grad",
+        0.02,
+        [((4 * half, width), BF)],
+        [low_grad, grad_y, grad_f, grad_yf],
+    )
+    grads_other = swap(grads_core, "tensor", 1)
     result, gate2_sum = call(
         order,
         lambda *refs: output_kernel(frames, spots, *refs),
         "output",
-        0.02,
+        1.0,
         [((half, width), BF), ((1, width), F32)],
         [lengths, tok, part2, part2_other, bias_row, mods, branch1, cot],
     )
@@ -791,6 +859,16 @@
         ],
     )
     sums_other = swap(sums, "tensor", 1)
+    (rows_core,) = call(
+        order,
+        rows_kernel,
+        "rows_norm",
+        0.02,
+        [((4 * half, width), BF)],
+        [low2, rows_y, rows_f, rows_yf],
+    )
+    rows_other = swap(rows_core, "tensor", 1)
+
     layout, at = {}, 0
     for name, size in (
         ("mod", ada_cols), ("fc2", width), ("proj", width), ("fc1", hidden), ("stack", n_qkv),
@@ -812,50 +890,55 @@
         other = swap(value, "dp", flip)
         return call(order, stack_kernel, name, 0.02, [((2 * n, cols), F32)], [value, other])[0]
 
-    def mlp_grads(name, bit, pack, chunks, far, mixed, at):
-        left = ((1, 0), (4, at + hidden), (2, 2 * hidden), (3, hidden))
-        right = ((0, 0), (4, at), (2, 0), (3, 0))
-        return first_grads(name, bit, [(left, right, hidden)], [pack, chunks, far, mixed, core_mlp])
-
-    vector = stack("stack0", vector, 1)
-    mixed_act, mixed_pre = forward(
-        "forward_mlp", [[(i, hidden, hidden), (i, 2 * hidden, wide)] for i in range(2)], [far_act, far_pre]
-    )
-    down_grad = mlp_grads("down_grad", 2, pack_act, chunks_act, far_act, mixed_act, 0)
-    up_grad = mlp_grads("up_grad", 0, pack_pre, chunks_pre, far_pre, mixed_pre, n_mix)
-    (mixed3,) = forward(
+    def mlp_grads(stay, other):
+        if n_dp == 8:
+            return call(
+                order,
+                lambda *refs: add_kernel([hidden] * 2, *refs),
+                "mlp_add",
+                0.02,
+                [((chunk, hidden), F32)] * 2,
+                [stay, other],
+            )
+        return [halve_all(g.reshape(n_dp // 4, chunk, hidden), [0, 2]) for g in (stay, other)]
+
+    sums2 = remake("remake_yf", [rows_yf], [grad_yf], [], sums2, False)
+    flips = [4, 1] + [1 << b for b in range(3, (n_dp - 1).bit_length())] + [2]
+    mixed3, mixed1 = forward(
         "forward3",
-        [[(0, s_wide, s_wide), (0, 2 * s_wide, wide), (1, s_wide, s_wide), (2, 0, wide)]],
-        [far3, pack3, chunks3],
-    )
-    vector = stack("stack1", vector, 2)
+        [
+            [(0, s_wide, s_wide), (0, 2 * s_wide, wide), (1, s_wide, s_wide), (2, 0, wide)],
+            [(3, n_att, att_core), (3, att_far, wide), (4, n_att, att_core), (5, 0, wide)],
+        ],
+        [far3, pack3, chunks3, far1, pack1, chunks1],
+        us=6.5,
+    )
+    vector = stack("stack0", vector, flips[0])
+    core_args = ([rows_other], [grads_other], [])
+    sums2 = remake("remake_core0", *core_args, sums2, False, (0, 2 * half), us=8.0)
+    for i, flip in enumerate(flips[1:-1]):
+        vector = stack("stack%d" % (i + 1), vector, flip)
     n_mix3 = s_wide + wide
-    left_qkv = ((1, 0), (3, at1 + n_mix1 + att_core), (2, att_far), (3, at1 + att_core))
-    right_qkv = ((4, 0), (7, n_mix3), (6, 0), (7, 0))
-    left_out = ((5, 0), (7, n_mix3 + s_wide), (6, 2 * s_wide), (7, s_wide))
-    right_out = ((0, 0), (3, at1 + n_mix1), (2, 0), (3, at1))
+    n_mix1 = att_core + wide
+    left_qkv = ((1, 0), (7, n_mix1 + att_core), (2, att_far), (7, att_core))
+    right_qkv = ((3, 0), (6, n_mix3), (5, 0), (6, 0))
+    left_out = ((4, 0), (6, n_mix3 + s_wide), (5, 2 * s_wide), (6, s_wide))
+    right_out = ((0, 0), (7, n_mix1), (2, 0), (7, 0))
     qkv_grad = first_grads(
         "qkv_grad",
         1,
         [(left_qkv, right_qkv, n_qkv), (left_out, right_out, n_att)],
-        [pack1, chunks1, far1, core_mlp, pack3, chunks3, far3, mixed3],
-    )
-    both_other = swap(behind(both, qkv_grad[0]), "tensor", 1)
-    down_grad = second_grads("down_halve", 2, *down_grad)
-    up_grad = second_grads("up_halve", 0, *up_grad)
-    result, tokens_grad = call(
-        order, join_kernel, "join", 0.02, [((rows, width), BF)] * 2, [both, both_other]
-    )
-    result, tokens_grad = result.reshape(tokens.shape), tokens_grad.reshape(tokens.shape)
-    flip = 4
-    while flip < n_dp:
-        vector = stack("stack%d" % flip, vector, flip)
-        flip *= 2
+        [pack1, chunks1, far1, pack3, chunks3, far3, mixed3, mixed1],
+    )
+    mlp_grad = remake("remake_core1", *core_args, sums2, True, (2 * half, 4 * half))
+    mlp_grad = (mlp_grad[0], swap(mlp_grad[1], "dp", 2) if n_dp == 8 else mlp_grad[1])
+    both_other = swap(behind(both, mlp_grad[0]), "tensor", 1)
+    vector = stack("stack_last", vector, flips[-1])
     ada_grad, ada_bias_grad, qv_grad, proj_grad, fc1_grad, fc2_grad, stay, send, cond_cols, labels_all = call(
         order,
-        lambda *refs: gathered_kernel(layout, n_dp, chunk, *refs),
+        lambda *refs: gathered_kernel(layout, n_dp, chunk, flips, *refs),
         "gathered",
-        0.02,
+        5.0,
         [((chunk, ada_cols), F32)]
         + [((n,), F32) for n in (ada_cols, qv_bias.shape[0], width, hidden, width)]
         + [((n_dp, 2 * pad_lanes(columns)), F32)] * 2
@@ -863,7 +946,10 @@
         [ada_weight.T, vector],
         [pltpu.VMEM((n_dp, at), F32)],
     )
-    qkv_grad = second_grads("qkv_halve", 1, *qkv_grad)
+    result, tokens_grad = call(
+        order, join_kernel, "join", 0.02, [((rows, width), BF)] * 2, [both, both_other]
+    )
+    result, tokens_grad = result.reshape(tokens.shape), tokens_grad.reshape(tokens.shape)
     mine, send = call(
         order,
         middle_kernel,
@@ -880,8 +966,8 @@
         [((columns, n_classes), F32)],
         [mine, swap(send, "tensor", 2), cond_cols, labels_all],
     )
-    (down_grad,) = last_grads("down_add", 2, [hidden], *down_grad)
-    (up_grad,) = last_grads("up_add", 0, [hidden], *up_grad)
+    qkv_grad = second_grads("qkv_halve", 1, *qkv_grad)
+    down_grad, up_grad = mlp_grads(*mlp_grad)
     qkv_grad, out_grad = last_grads("qkv_add", 1, [n_qkv, n_att], *qkv_grad)
     return (
         result,

time: 133 us -> 114 us (0.86)
  waiting for transfers between devices: 65.3 us -> 36.7 us
  Pallas kernels: 27.9 us -> 37.8 us
    ppermute x36 -> x37, waiting for transfers between devices: 65.3 us -> 36.7 us  [swap(): return lax.ppermute(value, axis, [(i, i ^ flip) for i in range(size)])]
    pallas_call x30, Pallas kernels: 27.9 us -> 37.8 us  [call(): pl.pallas_call(whole, out_shape=[jax.ShapeDtypeStruct(s, d) for s, d in [...]
    ppermute x36 -> x37, starting transfers between devices: 34.7 us -> 34.6 us  [swap(): return lax.ppermute(value, axis, [(i, i ^ flip) for i in range(size)])]
  transfers between devices with their start and end apart: 36 -> 37, of which waited for: 18 -> 13; matrix products, arithmetic and copies ran while one was open for 1% -> 1% of each run, Pallas kernels for 20% -> 32%
where the time goes in v4:
time: 114 us
  Pallas kernels  37.8 us (33%)
  waiting for transfers between devices  36.7 us (32%)
  starting transfers between devices  34.6 us (30%)
  between operations  2.96 us (3%)
    pallas_call x30, Pallas kernels, call(): pl.pallas_call(whole, out_shape=[jax.ShapeDtypeStruct(s, d) for s, d in [...  37.8 us
    ppermute x37, waiting for transfers between devices, swap(): return lax.ppermute(value, axis, [(i, i ^ flip) for i in range(size)])  36.7 us
    ppermute x37, starting transfers between devices, swap(): return lax.ppermute(value, axis, [(i, i ^ flip) for i in range(size)])  34.6 us
  transfers between devices with their start and end apart: 37, of which 13 were waited for; matrix products, arithmetic and copies ran while one was open for 1% of the time, Pallas kernels for 32%

profile of v4, /device:TPU:0, one launch (start us, length us, event | category | flops | bytes accessed | tf_op | source)
XLA Modules:
  0.0 113.7 jit_solution(5509760249044645134)
XLA Ops:
  1.3 0.2 copy-done
  1.7 3.0 %collective-permute-start.1 = (bf16[1,288]{1,0:T(2,128)(2,1)S(1)}, bf16[1,288]{1,0:T(2,128)(2,1)S(1)}, u32[]{:S(2)}, u32[]{:S(2)}) collective-permute-start(bf16[1,288]{1,0:T(2,128)(2,1)S(1)} %copy.31.refs_0_), channel_id=1, source_target_pairs={{0,2},{1,3},{2,0},{3,1},{4,6},{5,7},{6,4},{7,5},{8,10},{9,11},{10,... | collective-permute-start | bytes 1736 | tf_op jit(solution)/shard_map/ppermute | solution.py:30
  5.4 0.8 add_add_fusion
  6.3 0.6 collective-permute-start.2
  6.9 0.8 collective-permute-done.2.refs_3_
  7.7 0.5 collective-permute-start.6
  8.4 0.4 collective-permute-start.5
  8.7 0.4 copy-done.3
  9.1 1.2 %modulation.1 = (f32[1,1152]{1,0:T(1,128)S(1)}, f32[1,1728]{1,0:T(1,128)S(1)}, f32[8,128]{1,0:T(8,128)S(1)}) custom-call(bf16[1,288]{1,0:T(2,128)(2,1)S(1)} %copy.31.refs_0_, bf16[1,288]{1,0:T(2,128)(2,1)S(1)} %collective-permute-done.refs_1_, bf16[1,288]{1,0:T(2,128)(2,1)S(1)} %collective-permute-done.1.refs_2_, ...), custom_call_target="tpu_custom_call" | custom-call | flops 1100000000 | bytes 1024 | tf_op jit(solution)/shard_map/modulation/pallas_call | solution.py:49
  10.3 1.1 collective-permute-start.4
  11.5 0.3 start.1
  11.8 2.3 %collective-permute-done.4.refs_4_ = f32[1,1728]{1,0:T(1,128)S(1)} collective-permute-done((f32[1,1728]{1,0:T(1,128)S(1)}, f32[1,1728]{1,0:T(1,128)S(1)}, u32[]{:S(2)}, u32[]{:S(2)}) %collective-permute-start.4) | collective-permute-done | bytes 6944 | tf_op jit(solution)/shard_map/ppermute | solution.py:30
  14.1 1.1 %collective-permute-done.8.refs_5_ = f32[1,1728]{1,0:T(1,128)S(1)} collective-permute-done((f32[1,1728]{1,0:T(1,128)S(1)}, f32[1,1728]{1,0:T(1,128)S(1)}, u32[]{:S(2)}, u32[]{:S(2)}) %collective-permute-start.8) | collective-permute-done | bytes 6944 | tf_op jit(solution)/shard_map/ppermute | solution.py:30
  15.3 0.2 collective-permute-start.11
  15.4 0.3 collective-permute-start.10
  16.4 4.2 %attention.1 = (bf16[128,1152]{1,0:T(8,128)(2,1)S(1)}, f32[8,1152]{1,0:T(8,128)S(1)}, bf16[128,1152]{1,0:T(8,128)(2,1)S(1)}, bf16[128,864]{1,0:T(8,128)(2,1)S(1)...) custom-call(s32[1]{0:T(128)S(6)} %copy.32.refs_0_, ...), custom_call_target="tpu_custom_call" | custom-call | flops 4400000000 | bytes 1024 | tf_op jit(solution)/shard_map/attention/pallas_call | solution.py:49
  20.7 1.1 collective-permute-start.9
  21.8 1.3 %early_back.1 = (f32[128,1152]{1,0:T(8,128)S(1)}, f32[128,1152]{1,0:T(8,128)S(1)}, bf16[128,1152]{1,0:T(8,128)(2,1)S(1)}, bf16[128,1280]{1,0:T(8,128)(2,1)S(1)},...) custom-call(s32[1]{0:T(128)S(6)} %copy.32.refs_0_, ...), custom_call_target="tpu_custom_call" | custom-call | flops 2200000000 | bytes 1024 | tf_op jit(solution)/shard_map/early_back/pallas_call | solution.py:49
  23.1 1.6 %collective-permute-start.17 = (bf16[128,1152]{1,0:T(8,128)(2,1)S(1)}, bf16[128,1152]{1,0:T(8,128)(2,1)S(1)}, u32[]{:S(2)}, u32[]{:S(2)}) collective-permute-start(bf16[128,1152]{1,0:T(8,128)(2,1)S(1)} %get-tuple-element.164.refs_7_.refs_0_), channel_id=1, source_target_pairs={{0,4},{4,0},{8,12},{12,8},{16,20},{20,16},{24,28},{28,24},{1,5},{5... | collective-permute-start | bytes 884744 | tf_op jit(solution)/shard_map/ppermute | solution.py:30
  24.7 2.6 %collective-permute-start.14 = (bf16[128,1152]{1,0:T(8,128)(2,1)S(1)}, bf16[128,1152]{1,0:T(8,128)(2,1)S(1)}, u32[]{:S(2)}, u32[]{:S(2)}) collective-permute-start(bf16[128,1152]{1,0:T(8,128)(2,1)S(1)} %get-tuple-element.164.refs_7_.refs_0_), channel_id=1, source_target_pairs={{0,16},{4,20},{8,24},{12,28},{16,0},{20,4},{24,8},{28,12},{1,17},{... | collective-permute-start | bytes 884744 | tf_op jit(solution)/shard_map/ppermute | solution.py:30
  27.2 1.6 %collective-permute-start.13 = (bf16[128,1280]{1,0:T(8,128)(2,1)S(1)}, bf16[128,1280]{1,0:T(8,128)(2,1)S(1)}, u32[]{:S(2)}, u32[]{:S(2)}) collective-permute-start(bf16[128,1280]{1,0:T(8,128)(2,1)S(1)} %get-tuple-element.163.refs_4_.refs_0_), channel_id=1, source_target_pairs={{0,8},{4,12},{8,0},{12,4},{16,24},{20,28},{24,16},{28,20},{1,9},{5... | collective-permute-start | bytes 983048 | tf_op jit(solution)/shard_map/ppermute | solution.py:30
  28.8 1.0 collective-permute-done.9.refs_2_
  29.8 3.1 %mlp.1 = (bf16[128,1152]{1,0:T(8,128)(2,1)S(1)}, bf16[128,2304]{1,0:T(8,128)(2,1)S(1)}, bf16[128,1152]{1,0:T(8,128)(2,1)S(1)}, bf16[128,1152]{1,0:T(8,128)(2,1)S...) custom-call(bf16[128,1152]{1,0:T(8,128)(2,1)S(1)} %get-tuple-element, ...), custom_call_target="tpu_custom_call" | custom-call | flops 3300000000 | bytes 1024 | tf_op jit(solution)/shard_map/mlp/pallas_call | solution.py:49
  32.9 1.1 collective-permute-start.12
  34.0 2.6 %collective-permute-start.20 = (bf16[128,1152]{1,0:T(8,128)(2,1)S(1)}, bf16[128,1152]{1,0:T(8,128)(2,1)S(1)}, u32[]{:S(2)}, u32[]{:S(2)}) collective-permute-start(bf16[128,1152]{1,0:T(8,128)(2,1)S(1)} %get-tuple-element.173.refs_4_.refs_0_), channel_id=1, source_target_pairs={{0,16},{4,20},{8,24},{12,28},{16,0},{20,4},{24,8},{28,12},{1,17},{... | collective-permute-start | bytes 884744 | tf_op jit(solution)/shard_map/ppermute | solution.py:30
  36.6 1.5 %collective-permute-start.19 = (bf16[128,1152]{1,0:T(8,128)(2,1)S(1)}, bf16[128,1152]{1,0:T(8,128)(2,1)S(1)}, u32[]{:S(2)}, u32[]{:S(2)}) collective-permute-start(bf16[128,1152]{1,0:T(8,128)(2,1)S(1)} %get-tuple-element.173.refs_4_.refs_0_), channel_id=1, source_target_pairs={{0,4},{4,0},{8,12},{12,8},{16,20},{20,16},{24,28},{28,24},{1,5},{5... | collective-permute-start | bytes 884744 | tf_op jit(solution)/shard_map/ppermute | solution.py:30
  38.1 4.3 %collective-permute-done.14.refs_5_.refs_9_.refs_2_ = bf16[128,1152]{1,0:T(8,128)(2,1)S(1)} collective-permute-done((bf16[128,1152]{1,0:T(8,128)(2,1)S(1)}, bf16[128,1152]{1,0:T(8,128)(2,1)S(1)}, u32[]{:S(2)}, u32[]{:S(2)}) %collective-permute-start.14) | collective-permute-done | bytes 294944 | tf_op jit(solution)/shard_map/ppermute | solution.py:30
  42.4 0.5 collective-permute-start.18
  42.9 1.7 %mlp_tail.1 = (bf16[128,1152]{1,0:T(8,128)(2,1)S(1)}, f32[8,128]{1,0:T(8,128)S(1)}) custom-call(bf16[128,2304]{1,0:T(8,128)(2,1)S(1)} %get-tuple-element.161.refs_0_.refs_10_, bf16[1152,1152]{1,0:T(8,128)(2,1)S(1)} %copy-done.1, bf16[1152,1152]{1,0:T(8,128)(2,1)S(1)} %collective-permute-done.11.refs_4_.refs_2_, f32[8,128]{1,0:T(8,128)S(1)} %get-tuple-element.162.refs_3_, ...), custom_call_target="tpu_custom_call" | custom-call | flops 1100000000 | bytes 1024 | tf_op jit(solution)/shard_map/mlp_tail/pallas_call | solution.py:49
  44.6 1.1 collective-permute-start.16
  45.7 4.3 %attention_back.1 = (bf16[128,1152]{1,0:T(8,128)(2,1)S(1)}, f32[128,1152]{1,0:T(8,128)S(1)}, bf16[128,1152]{1,0:T(8,128)(2,1)S(1)}, bf16[128,1792]{1,0:T(8,128)(...) custom-call(s32[1]{0:T(128)S(6)} %copy.32.refs_0_, bf16[128,1152]{1,0:T(8,128)(2,1)S(1)} %get-tuple-element.154.refs_1_, ...), custom_call_target="tpu_custom_call" | custom-call | flops 5500000256 | bytes 1024 | tf_op jit(solution)/shard_map/attention_back/pallas_call | solution.py:49
  50.0 1.1 collective-permute-start.15
  51.0 2.0 %collective-permute-done.20.refs_6_.refs_2_ = bf16[128,1152]{1,0:T(8,128)(2,1)S(1)} collective-permute-done((bf16[128,1152]{1,0:T(8,128)(2,1)S(1)}, bf16[128,1152]{1,0:T(8,128)(2,1)S(1)}, u32[]{:S(2)}, u32[]{:S(2)}) %collective-permute-start.20) | collective-permute-done | bytes 294944 | tf_op jit(solution)/shard_map/ppermute | solution.py:30
  53.1 0.5 collective-permute-start.21
  53.6 0.2 pack_back.1
  53.8 0.7 collective-permute-start.26
  54.5 3.6 %remake_near.1 = (f32[288,1152]{1,0:T(8,128)S(1)}, f32[288,1152]{1,0:T(8,128)S(1)}, f32[8,128]{1,0:T(8,128)S(1)}) custom-call(bf16[288,1152]{1,0:T(8,128)(2,1)S(1)} %get-tuple-element.171.refs_0_, bf16[1152,1152]{1,0:T(8,128)(2,1)S(1)} %copy-done.2, bf16[1152,1152]{1,0:T(8,128)(2,1)S(1)} %copy-done.1, ...), custom_call_target="tpu_custom_call" | custom-call | flops 1100000000 | bytes 1024 | tf_op jit(solution)/shard_map/remake_near/pallas_call | solution.py:49
  58.3 0.3 output.1
  58.6 0.5 input_back.1
  59.2 1.8 %collective-permute-done.21.refs_3_.refs_4_ = bf16[128,1152]{1,0:T(8,128)(2,1)S(1)} collective-permute-done((bf16[128,1152]{1,0:T(8,128)(2,1)S(1)}, bf16[128,1152]{1,0:T(8,128)(2,1)S(1)}, u32[]{:S(2)}, u32[]{:S(2)}) %collective-permute-start.21) | collective-permute-done | bytes 294944 | tf_op jit(solution)/shard_map/ppermute | solution.py:30
  61.1 0.5 collective-permute-start.24
  61.6 2.4 %collective-permute-done.24.refs_2_ = f32[16,1152]{1,0:T(8,128)S(1)} collective-permute-done((f32[16,1152]{1,0:T(8,128)S(1)}, f32[16,1152]{1,0:T(8,128)S(1)}, u32[]{:S(2)}, u32[]{:S(2)}) %collective-permute-start.24) | collective-permute-done | bytes 73760 | tf_op jit(solution)/shard_map/ppermute | solution.py:30
  64.2 2.3 %collective-permute-start.25 = (f32[1,7424]{1,0:T(1,128)S(1)}, f32[1,7424]{1,0:T(1,128)S(1)}, u32[]{:S(2)}, u32[]{:S(2)}) collective-permute-start(f32[1,7424]{1,0:T(1,128)S(1)} %get-tuple-element.198.refs_0_), channel_id=1, source_target_pairs={{0,16},{4,20},{8,24},{12,28},{16,0},{20,4},{24,8},{28,12},{1,17},{... | collective-permute-start | bytes 89096 | tf_op jit(solution)/shard_map/ppermute | solution.py:30
  66.5 2.2 %remake_yf.1 = (f32[288,1152]{1,0:T(8,128)S(1)}, f32[288,1152]{1,0:T(8,128)S(1)}, f32[8,128]{1,0:T(8,128)S(1)}) custom-call(bf16[288,1152]{1,0:T(8,128)(2,1)S(1)} %get-tuple-element.171.refs_0_, bf16[1152,1152]{1,0:T(8,128)(2,1)S(1)} %copy-done.2, bf16[1152,1152]{1,0:T(8,128)(2,1)S(1)} %copy-done.1, ...), custom_call_target="tpu_custom_call" | custom-call | flops 22000000 | bytes 1024 | tf_op jit(solution)/shard_map/remake_yf/pallas_call | solution.py:49
  68.7 0.4 collective-permute-done.26.refs_0_.refs_5_
  69.3 1.6 %collective-permute-start.29 = (f32[2,7424]{1,0:T(2,128)S(1)}, f32[2,7424]{1,0:T(2,128)S(1)}, u32[]{:S(2)}, u32[]{:S(2)}) collective-permute-start(f32[2,7424]{1,0:T(2,128)S(1)} %get-tuple-element.209.refs_0_), channel_id=1, source_target_pairs={{0,4},{4,0},{8,12},{12,8},{16,20},{20,16},{24,28},{28,24},{1,5},{5... | collective-permute-start | bytes 178184 | tf_op jit(solution)/shard_map/ppermute | solution.py:30
  70.9 0.5 collective-permute-start.27
  71.4 3.3 %remake_core0.1 = (f32[288,1152]{1,0:T(8,128)S(1)}, f32[288,1152]{1,0:T(8,128)S(1)}, f32[8,128]{1,0:T(8,128)S(1)}) custom-call(bf16[288,1152]{1,0:T(8,128)(2,1)S(1)} %get-tuple-element.171.refs_0_, bf16[1152,1152]{1,0:T(8,128)(2,1)S(1)} %copy-done.2, bf16[1152,1152]{1,0:T(8,128)(2,1)S(1)} %copy-done.1, ...), custom_call_target="tpu_custom_call" | custom-call | flops 8800000000 | bytes 1024 | tf_op jit(solution)/shard_map/remake_core0/pallas_call | solution.py:49
  74.7 3.2 %collective-permute-start.31 = (f32[4,7424]{1,0:T(4,128)S(1)}, f32[4,7424]{1,0:T(4,128)S(1)}, u32[]{:S(2)}, u32[]{:S(2)}) collective-permute-start(f32[4,7424]{1,0:T(4,128)S(1)} %get-tuple-element.215.refs_0_), channel_id=1, source_target_pairs={{0,8},{4,12},{8,0},{12,4},{16,24},{20,28},{24,16},{28,20},{1,9},{5... | collective-permute-start | bytes 356360 | tf_op jit(solution)/shard_map/ppermute | solution.py:30
  77.9 1.4 %qkv_grad.1 = (f32[2,144,1152]{2,1,0:T(8,128)S(1)}, bf16[2,144,1152]{2,1,0:T(8,128)(2,1)S(1)}, f32[8,128]{1,0:T(8,128)S(1)}) custom-call(bf16[128,1280]{1,0:T(8,128)(2,1)S(1)} %get-tuple-element.163.refs_4_.refs_0_, bf16[128,640]{1,0:T(8,128)(2,1)S(1)} %get-tuple-element.201.refs_5_.refs_1_, ...), custom_call_target="tpu_custom_call" | custom-call | flops 22000000 | bytes 1024 | tf_op jit(solution)/shard_map/qkv_grad/pallas_call | solution.py:49
  79.3 0.5 collective-permute-start.32
  79.9 3.5 %remake_core1.1 = (f32[144,2304]{1,0:T(8,128)S(1)}, bf16[144,2304]{1,0:T(8,128)(2,1)S(1)}, f32[8,128]{1,0:T(8,128)S(1)}) custom-call(bf16[288,1152]{1,0:T(8,128)(2,1)S(1)} %get-tuple-element.171.refs_0_, bf16[1152,1152]{1,0:T(8,128)(2,1)S(1)} %copy-done.2, bf16[1152,1152]{1,0:T(8,128)(2,1)S(1)} %copy-done.1, ...), custom_call_target="tpu_custom_call" | custom-call | flops 22000000 | bytes 1024 | tf_op jit(solution)/shard_map/remake_core1/pallas_call | solution.py:49
  83.6 1.6 %gathered.1 = (f32[144,1728]{1,0:T(8,128)}, f32[1728]{0:T(1024)}, f32[576]{0:T(1024)}, f32[1152]{0:T(1024)}, f32[1152]{0:T(1024)}, /*index=5*/f32[1152]{0:T(1024...) custom-call(bf16[1728,1152]{1,0:T(8,128)(2,1)S(1)} %bitcast.13, ...), custom_call_target="tpu_custom_call" | custom-call | flops 5500000256 | bytes 1024 | tf_op jit(solution)/shard_map/gathered/pallas_call | solution.py:49
  85.2 0.4 collective-permute-start.33
  85.6 1.1 join.1
  86.8 1.1 collective-permute-start.34
  87.8 2.7 %collective-permute-done.34.refs_1_ = f32[8,288]{1,0:T(8,128)S(1)} collective-permute-done((f32[8,288]{1,0:T(8,128)S(1)}, f32[8,288]{1,0:T(8,128)S(1)}, u32[]{:S(2)}, u32[]{:S(2)}) %collective-permute-start.34) | collective-permute-done | bytes 9248 | tf_op jit(solution)/shard_map/ppermute | solution.py:30
  90.5 1.0 table.1
  91.5 4.4 %collective-permute-done.32.refs_1_ = bf16[2,144,1152]{2,1,0:T(8,128)(2,1)S(1)} collective-permute-done((bf16[2,144,1152]{2,1,0:T(8,128)(2,1)S(1)}, bf16[2,144,1152]{2,1,0:T(8,128)(2,1)S(1)}, u32[]{:S(2)}, u32[]{:S(2)}) %collective-permute-start.32) | collective-permute-done | bytes 663584 | tf_op jit(solution)/shard_map/ppermute | solution.py:30
  96.0 2.0 %collective-permute-start.35 = (bf16[144,1152]{1,0:T(8,128)(2,1)S(1)}, bf16[144,1152]{1,0:T(8,128)(2,1)S(1)}, u32[]{:S(2)}, u32[]{:S(2)}) collective-permute-start(bf16[144,1152]{1,0:T(8,128)(2,1)S(1)} %get-tuple-element.234), channel_id=1, source_target_pairs={{0,16},{4,20},{8,24},{12,28},{16,0},{20,4},{24,8},{28,12},{1,17},{... | collective-permute-start | bytes 995336 | tf_op jit(solution)/shard_map/ppermute | solution.py:30
  98.1 6.5 %collective-permute-done.36.refs_1_ = bf16[144,2304]{1,0:T(8,128)(2,1)S(1)} collective-permute-done((bf16[144,2304]{1,0:T(8,128)(2,1)S(1)}, bf16[144,2304]{1,0:T(8,128)(2,1)S(1)}, u32[]{:S(2)}, u32[]{:S(2)}) %collective-permute-start.36) | collective-permute-done | bytes 663584 | tf_op jit(solution)/shard_map/ppermute | solution.py:30
  104.5 1.2 %mlp_add.1 = (f32[144,1152]{1,0:T(8,128)}, f32[144,1152]{1,0:T(8,128)}, f32[8,128]{1,0:T(8,128)S(1)}) custom-call(f32[144,2304]{1,0:T(8,128)S(1)} %get-tuple-element.213.refs_0_, bf16[144,2304]{1,0:T(8,128)(2,1)S(1)} %collective-permute-done.36.refs_1_, f32[8,128]{1,0:T(8,128)S(1)} %get-tuple-element.236.refs_2_), custom_call_target="tpu_custom_call" | custom-call | flops 22000000 | bytes 1024 | tf_op jit(solution)/shard_map/mlp_add/pallas_call | solution.py:49
  105.7 7.0 %collective-permute-done.35.refs_1_ = bf16[144,1152]{1,0:T(8,128)(2,1)S(1)} collective-permute-done((bf16[144,1152]{1,0:T(8,128)(2,1)S(1)}, bf16[144,1152]{1,0:T(8,128)(2,1)S(1)}, u32[]{:S(2)}, u32[]{:S(2)}) %collective-permute-start.35) | collective-permute-done | bytes 331808 | tf_op jit(solution)/shard_map/ppermute | solution.py:30
  112.7 1.0 qkv_add.1
  (62 shorter events, 1.6 us)
Async XLA Ops:
  0.6 0.9 copy-start
  1.7 4.6 %collective-permute-start.1 = (bf16[1,288]{1,0:T(2,128)(2,1)S(1)}, bf16[1,288]{1,0:T(2,128)(2,1)S(1)}, u32[]{:S(2)}, u32[]{:S(2)}) collective-permute-start(bf16[1,288]{1,0:T(2,128)(2,1)S(1)} %copy.31.refs_0_), channel_id=1, source_target_pairs={{0,2},{1,3},{2,0},{3,1},{4,6},{5,7},{6,4},{7,5},{8,10},{9,11},{10,... | collective-permute-start | bytes 1736 | tf_op jit(solution)/shard_map/ppermute | solution.py:30
  4.7 2.2 %collective-permute-start = (bf16[1,288]{1,0:T(2,128)(2,1)S(1)}, bf16[1,288]{1,0:T(2,128)(2,1)S(1)}, u32[]{:S(2)}, u32[]{:S(2)}) collective-permute-start(bf16[1,288]{1,0:T(2,128)(2,1)S(1)} %copy.31.refs_0_), channel_id=1, source_target_pairs={{0,1},{1,0},{2,3},{3,2},{4,5},{5,4},{6,7},{7,6},{8,9},{9,8},{10,11... | collective-permute-start | bytes 1736 | tf_op jit(solution)/shard_map/ppermute | solution.py:30
  6.2 1.6 %copy-start.5 = (bf16[1152,864]{0,1:T(8,128)(2,1)S(1)}, bf16[1152,864]{0,1:T(8,128)(2,1)}, u32[]{:S(2)}) copy-start(bf16[1152,864]{0,1:T(8,128)(2,1)} %param.24) | copy-start | bytes 5971972
  6.2 2.1 %copy-start.6 = (bf16[1152,288]{0,1:T(8,128)(2,1)S(1)}, bf16[1152,288]{0,1:T(8,128)(2,1)}, u32[]{:S(2)}) copy-start(bf16[1152,288]{0,1:T(8,128)(2,1)} %param.26) | copy-start | bytes 1990660
  6.2 2.9 %copy-start.3 = (bf16[1152,1728]{0,1:T(8,128)(2,1)S(1)}, bf16[1152,1728]{0,1:T(8,128)(2,1)}, u32[]{:S(2)}) copy-start(bf16[1152,1728]{0,1:T(8,128)(2,1)} %param.22) | copy-start | bytes 11943940
  6.3 1.4 %collective-permute-start.2 = (bf16[1,288]{1,0:T(2,128)(2,1)S(1)}, bf16[1,288]{1,0:T(2,128)(2,1)S(1)}, u32[]{:S(2)}, u32[]{:S(2)}) collective-permute-start(bf16[1,288]{1,0:T(2,128)(2,1)S(1)} %collective-permute-done.1.refs_2_), channel_id=1, source_target_pairs={{0,1},{1,0},{2,3},{3,2},{4,5},{5,4},{6,7},{7,6},{8,9},{9,8},{10,11... | collective-permute-start | bytes 1736 | tf_op jit(solution)/shard_map/ppermute | solution.py:30
  7.7 6.3 %collective-permute-start.6 = (bf16[864,1152]{1,0:T(8,128)(2,1)S(1)}, bf16[864,1152]{1,0:T(8,128)(2,1)S(1)}, u32[]{:S(2)}, u32[]{:S(2)}) collective-permute-start(bf16[864,1152]{1,0:T(8,128)(2,1)S(1)} %bitcast.14), channel_id=1, source_target_pairs={{0,1},{1,0},{2,3},{3,2},{4,5},{5,4},{6,7},{7,6},{8,9},{9,8},{10,11... | collective-permute-start | bytes 5971976 | tf_op jit(solution)/shard_map/ppermute | solution.py:30
  8.2 5.8 %collective-permute-start.7 = (bf16[288,1152]{1,0:T(8,128)(2,1)S(1)}, bf16[288,1152]{1,0:T(8,128)(2,1)S(1)}, u32[]{:S(2)}, u32[]{:S(2)}) collective-permute-start(bf16[288,1152]{1,0:T(8,128)(2,1)S(1)} %bitcast.17), channel_id=1, source_target_pairs={{0,1},{1,0},{2,3},{3,2},{4,5},{5,4},{6,7},{7,6},{8,9},{9,8},{10,11... | collective-permute-start | bytes 1990664 | tf_op jit(solution)/shard_map/ppermute | solution.py:30
  8.4 5.7 %collective-permute-start.5 = (f32[1,6528]{1,0:T(1,128)S(1)}, f32[1,6528]{1,0:T(1,128)S(1)}, u32[]{:S(2)}, u32[]{:S(2)}) collective-permute-start(f32[1,6528]{1,0:T(1,128)S(1)} %reshape.43.refs_1_.refs_6_.refs_8_.refs_3_.refs_4_), channel_id=1, source_target_pairs={{0,1},{1,0},{2,3},{3,2},{4,5},{5,4},{6,7},{7,6},{8,9},{9,8},{10,11... | collective-permute-start | bytes 78344 | tf_op jit(solution)/shard_map/ppermute | solution.py:30
  9.1 2.3 %copy-start.7 = (bf16[1,16,16,1152]{3,2,1,0:T(8,128)(2,1)S(1)}, bf16[1,16,16,1152]{3,2,1,0:T(8,128)(2,1)}, u32[]{:S(2)}) copy-start(bf16[1,16,16,1152]{3,2,1,0:T(8,128)(2,1)} %param.17) | copy-start | bytes 1769476
  9.1 2.3 %copy-start.8 = (bf16[1,16,16,1152]{3,2,1,0:T(8,128)(2,1)S(1)}, bf16[1,16,16,1152]{3,2,1,0:T(8,128)(2,1)}, u32[]{:S(2)}) copy-start(bf16[1,16,16,1152]{3,2,1,0:T(8,128)(2,1)} %param.32) | copy-start | bytes 1769476
  9.1 6.3 %copy-start.2 = (bf16[1152,1152]{1,0:T(8,128)(2,1)S(1)}, bf16[1152,1152]{1,0:T(8,128)(2,1)}, u32[]{:S(2)}) copy-start(bf16[1152,1152]{1,0:T(8,128)(2,1)} %refs_1_.9) | copy-start | bytes 7962628
  10.3 3.7 %collective-permute-start.4 = (f32[1,1728]{1,0:T(1,128)S(1)}, f32[1,1728]{1,0:T(1,128)S(1)}, u32[]{:S(2)}, u32[]{:S(2)}) collective-permute-start(f32[1,1728]{1,0:T(1,128)S(1)} %get-tuple-element.137.refs_2_), channel_id=1, source_target_pairs={{0,2},{1,3},{2,0},{3,1},{4,6},{5,7},{6,4},{7,5},{8,10},{9,11},{10,... | collective-permute-start | bytes 20744 | tf_op jit(solution)/shard_map/ppermute | solution.py:30
  11.4 2.7 %collective-permute-start.3 = (f32[1,1728]{1,0:T(1,128)S(1)}, f32[1,1728]{1,0:T(1,128)S(1)}, u32[]{:S(2)}, u32[]{:S(2)}) collective-permute-start(f32[1,1728]{1,0:T(1,128)S(1)} %get-tuple-element.137.refs_2_), channel_id=1, source_target_pairs={{0,1},{1,0},{2,3},{3,2},{4,5},{5,4},{6,7},{7,6},{8,9},{9,8},{10,11... | collective-permute-start | bytes 20744 | tf_op jit(solution)/shard_map/ppermute | solution.py:30
  11.5 3.8 %copy-start.1 = (bf16[1152,1152]{1,0:T(8,128)(2,1)S(1)}, bf16[1152,1152]{1,0:T(8,128)(2,1)}, u32[]{:S(2)}) copy-start(bf16[1152,1152]{1,0:T(8,128)(2,1)} %refs_2_.7) | copy-start | bytes 7962628
  14.0 1.2 %collective-permute-start.8 = (f32[1,1728]{1,0:T(1,128)S(1)}, f32[1,1728]{1,0:T(1,128)S(1)}, u32[]{:S(2)}, u32[]{:S(2)}) collective-permute-start(f32[1,1728]{1,0:T(1,128)S(1)} %collective-permute-done.4.refs_4_), channel_id=1, source_target_pairs={{0,1},{1,0},{2,3},{3,2},{4,5},{5,4},{6,7},{7,6},{8,9},{9,8},{10,11... | collective-permute-start | bytes 20744 | tf_op jit(solution)/shard_map/ppermute | solution.py:30
  15.3 6.5 %collective-permute-start.11 = (bf16[1152,1152]{1,0:T(8,128)(2,1)S(1)}, bf16[1152,1152]{1,0:T(8,128)(2,1)S(1)}, u32[]{:S(2)}, u32[]{:S(2)}) collective-permute-start(bf16[1152,1152]{1,0:T(8,128)(2,1)S(1)} %copy-done.1), channel_id=1, source_target_pairs={{0,1},{1,0},{2,3},{3,2},{4,5},{5,4},{6,7},{7,6},{8,9},{9,8},{10,11... | collective-permute-start | bytes 7962632 | tf_op jit(solution)/shard_map/ppermute | solution.py:30
  15.4 14.4 %collective-permute-start.10 = (bf16[1152,1152]{1,0:T(8,128)(2,1)S(1)}, bf16[1152,1152]{1,0:T(8,128)(2,1)S(1)}, u32[]{:S(2)}, u32[]{:S(2)}) collective-permute-start(bf16[1152,1152]{1,0:T(8,128)(2,1)S(1)} %copy-done.2), channel_id=1, source_target_pairs={{0,1},{1,0},{2,3},{3,2},{4,5},{5,4},{6,7},{7,6},{8,9},{9,8},{10,11... | collective-permute-start | bytes 7962632 | tf_op jit(solution)/shard_map/ppermute | solution.py:30
  20.7 9.1 %collective-permute-start.9 = (bf16[128,1152]{1,0:T(8,128)(2,1)S(1)}, bf16[128,1152]{1,0:T(8,128)(2,1)S(1)}, u32[]{:S(2)}, u32[]{:S(2)}) collective-permute-start(bf16[128,1152]{1,0:T(8,128)(2,1)S(1)} %get-tuple-element.142.refs_1_), channel_id=1, source_target_pairs={{0,2},{1,3},{2,0},{3,1},{4,6},{5,7},{6,4},{7,5},{8,10},{9,11},{10,... | collective-permute-start | bytes 884744 | tf_op jit(solution)/shard_map/ppermute | solution.py:30
  23.1 13.5 %collective-permute-start.17 = (bf16[128,1152]{1,0:T(8,128)(2,1)S(1)}, bf16[128,1152]{1,0:T(8,128)(2,1)S(1)}, u32[]{:S(2)}, u32[]{:S(2)}) collective-permute-start(bf16[128,1152]{1,0:T(8,128)(2,1)S(1)} %get-tuple-element.164.refs_7_.refs_0_), channel_id=1, source_target_pairs={{0,4},{4,0},{8,12},{12,8},{16,20},{20,16},{24,28},{28,24},{1,5},{5... | collective-permute-start | bytes 884744 | tf_op jit(solution)/shard_map/ppermute | solution.py:30
  24.7 17.7 %collective-permute-start.14 = (bf16[128,1152]{1,0:T(8,128)(2,1)S(1)}, bf16[128,1152]{1,0:T(8,128)(2,1)S(1)}, u32[]{:S(2)}, u32[]{:S(2)}) collective-permute-start(bf16[128,1152]{1,0:T(8,128)(2,1)S(1)} %get-tuple-element.164.refs_7_.refs_0_), channel_id=1, source_target_pairs={{0,16},{4,20},{8,24},{12,28},{16,0},{20,4},{24,8},{28,12},{1,17},{... | collective-permute-start | bytes 884744 | tf_op jit(solution)/shard_map/ppermute | solution.py:30
  27.2 15.7 %collective-permute-start.13 = (bf16[128,1280]{1,0:T(8,128)(2,1)S(1)}, bf16[128,1280]{1,0:T(8,128)(2,1)S(1)}, u32[]{:S(2)}, u32[]{:S(2)}) collective-permute-start(bf16[128,1280]{1,0:T(8,128)(2,1)S(1)} %get-tuple-element.163.refs_4_.refs_0_), channel_id=1, source_target_pairs={{0,8},{4,12},{8,0},{12,4},{16,24},{20,28},{24,16},{28,20},{1,9},{5... | collective-permute-start | bytes 983048 | tf_op jit(solution)/shard_map/ppermute | solution.py:30
  32.9 12.8 %collective-permute-start.12 = (bf16[128,1152]{1,0:T(8,128)(2,1)S(1)}, bf16[128,1152]{1,0:T(8,128)(2,1)S(1)}, u32[]{:S(2)}, u32[]{:S(2)}) collective-permute-start(bf16[128,1152]{1,0:T(8,128)(2,1)S(1)} %get-tuple-element.154.refs_1_), channel_id=1, source_target_pairs={{0,2},{1,3},{2,0},{3,1},{4,6},{5,7},{6,4},{7,5},{8,10},{9,11},{10,... | collective-permute-start | bytes 884744 | tf_op jit(solution)/shard_map/ppermute | solution.py:30
  34.0 19.1 %collective-permute-start.20 = (bf16[128,1152]{1,0:T(8,128)(2,1)S(1)}, bf16[128,1152]{1,0:T(8,128)(2,1)S(1)}, u32[]{:S(2)}, u32[]{:S(2)}) collective-permute-start(bf16[128,1152]{1,0:T(8,128)(2,1)S(1)} %get-tuple-element.173.refs_4_.refs_0_), channel_id=1, source_target_pairs={{0,16},{4,20},{8,24},{12,28},{16,0},{20,4},{24,8},{28,12},{1,17},{... | collective-permute-start | bytes 884744 | tf_op jit(solution)/shard_map/ppermute | solution.py:30
  36.6 17.2 %collective-permute-start.19 = (bf16[128,1152]{1,0:T(8,128)(2,1)S(1)}, bf16[128,1152]{1,0:T(8,128)(2,1)S(1)}, u32[]{:S(2)}, u32[]{:S(2)}) collective-permute-start(bf16[128,1152]{1,0:T(8,128)(2,1)S(1)} %get-tuple-element.173.refs_4_.refs_0_), channel_id=1, source_target_pairs={{0,4},{4,0},{8,12},{12,8},{16,20},{20,16},{24,28},{28,24},{1,5},{5... | collective-permute-start | bytes 884744 | tf_op jit(solution)/shard_map/ppermute | solution.py:30
  42.4 15.7 %collective-permute-start.18 = (bf16[128,1152]{1,0:T(8,128)(2,1)S(1)}, bf16[128,1152]{1,0:T(8,128)(2,1)S(1)}, u32[]{:S(2)}, u32[]{:S(2)}) collective-permute-start(bf16[128,1152]{1,0:T(8,128)(2,1)S(1)} %collective-permute-done.14.refs_5_.refs_9_.refs_2_), channel_id=1, source_target_pairs={{0,4},{4,0},{8,12},{12,8},{16,20},{20,16},{24,28},{28,24},{1,5},{5... | collective-permute-start | bytes 884744 | tf_op jit(solution)/shard_map/ppermute | solution.py:30
  44.6 13.7 %collective-permute-start.16 = (bf16[128,1152]{1,0:T(8,128)(2,1)S(1)}, bf16[128,1152]{1,0:T(8,128)(2,1)S(1)}, u32[]{:S(2)}, u32[]{:S(2)}) collective-permute-start(bf16[128,1152]{1,0:T(8,128)(2,1)S(1)} %get-tuple-element.170.refs_2_), channel_id=1, source_target_pairs={{0,2},{1,3},{2,0},{3,1},{4,6},{5,7},{6,4},{7,5},{8,10},{9,11},{10,... | collective-permute-start | bytes 884744 | tf_op jit(solution)/shard_map/ppermute | solution.py:30
  50.0 8.7 %collective-permute-start.15 = (bf16[128,1152]{1,0:T(8,128)(2,1)S(1)}, bf16[128,1152]{1,0:T(8,128)(2,1)S(1)}, u32[]{:S(2)}, u32[]{:S(2)}) collective-permute-start(bf16[128,1152]{1,0:T(8,128)(2,1)S(1)} %get-tuple-element.166.refs_1_), channel_id=1, source_target_pairs={{0,2},{1,3},{2,0},{3,1},{4,6},{5,7},{6,4},{7,5},{8,10},{9,11},{10,... | collective-permute-start | bytes 884744 | tf_op jit(solution)/shard_map/ppermute | solution.py:30
  53.1 7.9 %collective-permute-start.21 = (bf16[128,1152]{1,0:T(8,128)(2,1)S(1)}, bf16[128,1152]{1,0:T(8,128)(2,1)S(1)}, u32[]{:S(2)}, u32[]{:S(2)}) collective-permute-start(bf16[128,1152]{1,0:T(8,128)(2,1)S(1)} %collective-permute-done.20.refs_6_.refs_2_), channel_id=1, source_target_pairs={{0,4},{4,0},{8,12},{12,8},{16,20},{20,16},{24,28},{28,24},{1,5},{5... | collective-permute-start | bytes 884744 | tf_op jit(solution)/shard_map/ppermute | solution.py:30
  53.8 15.3 %collective-permute-start.26 = (bf16[128,2432]{1,0:T(8,128)(2,1)S(1)}, bf16[128,2432]{1,0:T(8,128)(2,1)S(1)}, u32[]{:S(2)}, u32[]{:S(2)}) collective-permute-start(bf16[128,2432]{1,0:T(8,128)(2,1)S(1)} %get-tuple-element.199.refs_1_.refs_3_), channel_id=1, source_target_pairs={{0,8},{4,12},{8,0},{12,4},{16,24},{20,28},{24,16},{28,20},{1,9},{5... | collective-permute-start | bytes 1867784 | tf_op jit(solution)/shard_map/ppermute | solution.py:30
  58.2 13.2 %collective-permute-start.23 = (bf16[512,1152]{1,0:T(8,128)(2,1)S(1)}, bf16[512,1152]{1,0:T(8,128)(2,1)S(1)}, u32[]{:S(2)}, u32[]{:S(2)}) collective-permute-start(bf16[512,1152]{1,0:T(8,128)(2,1)S(1)} %get-tuple-element.189), channel_id=1, source_target_pairs={{0,1},{1,0},{2,3},{3,2},{4,5},{5,4},{6,7},{7,6},{8,9},{9,8},{10,11... | collective-permute-start | bytes 3538952 | tf_op jit(solution)/shard_map/ppermute | solution.py:30
  61.0 10.3 %collective-permute-start.22 = (bf16[512,1152]{1,0:T(8,128)(2,1)S(1)}, bf16[512,1152]{1,0:T(8,128)(2,1)S(1)}, u32[]{:S(2)}, u32[]{:S(2)}) collective-permute-start(bf16[512,1152]{1,0:T(8,128)(2,1)S(1)} %get-tuple-element.188), channel_id=1, source_target_pairs={{0,1},{1,0},{2,3},{3,2},{4,5},{5,4},{6,7},{7,6},{8,9},{9,8},{10,11... | collective-permute-start | bytes 3538952 | tf_op jit(solution)/shard_map/ppermute | solution.py:30
  61.1 2.9 %collective-permute-start.24 = (f32[16,1152]{1,0:T(8,128)S(1)}, f32[16,1152]{1,0:T(8,128)S(1)}, u32[]{:S(2)}, u32[]{:S(2)}) collective-permute-start(f32[16,1152]{1,0:T(8,128)S(1)} %get-tuple-element.192.refs_1_), channel_id=1, source_target_pairs={{0,1},{1,0},{2,3},{3,2},{4,5},{5,4},{6,7},{7,6},{8,9},{9,8},{10,11... | collective-permute-start | bytes 221192 | tf_op jit(solution)/shard_map/ppermute | solution.py:30
  64.2 5.1 %collective-permute-start.25 = (f32[1,7424]{1,0:T(1,128)S(1)}, f32[1,7424]{1,0:T(1,128)S(1)}, u32[]{:S(2)}, u32[]{:S(2)}) collective-permute-start(f32[1,7424]{1,0:T(1,128)S(1)} %get-tuple-element.198.refs_0_), channel_id=1, source_target_pairs={{0,16},{4,20},{8,24},{12,28},{16,0},{20,4},{24,8},{28,12},{1,17},{... | collective-permute-start | bytes 89096 | tf_op jit(solution)/shard_map/ppermute | solution.py:30
  69.3 5.4 %collective-permute-start.29 = (f32[2,7424]{1,0:T(2,128)S(1)}, f32[2,7424]{1,0:T(2,128)S(1)}, u32[]{:S(2)}, u32[]{:S(2)}) collective-permute-start(f32[2,7424]{1,0:T(2,128)S(1)} %get-tuple-element.209.refs_0_), channel_id=1, source_target_pairs={{0,4},{4,0},{8,12},{12,8},{16,20},{20,16},{24,28},{28,24},{1,5},{5... | collective-permute-start | bytes 178184 | tf_op jit(solution)/shard_map/ppermute | solution.py:30
  70.9 7.0 %collective-permute-start.28 = (bf16[128,2048]{1,0:T(8,128)(2,1)S(1)}, bf16[128,2048]{1,0:T(8,128)(2,1)S(1)}, u32[]{:S(2)}, u32[]{:S(2)}) collective-permute-start(bf16[128,2048]{1,0:T(8,128)(2,1)S(1)} %get-tuple-element.208), channel_id=1, source_target_pairs={{0,1},{1,0},{2,3},{3,2},{4,5},{5,4},{6,7},{7,6},{8,9},{9,8},{10,11... | collective-permute-start | bytes 1572872 | tf_op jit(solution)/shard_map/ppermute | solution.py:30
  70.9 7.0 %collective-permute-start.27 = (bf16[128,3072]{1,0:T(8,128)(2,1)S(1)}, bf16[128,3072]{1,0:T(8,128)(2,1)S(1)}, u32[]{:S(2)}, u32[]{:S(2)}) collective-permute-start(bf16[128,3072]{1,0:T(8,128)(2,1)S(1)} %get-tuple-element.207), channel_id=1, source_target_pairs={{0,1},{1,0},{2,3},{3,2},{4,5},{5,4},{6,7},{7,6},{8,9},{9,8},{10,11... | collective-permute-start | bytes 2359304 | tf_op jit(solution)/shard_map/ppermute | solution.py:30
  74.7 8.9 %collective-permute-start.31 = (f32[4,7424]{1,0:T(4,128)S(1)}, f32[4,7424]{1,0:T(4,128)S(1)}, u32[]{:S(2)}, u32[]{:S(2)}) collective-permute-start(f32[4,7424]{1,0:T(4,128)S(1)} %get-tuple-element.215.refs_0_), channel_id=1, source_target_pairs={{0,8},{4,12},{8,0},{12,4},{16,24},{20,28},{24,16},{28,20},{1,9},{5... | collective-permute-start | bytes 356360 | tf_op jit(solution)/shard_map/ppermute | solution.py:30
  79.3 16.6 %collective-permute-start.32 = (bf16[2,144,1152]{2,1,0:T(8,128)(2,1)S(1)}, bf16[2,144,1152]{2,1,0:T(8,128)(2,1)S(1)}, u32[]{:S(2)}, u32[]{:S(2)}) collective-permute-start(bf16[2,144,1152]{2,1,0:T(8,128)(2,1)S(1)} %get-tuple-element.223), channel_id=1, source_target_pairs={{0,4},{4,0},{8,12},{12,8},{16,20},{20,16},{24,28},{28,24},{1,5},{5... | collective-permute-start | bytes 1990664 | tf_op jit(solution)/shard_map/ppermute | solution.py:30
  79.8 3.7 %copy-start.4 = (bf16[1152,1728]{0,1:T(8,128)(2,1)S(1)}, bf16[1152,1728]{0,1:T(8,128)(2,1)}, u32[]{:S(2)}) copy-start(bf16[1152,1728]{0,1:T(8,128)(2,1)} %param.22) | copy-start | bytes 11943940
  83.4 2.3 %collective-permute-start.30 = (bf16[128,2304]{1,0:T(8,128)(2,1)S(1)}, bf16[128,2304]{1,0:T(8,128)(2,1)S(1)}, u32[]{:S(2)}, u32[]{:S(2)}) collective-permute-start(bf16[128,2304]{1,0:T(8,128)(2,1)S(1)} %get-tuple-element.214.refs_0_), channel_id=1, source_target_pairs={{0,1},{1,0},{2,3},{3,2},{4,5},{5,4},{6,7},{7,6},{8,9},{9,8},{10,11... | collective-permute-start | bytes 1769480 | tf_op jit(solution)/shard_map/ppermute | solution.py:30
  83.4 21.1 %collective-permute-start.36 = (bf16[144,2304]{1,0:T(8,128)(2,1)S(1)}, bf16[144,2304]{1,0:T(8,128)(2,1)S(1)}, u32[]{:S(2)}, u32[]{:S(2)}) collective-permute-start(bf16[144,2304]{1,0:T(8,128)(2,1)S(1)} %get-tuple-element.235), channel_id=1, source_target_pairs={{0,8},{4,12},{8,0},{12,4},{16,24},{20,28},{24,16},{28,20},{1,9},{5... | collective-permute-start | bytes 1990664 | tf_op jit(solution)/shard_map/ppermute | solution.py:30
  85.2 1.5 %collective-permute-start.33 = (f32[8,768]{1,0:T(8,128)S(1)}, f32[8,768]{1,0:T(8,128)S(1)}, u32[]{:S(2)}, u32[]{:S(2)}) collective-permute-start(f32[8,768]{1,0:T(8,128)S(1)} %get-tuple-element.225), channel_id=1, source_target_pairs={{0,1},{1,0},{2,3},{3,2},{4,5},{5,4},{6,7},{7,6},{8,9},{9,8},{10,11... | collective-permute-start | bytes 73736 | tf_op jit(solution)/shard_map/ppermute | solution.py:30
  86.8 3.8 %collective-permute-start.34 = (f32[8,288]{1,0:T(8,128)S(1)}, f32[8,288]{1,0:T(8,128)S(1)}, u32[]{:S(2)}, u32[]{:S(2)}) collective-permute-start(f32[8,288]{1,0:T(8,128)S(1)} %get-tuple-element.228), channel_id=1, source_target_pairs={{0,2},{1,3},{2,0},{3,1},{4,6},{5,7},{6,4},{7,5},{8,10},{9,11},{10,... | collective-permute-start | bytes 27656 | tf_op jit(solution)/shard_map/ppermute | solution.py:30
  96.0 16.7 %collective-permute-start.35 = (bf16[144,1152]{1,0:T(8,128)(2,1)S(1)}, bf16[144,1152]{1,0:T(8,128)(2,1)S(1)}, u32[]{:S(2)}, u32[]{:S(2)}) collective-permute-start(bf16[144,1152]{1,0:T(8,128)(2,1)S(1)} %get-tuple-element.234), channel_id=1, source_target_pairs={{0,16},{4,20},{8,24},{12,28},{16,0},{20,4},{24,8},{28,12},{1,17},{... | collective-permute-start | bytes 995336 | tf_op jit(solution)/shard_map/ppermute | solution.py:30

commit v5 on v4

--- a/solution.py
+++ b/solution.py
@@ -494,7 +494,7 @@
             at += size
 
 
-def weight_kernel(n_dp, split_bit, products, n_in, *refs):
+def weight_kernel(n_dp, split, products, n_in, *refs):
     outs, lefts = refs[n_in : -len(products)], refs[-len(products) :]
     half = refs[0].shape[0]
     part = lefts[0].shape[0]
@@ -506,28 +506,27 @@
             left[:, i * half : (i + 1) * half] = value.astype(F32).T.astype(BF)
         right = [refs[j][:, start : start + cols] for j, start in right_rows]
         right = jnp.concatenate(right, axis=0)
-        if split_bit is None:
+        if split is None:
             outs[0][:, at : at + cols] = dot(left[...], right)
         else:
-            stay, send = outs
-            mine = (lax.axis_index("dp") >> split_bit) & 1
-            for k in range(n_dp // 4):
-                for out, side in ((stay, mine), (send, 1 - mine)):
+            near, far = ((lax.axis_index("dp") >> bit) & 1 for bit in split)
+            for (stay, send), k in ((outs[0:2], 1 - far), (outs[2:4], far)):
+                for out, side in ((stay, near), (send, 1 - near)):
                     start = pl.multiple_of((2 * k + side) * r, r)
-                    out[k, :, at : at + cols] = dot(left[pl.ds(start, r), :], right).astype(out.dtype)
+                    out[:, at : at + cols] = dot(left[pl.ds(start, r), :], right).astype(out.dtype)
         at += cols
 
 
-def halve_kernel(bit, stay, other, out_stay, out_send):
-    mine = (lax.axis_index("dp") >> bit) & 1
-    out_stay[...] = stay[mine] + other[mine].astype(F32)
-    out_send[...] = (stay[1 - mine] + other[1 - mine].astype(F32)).astype(BF)
-
-
-def add_kernel(widths, stay, other, *outs):
-    total = stay[...] + other[...].astype(F32)
+def halve_kernel(stay, other, send):
+    send[...] = (stay[...] + other[...].astype(F32)).astype(BF)
+
+
+def add_kernel(widths, n_others, stay, *refs):
+    total = stay[...]
+    for other in refs[:n_others]:
+        total = total + other[...].astype(F32)
     at = 0
-    for out, cols in zip(outs, widths):
+    for out, cols in zip(refs[n_others:], widths):
         out[...] = total[:, at : at + cols]
         at += cols
 
@@ -711,14 +710,13 @@
         )
         return [swap(out, "tensor", 1) for out in outs]
 
-    def first_grads(name, bit, products, args):
+    def first_grads(name, products, args):
         cols = sum(p[2] for p in products)
         scratch = [pltpu.VMEM((part, 4 * half), BF)] * len(products)
         split, outs = None, [((part, cols), F32)]
         if n_dp == 8:
-            split = 0 if bit else 1
-            outs = [((2, chunk, cols), F32), ((2, chunk, cols), BF)]
-        outs = call(
+            split, outs = (0, 2), [((chunk, cols), F32), ((chunk, cols), BF)] * 2
+        return call(
             order,
             lambda *refs: weight_kernel(n_dp, split, products, len(args), *refs),
             name,
@@ -727,17 +725,16 @@
             args,
             scratch,
         )
-        return outs[0], swap(outs[1], "dp", 1 << split) if n_dp == 8 else None
-
-    def second_grads(name, bit, stay, other):
-        if n_dp != 8:
-            return stay, other
-        last = 1 if bit == 2 else 2
-        shape = (chunk, stay.shape[2])
-        stay, send = call(
-            order, lambda *refs: halve_kernel(last, *refs), name, 0.02, [(shape, F32), (shape, BF)], [stay, other]
+
+    def add(name, widths, stay, *others):
+        return call(
+            order,
+            lambda *refs: add_kernel(widths, len(others), *refs),
+            name,
+            0.02,
+            [((chunk, w), F32) for w in widths],
+            [stay, *others],
         )
-        return stay, swap(send, "dp", 1 << last)
 
     def halve_all(grad, done):
         for b in range((n_dp - 1).bit_length()):
@@ -749,19 +746,6 @@
                 grad = stay + swap(send, "dp", 1 << b).astype(F32)
         return grad[0]
 
-    def last_grads(name, bit, widths, stay, other):
-        if n_dp == 8:
-            return call(
-                order,
-                lambda *refs: add_kernel(widths, *refs),
-                name,
-                0.02,
-                [((chunk, w), F32) for w in widths],
-                [stay, other],
-            )
-        grad = halve_all(stay.reshape(n_dp // 2, chunk, -1), [bit])
-        return jnp.split(grad, [sum(widths[:i]) for i in range(1, len(widths))], axis=1)
-
     (part2,) = call(
         order,
         mlp_tail_kernel,
@@ -769,10 +753,9 @@
         1.0,
         [((half, width), BF)],
         [act, *down_ws],
-        also=[far1, grad_f],
-    )
-    part2_other = swap(part2, "tensor", 2)
-    grad_yf = swap(grad_f, "dp", 1)
+    )
+    part2_other = swap(behind(part2, far1), "tensor", 2)
+    grad_yf = swap(behind(grad_f, part2), "dp", 1)
 
     part4, mid_grad, low_back, stacked, back_sums = call(
         order,
@@ -790,10 +773,10 @@
             lengths, part3, part3_other, mods, normed2, inv2, branch1, cot,
             *out_ws, *qkv_ws, saved_a, saved_b, probs,
         ],
+        also=[grad_f],
     )
     part4_other = swap(part4, "tensor", 2)
     s_wide = pad_lanes(n_qkv)
-    rows_yf = swap(rows_f, "dp", 1)
     pack3, chunks3 = call(
         order,
         lambda *refs: pack_back_kernel(n_dp, *refs),
@@ -821,6 +804,15 @@
             limit=40,
         )
 
+    result, gate2_sum = call(
+        order,
+        lambda *refs: output_kernel(frames, spots, *refs),
+        "output",
+        2.0,
+        [((half, width), BF), ((1, width), F32)],
+        [lengths, tok, part2, part2_other, bias_row, mods, branch1, cot],
+    )
+    rows_yf = swap(behind(rows_f, gate2_sum), "dp", 1)
     sums2 = remake(
         "remake_near",
         [low2, rows_y, rows_f],
@@ -839,14 +831,6 @@
         [low_grad, grad_y, grad_f, grad_yf],
     )
     grads_other = swap(grads_core, "tensor", 1)
-    result, gate2_sum = call(
-        order,
-        lambda *refs: output_kernel(frames, spots, *refs),
-        "output",
-        1.0,
-        [((half, width), BF), ((1, width), F32)],
-        [lengths, tok, part2, part2_other, bias_row, mods, branch1, cot],
-    )
     both, sums = call(
         order,
         lambda *refs: input_back_kernel(frames, *refs),
@@ -863,9 +847,10 @@
         order,
         rows_kernel,
         "rows_norm",
-        0.02,
+        3.0,
         [((4 * half, width), BF)],
         [low2, rows_y, rows_f, rows_yf],
+        also=[sums_other],
     )
     rows_other = swap(rows_core, "tensor", 1)
 
@@ -885,21 +870,14 @@
         [labels, sums, sums_other, cond],
     )
 
-    def stack(name, value, flip):
+    def stack(name, value, flip, us=0.02):
         n, cols = value.shape
         other = swap(value, "dp", flip)
-        return call(order, stack_kernel, name, 0.02, [((2 * n, cols), F32)], [value, other])[0]
+        return call(order, stack_kernel, name, us, [((2 * n, cols), F32)], [value, other])[0]
 
     def mlp_grads(stay, other):
         if n_dp == 8:
-            return call(
-                order,
-                lambda *refs: add_kernel([hidden] * 2, *refs),
-                "mlp_add",
-                0.02,
-                [((chunk, hidden), F32)] * 2,
-                [stay, other],
-            )
+            return add("mlp_add", [hidden] * 2, stay, other)
         return [halve_all(g.reshape(n_dp // 4, chunk, hidden), [0, 2]) for g in (stay, other)]
 
     sums2 = remake("remake_yf", [rows_yf], [grad_yf], [], sums2, False)
@@ -911,13 +889,9 @@
             [(3, n_att, att_core), (3, att_far, wide), (4, n_att, att_core), (5, 0, wide)],
         ],
         [far3, pack3, chunks3, far1, pack1, chunks1],
-        us=6.5,
-    )
-    vector = stack("stack0", vector, flips[0])
-    core_args = ([rows_other], [grads_other], [])
-    sums2 = remake("remake_core0", *core_args, sums2, False, (0, 2 * half), us=8.0)
-    for i, flip in enumerate(flips[1:-1]):
-        vector = stack("stack%d" % (i + 1), vector, flip)
+        us=3.0,
+    )
+    vector = stack("stack0", vector, flips[0], us=8.0)
     n_mix3 = s_wide + wide
     n_mix1 = att_core + wide
     left_qkv = ((1, 0), (7, n_mix1 + att_core), (2, att_far), (7, att_core))
@@ -926,13 +900,30 @@
     right_out = ((0, 0), (7, n_mix1), (2, 0), (7, 0))
     qkv_grad = first_grads(
         "qkv_grad",
-        1,
         [(left_qkv, right_qkv, n_qkv), (left_out, right_out, n_att)],
         [pack1, chunks1, far1, pack3, chunks3, far3, mixed3, mixed1],
     )
+    if n_dp == 8:
+        far_other = swap(qkv_grad[1], "dp", 1)
+    for i, flip in enumerate(flips[1:-1]):
+        vector = stack("stack%d" % (i + 1), vector, flip)
+    core_args = ([rows_other], [grads_other], [])
+    sums2 = remake("remake_core0", *core_args, sums2, False, (0, 2 * half), us=2.0)
     mlp_grad = remake("remake_core1", *core_args, sums2, True, (2 * half, 4 * half))
     mlp_grad = (mlp_grad[0], swap(mlp_grad[1], "dp", 2) if n_dp == 8 else mlp_grad[1])
     both_other = swap(behind(both, mlp_grad[0]), "tensor", 1)
+    if n_dp == 8:
+        stay_far, send_far, stay_near, send_near = qkv_grad
+        near_other = swap(send_near, "dp", 1)
+        (send_far,) = call(
+            order,
+            halve_kernel,
+            "qkv_halve",
+            0.02,
+            [(send_far.shape, BF)],
+            [stay_far, far_other],
+        )
+        qkv_grad = stay_near, near_other, swap(send_far, "dp", 4)
     vector = stack("stack_last", vector, flips[-1])
     ada_grad, ada_bias_grad, qv_grad, proj_grad, fc1_grad, fc2_grad, stay, send, cond_cols, labels_all = call(
         order,
@@ -966,9 +957,12 @@
         [((columns, n_classes), F32)],
         [mine, swap(send, "tensor", 2), cond_cols, labels_all],
     )
-    qkv_grad = second_grads("qkv_halve", 1, *qkv_grad)
     down_grad, up_grad = mlp_grads(*mlp_grad)
-    qkv_grad, out_grad = last_grads("qkv_add", 1, [n_qkv, n_att], *qkv_grad)
+    if n_dp == 8:
+        qkv_grad, out_grad = add("qkv_add", [n_qkv, n_att], *qkv_grad)
+    else:
+        grad = halve_all(qkv_grad[0].reshape(n_dp // 2, chunk, -1), [1])
+        qkv_grad, out_grad = grad[:, :n_qkv], grad[:, n_qkv:]
     return (
         result,
         tokens_grad,

time: 114 us -> 107 us (0.939)
  waiting for transfers between devices: 36.7 us -> 28.9 us
  local copies, waits for them, and re-layouts: 0.83 us -> 2.95 us
    ppermute x37 -> x38, waiting for transfers between devices: 36.7 us -> 28.9 us  [swap(): return lax.ppermute(value, axis, [(i, i ^ flip) for i in range(size)])]
    unnamed x19, local copies, waits for them, and re-layouts: 0.72 us -> 2.84 us
    ppermute x37 -> x38, starting transfers between devices: 34.6 us -> 33.5 us  [swap(): return lax.ppermute(value, axis, [(i, i ^ flip) for i in range(size)])]
  transfers between devices with their start and end apart: 37 -> 38, of which waited for: 13 -> 15; matrix products, arithmetic and copies ran while one was open for 1% -> 1% of each run, Pallas kernels for 32% -> 34%
where the time goes in v5:
time: 107 us
  Pallas kernels  37.7 us (35%)
  starting transfers between devices  33.5 us (31%)
  waiting for transfers between devices  28.9 us (27%)
  local copies, waits for them, and re-layouts  2.95 us (3%)
  between operations  2.92 us (3%)
    pallas_call x30, Pallas kernels, call(): pl.pallas_call(whole, out_shape=[jax.ShapeDtypeStruct(s, d) for s, d in [...  37.7 us
    ppermute x38, starting transfers between devices, swap(): return lax.ppermute(value, axis, [(i, i ^ flip) for i in range(size)])  33.5 us
    ppermute x38, waiting for transfers between devices, swap(): return lax.ppermute(value, axis, [(i, i ^ flip) for i in range(size)])  28.9 us
    unnamed x19, local copies, waits for them, and re-layouts  2.84 us
  transfers between devices with their start and end apart: 38, of which 15 were waited for; matrix products, arithmetic and copies ran while one was open for 1% of the time, Pallas kernels for 34%

profile of v5, /device:TPU:0, one launch (start us, length us, event | category | flops | bytes accessed | tf_op | source)
XLA Modules:
  0.0 106.8 jit_solution(5387405821951305097)
XLA Ops:
  1.3 0.2 copy-done
  1.7 3.0 %collective-permute-start.1 = (bf16[1,288]{1,0:T(2,128)(2,1)S(1)}, bf16[1,288]{1,0:T(2,128)(2,1)S(1)}, u32[]{:S(2)}, u32[]{:S(2)}) collective-permute-start(bf16[1,288]{1,0:T(2,128)(2,1)S(1)} %copy.31.refs_0_), channel_id=1, source_target_pairs={{0,2},{1,3},{2,0},{3,1},{4,6},{5,7},{6,4},{7,5},{8,10},{9,11},{10,... | collective-permute-start | bytes 1736 | tf_op jit(solution)/shard_map/ppermute | solution.py:30
  5.4 0.8 add_add_fusion
  6.3 0.6 collective-permute-start.2
  6.9 0.8 collective-permute-done.2.refs_3_
  7.7 0.5 collective-permute-start.6
  8.4 0.4 collective-permute-start.5
  8.7 0.4 copy-done.3
  9.1 1.2 %modulation.1 = (f32[1,1152]{1,0:T(1,128)S(1)}, f32[1,1728]{1,0:T(1,128)S(1)}, f32[8,128]{1,0:T(8,128)S(1)}) custom-call(bf16[1,288]{1,0:T(2,128)(2,1)S(1)} %copy.31.refs_0_, bf16[1,288]{1,0:T(2,128)(2,1)S(1)} %collective-permute-done.refs_1_, bf16[1,288]{1,0:T(2,128)(2,1)S(1)} %collective-permute-done.1.refs_2_, ...), custom_call_target="tpu_custom_call" | custom-call | flops 1100000000 | bytes 1024 | tf_op jit(solution)/shard_map/modulation/pallas_call | solution.py:49
  10.3 1.1 %collective-permute-start.4 = (f32[1,1728]{1,0:T(1,128)S(1)}, f32[1,1728]{1,0:T(1,128)S(1)}, u32[]{:S(2)}, u32[]{:S(2)}) collective-permute-start(f32[1,1728]{1,0:T(1,128)S(1)} %get-tuple-element.141.refs_2_), channel_id=1, source_target_pairs={{0,2},{1,3},{2,0},{3,1},{4,6},{5,7},{6,4},{7,5},{8,10},{9,11},{10,... | collective-permute-start | bytes 20744 | tf_op jit(solution)/shard_map/ppermute | solution.py:30
  11.5 0.3 start.1
  11.8 2.3 %collective-permute-done.4.refs_4_ = f32[1,1728]{1,0:T(1,128)S(1)} collective-permute-done((f32[1,1728]{1,0:T(1,128)S(1)}, f32[1,1728]{1,0:T(1,128)S(1)}, u32[]{:S(2)}, u32[]{:S(2)}) %collective-permute-start.4) | collective-permute-done | bytes 6944 | tf_op jit(solution)/shard_map/ppermute | solution.py:30
  14.1 1.1 %collective-permute-done.8.refs_5_ = f32[1,1728]{1,0:T(1,128)S(1)} collective-permute-done((f32[1,1728]{1,0:T(1,128)S(1)}, f32[1,1728]{1,0:T(1,128)S(1)}, u32[]{:S(2)}, u32[]{:S(2)}) %collective-permute-start.8) | collective-permute-done | bytes 6944 | tf_op jit(solution)/shard_map/ppermute | solution.py:30
  15.4 0.3 collective-permute-start.10
  16.4 4.2 %attention.1 = (bf16[128,1152]{1,0:T(8,128)(2,1)S(1)}, f32[8,1152]{1,0:T(8,128)S(1)}, bf16[128,1152]{1,0:T(8,128)(2,1)S(1)}, bf16[128,864]{1,0:T(8,128)(2,1)S(1)...) custom-call(s32[1]{0:T(128)S(6)} %copy.32.refs_0_, ...), custom_call_target="tpu_custom_call" | custom-call | flops 4400000000 | bytes 1024 | tf_op jit(solution)/shard_map/attention/pallas_call | solution.py:49
  20.7 1.1 %collective-permute-start.9 = (bf16[128,1152]{1,0:T(8,128)(2,1)S(1)}, bf16[128,1152]{1,0:T(8,128)(2,1)S(1)}, u32[]{:S(2)}, u32[]{:S(2)}) collective-permute-start(bf16[128,1152]{1,0:T(8,128)(2,1)S(1)} %get-tuple-element.146.refs_1_), channel_id=1, source_target_pairs={{0,2},{1,3},{2,0},{3,1},{4,6},{5,7},{6,4},{7,5},{8,10},{9,11},{10,... | collective-permute-start | bytes 884744 | tf_op jit(solution)/shard_map/ppermute | solution.py:30
  21.8 1.3 %early_back.1 = (f32[128,1152]{1,0:T(8,128)S(1)}, f32[128,1152]{1,0:T(8,128)S(1)}, bf16[128,1152]{1,0:T(8,128)(2,1)S(1)}, bf16[128,1280]{1,0:T(8,128)(2,1)S(1)},...) custom-call(s32[1]{0:T(128)S(6)} %copy.32.refs_0_, ...), custom_call_target="tpu_custom_call" | custom-call | flops 2200000000 | bytes 1024 | tf_op jit(solution)/shard_map/early_back/pallas_call | solution.py:49
  23.1 1.6 %collective-permute-start.17 = (bf16[128,1152]{1,0:T(8,128)(2,1)S(1)}, bf16[128,1152]{1,0:T(8,128)(2,1)S(1)}, u32[]{:S(2)}, u32[]{:S(2)}) collective-permute-start(bf16[128,1152]{1,0:T(8,128)(2,1)S(1)} %get-tuple-element.168.refs_7_.refs_0_), channel_id=1, source_target_pairs={{0,4},{4,0},{8,12},{12,8},{16,20},{20,16},{24,28},{28,24},{1,5},{5... | collective-permute-start | bytes 884744 | tf_op jit(solution)/shard_map/ppermute | solution.py:30
  24.7 2.6 %collective-permute-start.13 = (bf16[128,1152]{1,0:T(8,128)(2,1)S(1)}, bf16[128,1152]{1,0:T(8,128)(2,1)S(1)}, u32[]{:S(2)}, u32[]{:S(2)}) collective-permute-start(bf16[128,1152]{1,0:T(8,128)(2,1)S(1)} %get-tuple-element.168.refs_7_.refs_0_), channel_id=1, source_target_pairs={{0,16},{4,20},{8,24},{12,28},{16,0},{20,4},{24,8},{28,12},{1,17},{... | collective-permute-start | bytes 884744 | tf_op jit(solution)/shard_map/ppermute | solution.py:30
  27.2 1.6 %collective-permute-start.15 = (bf16[128,1280]{1,0:T(8,128)(2,1)S(1)}, bf16[128,1280]{1,0:T(8,128)(2,1)S(1)}, u32[]{:S(2)}, u32[]{:S(2)}) collective-permute-start(bf16[128,1280]{1,0:T(8,128)(2,1)S(1)} %get-tuple-element.174.refs_4_.refs_0_), channel_id=1, source_target_pairs={{0,8},{4,12},{8,0},{12,4},{16,24},{20,28},{24,16},{28,20},{1,9},{5... | collective-permute-start | bytes 983048 | tf_op jit(solution)/shard_map/ppermute | solution.py:30
  28.8 1.0 collective-permute-done.9.refs_2_
  29.8 3.0 %mlp.1 = (bf16[128,1152]{1,0:T(8,128)(2,1)S(1)}, bf16[128,2304]{1,0:T(8,128)(2,1)S(1)}, bf16[128,1152]{1,0:T(8,128)(2,1)S(1)}, bf16[128,1152]{1,0:T(8,128)(2,1)S...) custom-call(bf16[128,1152]{1,0:T(8,128)(2,1)S(1)} %get-tuple-element, ...), custom_call_target="tpu_custom_call" | custom-call | flops 3300000000 | bytes 1024 | tf_op jit(solution)/shard_map/mlp/pallas_call | solution.py:49
  32.9 1.1 %collective-permute-start.12 = (bf16[128,1152]{1,0:T(8,128)(2,1)S(1)}, bf16[128,1152]{1,0:T(8,128)(2,1)S(1)}, u32[]{:S(2)}, u32[]{:S(2)}) collective-permute-start(bf16[128,1152]{1,0:T(8,128)(2,1)S(1)} %get-tuple-element.158.refs_1_), channel_id=1, source_target_pairs={{0,2},{1,3},{2,0},{3,1},{4,6},{5,7},{6,4},{7,5},{8,10},{9,11},{10,... | collective-permute-start | bytes 884744 | tf_op jit(solution)/shard_map/ppermute | solution.py:30
  34.0 2.6 %collective-permute-start.20 = (bf16[128,1152]{1,0:T(8,128)(2,1)S(1)}, bf16[128,1152]{1,0:T(8,128)(2,1)S(1)}, u32[]{:S(2)}, u32[]{:S(2)}) collective-permute-start(bf16[128,1152]{1,0:T(8,128)(2,1)S(1)} %get-tuple-element.187.refs_4_.refs_0_), channel_id=1, source_target_pairs={{0,16},{4,20},{8,24},{12,28},{16,0},{20,4},{24,8},{28,12},{1,17},{... | collective-permute-start | bytes 884744 | tf_op jit(solution)/shard_map/ppermute | solution.py:30
  36.6 1.7 %mlp_tail.1 = (bf16[128,1152]{1,0:T(8,128)(2,1)S(1)}, f32[8,128]{1,0:T(8,128)S(1)}) custom-call(bf16[128,2304]{1,0:T(8,128)(2,1)S(1)} %get-tuple-element.165.refs_0_.refs_10_, bf16[1152,1152]{1,0:T(8,128)(2,1)S(1)} %copy-done.1, bf16[1152,1152]{1,0:T(8,128)(2,1)S(1)} %collective-permute-done.11.refs_4_.refs_2_, f32[8,128]{1,0:T(8,128)S(1)} %get-tuple-element.166.refs_3_), custom_call_target="tpu_custom_call" | custom-call | flops 1100000000 | bytes 1024 | tf_op jit(solution)/shard_map/mlp_tail/pallas_call | solution.py:49
  38.3 1.6 %collective-permute-start.19 = (bf16[128,1152]{1,0:T(8,128)(2,1)S(1)}, bf16[128,1152]{1,0:T(8,128)(2,1)S(1)}, u32[]{:S(2)}, u32[]{:S(2)}) collective-permute-start(bf16[128,1152]{1,0:T(8,128)(2,1)S(1)} %get-tuple-element.187.refs_4_.refs_0_), channel_id=1, source_target_pairs={{0,4},{4,0},{8,12},{12,8},{16,20},{20,16},{24,28},{28,24},{1,5},{5... | collective-permute-start | bytes 884744 | tf_op jit(solution)/shard_map/ppermute | solution.py:30
  39.9 2.6 %collective-permute-done.13.refs_16_.refs_9_.refs_2_ = bf16[128,1152]{1,0:T(8,128)(2,1)S(1)} collective-permute-done((bf16[128,1152]{1,0:T(8,128)(2,1)S(1)}, bf16[128,1152]{1,0:T(8,128)(2,1)S(1)}, u32[]{:S(2)}, u32[]{:S(2)}) %collective-permute-start.13) | collective-permute-done | bytes 294944 | tf_op jit(solution)/shard_map/ppermute | solution.py:30
  42.4 0.5 collective-permute-start.18
  42.9 1.0 collective-permute-start.16
  43.9 4.3 %attention_back.1 = (bf16[128,1152]{1,0:T(8,128)(2,1)S(1)}, f32[128,1152]{1,0:T(8,128)S(1)}, bf16[128,1152]{1,0:T(8,128)(2,1)S(1)}, bf16[128,1792]{1,0:T(8,128)(...) custom-call(s32[1]{0:T(128)S(6)} %copy.32.refs_0_, bf16[128,1152]{1,0:T(8,128)(2,1)S(1)} %get-tuple-element.158.refs_1_, ...), custom_call_target="tpu_custom_call" | custom-call | flops 5500000256 | bytes 1024 | tf_op jit(solution)/shard_map/attention_back/pallas_call | solution.py:49
  48.2 1.1 %collective-permute-start.14 = (bf16[128,1152]{1,0:T(8,128)(2,1)S(1)}, bf16[128,1152]{1,0:T(8,128)(2,1)S(1)}, u32[]{:S(2)}, u32[]{:S(2)}) collective-permute-start(bf16[128,1152]{1,0:T(8,128)(2,1)S(1)} %get-tuple-element.169.refs_1_), channel_id=1, source_target_pairs={{0,2},{1,3},{2,0},{3,1},{4,6},{5,7},{6,4},{7,5},{8,10},{9,11},{10,... | collective-permute-start | bytes 884744 | tf_op jit(solution)/shard_map/ppermute | solution.py:30
  49.5 2.6 %collective-permute-done.16.refs_3_ = bf16[128,1152]{1,0:T(8,128)(2,1)S(1)} collective-permute-done((bf16[128,1152]{1,0:T(8,128)(2,1)S(1)}, bf16[128,1152]{1,0:T(8,128)(2,1)S(1)}, u32[]{:S(2)}, u32[]{:S(2)}) %collective-permute-start.16) | collective-permute-done | bytes 294944 | tf_op jit(solution)/shard_map/ppermute | solution.py:30
  52.0 0.7 collective-permute-start.26
  52.7 0.3 output.1
  53.2 0.8 collective-permute-start.21
  54.0 3.6 %remake_near.1 = (f32[288,1152]{1,0:T(8,128)S(1)}, f32[288,1152]{1,0:T(8,128)S(1)}, f32[8,128]{1,0:T(8,128)S(1)}) custom-call(bf16[288,1152]{1,0:T(8,128)(2,1)S(1)} %get-tuple-element.185.refs_0_, bf16[1152,1152]{1,0:T(8,128)(2,1)S(1)} %copy-done.2, bf16[1152,1152]{1,0:T(8,128)(2,1)S(1)} %copy-done.1, ...), custom_call_target="tpu_custom_call" | custom-call | flops 1100000000 | bytes 1024 | tf_op jit(solution)/shard_map/remake_near/pallas_call | solution.py:49
  57.7 0.5 input_back.1
  58.3 0.5 collective-permute-start.24
  58.8 0.8 collective-permute-done.22.refs_5_.refs_2_
  59.6 1.4 %collective-permute-done.21.refs_3_.refs_4_ = bf16[128,1152]{1,0:T(8,128)(2,1)S(1)} collective-permute-done((bf16[128,1152]{1,0:T(8,128)(2,1)S(1)}, bf16[128,1152]{1,0:T(8,128)(2,1)S(1)}, u32[]{:S(2)}, u32[]{:S(2)}) %collective-permute-start.21) | collective-permute-done | bytes 294944 | tf_op jit(solution)/shard_map/ppermute | solution.py:30
  61.2 2.0 %collective-permute-start.25 = (f32[1,7424]{1,0:T(1,128)S(1)}, f32[1,7424]{1,0:T(1,128)S(1)}, u32[]{:S(2)}, u32[]{:S(2)}) collective-permute-start(f32[1,7424]{1,0:T(1,128)S(1)} %get-tuple-element.205.refs_0_), channel_id=1, source_target_pairs={{0,16},{4,20},{8,24},{12,28},{16,0},{20,4},{24,8},{28,12},{1,17},{... | collective-permute-start | bytes 89096 | tf_op jit(solution)/shard_map/ppermute | solution.py:30
  63.2 2.2 %remake_yf.1 = (f32[288,1152]{1,0:T(8,128)S(1)}, f32[288,1152]{1,0:T(8,128)S(1)}, f32[8,128]{1,0:T(8,128)S(1)}) custom-call(bf16[288,1152]{1,0:T(8,128)(2,1)S(1)} %get-tuple-element.185.refs_0_, bf16[1152,1152]{1,0:T(8,128)(2,1)S(1)} %copy-done.2, bf16[1152,1152]{1,0:T(8,128)(2,1)S(1)} %copy-done.1, ...), custom_call_target="tpu_custom_call" | custom-call | flops 22000000 | bytes 1024 | tf_op jit(solution)/shard_map/remake_yf/pallas_call | solution.py:49
  65.4 1.5 %collective-permute-done.26.refs_0_.refs_5_ = bf16[128,2432]{1,0:T(8,128)(2,1)S(1)} collective-permute-done((bf16[128,2432]{1,0:T(8,128)(2,1)S(1)}, bf16[128,2432]{1,0:T(8,128)(2,1)S(1)}, u32[]{:S(2)}, u32[]{:S(2)}) %collective-permute-start.26) | collective-permute-done | bytes 622624 | tf_op jit(solution)/shard_map/ppermute | solution.py:30
  67.2 0.5 collective-permute-start.28
  67.7 0.7 collective-permute-start.27
  68.4 0.7 collective-permute-done.29.refs_7_
  69.1 1.1 %collective-permute-done.28.refs_6_ = bf16[128,3072]{1,0:T(8,128)(2,1)S(1)} collective-permute-done((bf16[128,3072]{1,0:T(8,128)(2,1)S(1)}, bf16[128,3072]{1,0:T(8,128)(2,1)S(1)}, u32[]{:S(2)}, u32[]{:S(2)}) %collective-permute-start.28) | collective-permute-done | bytes 786464 | tf_op jit(solution)/shard_map/ppermute | solution.py:30
  70.2 1.4 %qkv_grad.1 = (f32[144,1152]{1,0:T(8,128)S(1)}, bf16[144,1152]{1,0:T(8,128)(2,1)S(1)}, f32[144,1152]{1,0:T(8,128)S(1)}, bf16[144,1152]{1,0:T(8,128)(2,1)S(1)}, f32[8,128]{1,0:T(8,128)S(1)}) custom-call(bf16[128,1280]{1,0:T(8,128)(2,1)S(1)} %get-tuple-element.174.refs_4_.refs_0_, bf16[128,640]{1,0:T(8,128)(2,1)S(1)} %get-tuple-element.208.refs_5_.refs_1_, ...), custom_call_target="tpu_custom_call" | custom-call | flops 22000000 | bytes 1024 | tf_op jit(solution)/shard_map/qkv_grad/pallas_call | solution.py:49
  71.6 0.7 collective-permute-start.32
  72.3 1.7 %collective-permute-start.31 = (f32[4,7424]{1,0:T(4,128)S(1)}, f32[4,7424]{1,0:T(4,128)S(1)}, u32[]{:S(2)}, u32[]{:S(2)}) collective-permute-start(f32[4,7424]{1,0:T(4,128)S(1)} %get-tuple-element.222.refs_0_), channel_id=1, source_target_pairs={{0,8},{4,12},{8,0},{12,4},{16,24},{20,28},{24,16},{28,20},{1,9},{5... | collective-permute-start | bytes 356360 | tf_op jit(solution)/shard_map/ppermute | solution.py:30
  74.0 3.2 %remake_core0.1 = (f32[288,1152]{1,0:T(8,128)S(1)}, f32[288,1152]{1,0:T(8,128)S(1)}, f32[8,128]{1,0:T(8,128)S(1)}) custom-call(bf16[288,1152]{1,0:T(8,128)(2,1)S(1)} %get-tuple-element.185.refs_0_, bf16[1152,1152]{1,0:T(8,128)(2,1)S(1)} %copy-done.2, bf16[1152,1152]{1,0:T(8,128)(2,1)S(1)} %copy-done.1, ...), custom_call_target="tpu_custom_call" | custom-call | flops 2200000000 | bytes 1024 | tf_op jit(solution)/shard_map/remake_core0/pallas_call | solution.py:49
  77.2 3.5 %remake_core1.1 = (f32[144,2304]{1,0:T(8,128)S(1)}, bf16[144,2304]{1,0:T(8,128)(2,1)S(1)}, f32[8,128]{1,0:T(8,128)S(1)}) custom-call(bf16[288,1152]{1,0:T(8,128)(2,1)S(1)} %get-tuple-element.185.refs_0_, bf16[1152,1152]{1,0:T(8,128)(2,1)S(1)} %copy-done.2, bf16[1152,1152]{1,0:T(8,128)(2,1)S(1)} %copy-done.1, ...), custom_call_target="tpu_custom_call" | custom-call | flops 22000000 | bytes 1024 | tf_op jit(solution)/shard_map/remake_core1/pallas_call | solution.py:49
  80.8 0.5 collective-permute-start.35
  81.2 1.4 %collective-permute-start.33 = (bf16[144,1152]{1,0:T(8,128)(2,1)S(1)}, bf16[144,1152]{1,0:T(8,128)(2,1)S(1)}, u32[]{:S(2)}, u32[]{:S(2)}) collective-permute-start(bf16[144,1152]{1,0:T(8,128)(2,1)S(1)} %get-tuple-element.233), channel_id=1, source_target_pairs={{0,4},{4,0},{8,12},{12,8},{16,20},{20,16},{24,28},{28,24},{1,5},{5... | collective-permute-start | bytes 995336 | tf_op jit(solution)/shard_map/ppermute | solution.py:30
  82.7 2.0 %collective-permute-start.34 = (bf16[144,1152]{1,0:T(8,128)(2,1)S(1)}, bf16[144,1152]{1,0:T(8,128)(2,1)S(1)}, u32[]{:S(2)}, u32[]{:S(2)}) collective-permute-start(bf16[144,1152]{1,0:T(8,128)(2,1)S(1)} %get-tuple-element.234), channel_id=1, source_target_pairs={{0,16},{4,20},{8,24},{12,28},{16,0},{20,4},{24,8},{28,12},{1,17},{... | collective-permute-start | bytes 995336 | tf_op jit(solution)/shard_map/ppermute | solution.py:30
  84.8 2.1 %copy-done.4 = bf16[1152,1728]{0,1:T(8,128)(2,1)S(1)} copy-done((bf16[1152,1728]{0,1:T(8,128)(2,1)S(1)}, bf16[1152,1728]{0,1:T(8,128)(2,1)}, u32[]{:S(2)}) %copy-start.4) | copy-done | bytes 3981336
  86.9 1.6 %gathered.1 = (f32[144,1728]{1,0:T(8,128)}, f32[1728]{0:T(1024)}, f32[576]{0:T(1024)}, f32[1152]{0:T(1024)}, f32[1152]{0:T(1024)}, /*index=5*/f32[1152]{0:T(1024...) custom-call(bf16[1728,1152]{1,0:T(8,128)(2,1)S(1)} %bitcast.13, ...), custom_call_target="tpu_custom_call" | custom-call | flops 5500000256 | bytes 1024 | tf_op jit(solution)/shard_map/gathered/pallas_call | solution.py:49
  88.6 1.1 %join.1 = (bf16[256,1152]{1,0:T(8,128)(2,1)}, bf16[256,1152]{1,0:T(8,128)(2,1)}, f32[8,128]{1,0:T(8,128)S(1)}) custom-call(bf16[128,2304]{1,0:T(8,128)(2,1)S(1)} %get-tuple-element.221.refs_0_, bf16[128,2304]{1,0:T(8,128)(2,1)S(1)} %collective-permute-done.30.refs_1_, f32[8,128]{1,0:T(8,128)S(1)} %get-tuple-element.229.refs_2_), custom_call_target="tpu_custom_call" | custom-call | flops 22000000 | bytes 1024 | tf_op jit(solution)/shard_map/join/pallas_call | solution.py:49
  89.8 1.0 collective-permute-start.37
  90.8 2.7 %collective-permute-done.37.refs_1_ = f32[8,288]{1,0:T(8,128)S(1)} collective-permute-done((f32[8,288]{1,0:T(8,128)S(1)}, f32[8,288]{1,0:T(8,128)S(1)}, u32[]{:S(2)}, u32[]{:S(2)}) %collective-permute-start.37) | collective-permute-done | bytes 9248 | tf_op jit(solution)/shard_map/ppermute | solution.py:30
  93.5 1.0 table.1
  94.5 10.1 %collective-permute-done.35.refs_1_ = bf16[144,2304]{1,0:T(8,128)(2,1)S(1)} collective-permute-done((bf16[144,2304]{1,0:T(8,128)(2,1)S(1)}, bf16[144,2304]{1,0:T(8,128)(2,1)S(1)}, u32[]{:S(2)}, u32[]{:S(2)}) %collective-permute-start.35) | collective-permute-done | bytes 663584 | tf_op jit(solution)/shard_map/ppermute | solution.py:30
  104.5 1.2 %mlp_add.1 = (f32[144,1152]{1,0:T(8,128)}, f32[144,1152]{1,0:T(8,128)}, f32[8,128]{1,0:T(8,128)S(1)}) custom-call(f32[144,2304]{1,0:T(8,128)S(1)} %get-tuple-element.220.refs_0_, bf16[144,2304]{1,0:T(8,128)(2,1)S(1)} %collective-permute-done.35.refs_1_, f32[8,128]{1,0:T(8,128)S(1)} %get-tuple-element.244.refs_2_), custom_call_target="tpu_custom_call" | custom-call | flops 22000000 | bytes 1024 | tf_op jit(solution)/shard_map/mlp_add/pallas_call | solution.py:49
  105.7 1.0 qkv_add.1
  (64 shorter events, 2.0 us)
Async XLA Ops:
  0.6 0.9 copy-start
  1.7 4.6 %collective-permute-start.1 = (bf16[1,288]{1,0:T(2,128)(2,1)S(1)}, bf16[1,288]{1,0:T(2,128)(2,1)S(1)}, u32[]{:S(2)}, u32[]{:S(2)}) collective-permute-start(bf16[1,288]{1,0:T(2,128)(2,1)S(1)} %copy.31.refs_0_), channel_id=1, source_target_pairs={{0,2},{1,3},{2,0},{3,1},{4,6},{5,7},{6,4},{7,5},{8,10},{9,11},{10,... | collective-permute-start | bytes 1736 | tf_op jit(solution)/shard_map/ppermute | solution.py:30
  4.7 2.2 %collective-permute-start = (bf16[1,288]{1,0:T(2,128)(2,1)S(1)}, bf16[1,288]{1,0:T(2,128)(2,1)S(1)}, u32[]{:S(2)}, u32[]{:S(2)}) collective-permute-start(bf16[1,288]{1,0:T(2,128)(2,1)S(1)} %copy.31.refs_0_), channel_id=1, source_target_pairs={{0,1},{1,0},{2,3},{3,2},{4,5},{5,4},{6,7},{7,6},{8,9},{9,8},{10,11... | collective-permute-start | bytes 1736 | tf_op jit(solution)/shard_map/ppermute | solution.py:30
  6.2 1.6 %copy-start.5 = (bf16[1152,864]{0,1:T(8,128)(2,1)S(1)}, bf16[1152,864]{0,1:T(8,128)(2,1)}, u32[]{:S(2)}) copy-start(bf16[1152,864]{0,1:T(8,128)(2,1)} %param.24) | copy-start | bytes 5971972
  6.2 2.1 %copy-start.6 = (bf16[1152,288]{0,1:T(8,128)(2,1)S(1)}, bf16[1152,288]{0,1:T(8,128)(2,1)}, u32[]{:S(2)}) copy-start(bf16[1152,288]{0,1:T(8,128)(2,1)} %param.26) | copy-start | bytes 1990660
  6.2 2.9 %copy-start.3 = (bf16[1152,1728]{0,1:T(8,128)(2,1)S(1)}, bf16[1152,1728]{0,1:T(8,128)(2,1)}, u32[]{:S(2)}) copy-start(bf16[1152,1728]{0,1:T(8,128)(2,1)} %param.22) | copy-start | bytes 11943940
  6.3 1.4 %collective-permute-start.2 = (bf16[1,288]{1,0:T(2,128)(2,1)S(1)}, bf16[1,288]{1,0:T(2,128)(2,1)S(1)}, u32[]{:S(2)}, u32[]{:S(2)}) collective-permute-start(bf16[1,288]{1,0:T(2,128)(2,1)S(1)} %collective-permute-done.1.refs_2_), channel_id=1, source_target_pairs={{0,1},{1,0},{2,3},{3,2},{4,5},{5,4},{6,7},{7,6},{8,9},{9,8},{10,11... | collective-permute-start | bytes 1736 | tf_op jit(solution)/shard_map/ppermute | solution.py:30
  7.7 6.3 %collective-permute-start.6 = (bf16[864,1152]{1,0:T(8,128)(2,1)S(1)}, bf16[864,1152]{1,0:T(8,128)(2,1)S(1)}, u32[]{:S(2)}, u32[]{:S(2)}) collective-permute-start(bf16[864,1152]{1,0:T(8,128)(2,1)S(1)} %bitcast.14), channel_id=1, source_target_pairs={{0,1},{1,0},{2,3},{3,2},{4,5},{5,4},{6,7},{7,6},{8,9},{9,8},{10,11... | collective-permute-start | bytes 5971976 | tf_op jit(solution)/shard_map/ppermute | solution.py:30
  8.2 5.8 %collective-permute-start.7 = (bf16[288,1152]{1,0:T(8,128)(2,1)S(1)}, bf16[288,1152]{1,0:T(8,128)(2,1)S(1)}, u32[]{:S(2)}, u32[]{:S(2)}) collective-permute-start(bf16[288,1152]{1,0:T(8,128)(2,1)S(1)} %bitcast.17), channel_id=1, source_target_pairs={{0,1},{1,0},{2,3},{3,2},{4,5},{5,4},{6,7},{7,6},{8,9},{9,8},{10,11... | collective-permute-start | bytes 1990664 | tf_op jit(solution)/shard_map/ppermute | solution.py:30
  8.4 5.7 %collective-permute-start.5 = (f32[1,6528]{1,0:T(1,128)S(1)}, f32[1,6528]{1,0:T(1,128)S(1)}, u32[]{:S(2)}, u32[]{:S(2)}) collective-permute-start(f32[1,6528]{1,0:T(1,128)S(1)} %reshape.43.refs_1_.refs_6_.refs_8_.refs_4_.refs_3_), channel_id=1, source_target_pairs={{0,1},{1,0},{2,3},{3,2},{4,5},{5,4},{6,7},{7,6},{8,9},{9,8},{10,11... | collective-permute-start | bytes 78344 | tf_op jit(solution)/shard_map/ppermute | solution.py:30
  9.1 2.3 %copy-start.7 = (bf16[1,16,16,1152]{3,2,1,0:T(8,128)(2,1)S(1)}, bf16[1,16,16,1152]{3,2,1,0:T(8,128)(2,1)}, u32[]{:S(2)}) copy-start(bf16[1,16,16,1152]{3,2,1,0:T(8,128)(2,1)} %param.17) | copy-start | bytes 1769476
  9.1 2.3 %copy-start.8 = (bf16[1,16,16,1152]{3,2,1,0:T(8,128)(2,1)S(1)}, bf16[1,16,16,1152]{3,2,1,0:T(8,128)(2,1)}, u32[]{:S(2)}) copy-start(bf16[1,16,16,1152]{3,2,1,0:T(8,128)(2,1)} %param.32) | copy-start | bytes 1769476
  9.1 6.3 %copy-start.2 = (bf16[1152,1152]{1,0:T(8,128)(2,1)S(1)}, bf16[1152,1152]{1,0:T(8,128)(2,1)}, u32[]{:S(2)}) copy-start(bf16[1152,1152]{1,0:T(8,128)(2,1)} %refs_1_.9) | copy-start | bytes 7962628
  10.3 3.7 %collective-permute-start.4 = (f32[1,1728]{1,0:T(1,128)S(1)}, f32[1,1728]{1,0:T(1,128)S(1)}, u32[]{:S(2)}, u32[]{:S(2)}) collective-permute-start(f32[1,1728]{1,0:T(1,128)S(1)} %get-tuple-element.141.refs_2_), channel_id=1, source_target_pairs={{0,2},{1,3},{2,0},{3,1},{4,6},{5,7},{6,4},{7,5},{8,10},{9,11},{10,... | collective-permute-start | bytes 20744 | tf_op jit(solution)/shard_map/ppermute | solution.py:30
  11.4 2.7 %collective-permute-start.3 = (f32[1,1728]{1,0:T(1,128)S(1)}, f32[1,1728]{1,0:T(1,128)S(1)}, u32[]{:S(2)}, u32[]{:S(2)}) collective-permute-start(f32[1,1728]{1,0:T(1,128)S(1)} %get-tuple-element.141.refs_2_), channel_id=1, source_target_pairs={{0,1},{1,0},{2,3},{3,2},{4,5},{5,4},{6,7},{7,6},{8,9},{9,8},{10,11... | collective-permute-start | bytes 20744 | tf_op jit(solution)/shard_map/ppermute | solution.py:30
  11.5 3.8 %copy-start.1 = (bf16[1152,1152]{1,0:T(8,128)(2,1)S(1)}, bf16[1152,1152]{1,0:T(8,128)(2,1)}, u32[]{:S(2)}) copy-start(bf16[1152,1152]{1,0:T(8,128)(2,1)} %refs_2_.7) | copy-start | bytes 7962628
  14.0 1.2 %collective-permute-start.8 = (f32[1,1728]{1,0:T(1,128)S(1)}, f32[1,1728]{1,0:T(1,128)S(1)}, u32[]{:S(2)}, u32[]{:S(2)}) collective-permute-start(f32[1,1728]{1,0:T(1,128)S(1)} %collective-permute-done.4.refs_4_), channel_id=1, source_target_pairs={{0,1},{1,0},{2,3},{3,2},{4,5},{5,4},{6,7},{7,6},{8,9},{9,8},{10,11... | collective-permute-start | bytes 20744 | tf_op jit(solution)/shard_map/ppermute | solution.py:30
  15.3 6.5 %collective-permute-start.11 = (bf16[1152,1152]{1,0:T(8,128)(2,1)S(1)}, bf16[1152,1152]{1,0:T(8,128)(2,1)S(1)}, u32[]{:S(2)}, u32[]{:S(2)}) collective-permute-start(bf16[1152,1152]{1,0:T(8,128)(2,1)S(1)} %copy-done.1), channel_id=1, source_target_pairs={{0,1},{1,0},{2,3},{3,2},{4,5},{5,4},{6,7},{7,6},{8,9},{9,8},{10,11... | collective-permute-start | bytes 7962632 | tf_op jit(solution)/shard_map/ppermute | solution.py:30
  15.4 14.4 %collective-permute-start.10 = (bf16[1152,1152]{1,0:T(8,128)(2,1)S(1)}, bf16[1152,1152]{1,0:T(8,128)(2,1)S(1)}, u32[]{:S(2)}, u32[]{:S(2)}) collective-permute-start(bf16[1152,1152]{1,0:T(8,128)(2,1)S(1)} %copy-done.2), channel_id=1, source_target_pairs={{0,1},{1,0},{2,3},{3,2},{4,5},{5,4},{6,7},{7,6},{8,9},{9,8},{10,11... | collective-permute-start | bytes 7962632 | tf_op jit(solution)/shard_map/ppermute | solution.py:30
  20.7 9.2 %collective-permute-start.9 = (bf16[128,1152]{1,0:T(8,128)(2,1)S(1)}, bf16[128,1152]{1,0:T(8,128)(2,1)S(1)}, u32[]{:S(2)}, u32[]{:S(2)}) collective-permute-start(bf16[128,1152]{1,0:T(8,128)(2,1)S(1)} %get-tuple-element.146.refs_1_), channel_id=1, source_target_pairs={{0,2},{1,3},{2,0},{3,1},{4,6},{5,7},{6,4},{7,5},{8,10},{9,11},{10,... | collective-permute-start | bytes 884744 | tf_op jit(solution)/shard_map/ppermute | solution.py:30
  23.1 15.2 %collective-permute-start.17 = (bf16[128,1152]{1,0:T(8,128)(2,1)S(1)}, bf16[128,1152]{1,0:T(8,128)(2,1)S(1)}, u32[]{:S(2)}, u32[]{:S(2)}) collective-permute-start(bf16[128,1152]{1,0:T(8,128)(2,1)S(1)} %get-tuple-element.168.refs_7_.refs_0_), channel_id=1, source_target_pairs={{0,4},{4,0},{8,12},{12,8},{16,20},{20,16},{24,28},{28,24},{1,5},{5... | collective-permute-start | bytes 884744 | tf_op jit(solution)/shard_map/ppermute | solution.py:30
  24.7 17.8 %collective-permute-start.13 = (bf16[128,1152]{1,0:T(8,128)(2,1)S(1)}, bf16[128,1152]{1,0:T(8,128)(2,1)S(1)}, u32[]{:S(2)}, u32[]{:S(2)}) collective-permute-start(bf16[128,1152]{1,0:T(8,128)(2,1)S(1)} %get-tuple-element.168.refs_7_.refs_0_), channel_id=1, source_target_pairs={{0,16},{4,20},{8,24},{12,28},{16,0},{20,4},{24,8},{28,12},{1,17},{... | collective-permute-start | bytes 884744 | tf_op jit(solution)/shard_map/ppermute | solution.py:30
  27.2 15.7 %collective-permute-start.15 = (bf16[128,1280]{1,0:T(8,128)(2,1)S(1)}, bf16[128,1280]{1,0:T(8,128)(2,1)S(1)}, u32[]{:S(2)}, u32[]{:S(2)}) collective-permute-start(bf16[128,1280]{1,0:T(8,128)(2,1)S(1)} %get-tuple-element.174.refs_4_.refs_0_), channel_id=1, source_target_pairs={{0,8},{4,12},{8,0},{12,4},{16,24},{20,28},{24,16},{28,20},{1,9},{5... | collective-permute-start | bytes 983048 | tf_op jit(solution)/shard_map/ppermute | solution.py:30
  32.9 11.0 %collective-permute-start.12 = (bf16[128,1152]{1,0:T(8,128)(2,1)S(1)}, bf16[128,1152]{1,0:T(8,128)(2,1)S(1)}, u32[]{:S(2)}, u32[]{:S(2)}) collective-permute-start(bf16[128,1152]{1,0:T(8,128)(2,1)S(1)} %get-tuple-element.158.refs_1_), channel_id=1, source_target_pairs={{0,2},{1,3},{2,0},{3,1},{4,6},{5,7},{6,4},{7,5},{8,10},{9,11},{10,... | collective-permute-start | bytes 884744 | tf_op jit(solution)/shard_map/ppermute | solution.py:30
  34.0 19.2 %collective-permute-start.20 = (bf16[128,1152]{1,0:T(8,128)(2,1)S(1)}, bf16[128,1152]{1,0:T(8,128)(2,1)S(1)}, u32[]{:S(2)}, u32[]{:S(2)}) collective-permute-start(bf16[128,1152]{1,0:T(8,128)(2,1)S(1)} %get-tuple-element.187.refs_4_.refs_0_), channel_id=1, source_target_pairs={{0,16},{4,20},{8,24},{12,28},{16,0},{20,4},{24,8},{28,12},{1,17},{... | collective-permute-start | bytes 884744 | tf_op jit(solution)/shard_map/ppermute | solution.py:30
  38.3 15.7 %collective-permute-start.19 = (bf16[128,1152]{1,0:T(8,128)(2,1)S(1)}, bf16[128,1152]{1,0:T(8,128)(2,1)S(1)}, u32[]{:S(2)}, u32[]{:S(2)}) collective-permute-start(bf16[128,1152]{1,0:T(8,128)(2,1)S(1)} %get-tuple-element.187.refs_4_.refs_0_), channel_id=1, source_target_pairs={{0,4},{4,0},{8,12},{12,8},{16,20},{20,16},{24,28},{28,24},{1,5},{5... | collective-permute-start | bytes 884744 | tf_op jit(solution)/shard_map/ppermute | solution.py:30
  42.4 15.2 %collective-permute-start.18 = (bf16[128,1152]{1,0:T(8,128)(2,1)S(1)}, bf16[128,1152]{1,0:T(8,128)(2,1)S(1)}, u32[]{:S(2)}, u32[]{:S(2)}) collective-permute-start(bf16[128,1152]{1,0:T(8,128)(2,1)S(1)} %collective-permute-done.13.refs_16_.refs_9_.refs_2_), channel_id=1, source_target_pairs={{0,4},{4,0},{8,12},{12,8},{16,20},{20,16},{24,28},{28,24},{1,5},{5... | collective-permute-start | bytes 884744 | tf_op jit(solution)/shard_map/ppermute | solution.py:30
  42.9 9.1 %collective-permute-start.16 = (bf16[128,1152]{1,0:T(8,128)(2,1)S(1)}, bf16[128,1152]{1,0:T(8,128)(2,1)S(1)}, u32[]{:S(2)}, u32[]{:S(2)}) collective-permute-start(bf16[128,1152]{1,0:T(8,128)(2,1)S(1)} %get-tuple-element.175.refs_2_), channel_id=1, source_target_pairs={{0,2},{1,3},{2,0},{3,1},{4,6},{5,7},{6,4},{7,5},{8,10},{9,11},{10,... | collective-permute-start | bytes 884744 | tf_op jit(solution)/shard_map/ppermute | solution.py:30
  48.2 9.5 %collective-permute-start.14 = (bf16[128,1152]{1,0:T(8,128)(2,1)S(1)}, bf16[128,1152]{1,0:T(8,128)(2,1)S(1)}, u32[]{:S(2)}, u32[]{:S(2)}) collective-permute-start(bf16[128,1152]{1,0:T(8,128)(2,1)S(1)} %get-tuple-element.169.refs_1_), channel_id=1, source_target_pairs={{0,2},{1,3},{2,0},{3,1},{4,6},{5,7},{6,4},{7,5},{8,10},{9,11},{10,... | collective-permute-start | bytes 884744 | tf_op jit(solution)/shard_map/ppermute | solution.py:30
  52.0 14.9 %collective-permute-start.26 = (bf16[128,2432]{1,0:T(8,128)(2,1)S(1)}, bf16[128,2432]{1,0:T(8,128)(2,1)S(1)}, u32[]{:S(2)}, u32[]{:S(2)}) collective-permute-start(bf16[128,2432]{1,0:T(8,128)(2,1)S(1)} %get-tuple-element.206.refs_1_.refs_3_), channel_id=1, source_target_pairs={{0,8},{4,12},{8,0},{12,4},{16,24},{20,28},{24,16},{28,20},{1,9},{5... | collective-permute-start | bytes 1867784 | tf_op jit(solution)/shard_map/ppermute | solution.py:30
  53.2 7.8 %collective-permute-start.21 = (bf16[128,1152]{1,0:T(8,128)(2,1)S(1)}, bf16[128,1152]{1,0:T(8,128)(2,1)S(1)}, u32[]{:S(2)}, u32[]{:S(2)}) collective-permute-start(bf16[128,1152]{1,0:T(8,128)(2,1)S(1)} %collective-permute-done.20.refs_6_.refs_2_), channel_id=1, source_target_pairs={{0,4},{4,0},{8,12},{12,8},{16,20},{20,16},{24,28},{28,24},{1,5},{5... | collective-permute-start | bytes 884744 | tf_op jit(solution)/shard_map/ppermute | solution.py:30
  58.3 1.3 %collective-permute-start.22 = (f32[16,1152]{1,0:T(8,128)S(1)}, f32[16,1152]{1,0:T(8,128)S(1)}, u32[]{:S(2)}, u32[]{:S(2)}) collective-permute-start(f32[16,1152]{1,0:T(8,128)S(1)} %get-tuple-element.195.refs_1_), channel_id=1, source_target_pairs={{0,1},{1,0},{2,3},{3,2},{4,5},{5,4},{6,7},{7,6},{8,9},{9,8},{10,11... | collective-permute-start | bytes 221192 | tf_op jit(solution)/shard_map/ppermute | solution.py:30
  58.3 15.6 %collective-permute-start.24 = (bf16[512,1152]{1,0:T(8,128)(2,1)S(1)}, bf16[512,1152]{1,0:T(8,128)(2,1)S(1)}, u32[]{:S(2)}, u32[]{:S(2)}) collective-permute-start(bf16[512,1152]{1,0:T(8,128)(2,1)S(1)} %get-tuple-element.197), channel_id=1, source_target_pairs={{0,1},{1,0},{2,3},{3,2},{4,5},{5,4},{6,7},{7,6},{8,9},{9,8},{10,11... | collective-permute-start | bytes 3538952 | tf_op jit(solution)/shard_map/ppermute | solution.py:30
  61.2 6.5 %collective-permute-start.25 = (f32[1,7424]{1,0:T(1,128)S(1)}, f32[1,7424]{1,0:T(1,128)S(1)}, u32[]{:S(2)}, u32[]{:S(2)}) collective-permute-start(f32[1,7424]{1,0:T(1,128)S(1)} %get-tuple-element.205.refs_0_), channel_id=1, source_target_pairs={{0,16},{4,20},{8,24},{12,28},{16,0},{20,4},{24,8},{28,12},{1,17},{... | collective-permute-start | bytes 89096 | tf_op jit(solution)/shard_map/ppermute | solution.py:30
  63.2 10.8 %collective-permute-start.23 = (bf16[512,1152]{1,0:T(8,128)(2,1)S(1)}, bf16[512,1152]{1,0:T(8,128)(2,1)S(1)}, u32[]{:S(2)}, u32[]{:S(2)}) collective-permute-start(bf16[512,1152]{1,0:T(8,128)(2,1)S(1)} %get-tuple-element.196), channel_id=1, source_target_pairs={{0,1},{1,0},{2,3},{3,2},{4,5},{5,4},{6,7},{7,6},{8,9},{9,8},{10,11... | collective-permute-start | bytes 3538952 | tf_op jit(solution)/shard_map/ppermute | solution.py:30
  67.1 2.0 %collective-permute-start.29 = (bf16[128,2048]{1,0:T(8,128)(2,1)S(1)}, bf16[128,2048]{1,0:T(8,128)(2,1)S(1)}, u32[]{:S(2)}, u32[]{:S(2)}) collective-permute-start(bf16[128,2048]{1,0:T(8,128)(2,1)S(1)} %get-tuple-element.213), channel_id=1, source_target_pairs={{0,1},{1,0},{2,3},{3,2},{4,5},{5,4},{6,7},{7,6},{8,9},{9,8},{10,11... | collective-permute-start | bytes 1572872 | tf_op jit(solution)/shard_map/ppermute | solution.py:30
  67.2 3.0 %collective-permute-start.28 = (bf16[128,3072]{1,0:T(8,128)(2,1)S(1)}, bf16[128,3072]{1,0:T(8,128)(2,1)S(1)}, u32[]{:S(2)}, u32[]{:S(2)}) collective-permute-start(bf16[128,3072]{1,0:T(8,128)(2,1)S(1)} %get-tuple-element.212), channel_id=1, source_target_pairs={{0,1},{1,0},{2,3},{3,2},{4,5},{5,4},{6,7},{7,6},{8,9},{9,8},{10,11... | collective-permute-start | bytes 2359304 | tf_op jit(solution)/shard_map/ppermute | solution.py:30
  67.7 4.6 %collective-permute-start.27 = (f32[2,7424]{1,0:T(2,128)S(1)}, f32[2,7424]{1,0:T(2,128)S(1)}, u32[]{:S(2)}, u32[]{:S(2)}) collective-permute-start(f32[2,7424]{1,0:T(2,128)S(1)} %get-tuple-element.211.refs_0_), channel_id=1, source_target_pairs={{0,4},{4,0},{8,12},{12,8},{16,20},{20,16},{24,28},{28,24},{1,5},{5... | collective-permute-start | bytes 178184 | tf_op jit(solution)/shard_map/ppermute | solution.py:30
  71.6 11.1 %collective-permute-start.32 = (bf16[144,1152]{1,0:T(8,128)(2,1)S(1)}, bf16[144,1152]{1,0:T(8,128)(2,1)S(1)}, u32[]{:S(2)}, u32[]{:S(2)}) collective-permute-start(bf16[144,1152]{1,0:T(8,128)(2,1)S(1)} %get-tuple-element.224), channel_id=1, source_target_pairs={{0,4},{4,0},{8,12},{12,8},{16,20},{20,16},{24,28},{28,24},{1,5},{5... | collective-permute-start | bytes 995336 | tf_op jit(solution)/shard_map/ppermute | solution.py:30
  72.3 12.4 %collective-permute-start.31 = (f32[4,7424]{1,0:T(4,128)S(1)}, f32[4,7424]{1,0:T(4,128)S(1)}, u32[]{:S(2)}, u32[]{:S(2)}) collective-permute-start(f32[4,7424]{1,0:T(4,128)S(1)} %get-tuple-element.222.refs_0_), channel_id=1, source_target_pairs={{0,8},{4,12},{8,0},{12,4},{16,24},{20,28},{24,16},{28,20},{1,9},{5... | collective-permute-start | bytes 356360 | tf_op jit(solution)/shard_map/ppermute | solution.py:30
  80.8 23.8 %collective-permute-start.35 = (bf16[144,2304]{1,0:T(8,128)(2,1)S(1)}, bf16[144,2304]{1,0:T(8,128)(2,1)S(1)}, u32[]{:S(2)}, u32[]{:S(2)}) collective-permute-start(bf16[144,2304]{1,0:T(8,128)(2,1)S(1)} %get-tuple-element.235), channel_id=1, source_target_pairs={{0,8},{4,12},{8,0},{12,4},{16,24},{20,28},{24,16},{28,20},{1,9},{5... | collective-permute-start | bytes 1990664 | tf_op jit(solution)/shard_map/ppermute | solution.py:30
  81.2 7.3 %collective-permute-start.30 = (bf16[128,2304]{1,0:T(8,128)(2,1)S(1)}, bf16[128,2304]{1,0:T(8,128)(2,1)S(1)}, u32[]{:S(2)}, u32[]{:S(2)}) collective-permute-start(bf16[128,2304]{1,0:T(8,128)(2,1)S(1)} %get-tuple-element.221.refs_0_), channel_id=1, source_target_pairs={{0,1},{1,0},{2,3},{3,2},{4,5},{5,4},{6,7},{7,6},{8,9},{9,8},{10,11... | collective-permute-start | bytes 1769480 | tf_op jit(solution)/shard_map/ppermute | solution.py:30
  81.2 24.5 %collective-permute-start.33 = (bf16[144,1152]{1,0:T(8,128)(2,1)S(1)}, bf16[144,1152]{1,0:T(8,128)(2,1)S(1)}, u32[]{:S(2)}, u32[]{:S(2)}) collective-permute-start(bf16[144,1152]{1,0:T(8,128)(2,1)S(1)} %get-tuple-element.233), channel_id=1, source_target_pairs={{0,4},{4,0},{8,12},{12,8},{16,20},{20,16},{24,28},{28,24},{1,5},{5... | collective-permute-start | bytes 995336 | tf_op jit(solution)/shard_map/ppermute | solution.py:30
  82.7 23.0 %collective-permute-start.34 = (bf16[144,1152]{1,0:T(8,128)(2,1)S(1)}, bf16[144,1152]{1,0:T(8,128)(2,1)S(1)}, u32[]{:S(2)}, u32[]{:S(2)}) collective-permute-start(bf16[144,1152]{1,0:T(8,128)(2,1)S(1)} %get-tuple-element.234), channel_id=1, source_target_pairs={{0,16},{4,20},{8,24},{12,28},{16,0},{20,4},{24,8},{28,12},{1,17},{... | collective-permute-start | bytes 995336 | tf_op jit(solution)/shard_map/ppermute | solution.py:30
  84.8 2.1 %copy-start.4 = (bf16[1152,1728]{0,1:T(8,128)(2,1)S(1)}, bf16[1152,1728]{0,1:T(8,128)(2,1)}, u32[]{:S(2)}) copy-start(bf16[1152,1728]{0,1:T(8,128)(2,1)} %param.22) | copy-start | bytes 11943940
  88.6 1.2 %collective-permute-start.36 = (f32[8,768]{1,0:T(8,128)S(1)}, f32[8,768]{1,0:T(8,128)S(1)}, u32[]{:S(2)}, u32[]{:S(2)}) collective-permute-start(f32[8,768]{1,0:T(8,128)S(1)} %get-tuple-element.237), channel_id=1, source_target_pairs={{0,1},{1,0},{2,3},{3,2},{4,5},{5,4},{6,7},{7,6},{8,9},{9,8},{10,11... | collective-permute-start | bytes 73736 | tf_op jit(solution)/shard_map/ppermute | solution.py:30
  89.8 3.7 %collective-permute-start.37 = (f32[8,288]{1,0:T(8,128)S(1)}, f32[8,288]{1,0:T(8,128)S(1)}, u32[]{:S(2)}, u32[]{:S(2)}) collective-permute-start(f32[8,288]{1,0:T(8,128)S(1)} %get-tuple-element.240), channel_id=1, source_target_pairs={{0,2},{1,3},{2,0},{3,1},{4,6},{5,7},{6,4},{7,5},{8,10},{9,11},{10,... | collective-permute-start | bytes 27656 | tf_op jit(solution)/shard_map/ppermute | solution.py:30

commit v6 on v5

--- a/solution.py
+++ b/solution.py
@@ -145,6 +145,14 @@
     act = (cond / (1.0 + jnp.exp(-cond))).astype(BF)
     act = jnp.broadcast_to(act, (16, act.shape[1]))
     part[...] = dot_trans(act, weight[...])[0:1, :] + row_part(bias, spots, "ada")
+
+
+def split_heads(qkv, heads):
+    at = lambda h, j: (3 * h + j) * HEAD_DIM
+    return [
+        tuple(qkv[:, at(h, j) : at(h, j) + HEAD_DIM].astype(BF) for j in range(3))
+        for h in range(heads)
+    ]
 
 
 def attention_kernel(
@@ -171,9 +179,8 @@
     seen = ((row_id // frames) == (col_id // frames)) & ((col_id % frames) < length[0])
     factor = HEAD_DIM ** (-0.5)
     heads = out_a.shape[0] // HEAD_DIM
-    total = None
-    blocks = ((qkv_a, bias_a, out_a, saved_a, att_a), (qkv_b, bias_b, out_b, saved_b, att_b))
-    for block, (w, b, o, saved, att_ref) in enumerate(blocks):
+    heads_in = []
+    for w, b, saved in ((qkv_a, bias_a, saved_a), (qkv_b, bias_b, saved_b)):
         qv = row_part(b, spots, "qv")
         zero = jnp.zeros((1, HEAD_DIM), F32)
         pieces = [
@@ -187,17 +194,20 @@
         ]
         qkv = dot_trans(low, w[...]) + jnp.concatenate(pieces, axis=1)
         saved[...] = qkv.astype(BF)
+        heads_in += split_heads(qkv, heads)
+    all_scores = [dot_trans(q, k) for q, k, _ in heads_in]
+    all_probs = []
+    for i, scores in enumerate(all_scores):
+        scores = jnp.where(seen, scores * factor, -1e30)
+        raised = jnp.exp(scores - jnp.max(scores, axis=-1, keepdims=True))
+        probs = raised / jnp.sum(raised, axis=-1, keepdims=True)
+        probs_out[i] = probs
+        all_probs.append(probs.astype(BF))
+    outs = [dot(probs, v) for probs, (_, _, v) in zip(all_probs, heads_in)]
+    total = None
+    for block, (o, att_ref) in enumerate(((out_a, att_a), (out_b, att_b))):
         for h in range(heads):
-            base = h * 3 * HEAD_DIM
-            q, k, v = (
-                qkv[:, base + j * HEAD_DIM : base + (j + 1) * HEAD_DIM].astype(BF)
-                for j in range(3)
-            )
-            scores = jnp.where(seen, dot_trans(q, k) * factor, -1e30)
-            raised = jnp.exp(scores - jnp.max(scores, axis=-1, keepdims=True))
-            probs = raised / jnp.sum(raised, axis=-1, keepdims=True)
-            probs_out[block * heads + h] = probs
-            att_ref[:, h * HEAD_DIM : (h + 1) * HEAD_DIM] = dot(probs.astype(BF), v).astype(BF)
+            att_ref[:, h * HEAD_DIM : (h + 1) * HEAD_DIM] = outs[block * heads + h].astype(BF)
         term = dot(att_ref[...], o[...])
         total = term if total is None else total + term
     part[...] = total.astype(BF)
@@ -247,18 +257,19 @@
     inv_out[...] = inv
     low = (normed * (1.0 + mods[4:5, :]) + mods[3:4, :]).astype(BF)
     low_out[...] = low
-    total = None
     cols = up_a.shape[1]
-    for block, (u, b, g) in enumerate(((up_a, fc1_a, grad_a), (up_b, fc1_b, grad_b))):
-        act, slope = gelu_pair(dot(low, u[...]) + row_part(b, spots, "fc1"))
+    blocks = ((up_a, fc1_a, grad_a), (up_b, fc1_b, grad_b))
+    hidden = [dot(low, u[...]) + row_part(b, spots, "fc1") for u, b, _ in blocks]
+    pres = []
+    for block, (value, (_, _, g)) in enumerate(zip(hidden, blocks)):
+        act, slope = gelu_pair(value)
         act_out[:, block * cols : (block + 1) * cols] = act.astype(BF)
         pre = (g[...] * slope).astype(BF)
         if block == 0:
             pre_out[...] = pre
         sums[block : block + 1, :] = column_sum(pre.astype(F32))
-        term = dot_trans(pre, u[...])
-        total = term if total is None else total + term
-    part3[...] = total.astype(BF)
+        pres.append(pre)
+    part3[...] = (dot_trans(pres[0], up_a[...]) + dot_trans(pres[1], up_b[...])).astype(BF)
 
 
 def mlp_tail_kernel(act, down_a, down_b, part2):
@@ -274,11 +285,11 @@
         refs[-1][i * half : (i + 1) * half, :] = source[...]
 
 
-def remake_kernel(n_dp, spots, own, before, last, n_blocks, span, pick, up, down, bias, *refs):
+def remake_kernel(n_dp, spots, own, before, last, n_blocks, grads_rows, pick, up, down, bias, *refs):
     cols = up.shape[1]
     normed, grads, refs = refs[:n_blocks], refs[n_blocks : 2 * n_blocks], refs[2 * n_blocks :]
-    if span is not None:
-        normed, grads = ([ref.at[span[0] : span[1], :] for ref in v] for v in (normed, grads))
+    if n_blocks == 1 and normed[0].shape[0] > grads_rows:
+        normed, grads = [normed[0].at[0:grads_rows, :]], [grads[0].at[grads_rows : 2 * grads_rows, :]]
     down_sum, up_sum = 0.0, 0.0
     if own:
         act_own, pre_own, refs = refs[0][:, 0:cols], refs[1][...], refs[2:]
@@ -328,26 +339,28 @@
     heads = out_a.shape[0] // HEAD_DIM
     cols = heads * 3 * HEAD_DIM
     wide = pad_lanes(cols)
+    heads_in, att_grads = [], []
+    for o, saved in ((out_a, saved_a), (out_b, saved_b)):
+        att_grad = dot_trans(low, o[...])
+        heads_in += split_heads(saved[...].astype(F32), heads)
+        att_grads += [
+            att_grad[:, h * HEAD_DIM : (h + 1) * HEAD_DIM].astype(BF) for h in range(heads)
+        ]
+    all_probs_grad = [dot_trans(ag, v) for ag, (_, _, v) in zip(att_grads, heads_in)]
+    value_grads = [dot_rows(probs_in[i].astype(BF), ag) for i, ag in enumerate(att_grads)]
+    all_low = []
+    for i, probs_grad in enumerate(all_probs_grad):
+        probs = probs_in[i]
+        inner = jnp.sum(probs * probs_grad, axis=-1, keepdims=True)
+        all_low.append((probs * (probs_grad - inner)).astype(BF))
+    query_grads = [dot(scores_low, k) * factor for scores_low, (_, k, _) in zip(all_low, heads_in)]
+    key_grads = [dot_rows(scores_low, q) * factor for scores_low, (q, _, _) in zip(all_low, heads_in)]
     total = None
-    for block, (w, o, saved) in enumerate(((qkv_a, out_a, saved_a), (qkv_b, out_b, saved_b))):
-        att_grad = dot_trans(low, o[...])
-        qkv = saved[...].astype(F32)
+    for block, w in enumerate((qkv_a, qkv_b)):
         for h in range(heads):
-            base = h * 3 * HEAD_DIM
-            q, k, v = (
-                qkv[:, base + j * HEAD_DIM : base + (j + 1) * HEAD_DIM].astype(BF)
-                for j in range(3)
-            )
-            ag = att_grad[:, h * HEAD_DIM : (h + 1) * HEAD_DIM].astype(BF)
-            probs = probs_in[block * heads + h]
-            value_grad = dot_rows(probs.astype(BF), ag)
-            probs_grad = dot_trans(ag, v)
-            inner = jnp.sum(probs * probs_grad, axis=-1, keepdims=True)
-            scores_low = (probs * (probs_grad - inner)).astype(BF)
-            query_grad = dot(scores_low, k) * factor
-            key_grad = dot_rows(scores_low, q) * factor
-            at = block * wide + base
-            for j, piece in enumerate((query_grad, key_grad, value_grad)):
+            i = block * heads + h
+            at = block * wide + h * 3 * HEAD_DIM
+            for j, piece in enumerate((query_grads[i], key_grads[i], value_grads[i])):
                 stacked[:, at + j * HEAD_DIM : at + (j + 1) * HEAD_DIM] = piece.astype(BF)
         mine = stacked[:, block * wide : block * wide + cols]
         sums[4 + block : 5 + block, 0:cols] = column_sum(mine.astype(F32))
@@ -776,6 +789,15 @@
         also=[grad_f],
     )
     part4_other = swap(part4, "tensor", 2)
+    (near_rows,) = call(
+        order,
+        rows_kernel,
+        "rows_near",
+        0.02,
+        [((4 * half, width), BF)],
+        [low2, rows_y, low_grad, grad_y],
+    )
+    near_other = swap(near_rows, "tensor", 1)
     s_wide = pad_lanes(n_qkv)
     pack3, chunks3 = call(
         order,
@@ -788,14 +810,14 @@
     )
     far3 = swap(pack3, "dp", 2)
 
-    def remake(name, normed, grads, own, before, last, span=None, us=0.02):
+    def remake(name, normed, grads, own, before, last, us=0.02):
         outs = [((part // 2, hidden), F32)] * 2
         if last and n_dp == 8:
             outs = [((chunk, 2 * hidden), F32), ((chunk, 2 * hidden), BF)]
         return call(
             order,
             lambda *refs: remake_kernel(
-                n_dp, spots, bool(own), bool(before), last, len(normed), span, *refs
+                n_dp, spots, bool(own), bool(before), last, len(normed), 2 * half, *refs
             ),
             name,
             us,
@@ -822,20 +844,11 @@
         False,
         us=1.0,
     )
-    (grads_core,) = call(
-        order,
-        rows_kernel,
-        "rows_grad",
-        0.02,
-        [((4 * half, width), BF)],
-        [low_grad, grad_y, grad_f, grad_yf],
-    )
-    grads_other = swap(grads_core, "tensor", 1)
     both, sums = call(
         order,
         lambda *refs: input_back_kernel(frames, *refs),
         "input_back",
-        0.02,
+        10.0,
         [((half, 2 * width), BF), ((16, width), F32)],
         [
             lengths, part4, part4_other, mods, normed1, inv1, mid_grad, cot,
@@ -843,16 +856,17 @@
         ],
     )
     sums_other = swap(sums, "tensor", 1)
-    (rows_core,) = call(
+    sums2 = remake("remake_core0", [near_other], [near_other], [], sums2, False, us=2.0)
+    (far_rows,) = call(
         order,
         rows_kernel,
-        "rows_norm",
+        "rows_far",
         3.0,
         [((4 * half, width), BF)],
-        [low2, rows_y, rows_f, rows_yf],
+        [rows_f, rows_yf, grad_f, grad_yf],
         also=[sums_other],
     )
-    rows_other = swap(rows_core, "tensor", 1)
+    far_rows_other = swap(far_rows, "tensor", 1)
 
     layout, at = {}, 0
     for name, size in (
@@ -906,10 +920,8 @@
     if n_dp == 8:
         far_other = swap(qkv_grad[1], "dp", 1)
     for i, flip in enumerate(flips[1:-1]):
-        vector = stack("stack%d" % (i + 1), vector, flip)
-    core_args = ([rows_other], [grads_other], [])
-    sums2 = remake("remake_core0", *core_args, sums2, False, (0, 2 * half), us=2.0)
-    mlp_grad = remake("remake_core1", *core_args, sums2, True, (2 * half, 4 * half))
+        vector = stack("stack%d" % (i + 1), vector, flip, us=2.0)
+    mlp_grad = remake("remake_core1", [far_rows_other], [far_rows_other], [], sums2, True)
     mlp_grad = (mlp_grad[0], swap(mlp_grad[1], "dp", 2) if n_dp == 8 else mlp_grad[1])
     both_other = swap(behind(both, mlp_grad[0]), "tensor", 1)
     if n_dp == 8:
@@ -957,12 +969,12 @@
         [((columns, n_classes), F32)],
         [mine, swap(send, "tensor", 2), cond_cols, labels_all],
     )
-    down_grad, up_grad = mlp_grads(*mlp_grad)
     if n_dp == 8:
         qkv_grad, out_grad = add("qkv_add", [n_qkv, n_att], *qkv_grad)
     else:
         grad = halve_all(qkv_grad[0].reshape(n_dp // 2, chunk, -1), [1])
         qkv_grad, out_grad = grad[:, :n_qkv], grad[:, n_qkv:]
+    down_grad, up_grad = mlp_grads(*mlp_grad)
     return (
         result,
         tokens_grad,

time: 107 us -> 102 us (0.953)
  Pallas kernels: 37.7 us -> 35.3 us
  waiting for transfers between devices: 28.9 us -> 26.8 us
    pallas_call x30, Pallas kernels: 37.7 us -> 35.3 us  [call(): pl.pallas_call(whole, out_shape=[jax.ShapeDtypeStruct(s, d) for s, d in [...]
    ppermute x38, waiting for transfers between devices: 28.9 us -> 26.8 us  [swap(): return lax.ppermute(value, axis, [(i, i ^ flip) for i in range(size)])]
  transfers between devices with their start and end apart: 38 -> 38, of which waited for: 15 -> 18; matrix products, arithmetic and copies ran while one was open for 1% -> 1% of each run, Pallas kernels for 34% -> 34%
where the time goes in v6:
time: 102 us; the launch traced here: 101 us
  Pallas kernels  35.3 us (35%)
  starting transfers between devices  32.8 us (32%)
  waiting for transfers between devices  26.8 us (26%)
  local copies, waits for them, and re-layouts  2.95 us (3%)
  between operations  2.94 us (3%)
    pallas_call x30, Pallas kernels, call(): pl.pallas_call(whole, out_shape=[jax.ShapeDtypeStruct(s, d) for s, d in [...  35.3 us
    ppermute x38, starting transfers between devices, swap(): return lax.ppermute(value, axis, [(i, i ^ flip) for i in range(size)])  32.8 us
    ppermute x38, waiting for transfers between devices, swap(): return lax.ppermute(value, axis, [(i, i ^ flip) for i in range(size)])  26.8 us
    unnamed x19, local copies, waits for them, and re-layouts  2.84 us
  transfers between devices with their start and end apart: 38, of which 18 were waited for; matrix products, arithmetic and copies ran while one was open for 1% of the time, Pallas kernels for 34%

profile of v6, /device:TPU:0, one launch (start us, length us, event | category | flops | bytes accessed | tf_op | source)
XLA Modules:
  0.0 101.5 jit_solution(6196439535078423616)
XLA Ops:
  1.7 3.0 %collective-permute-start.1 = (bf16[1,288]{1,0:T(2,128)(2,1)S(1)}, bf16[1,288]{1,0:T(2,128)(2,1)S(1)}, u32[]{:S(2)}, u32[]{:S(2)}) collective-permute-start(bf16[1,288]{1,0:T(2,128)(2,1)S(1)} %copy.31.refs_0_), channel_id=1, source_target_pairs={{0,2},{1,3},{2,0},{3,1},{4,6},{5,7},{6,4},{7,5},{8,10},{9,11},{10,... | collective-permute-start | bytes 1736 | tf_op jit(solution)/shard_map/ppermute | solution.py:30
  5.4 0.8 add_add_fusion
  6.3 0.6 collective-permute-start.2
  6.9 0.8 collective-permute-done.2.refs_3_
  7.7 0.5 collective-permute-start.6
  8.4 0.4 collective-permute-start.5
  8.7 0.4 copy-done.3
  9.1 1.2 %modulation.1 = (f32[1,1152]{1,0:T(1,128)S(1)}, f32[1,1728]{1,0:T(1,128)S(1)}, f32[8,128]{1,0:T(8,128)S(1)}) custom-call(bf16[1,288]{1,0:T(2,128)(2,1)S(1)} %copy.31.refs_0_, bf16[1,288]{1,0:T(2,128)(2,1)S(1)} %collective-permute-done.refs_1_, bf16[1,288]{1,0:T(2,128)(2,1)S(1)} %collective-permute-done.1.refs_2_, ...), custom_call_target="tpu_custom_call" | custom-call | flops 1100000000 | bytes 1024 | tf_op jit(solution)/shard_map/modulation/pallas_call | solution.py:49
  10.3 1.1 %collective-permute-start.4 = (f32[1,1728]{1,0:T(1,128)S(1)}, f32[1,1728]{1,0:T(1,128)S(1)}, u32[]{:S(2)}, u32[]{:S(2)}) collective-permute-start(f32[1,1728]{1,0:T(1,128)S(1)} %get-tuple-element.141.refs_2_), channel_id=1, source_target_pairs={{0,2},{1,3},{2,0},{3,1},{4,6},{5,7},{6,4},{7,5},{8,10},{9,11},{10,... | collective-permute-start | bytes 20744 | tf_op jit(solution)/shard_map/ppermute | solution.py:30
  11.5 0.3 start.1
  11.8 2.3 %collective-permute-done.4.refs_4_ = f32[1,1728]{1,0:T(1,128)S(1)} collective-permute-done((f32[1,1728]{1,0:T(1,128)S(1)}, f32[1,1728]{1,0:T(1,128)S(1)}, u32[]{:S(2)}, u32[]{:S(2)}) %collective-permute-start.4) | collective-permute-done | bytes 6944 | tf_op jit(solution)/shard_map/ppermute | solution.py:30
  14.1 1.1 %collective-permute-done.8.refs_5_ = f32[1,1728]{1,0:T(1,128)S(1)} collective-permute-done((f32[1,1728]{1,0:T(1,128)S(1)}, f32[1,1728]{1,0:T(1,128)S(1)}, u32[]{:S(2)}, u32[]{:S(2)}) %collective-permute-start.8) | collective-permute-done | bytes 6944 | tf_op jit(solution)/shard_map/ppermute | solution.py:30
  15.4 0.3 collective-permute-start.10
  16.4 2.6 %attention.1 = (bf16[128,1152]{1,0:T(8,128)(2,1)S(1)}, f32[8,1152]{1,0:T(8,128)S(1)}, bf16[128,1152]{1,0:T(8,128)(2,1)S(1)}, bf16[128,864]{1,0:T(8,128)(2,1)S(1)...) custom-call(s32[1]{0:T(128)S(6)} %copy.32.refs_0_, ...), custom_call_target="tpu_custom_call" | custom-call | flops 4400000000 | bytes 1024 | tf_op jit(solution)/shard_map/attention/pallas_call | solution.py:49
  19.1 1.1 %collective-permute-start.9 = (bf16[128,1152]{1,0:T(8,128)(2,1)S(1)}, bf16[128,1152]{1,0:T(8,128)(2,1)S(1)}, u32[]{:S(2)}, u32[]{:S(2)}) collective-permute-start(bf16[128,1152]{1,0:T(8,128)(2,1)S(1)} %get-tuple-element.146.refs_1_), channel_id=1, source_target_pairs={{0,2},{1,3},{2,0},{3,1},{4,6},{5,7},{6,4},{7,5},{8,10},{9,11},{10,... | collective-permute-start | bytes 884744 | tf_op jit(solution)/shard_map/ppermute | solution.py:30
  20.2 1.3 %early_back.1 = (f32[128,1152]{1,0:T(8,128)S(1)}, f32[128,1152]{1,0:T(8,128)S(1)}, bf16[128,1152]{1,0:T(8,128)(2,1)S(1)}, bf16[128,1280]{1,0:T(8,128)(2,1)S(1)},...) custom-call(s32[1]{0:T(128)S(6)} %copy.32.refs_0_, ...), custom_call_target="tpu_custom_call" | custom-call | flops 2200000000 | bytes 1024 | tf_op jit(solution)/shard_map/early_back/pallas_call | solution.py:49
  21.5 1.6 %collective-permute-start.17 = (bf16[128,1152]{1,0:T(8,128)(2,1)S(1)}, bf16[128,1152]{1,0:T(8,128)(2,1)S(1)}, u32[]{:S(2)}, u32[]{:S(2)}) collective-permute-start(bf16[128,1152]{1,0:T(8,128)(2,1)S(1)} %get-tuple-element.168.refs_2_.refs_7_), channel_id=1, source_target_pairs={{0,4},{4,0},{8,12},{12,8},{16,20},{20,16},{24,28},{28,24},{1,5},{5... | collective-permute-start | bytes 884744 | tf_op jit(solution)/shard_map/ppermute | solution.py:30
  23.1 2.6 %collective-permute-start.13 = (bf16[128,1152]{1,0:T(8,128)(2,1)S(1)}, bf16[128,1152]{1,0:T(8,128)(2,1)S(1)}, u32[]{:S(2)}, u32[]{:S(2)}) collective-permute-start(bf16[128,1152]{1,0:T(8,128)(2,1)S(1)} %get-tuple-element.168.refs_2_.refs_7_), channel_id=1, source_target_pairs={{0,16},{4,20},{8,24},{12,28},{16,0},{20,4},{24,8},{28,12},{1,17},{... | collective-permute-start | bytes 884744 | tf_op jit(solution)/shard_map/ppermute | solution.py:30
  25.7 1.6 %collective-permute-start.15 = (bf16[128,1280]{1,0:T(8,128)(2,1)S(1)}, bf16[128,1280]{1,0:T(8,128)(2,1)S(1)}, u32[]{:S(2)}, u32[]{:S(2)}) collective-permute-start(bf16[128,1280]{1,0:T(8,128)(2,1)S(1)} %get-tuple-element.174.refs_4_.refs_0_), channel_id=1, source_target_pairs={{0,8},{4,12},{8,0},{12,4},{16,24},{20,28},{24,16},{28,20},{1,9},{5... | collective-permute-start | bytes 983048 | tf_op jit(solution)/shard_map/ppermute | solution.py:30
  27.3 0.9 collective-permute-done.9.refs_2_
  28.2 3.1 %mlp.1 = (bf16[128,1152]{1,0:T(8,128)(2,1)S(1)}, bf16[128,2304]{1,0:T(8,128)(2,1)S(1)}, bf16[128,1152]{1,0:T(8,128)(2,1)S(1)}, bf16[128,1152]{1,0:T(8,128)(2,1)S...) custom-call(bf16[128,1152]{1,0:T(8,128)(2,1)S(1)} %get-tuple-element, ...), custom_call_target="tpu_custom_call" | custom-call | flops 3300000000 | bytes 1024 | tf_op jit(solution)/shard_map/mlp/pallas_call | solution.py:49
  31.3 1.1 %collective-permute-start.12 = (bf16[128,1152]{1,0:T(8,128)(2,1)S(1)}, bf16[128,1152]{1,0:T(8,128)(2,1)S(1)}, u32[]{:S(2)}, u32[]{:S(2)}) collective-permute-start(bf16[128,1152]{1,0:T(8,128)(2,1)S(1)} %get-tuple-element.158.refs_1_), channel_id=1, source_target_pairs={{0,2},{1,3},{2,0},{3,1},{4,6},{5,7},{6,4},{7,5},{8,10},{9,11},{10,... | collective-permute-start | bytes 884744 | tf_op jit(solution)/shard_map/ppermute | solution.py:30
  32.4 2.6 %collective-permute-start.19 = (bf16[128,1152]{1,0:T(8,128)(2,1)S(1)}, bf16[128,1152]{1,0:T(8,128)(2,1)S(1)}, u32[]{:S(2)}, u32[]{:S(2)}) collective-permute-start(bf16[128,1152]{1,0:T(8,128)(2,1)S(1)} %get-tuple-element.177.refs_0_.refs_4_), channel_id=1, source_target_pairs={{0,16},{4,20},{8,24},{12,28},{16,0},{20,4},{24,8},{28,12},{1,17},{... | collective-permute-start | bytes 884744 | tf_op jit(solution)/shard_map/ppermute | solution.py:30
  35.0 1.7 %mlp_tail.1 = (bf16[128,1152]{1,0:T(8,128)(2,1)S(1)}, f32[8,128]{1,0:T(8,128)S(1)}) custom-call(bf16[128,2304]{1,0:T(8,128)(2,1)S(1)} %get-tuple-element.165.refs_0_.refs_10_, bf16[1152,1152]{1,0:T(8,128)(2,1)S(1)} %copy-done.1, bf16[1152,1152]{1,0:T(8,128)(2,1)S(1)} %collective-permute-done.11.refs_4_.refs_2_, f32[8,128]{1,0:T(8,128)S(1)} %get-tuple-element.166.refs_3_), custom_call_target="tpu_custom_call" | custom-call | flops 1100000000 | bytes 1024 | tf_op jit(solution)/shard_map/mlp_tail/pallas_call | solution.py:49
  36.7 1.6 %collective-permute-start.18 = (bf16[128,1152]{1,0:T(8,128)(2,1)S(1)}, bf16[128,1152]{1,0:T(8,128)(2,1)S(1)}, u32[]{:S(2)}, u32[]{:S(2)}) collective-permute-start(bf16[128,1152]{1,0:T(8,128)(2,1)S(1)} %get-tuple-element.177.refs_0_.refs_4_), channel_id=1, source_target_pairs={{0,4},{4,0},{8,12},{12,8},{16,20},{20,16},{24,28},{28,24},{1,5},{5... | collective-permute-start | bytes 884744 | tf_op jit(solution)/shard_map/ppermute | solution.py:30
  38.3 2.4 %collective-permute-done.13.refs_16_.refs_9_.refs_2_ = bf16[128,1152]{1,0:T(8,128)(2,1)S(1)} collective-permute-done((bf16[128,1152]{1,0:T(8,128)(2,1)S(1)}, bf16[128,1152]{1,0:T(8,128)(2,1)S(1)}, u32[]{:S(2)}, u32[]{:S(2)}) %collective-permute-start.13) | collective-permute-done | bytes 294944 | tf_op jit(solution)/shard_map/ppermute | solution.py:30
  40.7 0.5 collective-permute-start.21
  41.2 0.6 collective-permute-done.15.refs_3_.refs_2_
  41.8 1.0 %collective-permute-start.16 = (bf16[128,1152]{1,0:T(8,128)(2,1)S(1)}, bf16[128,1152]{1,0:T(8,128)(2,1)S(1)}, u32[]{:S(2)}, u32[]{:S(2)}) collective-permute-start(bf16[128,1152]{1,0:T(8,128)(2,1)S(1)} %get-tuple-element.175.refs_2_), channel_id=1, source_target_pairs={{0,2},{1,3},{2,0},{3,1},{4,6},{5,7},{6,4},{7,5},{8,10},{9,11},{10,... | collective-permute-start | bytes 884744 | tf_op jit(solution)/shard_map/ppermute | solution.py:30
  42.8 3.4 %attention_back.1 = (bf16[128,1152]{1,0:T(8,128)(2,1)S(1)}, f32[128,1152]{1,0:T(8,128)S(1)}, bf16[128,1152]{1,0:T(8,128)(2,1)S(1)}, bf16[128,1792]{1,0:T(8,128)(...) custom-call(s32[1]{0:T(128)S(6)} %copy.32.refs_0_, bf16[128,1152]{1,0:T(8,128)(2,1)S(1)} %get-tuple-element.158.refs_1_, ...), custom_call_target="tpu_custom_call" | custom-call | flops 5500000256 | bytes 1024 | tf_op jit(solution)/shard_map/attention_back/pallas_call | solution.py:49
  46.2 1.2 %collective-permute-start.14 = (bf16[128,1152]{1,0:T(8,128)(2,1)S(1)}, bf16[128,1152]{1,0:T(8,128)(2,1)S(1)}, u32[]{:S(2)}, u32[]{:S(2)}) collective-permute-start(bf16[128,1152]{1,0:T(8,128)(2,1)S(1)} %get-tuple-element.169.refs_1_), channel_id=1, source_target_pairs={{0,2},{1,3},{2,0},{3,1},{4,6},{5,7},{6,4},{7,5},{8,10},{9,11},{10,... | collective-permute-start | bytes 884744 | tf_op jit(solution)/shard_map/ppermute | solution.py:30
  47.7 1.0 collective-permute-start.26
  48.7 2.8 %collective-permute-done.16.refs_3_ = bf16[128,1152]{1,0:T(8,128)(2,1)S(1)} collective-permute-done((bf16[128,1152]{1,0:T(8,128)(2,1)S(1)}, bf16[128,1152]{1,0:T(8,128)(2,1)S(1)}, u32[]{:S(2)}, u32[]{:S(2)}) %collective-permute-start.16) | collective-permute-done | bytes 294944 | tf_op jit(solution)/shard_map/ppermute | solution.py:30
  51.5 0.3 output.1
  51.9 0.5 collective-permute-start.20
  52.4 3.6 %remake_near.1 = (f32[288,1152]{1,0:T(8,128)S(1)}, f32[288,1152]{1,0:T(8,128)S(1)}, f32[8,128]{1,0:T(8,128)S(1)}) custom-call(bf16[288,1152]{1,0:T(8,128)(2,1)S(1)} %get-tuple-element.187.refs_0_, bf16[1152,1152]{1,0:T(8,128)(2,1)S(1)} %copy-done.2, bf16[1152,1152]{1,0:T(8,128)(2,1)S(1)} %copy-done.1, ...), custom_call_target="tpu_custom_call" | custom-call | flops 1100000000 | bytes 1024 | tf_op jit(solution)/shard_map/remake_near/pallas_call | solution.py:49
  56.1 0.5 input_back.1
  56.6 0.2 collective-permute-start.23
  56.9 3.2 %remake_core0.1 = (f32[288,1152]{1,0:T(8,128)S(1)}, f32[288,1152]{1,0:T(8,128)S(1)}, f32[8,128]{1,0:T(8,128)S(1)}) custom-call(bf16[288,1152]{1,0:T(8,128)(2,1)S(1)} %get-tuple-element.187.refs_0_, bf16[1152,1152]{1,0:T(8,128)(2,1)S(1)} %copy-done.2, bf16[1152,1152]{1,0:T(8,128)(2,1)S(1)} %copy-done.1, ...), custom_call_target="tpu_custom_call" | custom-call | flops 2200000000 | bytes 1024 | tf_op jit(solution)/shard_map/remake_core0/pallas_call | solution.py:49
  60.1 1.2 %collective-permute-done.20.refs_1_.refs_4_ = bf16[128,1152]{1,0:T(8,128)(2,1)S(1)} collective-permute-done((bf16[128,1152]{1,0:T(8,128)(2,1)S(1)}, bf16[128,1152]{1,0:T(8,128)(2,1)S(1)}, u32[]{:S(2)}, u32[]{:S(2)}) %collective-permute-start.20) | collective-permute-done | bytes 294944 | tf_op jit(solution)/shard_map/ppermute | solution.py:30
  61.7 2.2 %remake_yf.1 = (f32[288,1152]{1,0:T(8,128)S(1)}, f32[288,1152]{1,0:T(8,128)S(1)}, f32[8,128]{1,0:T(8,128)S(1)}) custom-call(bf16[288,1152]{1,0:T(8,128)(2,1)S(1)} %get-tuple-element.187.refs_0_, bf16[1152,1152]{1,0:T(8,128)(2,1)S(1)} %copy-done.2, bf16[1152,1152]{1,0:T(8,128)(2,1)S(1)} %copy-done.1, ...), custom_call_target="tpu_custom_call" | custom-call | flops 22000000 | bytes 1024 | tf_op jit(solution)/shard_map/remake_yf/pallas_call | solution.py:49
  63.9 0.8 collective-permute-done.26.refs_0_.refs_5_
  65.0 0.5 collective-permute-start.28
  65.5 1.2 %collective-permute-done.25.refs_1_ = f32[1,7424]{1,0:T(1,128)S(1)} collective-permute-done((f32[1,7424]{1,0:T(1,128)S(1)}, f32[1,7424]{1,0:T(1,128)S(1)}, u32[]{:S(2)}, u32[]{:S(2)}) %collective-permute-start.25) | collective-permute-done | bytes 29728 | tf_op jit(solution)/shard_map/ppermute | solution.py:30
  66.7 0.8 collective-permute-start.27
  67.5 0.5 collective-permute-done.28.refs_6_
  68.0 1.4 %qkv_grad.1 = (f32[144,1152]{1,0:T(8,128)S(1)}, bf16[144,1152]{1,0:T(8,128)(2,1)S(1)}, f32[144,1152]{1,0:T(8,128)S(1)}, bf16[144,1152]{1,0:T(8,128)(2,1)S(1)}, f32[8,128]{1,0:T(8,128)S(1)}) custom-call(bf16[128,1280]{1,0:T(8,128)(2,1)S(1)} %get-tuple-element.174.refs_4_.refs_0_, bf16[128,640]{1,0:T(8,128)(2,1)S(1)} %get-tuple-element.211.refs_5_.refs_1_, ...), custom_call_target="tpu_custom_call" | custom-call | flops 22000000 | bytes 1024 | tf_op jit(solution)/shard_map/qkv_grad/pallas_call | solution.py:49
  69.4 1.0 collective-permute-start.32
  70.4 0.5 collective-permute-done.27.refs_1_
  70.9 2.1 %collective-permute-start.31 = (f32[4,7424]{1,0:T(4,128)S(1)}, f32[4,7424]{1,0:T(4,128)S(1)}, u32[]{:S(2)}, u32[]{:S(2)}) collective-permute-start(f32[4,7424]{1,0:T(4,128)S(1)} %get-tuple-element.222.refs_0_), channel_id=1, source_target_pairs={{0,8},{4,12},{8,0},{12,4},{16,24},{20,28},{24,16},{28,20},{1,9},{5... | collective-permute-start | bytes 356360 | tf_op jit(solution)/shard_map/ppermute | solution.py:30
  73.1 3.5 %remake_core1.1 = (f32[144,2304]{1,0:T(8,128)S(1)}, bf16[144,2304]{1,0:T(8,128)(2,1)S(1)}, f32[8,128]{1,0:T(8,128)S(1)}) custom-call(bf16[288,1152]{1,0:T(8,128)(2,1)S(1)} %get-tuple-element.187.refs_0_, bf16[1152,1152]{1,0:T(8,128)(2,1)S(1)} %copy-done.2, bf16[1152,1152]{1,0:T(8,128)(2,1)S(1)} %copy-done.1, ...), custom_call_target="tpu_custom_call" | custom-call | flops 22000000 | bytes 1024 | tf_op jit(solution)/shard_map/remake_core1/pallas_call | solution.py:49
  76.7 1.3 %collective-permute-start.33 = (bf16[144,1152]{1,0:T(8,128)(2,1)S(1)}, bf16[144,1152]{1,0:T(8,128)(2,1)S(1)}, u32[]{:S(2)}, u32[]{:S(2)}) collective-permute-start(bf16[144,1152]{1,0:T(8,128)(2,1)S(1)} %get-tuple-element.233), channel_id=1, source_target_pairs={{0,4},{4,0},{8,12},{12,8},{16,20},{20,16},{24,28},{28,24},{1,5},{5... | collective-permute-start | bytes 995336 | tf_op jit(solution)/shard_map/ppermute | solution.py:30
  78.1 1.2 %collective-permute-done.32.refs_1_ = bf16[144,1152]{1,0:T(8,128)(2,1)S(1)} collective-permute-done((bf16[144,1152]{1,0:T(8,128)(2,1)S(1)}, bf16[144,1152]{1,0:T(8,128)(2,1)S(1)}, u32[]{:S(2)}, u32[]{:S(2)}) %collective-permute-start.32) | collective-permute-done | bytes 331808 | tf_op jit(solution)/shard_map/ppermute | solution.py:30
  79.4 2.7 %collective-permute-start.34 = (bf16[144,1152]{1,0:T(8,128)(2,1)S(1)}, bf16[144,1152]{1,0:T(8,128)(2,1)S(1)}, u32[]{:S(2)}, u32[]{:S(2)}) collective-permute-start(bf16[144,1152]{1,0:T(8,128)(2,1)S(1)} %get-tuple-element.234), channel_id=1, source_target_pairs={{0,16},{4,20},{8,24},{12,28},{16,0},{20,4},{24,8},{28,12},{1,17},{... | collective-permute-start | bytes 995336 | tf_op jit(solution)/shard_map/ppermute | solution.py:30
  82.2 2.1 %copy-done.4 = bf16[1152,1728]{0,1:T(8,128)(2,1)S(1)} copy-done((bf16[1152,1728]{0,1:T(8,128)(2,1)S(1)}, bf16[1152,1728]{0,1:T(8,128)(2,1)}, u32[]{:S(2)}) %copy-start.4) | copy-done | bytes 3981336
  84.3 1.6 %gathered.1 = (f32[144,1728]{1,0:T(8,128)}, f32[1728]{0:T(1024)}, f32[576]{0:T(1024)}, f32[1152]{0:T(1024)}, f32[1152]{0:T(1024)}, /*index=5*/f32[1152]{0:T(1024...) custom-call(bf16[1728,1152]{1,0:T(8,128)(2,1)S(1)} %bitcast.13, ...), custom_call_target="tpu_custom_call" | custom-call | flops 5500000256 | bytes 1024 | tf_op jit(solution)/shard_map/gathered/pallas_call | solution.py:49
  85.9 1.1 %join.1 = (bf16[256,1152]{1,0:T(8,128)(2,1)}, bf16[256,1152]{1,0:T(8,128)(2,1)}, f32[8,128]{1,0:T(8,128)S(1)}) custom-call(bf16[128,2304]{1,0:T(8,128)(2,1)S(1)} %get-tuple-element.221.refs_0_, bf16[128,2304]{1,0:T(8,128)(2,1)S(1)} %collective-permute-done.30.refs_1_, f32[8,128]{1,0:T(8,128)S(1)} %get-tuple-element.229.refs_2_), custom_call_target="tpu_custom_call" | custom-call | flops 22000000 | bytes 1024 | tf_op jit(solution)/shard_map/join/pallas_call | solution.py:49
  87.1 1.1 %collective-permute-start.36 = (f32[8,288]{1,0:T(8,128)S(1)}, f32[8,288]{1,0:T(8,128)S(1)}, u32[]{:S(2)}, u32[]{:S(2)}) collective-permute-start(f32[8,288]{1,0:T(8,128)S(1)} %get-tuple-element.239), channel_id=1, source_target_pairs={{0,2},{1,3},{2,0},{3,1},{4,6},{5,7},{6,4},{7,5},{8,10},{9,11},{10,... | collective-permute-start | bytes 27656 | tf_op jit(solution)/shard_map/ppermute | solution.py:30
  88.2 2.6 %collective-permute-done.36.refs_1_ = f32[8,288]{1,0:T(8,128)S(1)} collective-permute-done((f32[8,288]{1,0:T(8,128)S(1)}, f32[8,288]{1,0:T(8,128)S(1)}, u32[]{:S(2)}, u32[]{:S(2)}) %collective-permute-start.36) | collective-permute-done | bytes 9248 | tf_op jit(solution)/shard_map/ppermute | solution.py:30
  90.8 1.0 %table.1 = (f32[288,101]{1,0:T(8,128)}, f32[8,128]{1,0:T(8,128)S(1)}) custom-call(f32[8,288]{1,0:T(8,128)S(1)} %get-tuple-element.238.refs_0_, f32[8,288]{1,0:T(8,128)S(1)} %collective-permute-done.36.refs_1_, f32[8,288]{1,0:T(8,128)S(1)} %get-tuple-element.240.refs_2_, f32[8,128]{1,0:T(8,128)S(1)} %get-tuple-element.241.refs_3_, ...), custom_call_target="tpu_custom_call" | custom-call | flops 22000000 | bytes 1024 | tf_op jit(solution)/shard_map/table/pallas_call | solution.py:49
  91.8 6.3 %collective-permute-done.34.refs_2_ = bf16[144,1152]{1,0:T(8,128)(2,1)S(1)} collective-permute-done((bf16[144,1152]{1,0:T(8,128)(2,1)S(1)}, bf16[144,1152]{1,0:T(8,128)(2,1)S(1)}, u32[]{:S(2)}, u32[]{:S(2)}) %collective-permute-start.34) | collective-permute-done | bytes 331808 | tf_op jit(solution)/shard_map/ppermute | solution.py:30
  98.1 1.0 %qkv_add.1 = (f32[144,864]{1,0:T(8,128)}, f32[144,288]{1,0:T(8,128)}, f32[8,128]{1,0:T(8,128)S(1)}) custom-call(f32[144,1152]{1,0:T(8,128)S(1)} %get-tuple-element.232.refs_0_, bf16[144,1152]{1,0:T(8,128)(2,1)S(1)} %collective-permute-done.33.refs_1_, bf16[144,1152]{1,0:T(8,128)(2,1)S(1)} %collective-permute-done.34.refs_2_, ...), custom_call_target="tpu_custom_call" | custom-call | flops 22000000 | bytes 1024 | tf_op jit(solution)/shard_map/qkv_add/pallas_call | solution.py:49
  99.2 1.2 %collective-permute-done.37.refs_1_ = bf16[144,2304]{1,0:T(8,128)(2,1)S(1)} collective-permute-done((bf16[144,2304]{1,0:T(8,128)(2,1)S(1)}, bf16[144,2304]{1,0:T(8,128)(2,1)S(1)}, u32[]{:S(2)}, u32[]{:S(2)}) %collective-permute-start.37) | collective-permute-done | bytes 663584 | tf_op jit(solution)/shard_map/ppermute | solution.py:30
  100.3 1.2 %mlp_add.1 = (f32[144,1152]{1,0:T(8,128)}, f32[144,1152]{1,0:T(8,128)}, f32[8,128]{1,0:T(8,128)}) custom-call(f32[144,2304]{1,0:T(8,128)S(1)} %get-tuple-element.220.refs_0_, bf16[144,2304]{1,0:T(8,128)(2,1)S(1)} %collective-permute-done.37.refs_1_, f32[8,128]{1,0:T(8,128)S(1)} %get-tuple-element.247.refs_2_), custom_call_target="tpu_custom_call" | custom-call | flops 22000000 | bytes 1024 | tf_op jit(solution)/shard_map/mlp_add/pallas_call | solution.py:49
  (64 shorter events, 2.4 us)
Async XLA Ops:
  0.6 0.9 copy-start
  1.7 4.6 %collective-permute-start.1 = (bf16[1,288]{1,0:T(2,128)(2,1)S(1)}, bf16[1,288]{1,0:T(2,128)(2,1)S(1)}, u32[]{:S(2)}, u32[]{:S(2)}) collective-permute-start(bf16[1,288]{1,0:T(2,128)(2,1)S(1)} %copy.31.refs_0_), channel_id=1, source_target_pairs={{0,2},{1,3},{2,0},{3,1},{4,6},{5,7},{6,4},{7,5},{8,10},{9,11},{10,... | collective-permute-start | bytes 1736 | tf_op jit(solution)/shard_map/ppermute | solution.py:30
  4.7 2.2 %collective-permute-start = (bf16[1,288]{1,0:T(2,128)(2,1)S(1)}, bf16[1,288]{1,0:T(2,128)(2,1)S(1)}, u32[]{:S(2)}, u32[]{:S(2)}) collective-permute-start(bf16[1,288]{1,0:T(2,128)(2,1)S(1)} %copy.31.refs_0_), channel_id=1, source_target_pairs={{0,1},{1,0},{2,3},{3,2},{4,5},{5,4},{6,7},{7,6},{8,9},{9,8},{10,11... | collective-permute-start | bytes 1736 | tf_op jit(solution)/shard_map/ppermute | solution.py:30
  6.2 1.6 %copy-start.5 = (bf16[1152,864]{0,1:T(8,128)(2,1)S(1)}, bf16[1152,864]{0,1:T(8,128)(2,1)}, u32[]{:S(2)}) copy-start(bf16[1152,864]{0,1:T(8,128)(2,1)} %param.24) | copy-start | bytes 5971972
  6.2 2.1 %copy-start.6 = (bf16[1152,288]{0,1:T(8,128)(2,1)S(1)}, bf16[1152,288]{0,1:T(8,128)(2,1)}, u32[]{:S(2)}) copy-start(bf16[1152,288]{0,1:T(8,128)(2,1)} %param.26) | copy-start | bytes 1990660
  6.2 2.9 %copy-start.3 = (bf16[1152,1728]{0,1:T(8,128)(2,1)S(1)}, bf16[1152,1728]{0,1:T(8,128)(2,1)}, u32[]{:S(2)}) copy-start(bf16[1152,1728]{0,1:T(8,128)(2,1)} %param.22) | copy-start | bytes 11943940
  6.3 1.4 %collective-permute-start.2 = (bf16[1,288]{1,0:T(2,128)(2,1)S(1)}, bf16[1,288]{1,0:T(2,128)(2,1)S(1)}, u32[]{:S(2)}, u32[]{:S(2)}) collective-permute-start(bf16[1,288]{1,0:T(2,128)(2,1)S(1)} %collective-permute-done.1.refs_2_), channel_id=1, source_target_pairs={{0,1},{1,0},{2,3},{3,2},{4,5},{5,4},{6,7},{7,6},{8,9},{9,8},{10,11... | collective-permute-start | bytes 1736 | tf_op jit(solution)/shard_map/ppermute | solution.py:30
  7.7 6.3 %collective-permute-start.6 = (bf16[864,1152]{1,0:T(8,128)(2,1)S(1)}, bf16[864,1152]{1,0:T(8,128)(2,1)S(1)}, u32[]{:S(2)}, u32[]{:S(2)}) collective-permute-start(bf16[864,1152]{1,0:T(8,128)(2,1)S(1)} %bitcast.14), channel_id=1, source_target_pairs={{0,1},{1,0},{2,3},{3,2},{4,5},{5,4},{6,7},{7,6},{8,9},{9,8},{10,11... | collective-permute-start | bytes 5971976 | tf_op jit(solution)/shard_map/ppermute | solution.py:30
  8.2 5.8 %collective-permute-start.7 = (bf16[288,1152]{1,0:T(8,128)(2,1)S(1)}, bf16[288,1152]{1,0:T(8,128)(2,1)S(1)}, u32[]{:S(2)}, u32[]{:S(2)}) collective-permute-start(bf16[288,1152]{1,0:T(8,128)(2,1)S(1)} %bitcast.17), channel_id=1, source_target_pairs={{0,1},{1,0},{2,3},{3,2},{4,5},{5,4},{6,7},{7,6},{8,9},{9,8},{10,11... | collective-permute-start | bytes 1990664 | tf_op jit(solution)/shard_map/ppermute | solution.py:30
  8.4 5.7 %collective-permute-start.5 = (f32[1,6528]{1,0:T(1,128)S(1)}, f32[1,6528]{1,0:T(1,128)S(1)}, u32[]{:S(2)}, u32[]{:S(2)}) collective-permute-start(f32[1,6528]{1,0:T(1,128)S(1)} %reshape.43.refs_1_.refs_6_.refs_8_.refs_4_.refs_3_), channel_id=1, source_target_pairs={{0,1},{1,0},{2,3},{3,2},{4,5},{5,4},{6,7},{7,6},{8,9},{9,8},{10,11... | collective-permute-start | bytes 78344 | tf_op jit(solution)/shard_map/ppermute | solution.py:30
  9.1 2.3 %copy-start.7 = (bf16[1,16,16,1152]{3,2,1,0:T(8,128)(2,1)S(1)}, bf16[1,16,16,1152]{3,2,1,0:T(8,128)(2,1)}, u32[]{:S(2)}) copy-start(bf16[1,16,16,1152]{3,2,1,0:T(8,128)(2,1)} %param.17) | copy-start | bytes 1769476
  9.1 2.3 %copy-start.8 = (bf16[1,16,16,1152]{3,2,1,0:T(8,128)(2,1)S(1)}, bf16[1,16,16,1152]{3,2,1,0:T(8,128)(2,1)}, u32[]{:S(2)}) copy-start(bf16[1,16,16,1152]{3,2,1,0:T(8,128)(2,1)} %param.32) | copy-start | bytes 1769476
  9.1 6.3 %copy-start.2 = (bf16[1152,1152]{1,0:T(8,128)(2,1)S(1)}, bf16[1152,1152]{1,0:T(8,128)(2,1)}, u32[]{:S(2)}) copy-start(bf16[1152,1152]{1,0:T(8,128)(2,1)} %refs_1_.9) | copy-start | bytes 7962628
  10.3 3.7 %collective-permute-start.4 = (f32[1,1728]{1,0:T(1,128)S(1)}, f32[1,1728]{1,0:T(1,128)S(1)}, u32[]{:S(2)}, u32[]{:S(2)}) collective-permute-start(f32[1,1728]{1,0:T(1,128)S(1)} %get-tuple-element.141.refs_2_), channel_id=1, source_target_pairs={{0,2},{1,3},{2,0},{3,1},{4,6},{5,7},{6,4},{7,5},{8,10},{9,11},{10,... | collective-permute-start | bytes 20744 | tf_op jit(solution)/shard_map/ppermute | solution.py:30
  11.4 2.7 %collective-permute-start.3 = (f32[1,1728]{1,0:T(1,128)S(1)}, f32[1,1728]{1,0:T(1,128)S(1)}, u32[]{:S(2)}, u32[]{:S(2)}) collective-permute-start(f32[1,1728]{1,0:T(1,128)S(1)} %get-tuple-element.141.refs_2_), channel_id=1, source_target_pairs={{0,1},{1,0},{2,3},{3,2},{4,5},{5,4},{6,7},{7,6},{8,9},{9,8},{10,11... | collective-permute-start | bytes 20744 | tf_op jit(solution)/shard_map/ppermute | solution.py:30
  11.5 3.8 %copy-start.1 = (bf16[1152,1152]{1,0:T(8,128)(2,1)S(1)}, bf16[1152,1152]{1,0:T(8,128)(2,1)}, u32[]{:S(2)}) copy-start(bf16[1152,1152]{1,0:T(8,128)(2,1)} %refs_2_.7) | copy-start | bytes 7962628
  14.0 1.2 %collective-permute-start.8 = (f32[1,1728]{1,0:T(1,128)S(1)}, f32[1,1728]{1,0:T(1,128)S(1)}, u32[]{:S(2)}, u32[]{:S(2)}) collective-permute-start(f32[1,1728]{1,0:T(1,128)S(1)} %collective-permute-done.4.refs_4_), channel_id=1, source_target_pairs={{0,1},{1,0},{2,3},{3,2},{4,5},{5,4},{6,7},{7,6},{8,9},{9,8},{10,11... | collective-permute-start | bytes 20744 | tf_op jit(solution)/shard_map/ppermute | solution.py:30
  15.3 5.0 %collective-permute-start.11 = (bf16[1152,1152]{1,0:T(8,128)(2,1)S(1)}, bf16[1152,1152]{1,0:T(8,128)(2,1)S(1)}, u32[]{:S(2)}, u32[]{:S(2)}) collective-permute-start(bf16[1152,1152]{1,0:T(8,128)(2,1)S(1)} %copy-done.1), channel_id=1, source_target_pairs={{0,1},{1,0},{2,3},{3,2},{4,5},{5,4},{6,7},{7,6},{8,9},{9,8},{10,11... | collective-permute-start | bytes 7962632 | tf_op jit(solution)/shard_map/ppermute | solution.py:30
  15.4 12.8 %collective-permute-start.10 = (bf16[1152,1152]{1,0:T(8,128)(2,1)S(1)}, bf16[1152,1152]{1,0:T(8,128)(2,1)S(1)}, u32[]{:S(2)}, u32[]{:S(2)}) collective-permute-start(bf16[1152,1152]{1,0:T(8,128)(2,1)S(1)} %copy-done.2), channel_id=1, source_target_pairs={{0,1},{1,0},{2,3},{3,2},{4,5},{5,4},{6,7},{7,6},{8,9},{9,8},{10,11... | collective-permute-start | bytes 7962632 | tf_op jit(solution)/shard_map/ppermute | solution.py:30
  19.1 9.1 %collective-permute-start.9 = (bf16[128,1152]{1,0:T(8,128)(2,1)S(1)}, bf16[128,1152]{1,0:T(8,128)(2,1)S(1)}, u32[]{:S(2)}, u32[]{:S(2)}) collective-permute-start(bf16[128,1152]{1,0:T(8,128)(2,1)S(1)} %get-tuple-element.146.refs_1_), channel_id=1, source_target_pairs={{0,2},{1,3},{2,0},{3,1},{4,6},{5,7},{6,4},{7,5},{8,10},{9,11},{10,... | collective-permute-start | bytes 884744 | tf_op jit(solution)/shard_map/ppermute | solution.py:30
  21.5 15.1 %collective-permute-start.17 = (bf16[128,1152]{1,0:T(8,128)(2,1)S(1)}, bf16[128,1152]{1,0:T(8,128)(2,1)S(1)}, u32[]{:S(2)}, u32[]{:S(2)}) collective-permute-start(bf16[128,1152]{1,0:T(8,128)(2,1)S(1)} %get-tuple-element.168.refs_2_.refs_7_), channel_id=1, source_target_pairs={{0,4},{4,0},{8,12},{12,8},{16,20},{20,16},{24,28},{28,24},{1,5},{5... | collective-permute-start | bytes 884744 | tf_op jit(solution)/shard_map/ppermute | solution.py:30
  23.1 17.6 %collective-permute-start.13 = (bf16[128,1152]{1,0:T(8,128)(2,1)S(1)}, bf16[128,1152]{1,0:T(8,128)(2,1)S(1)}, u32[]{:S(2)}, u32[]{:S(2)}) collective-permute-start(bf16[128,1152]{1,0:T(8,128)(2,1)S(1)} %get-tuple-element.168.refs_2_.refs_7_), channel_id=1, source_target_pairs={{0,16},{4,20},{8,24},{12,28},{16,0},{20,4},{24,8},{28,12},{1,17},{... | collective-permute-start | bytes 884744 | tf_op jit(solution)/shard_map/ppermute | solution.py:30
  25.7 16.0 %collective-permute-start.15 = (bf16[128,1280]{1,0:T(8,128)(2,1)S(1)}, bf16[128,1280]{1,0:T(8,128)(2,1)S(1)}, u32[]{:S(2)}, u32[]{:S(2)}) collective-permute-start(bf16[128,1280]{1,0:T(8,128)(2,1)S(1)} %get-tuple-element.174.refs_4_.refs_0_), channel_id=1, source_target_pairs={{0,8},{4,12},{8,0},{12,4},{16,24},{20,28},{24,16},{28,20},{1,9},{5... | collective-permute-start | bytes 983048 | tf_op jit(solution)/shard_map/ppermute | solution.py:30
  31.3 11.5 %collective-permute-start.12 = (bf16[128,1152]{1,0:T(8,128)(2,1)S(1)}, bf16[128,1152]{1,0:T(8,128)(2,1)S(1)}, u32[]{:S(2)}, u32[]{:S(2)}) collective-permute-start(bf16[128,1152]{1,0:T(8,128)(2,1)S(1)} %get-tuple-element.158.refs_1_), channel_id=1, source_target_pairs={{0,2},{1,3},{2,0},{3,1},{4,6},{5,7},{6,4},{7,5},{8,10},{9,11},{10,... | collective-permute-start | bytes 884744 | tf_op jit(solution)/shard_map/ppermute | solution.py:30
  32.4 19.5 %collective-permute-start.19 = (bf16[128,1152]{1,0:T(8,128)(2,1)S(1)}, bf16[128,1152]{1,0:T(8,128)(2,1)S(1)}, u32[]{:S(2)}, u32[]{:S(2)}) collective-permute-start(bf16[128,1152]{1,0:T(8,128)(2,1)S(1)} %get-tuple-element.177.refs_0_.refs_4_), channel_id=1, source_target_pairs={{0,16},{4,20},{8,24},{12,28},{16,0},{20,4},{24,8},{28,12},{1,17},{... | collective-permute-start | bytes 884744 | tf_op jit(solution)/shard_map/ppermute | solution.py:30
  36.7 10.8 %collective-permute-start.18 = (bf16[128,1152]{1,0:T(8,128)(2,1)S(1)}, bf16[128,1152]{1,0:T(8,128)(2,1)S(1)}, u32[]{:S(2)}, u32[]{:S(2)}) collective-permute-start(bf16[128,1152]{1,0:T(8,128)(2,1)S(1)} %get-tuple-element.177.refs_0_.refs_4_), channel_id=1, source_target_pairs={{0,4},{4,0},{8,12},{12,8},{16,20},{20,16},{24,28},{28,24},{1,5},{5... | collective-permute-start | bytes 884744 | tf_op jit(solution)/shard_map/ppermute | solution.py:30
  40.7 19.4 %collective-permute-start.21 = (bf16[128,1152]{1,0:T(8,128)(2,1)S(1)}, bf16[128,1152]{1,0:T(8,128)(2,1)S(1)}, u32[]{:S(2)}, u32[]{:S(2)}) collective-permute-start(bf16[128,1152]{1,0:T(8,128)(2,1)S(1)} %collective-permute-done.13.refs_16_.refs_9_.refs_2_), channel_id=1, source_target_pairs={{0,4},{4,0},{8,12},{12,8},{16,20},{20,16},{24,28},{28,24},{1,5},{5... | collective-permute-start | bytes 884744 | tf_op jit(solution)/shard_map/ppermute | solution.py:30
  41.8 9.8 %collective-permute-start.16 = (bf16[128,1152]{1,0:T(8,128)(2,1)S(1)}, bf16[128,1152]{1,0:T(8,128)(2,1)S(1)}, u32[]{:S(2)}, u32[]{:S(2)}) collective-permute-start(bf16[128,1152]{1,0:T(8,128)(2,1)S(1)} %get-tuple-element.175.refs_2_), channel_id=1, source_target_pairs={{0,2},{1,3},{2,0},{3,1},{4,6},{5,7},{6,4},{7,5},{8,10},{9,11},{10,... | collective-permute-start | bytes 884744 | tf_op jit(solution)/shard_map/ppermute | solution.py:30
  46.2 9.9 %collective-permute-start.14 = (bf16[128,1152]{1,0:T(8,128)(2,1)S(1)}, bf16[128,1152]{1,0:T(8,128)(2,1)S(1)}, u32[]{:S(2)}, u32[]{:S(2)}) collective-permute-start(bf16[128,1152]{1,0:T(8,128)(2,1)S(1)} %get-tuple-element.169.refs_1_), channel_id=1, source_target_pairs={{0,2},{1,3},{2,0},{3,1},{4,6},{5,7},{6,4},{7,5},{8,10},{9,11},{10,... | collective-permute-start | bytes 884744 | tf_op jit(solution)/shard_map/ppermute | solution.py:30
  47.7 17.0 %collective-permute-start.26 = (bf16[128,2432]{1,0:T(8,128)(2,1)S(1)}, bf16[128,2432]{1,0:T(8,128)(2,1)S(1)}, u32[]{:S(2)}, u32[]{:S(2)}) collective-permute-start(bf16[128,2432]{1,0:T(8,128)(2,1)S(1)} %get-tuple-element.209.refs_1_.refs_3_), channel_id=1, source_target_pairs={{0,8},{4,12},{8,0},{12,4},{16,24},{20,28},{24,16},{28,20},{1,9},{5... | collective-permute-start | bytes 1867784 | tf_op jit(solution)/shard_map/ppermute | solution.py:30
  51.5 5.3 %collective-permute-start.22 = (bf16[512,1152]{1,0:T(8,128)(2,1)S(1)}, bf16[512,1152]{1,0:T(8,128)(2,1)S(1)}, u32[]{:S(2)}, u32[]{:S(2)}) collective-permute-start(bf16[512,1152]{1,0:T(8,128)(2,1)S(1)} %get-tuple-element.194), channel_id=1, source_target_pairs={{0,1},{1,0},{2,3},{3,2},{4,5},{5,4},{6,7},{7,6},{8,9},{9,8},{10,11... | collective-permute-start | bytes 3538952 | tf_op jit(solution)/shard_map/ppermute | solution.py:30
  51.9 9.4 %collective-permute-start.20 = (bf16[128,1152]{1,0:T(8,128)(2,1)S(1)}, bf16[128,1152]{1,0:T(8,128)(2,1)S(1)}, u32[]{:S(2)}, u32[]{:S(2)}) collective-permute-start(bf16[128,1152]{1,0:T(8,128)(2,1)S(1)} %collective-permute-done.19.refs_6_.refs_0_), channel_id=1, source_target_pairs={{0,4},{4,0},{8,12},{12,8},{16,20},{20,16},{24,28},{28,24},{1,5},{5... | collective-permute-start | bytes 884744 | tf_op jit(solution)/shard_map/ppermute | solution.py:30
  56.6 3.5 %collective-permute-start.23 = (f32[16,1152]{1,0:T(8,128)S(1)}, f32[16,1152]{1,0:T(8,128)S(1)}, u32[]{:S(2)}, u32[]{:S(2)}) collective-permute-start(f32[16,1152]{1,0:T(8,128)S(1)} %get-tuple-element.199.refs_1_), channel_id=1, source_target_pairs={{0,1},{1,0},{2,3},{3,2},{4,5},{5,4},{6,7},{7,6},{8,9},{9,8},{10,11... | collective-permute-start | bytes 221192 | tf_op jit(solution)/shard_map/ppermute | solution.py:30
  61.6 5.1 %collective-permute-start.25 = (f32[1,7424]{1,0:T(1,128)S(1)}, f32[1,7424]{1,0:T(1,128)S(1)}, u32[]{:S(2)}, u32[]{:S(2)}) collective-permute-start(f32[1,7424]{1,0:T(1,128)S(1)} %get-tuple-element.208.refs_0_), channel_id=1, source_target_pairs={{0,16},{4,20},{8,24},{12,28},{16,0},{20,4},{24,8},{28,12},{1,17},{... | collective-permute-start | bytes 89096 | tf_op jit(solution)/shard_map/ppermute | solution.py:30
  61.6 11.4 %collective-permute-start.24 = (bf16[512,1152]{1,0:T(8,128)(2,1)S(1)}, bf16[512,1152]{1,0:T(8,128)(2,1)S(1)}, u32[]{:S(2)}, u32[]{:S(2)}) collective-permute-start(bf16[512,1152]{1,0:T(8,128)(2,1)S(1)} %get-tuple-element.200), channel_id=1, source_target_pairs={{0,1},{1,0},{2,3},{3,2},{4,5},{5,4},{6,7},{7,6},{8,9},{9,8},{10,11... | collective-permute-start | bytes 3538952 | tf_op jit(solution)/shard_map/ppermute | solution.py:30
  64.9 2.6 %collective-permute-start.29 = (bf16[128,2048]{1,0:T(8,128)(2,1)S(1)}, bf16[128,2048]{1,0:T(8,128)(2,1)S(1)}, u32[]{:S(2)}, u32[]{:S(2)}) collective-permute-start(bf16[128,2048]{1,0:T(8,128)(2,1)S(1)} %get-tuple-element.216), channel_id=1, source_target_pairs={{0,1},{1,0},{2,3},{3,2},{4,5},{5,4},{6,7},{7,6},{8,9},{9,8},{10,11... | collective-permute-start | bytes 1572872 | tf_op jit(solution)/shard_map/ppermute | solution.py:30
  65.0 3.0 %collective-permute-start.28 = (bf16[128,3072]{1,0:T(8,128)(2,1)S(1)}, bf16[128,3072]{1,0:T(8,128)(2,1)S(1)}, u32[]{:S(2)}, u32[]{:S(2)}) collective-permute-start(bf16[128,3072]{1,0:T(8,128)(2,1)S(1)} %get-tuple-element.215), channel_id=1, source_target_pairs={{0,1},{1,0},{2,3},{3,2},{4,5},{5,4},{6,7},{7,6},{8,9},{9,8},{10,11... | collective-permute-start | bytes 2359304 | tf_op jit(solution)/shard_map/ppermute | solution.py:30
  66.7 4.2 %collective-permute-start.27 = (f32[2,7424]{1,0:T(2,128)S(1)}, f32[2,7424]{1,0:T(2,128)S(1)}, u32[]{:S(2)}, u32[]{:S(2)}) collective-permute-start(f32[2,7424]{1,0:T(2,128)S(1)} %get-tuple-element.214.refs_0_), channel_id=1, source_target_pairs={{0,4},{4,0},{8,12},{12,8},{16,20},{20,16},{24,28},{28,24},{1,5},{5... | collective-permute-start | bytes 178184 | tf_op jit(solution)/shard_map/ppermute | solution.py:30
  69.4 9.9 %collective-permute-start.32 = (bf16[144,1152]{1,0:T(8,128)(2,1)S(1)}, bf16[144,1152]{1,0:T(8,128)(2,1)S(1)}, u32[]{:S(2)}, u32[]{:S(2)}) collective-permute-start(bf16[144,1152]{1,0:T(8,128)(2,1)S(1)} %get-tuple-element.224), channel_id=1, source_target_pairs={{0,4},{4,0},{8,12},{12,8},{16,20},{20,16},{24,28},{28,24},{1,5},{5... | collective-permute-start | bytes 995336 | tf_op jit(solution)/shard_map/ppermute | solution.py:30
  70.9 11.2 %collective-permute-start.31 = (f32[4,7424]{1,0:T(4,128)S(1)}, f32[4,7424]{1,0:T(4,128)S(1)}, u32[]{:S(2)}, u32[]{:S(2)}) collective-permute-start(f32[4,7424]{1,0:T(4,128)S(1)} %get-tuple-element.222.refs_0_), channel_id=1, source_target_pairs={{0,8},{4,12},{8,0},{12,4},{16,24},{20,28},{24,16},{28,20},{1,9},{5... | collective-permute-start | bytes 356360 | tf_op jit(solution)/shard_map/ppermute | solution.py:30
  76.6 23.7 %collective-permute-start.37 = (bf16[144,2304]{1,0:T(8,128)(2,1)S(1)}, bf16[144,2304]{1,0:T(8,128)(2,1)S(1)}, u32[]{:S(2)}, u32[]{:S(2)}) collective-permute-start(bf16[144,2304]{1,0:T(8,128)(2,1)S(1)} %get-tuple-element.246), channel_id=1, source_target_pairs={{0,8},{4,12},{8,0},{12,4},{16,24},{20,28},{24,16},{28,20},{1,9},{5... | collective-permute-start | bytes 1990664 | tf_op jit(solution)/shard_map/ppermute | solution.py:30
  76.7 9.2 %collective-permute-start.30 = (bf16[128,2304]{1,0:T(8,128)(2,1)S(1)}, bf16[128,2304]{1,0:T(8,128)(2,1)S(1)}, u32[]{:S(2)}, u32[]{:S(2)}) collective-permute-start(bf16[128,2304]{1,0:T(8,128)(2,1)S(1)} %get-tuple-element.221.refs_0_), channel_id=1, source_target_pairs={{0,1},{1,0},{2,3},{3,2},{4,5},{5,4},{6,7},{7,6},{8,9},{9,8},{10,11... | collective-permute-start | bytes 1769480 | tf_op jit(solution)/shard_map/ppermute | solution.py:30
  76.7 15.1 %collective-permute-start.33 = (bf16[144,1152]{1,0:T(8,128)(2,1)S(1)}, bf16[144,1152]{1,0:T(8,128)(2,1)S(1)}, u32[]{:S(2)}, u32[]{:S(2)}) collective-permute-start(bf16[144,1152]{1,0:T(8,128)(2,1)S(1)} %get-tuple-element.233), channel_id=1, source_target_pairs={{0,4},{4,0},{8,12},{12,8},{16,20},{20,16},{24,28},{28,24},{1,5},{5... | collective-permute-start | bytes 995336 | tf_op jit(solution)/shard_map/ppermute | solution.py:30
  79.4 18.8 %collective-permute-start.34 = (bf16[144,1152]{1,0:T(8,128)(2,1)S(1)}, bf16[144,1152]{1,0:T(8,128)(2,1)S(1)}, u32[]{:S(2)}, u32[]{:S(2)}) collective-permute-start(bf16[144,1152]{1,0:T(8,128)(2,1)S(1)} %get-tuple-element.234), channel_id=1, source_target_pairs={{0,16},{4,20},{8,24},{12,28},{16,0},{20,4},{24,8},{28,12},{1,17},{... | collective-permute-start | bytes 995336 | tf_op jit(solution)/shard_map/ppermute | solution.py:30
  82.1 2.1 %copy-start.4 = (bf16[1152,1728]{0,1:T(8,128)(2,1)S(1)}, bf16[1152,1728]{0,1:T(8,128)(2,1)}, u32[]{:S(2)}) copy-start(bf16[1152,1728]{0,1:T(8,128)(2,1)} %param.22) | copy-start | bytes 11943940
  85.9 1.2 %collective-permute-start.35 = (f32[8,768]{1,0:T(8,128)S(1)}, f32[8,768]{1,0:T(8,128)S(1)}, u32[]{:S(2)}, u32[]{:S(2)}) collective-permute-start(f32[8,768]{1,0:T(8,128)S(1)} %get-tuple-element.236), channel_id=1, source_target_pairs={{0,1},{1,0},{2,3},{3,2},{4,5},{5,4},{6,7},{7,6},{8,9},{9,8},{10,11... | collective-permute-start | bytes 73736 | tf_op jit(solution)/shard_map/ppermute | solution.py:30
  87.1 3.7 %collective-permute-start.36 = (f32[8,288]{1,0:T(8,128)S(1)}, f32[8,288]{1,0:T(8,128)S(1)}, u32[]{:S(2)}, u32[]{:S(2)}) collective-permute-start(f32[8,288]{1,0:T(8,128)S(1)} %get-tuple-element.239), channel_id=1, source_target_pairs={{0,2},{1,3},{2,0},{3,1},{4,6},{5,7},{6,4},{7,5},{8,10},{9,11},{10,... | collective-permute-start | bytes 27656 | tf_op jit(solution)/shard_map/ppermute | solution.py:30

commit v7 on v6

--- a/solution.py
+++ b/solution.py
@@ -156,8 +156,9 @@
 
 
 def attention_kernel(
-    frames, spots, length, normed, m0, m1, m2, m3, qkv_a, qkv_b, bias_a, bias_b, out_a, out_b,
-    part, mods, normed_low, saved_a, saved_b, probs_out, att_a, att_b, rows,
+    frames, spots, length, normed, cotangent, m0, m1, m2, m3,
+    qkv_a, qkv_b, bias_a, bias_b, out_a, out_b,
+    part, mods, normed_low, saved_a, saved_b, probs_out, att_a, att_b, low_grad, rows,
 ):
     rank = lax.axis_index("tensor")
     width = normed.shape[1]
@@ -211,17 +212,16 @@
         term = dot(att_ref[...], o[...])
         total = term if total is None else total + term
     part[...] = total.astype(BF)
+    keep = kept_rows(length, half, frames)
+    low_grad[...] = (mods[5:6, :] * jnp.where(keep, cotangent[...].astype(F32), 0.0)).astype(BF)
 
 
 def early_back_kernel(
-    frames, n_dp, length, mods, cotangent, down_a, down_b, normed_low, att_a, att_b,
-    grad_a, grad_b, low_out, pack_far, own_chunks, fc2_sum, pick,
+    n_dp, low_ref, down_a, down_b, normed_low, att_a, att_b,
+    grad_a, grad_b, pack_far, own_chunks, fc2_sum, pick,
 ):
-    upstream = cotangent[...].astype(F32)
-    half, width = upstream.shape
-    keep = kept_rows(length, half, frames)
-    low = (mods[5:6, :] * jnp.where(keep, upstream, 0.0)).astype(BF)
-    low_out[...] = low
+    low = low_ref[...]
+    width = low.shape[1]
     grad_a[...] = dot(low, down_a[...])
     grad_b[...] = dot(low, down_b[...])
     fc2_sum[...] = column_sum(low.astype(F32))
@@ -534,14 +534,14 @@
     send[...] = (stay[...] + other[...].astype(F32)).astype(BF)
 
 
-def add_kernel(widths, n_others, stay, *refs):
-    total = stay[...]
-    for other in refs[:n_others]:
-        total = total + other[...].astype(F32)
-    at = 0
-    for out, cols in zip(refs[n_others:], widths):
-        out[...] = total[:, at : at + cols]
-        at += cols
+def last_kernel(near, near_other, far_other, mlp, mlp_other, qkv, out, down, up):
+    cols = qkv.shape[1]
+    for source, target, start in ((mlp, down, 0), (mlp, up, down.shape[1])):
+        at = slice(start, start + target.shape[1])
+        target[...] = source[:, at] + mlp_other[:, at].astype(F32)
+    total = near[...] + near_other[...].astype(F32) + far_other[...].astype(F32)
+    qkv[...] = total[:, :cols]
+    out[...] = total[:, cols:]
 
 
 def join_kernel(mine, other, *outs):
@@ -654,7 +654,7 @@
     up_ws = pair(up_weight, *mod_pieces)
     down_ws = pair(down_weight, *mod_pieces)
 
-    part1, mods, low1, saved_a, saved_b, probs, att_a, att_b = call(
+    part1, mods, low1, saved_a, saved_b, probs, att_a, att_b, low_grad = call(
         order,
         lambda *refs: attention_kernel(frames, spots, *refs),
         "attention",
@@ -668,28 +668,28 @@
             ((2 * heads, half, half), F32),
             ((half, n_att), BF),
             ((half, n_att), BF),
+            ((half, width), BF),
         ],
-        [lengths, normed1, *mod_pieces, *qkv_ws, *bias_ws, *out_ws],
+        [lengths, normed1, cot, *mod_pieces, *qkv_ws, *bias_ws, *out_ws],
         [pltpu.VMEM((8, ada_cols), F32)],
     )
     part1_other = swap(part1, "tensor", 2)
 
     att_far, att_core = pad_lanes(2 * n_att), pad_lanes(n_att)
-    grad_a, grad_b, low_grad, pack1, chunks1, fc2_sum, pick = call(
-        order,
-        lambda *refs: early_back_kernel(frames, n_dp, *refs),
+    grad_a, grad_b, pack1, chunks1, fc2_sum, pick = call(
+        order,
+        lambda *refs: early_back_kernel(n_dp, *refs),
         "early_back",
         2.0,
         [
             ((half, hidden), F32),
             ((half, hidden), F32),
-            ((half, width), BF),
             ((half, att_far + wide), BF),
             ((half, wide), BF),
             ((1, width), F32),
             ((part // 2, width), BF),
         ],
-        [lengths, mods, cot, *down_ws, low1, att_a, att_b],
+        [low_grad, *down_ws, low1, att_a, att_b],
     )
     far1 = swap(pack1, "dp", 2)
     grad_y = swap(low_grad, "dp", 1)
@@ -739,16 +739,6 @@
             scratch,
         )
 
-    def add(name, widths, stay, *others):
-        return call(
-            order,
-            lambda *refs: add_kernel(widths, len(others), *refs),
-            name,
-            0.02,
-            [((chunk, w), F32) for w in widths],
-            [stay, *others],
-        )
-
     def halve_all(grad, done):
         for b in range((n_dp - 1).bit_length()):
             if b not in done:
@@ -888,11 +878,6 @@
         n, cols = value.shape
         other = swap(value, "dp", flip)
         return call(order, stack_kernel, name, us, [((2 * n, cols), F32)], [value, other])[0]
-
-    def mlp_grads(stay, other):
-        if n_dp == 8:
-            return add("mlp_add", [hidden] * 2, stay, other)
-        return [halve_all(g.reshape(n_dp // 4, chunk, hidden), [0, 2]) for g in (stay, other)]
 
     sums2 = remake("remake_yf", [rows_yf], [grad_yf], [], sums2, False)
     flips = [4, 1] + [1 << b for b in range(3, (n_dp - 1).bit_length())] + [2]
@@ -970,11 +955,20 @@
         [mine, swap(send, "tensor", 2), cond_cols, labels_all],
     )
     if n_dp == 8:
-        qkv_grad, out_grad = add("qkv_add", [n_qkv, n_att], *qkv_grad)
+        qkv_grad, out_grad, down_grad, up_grad = call(
+            order,
+            last_kernel,
+            "last_add",
+            0.02,
+            [((chunk, w), F32) for w in (n_qkv, n_att, hidden, hidden)],
+            [*qkv_grad, *mlp_grad],
+        )
     else:
         grad = halve_all(qkv_grad[0].reshape(n_dp // 2, chunk, -1), [1])
         qkv_grad, out_grad = grad[:, :n_qkv], grad[:, n_qkv:]
-    down_grad, up_grad = mlp_grads(*mlp_grad)
+        down_grad, up_grad = (
+            halve_all(g.reshape(n_dp // 4, chunk, hidden), [0, 2]) for g in mlp_grad
+        )
     return (
         result,
         tokens_grad,

time: 102 us -> 100 us (0.980)
    pallas_call x30 -> x29, Pallas kernels: 35.3 us -> 34.8 us  [call(): pl.pallas_call(whole, out_shape=[jax.ShapeDtypeStruct(s, d) for s, d in [...]
  transfers between devices with their start and end apart: 38 -> 38, of which waited for: 18 -> 13; matrix products, arithmetic and copies ran while one was open for 1% -> 1% of each run, Pallas kernels for 34% -> 33%
where the time goes in v7:
time: 100 us
  Pallas kernels  34.8 us (35%)
  starting transfers between devices  32.1 us (32%)
  waiting for transfers between devices  26.6 us (27%)
  between operations  2.96 us (3%)
  local copies, waits for them, and re-layouts  2.95 us (3%)
    pallas_call x29, Pallas kernels, call(): pl.pallas_call(whole, out_shape=[jax.ShapeDtypeStruct(s, d) for s, d in [...  34.8 us
    ppermute x38, starting transfers between devices, swap(): return lax.ppermute(value, axis, [(i, i ^ flip) for i in range(size)])  32.1 us
    ppermute x38, waiting for transfers between devices, swap(): return lax.ppermute(value, axis, [(i, i ^ flip) for i in range(size)])  26.6 us
    unnamed x19, local copies, waits for them, and re-layouts  2.84 us
  transfers between devices with their start and end apart: 38, of which 13 were waited for; matrix products, arithmetic and copies ran while one was open for 1% of the time, Pallas kernels for 33%

profile of v7, /device:TPU:0, one launch (start us, length us, event | category | flops | bytes accessed | tf_op | source)
XLA Modules:
  0.0 100.2 jit_solution(16922307435977990531)
XLA Ops:
  1.3 0.2 copy-done
  1.7 3.0 %collective-permute-start.1 = (bf16[1,288]{1,0:T(2,128)(2,1)S(1)}, bf16[1,288]{1,0:T(2,128)(2,1)S(1)}, u32[]{:S(2)}, u32[]{:S(2)}) collective-permute-start(bf16[1,288]{1,0:T(2,128)(2,1)S(1)} %copy.31.refs_0_), channel_id=1, source_target_pairs={{0,2},{1,3},{2,0},{3,1},{4,6},{5,7},{6,4},{7,5},{8,10},{9,11},{10,... | collective-permute-start | bytes 1736 | tf_op jit(solution)/shard_map/ppermute | solution.py:30
  4.7 0.8 add_add_fusion
  6.3 0.6 collective-permute-start.2
  6.9 0.8 collective-permute-done.2.refs_3_
  7.7 0.5 collective-permute-start.6
  8.4 0.4 collective-permute-start.5
  8.7 0.4 copy-done.3
  9.1 1.2 %modulation.1 = (f32[1,1152]{1,0:T(1,128)S(1)}, f32[1,1728]{1,0:T(1,128)S(1)}, f32[8,128]{1,0:T(8,128)S(1)}) custom-call(bf16[1,288]{1,0:T(2,128)(2,1)S(1)} %copy.31.refs_0_, bf16[1,288]{1,0:T(2,128)(2,1)S(1)} %collective-permute-done.refs_1_, bf16[1,288]{1,0:T(2,128)(2,1)S(1)} %collective-permute-done.1.refs_2_, ...), custom_call_target="tpu_custom_call" | custom-call | flops 1100000000 | bytes 1024 | tf_op jit(solution)/shard_map/modulation/pallas_call | solution.py:49
  10.3 1.1 %collective-permute-start.4 = (f32[1,1728]{1,0:T(1,128)S(1)}, f32[1,1728]{1,0:T(1,128)S(1)}, u32[]{:S(2)}, u32[]{:S(2)}) collective-permute-start(f32[1,1728]{1,0:T(1,128)S(1)} %get-tuple-element.141.refs_3_), channel_id=1, source_target_pairs={{0,2},{1,3},{2,0},{3,1},{4,6},{5,7},{6,4},{7,5},{8,10},{9,11},{10,... | collective-permute-start | bytes 20744 | tf_op jit(solution)/shard_map/ppermute | solution.py:30
  11.5 0.3 start.1
  11.8 2.2 %collective-permute-done.4.refs_5_ = f32[1,1728]{1,0:T(1,128)S(1)} collective-permute-done((f32[1,1728]{1,0:T(1,128)S(1)}, f32[1,1728]{1,0:T(1,128)S(1)}, u32[]{:S(2)}, u32[]{:S(2)}) %collective-permute-start.4) | collective-permute-done | bytes 6944 | tf_op jit(solution)/shard_map/ppermute | solution.py:30
  14.1 1.1 %collective-permute-done.8.refs_6_ = f32[1,1728]{1,0:T(1,128)S(1)} collective-permute-done((f32[1,1728]{1,0:T(1,128)S(1)}, f32[1,1728]{1,0:T(1,128)S(1)}, u32[]{:S(2)}, u32[]{:S(2)}) %collective-permute-start.8) | collective-permute-done | bytes 6944 | tf_op jit(solution)/shard_map/ppermute | solution.py:30
  15.3 0.2 collective-permute-start.11
  15.4 0.3 collective-permute-start.10
  16.4 2.6 %attention.1 = (bf16[128,1152]{1,0:T(8,128)(2,1)S(1)}, f32[8,1152]{1,0:T(8,128)S(1)}, bf16[128,1152]{1,0:T(8,128)(2,1)S(1)}, bf16[128,864]{1,0:T(8,128)(2,1)S(1)...) custom-call(s32[1]{0:T(128)S(6)} %copy.32.refs_0_, ...), custom_call_target="tpu_custom_call" | custom-call | flops 4400000000 | bytes 1024 | tf_op jit(solution)/shard_map/attention/pallas_call | solution.py:49
  19.1 1.1 %collective-permute-start.9 = (bf16[128,1152]{1,0:T(8,128)(2,1)S(1)}, bf16[128,1152]{1,0:T(8,128)(2,1)S(1)}, u32[]{:S(2)}, u32[]{:S(2)}) collective-permute-start(bf16[128,1152]{1,0:T(8,128)(2,1)S(1)} %get-tuple-element.146.refs_1_), channel_id=1, source_target_pairs={{0,2},{1,3},{2,0},{3,1},{4,6},{5,7},{6,4},{7,5},{8,10},{9,11},{10,... | collective-permute-start | bytes 884744 | tf_op jit(solution)/shard_map/ppermute | solution.py:30
  20.2 1.5 %collective-permute-start.17 = (bf16[128,1152]{1,0:T(8,128)(2,1)S(1)}, bf16[128,1152]{1,0:T(8,128)(2,1)S(1)}, u32[]{:S(2)}, u32[]{:S(2)}) collective-permute-start(bf16[128,1152]{1,0:T(8,128)(2,1)S(1)} %get-tuple-element.149.refs_0_.refs_2_.refs_7_), channel_id=1, source_target_pairs={{0,4},{4,0},{8,12},{12,8},{16,20},{20,16},{24,28},{28,24},{1,5},{5... | collective-permute-start | bytes 884744 | tf_op jit(solution)/shard_map/ppermute | solution.py:30
  21.7 2.6 %collective-permute-start.13 = (bf16[128,1152]{1,0:T(8,128)(2,1)S(1)}, bf16[128,1152]{1,0:T(8,128)(2,1)S(1)}, u32[]{:S(2)}, u32[]{:S(2)}) collective-permute-start(bf16[128,1152]{1,0:T(8,128)(2,1)S(1)} %get-tuple-element.149.refs_0_.refs_2_.refs_7_), channel_id=1, source_target_pairs={{0,16},{4,20},{8,24},{12,28},{16,0},{20,4},{24,8},{28,12},{1,17},{... | collective-permute-start | bytes 884744 | tf_op jit(solution)/shard_map/ppermute | solution.py:30
  24.3 1.4 %early_back.1 = (f32[128,1152]{1,0:T(8,128)S(1)}, f32[128,1152]{1,0:T(8,128)S(1)}, bf16[128,1280]{1,0:T(8,128)(2,1)S(1)}, bf16[128,640]{1,0:T(8,128)(2,1)S(1)}, ...) custom-call(bf16[128,1152]{1,0:T(8,128)(2,1)S(1)} %get-tuple-element.149.refs_0_.refs_2_.refs_7_, ...), custom_call_target="tpu_custom_call" | custom-call | flops 2200000000 | bytes 1024 | tf_op jit(solution)/shard_map/early_back/pallas_call | solution.py:49
  25.7 1.6 %collective-permute-start.15 = (bf16[128,1280]{1,0:T(8,128)(2,1)S(1)}, bf16[128,1280]{1,0:T(8,128)(2,1)S(1)}, u32[]{:S(2)}, u32[]{:S(2)}) collective-permute-start(bf16[128,1280]{1,0:T(8,128)(2,1)S(1)} %get-tuple-element.173.refs_4_.refs_0_), channel_id=1, source_target_pairs={{0,8},{4,12},{8,0},{12,4},{16,24},{20,28},{24,16},{28,20},{1,9},{5... | collective-permute-start | bytes 983048 | tf_op jit(solution)/shard_map/ppermute | solution.py:30
  27.3 0.9 collective-permute-done.9.refs_2_
  28.2 3.1 %mlp.1 = (bf16[128,1152]{1,0:T(8,128)(2,1)S(1)}, bf16[128,2304]{1,0:T(8,128)(2,1)S(1)}, bf16[128,1152]{1,0:T(8,128)(2,1)S(1)}, bf16[128,1152]{1,0:T(8,128)(2,1)S...) custom-call(bf16[128,1152]{1,0:T(8,128)(2,1)S(1)} %get-tuple-element, ...), custom_call_target="tpu_custom_call" | custom-call | flops 3300000000 | bytes 1024 | tf_op jit(solution)/shard_map/mlp/pallas_call | solution.py:49
  31.3 1.1 %collective-permute-start.12 = (bf16[128,1152]{1,0:T(8,128)(2,1)S(1)}, bf16[128,1152]{1,0:T(8,128)(2,1)S(1)}, u32[]{:S(2)}, u32[]{:S(2)}) collective-permute-start(bf16[128,1152]{1,0:T(8,128)(2,1)S(1)} %get-tuple-element.158.refs_1_), channel_id=1, source_target_pairs={{0,2},{1,3},{2,0},{3,1},{4,6},{5,7},{6,4},{7,5},{8,10},{9,11},{10,... | collective-permute-start | bytes 884744 | tf_op jit(solution)/shard_map/ppermute | solution.py:30
  32.4 2.6 %collective-permute-start.19 = (bf16[128,1152]{1,0:T(8,128)(2,1)S(1)}, bf16[128,1152]{1,0:T(8,128)(2,1)S(1)}, u32[]{:S(2)}, u32[]{:S(2)}) collective-permute-start(bf16[128,1152]{1,0:T(8,128)(2,1)S(1)} %get-tuple-element.176.refs_0_.refs_4_), channel_id=1, source_target_pairs={{0,16},{4,20},{8,24},{12,28},{16,0},{20,4},{24,8},{28,12},{1,17},{... | collective-permute-start | bytes 884744 | tf_op jit(solution)/shard_map/ppermute | solution.py:30
  35.0 1.5 %collective-permute-start.18 = (bf16[128,1152]{1,0:T(8,128)(2,1)S(1)}, bf16[128,1152]{1,0:T(8,128)(2,1)S(1)}, u32[]{:S(2)}, u32[]{:S(2)}) collective-permute-start(bf16[128,1152]{1,0:T(8,128)(2,1)S(1)} %get-tuple-element.176.refs_0_.refs_4_), channel_id=1, source_target_pairs={{0,4},{4,0},{8,12},{12,8},{16,20},{20,16},{24,28},{28,24},{1,5},{5... | collective-permute-start | bytes 884744 | tf_op jit(solution)/shard_map/ppermute | solution.py:30
  36.5 1.7 %mlp_tail.1 = (bf16[128,1152]{1,0:T(8,128)(2,1)S(1)}, f32[8,128]{1,0:T(8,128)S(1)}) custom-call(bf16[128,2304]{1,0:T(8,128)(2,1)S(1)} %get-tuple-element.165.refs_0_.refs_10_, bf16[1152,1152]{1,0:T(8,128)(2,1)S(1)} %copy-done.1, bf16[1152,1152]{1,0:T(8,128)(2,1)S(1)} %collective-permute-done.11.refs_2_, f32[8,128]{1,0:T(8,128)S(1)} %get-tuple-element.166.refs_3_), custom_call_target="tpu_custom_call" | custom-call | flops 1100000000 | bytes 1024 | tf_op jit(solution)/shard_map/mlp_tail/pallas_call | solution.py:49
  38.2 1.2 %collective-permute-done.13.refs_16_.refs_9_.refs_2_ = bf16[128,1152]{1,0:T(8,128)(2,1)S(1)} collective-permute-done((bf16[128,1152]{1,0:T(8,128)(2,1)S(1)}, bf16[128,1152]{1,0:T(8,128)(2,1)S(1)}, u32[]{:S(2)}, u32[]{:S(2)}) %collective-permute-start.13) | collective-permute-done | bytes 294944 | tf_op jit(solution)/shard_map/ppermute | solution.py:30
  39.4 0.5 collective-permute-start.21
  40.0 1.7 %collective-permute-done.15.refs_3_.refs_2_ = bf16[128,1280]{1,0:T(8,128)(2,1)S(1)} collective-permute-done((bf16[128,1280]{1,0:T(8,128)(2,1)S(1)}, bf16[128,1280]{1,0:T(8,128)(2,1)S(1)}, u32[]{:S(2)}, u32[]{:S(2)}) %collective-permute-start.15) | collective-permute-done | bytes 327712 | tf_op jit(solution)/shard_map/ppermute | solution.py:30
  41.7 1.0 collective-permute-start.16
  42.7 3.6 %attention_back.1 = (bf16[128,1152]{1,0:T(8,128)(2,1)S(1)}, f32[128,1152]{1,0:T(8,128)S(1)}, bf16[128,1152]{1,0:T(8,128)(2,1)S(1)}, bf16[128,1792]{1,0:T(8,128)(...) custom-call(s32[1]{0:T(128)S(6)} %copy.32.refs_0_, bf16[128,1152]{1,0:T(8,128)(2,1)S(1)} %get-tuple-element.158.refs_1_, ...), custom_call_target="tpu_custom_call" | custom-call | flops 5500000256 | bytes 1024 | tf_op jit(solution)/shard_map/attention_back/pallas_call | solution.py:49
  46.2 1.1 %collective-permute-start.14 = (bf16[128,1152]{1,0:T(8,128)(2,1)S(1)}, bf16[128,1152]{1,0:T(8,128)(2,1)S(1)}, u32[]{:S(2)}, u32[]{:S(2)}) collective-permute-start(bf16[128,1152]{1,0:T(8,128)(2,1)S(1)} %get-tuple-element.168.refs_1_), channel_id=1, source_target_pairs={{0,2},{1,3},{2,0},{3,1},{4,6},{5,7},{6,4},{7,5},{8,10},{9,11},{10,... | collective-permute-start | bytes 884744 | tf_op jit(solution)/shard_map/ppermute | solution.py:30
  47.5 0.2 pack_back.1
  47.7 2.9 %collective-permute-done.16.refs_3_ = bf16[128,1152]{1,0:T(8,128)(2,1)S(1)} collective-permute-done((bf16[128,1152]{1,0:T(8,128)(2,1)S(1)}, bf16[128,1152]{1,0:T(8,128)(2,1)S(1)}, u32[]{:S(2)}, u32[]{:S(2)}) %collective-permute-start.16) | collective-permute-done | bytes 294944 | tf_op jit(solution)/shard_map/ppermute | solution.py:30
  50.6 0.3 output.1
  50.9 0.5 collective-permute-start.20
  51.5 3.6 %remake_near.1 = (f32[288,1152]{1,0:T(8,128)S(1)}, f32[288,1152]{1,0:T(8,128)S(1)}, f32[8,128]{1,0:T(8,128)S(1)}) custom-call(bf16[288,1152]{1,0:T(8,128)(2,1)S(1)} %get-tuple-element.186.refs_0_, bf16[1152,1152]{1,0:T(8,128)(2,1)S(1)} %copy-done.2, bf16[1152,1152]{1,0:T(8,128)(2,1)S(1)} %copy-done.1, ...), custom_call_target="tpu_custom_call" | custom-call | flops 1100000000 | bytes 1024 | tf_op jit(solution)/shard_map/remake_near/pallas_call | solution.py:49
  55.1 0.6 input_back.1
  55.7 3.2 %remake_core0.1 = (f32[288,1152]{1,0:T(8,128)S(1)}, f32[288,1152]{1,0:T(8,128)S(1)}, f32[8,128]{1,0:T(8,128)S(1)}) custom-call(bf16[288,1152]{1,0:T(8,128)(2,1)S(1)} %get-tuple-element.186.refs_0_, bf16[1152,1152]{1,0:T(8,128)(2,1)S(1)} %copy-done.2, bf16[1152,1152]{1,0:T(8,128)(2,1)S(1)} %copy-done.1, ...), custom_call_target="tpu_custom_call" | custom-call | flops 2200000000 | bytes 1024 | tf_op jit(solution)/shard_map/remake_core0/pallas_call | solution.py:49
  59.2 3.4 %collective-permute-start.25 = (f32[1,7424]{1,0:T(1,128)S(1)}, f32[1,7424]{1,0:T(1,128)S(1)}, u32[]{:S(2)}, u32[]{:S(2)}) collective-permute-start(f32[1,7424]{1,0:T(1,128)S(1)} %get-tuple-element.207.refs_0_), channel_id=1, source_target_pairs={{0,16},{4,20},{8,24},{12,28},{16,0},{20,4},{24,8},{28,12},{1,17},{... | collective-permute-start | bytes 89096 | tf_op jit(solution)/shard_map/ppermute | solution.py:30
  62.6 0.2 collective-permute-start.24
  62.9 2.3 %remake_yf.1 = (f32[288,1152]{1,0:T(8,128)S(1)}, f32[288,1152]{1,0:T(8,128)S(1)}, f32[8,128]{1,0:T(8,128)S(1)}) custom-call(bf16[288,1152]{1,0:T(8,128)(2,1)S(1)} %get-tuple-element.186.refs_0_, bf16[1152,1152]{1,0:T(8,128)(2,1)S(1)} %copy-done.2, bf16[1152,1152]{1,0:T(8,128)(2,1)S(1)} %copy-done.1, ...), custom_call_target="tpu_custom_call" | custom-call | flops 22000000 | bytes 1024 | tf_op jit(solution)/shard_map/remake_yf/pallas_call | solution.py:49
  65.1 0.1 forward3.1
  65.3 0.4 collective-permute-start.28
  65.7 0.2 collective-permute-start.29
  65.9 0.9 collective-permute-start.27
  66.8 1.6 %collective-permute-done.29.refs_7_ = bf16[128,2048]{1,0:T(8,128)(2,1)S(1)} collective-permute-done((bf16[128,2048]{1,0:T(8,128)(2,1)S(1)}, bf16[128,2048]{1,0:T(8,128)(2,1)S(1)}, u32[]{:S(2)}, u32[]{:S(2)}) %collective-permute-start.29) | collective-permute-done | bytes 524320 | tf_op jit(solution)/shard_map/ppermute | solution.py:30
  68.4 1.4 %qkv_grad.1 = (f32[144,1152]{1,0:T(8,128)S(1)}, bf16[144,1152]{1,0:T(8,128)(2,1)S(1)}, f32[144,1152]{1,0:T(8,128)S(1)}, bf16[144,1152]{1,0:T(8,128)(2,1)S(1)}, f32[8,128]{1,0:T(8,128)S(1)}) custom-call(bf16[128,1280]{1,0:T(8,128)(2,1)S(1)} %get-tuple-element.173.refs_4_.refs_0_, bf16[128,640]{1,0:T(8,128)(2,1)S(1)} %get-tuple-element.210.refs_5_.refs_1_, ...), custom_call_target="tpu_custom_call" | custom-call | flops 22000000 | bytes 1024 | tf_op jit(solution)/shard_map/qkv_grad/pallas_call | solution.py:49
  69.8 0.9 collective-permute-start.32
  70.7 0.7 collective-permute-start.31
  71.4 3.5 %remake_core1.1 = (f32[144,2304]{1,0:T(8,128)S(1)}, bf16[144,2304]{1,0:T(8,128)(2,1)S(1)}, f32[8,128]{1,0:T(8,128)S(1)}) custom-call(bf16[288,1152]{1,0:T(8,128)(2,1)S(1)} %get-tuple-element.186.refs_0_, bf16[1152,1152]{1,0:T(8,128)(2,1)S(1)} %copy-done.2, bf16[1152,1152]{1,0:T(8,128)(2,1)S(1)} %copy-done.1, ...), custom_call_target="tpu_custom_call" | custom-call | flops 22000000 | bytes 1024 | tf_op jit(solution)/shard_map/remake_core1/pallas_call | solution.py:49
  75.0 1.4 %collective-permute-start.35 = (bf16[144,2304]{1,0:T(8,128)(2,1)S(1)}, bf16[144,2304]{1,0:T(8,128)(2,1)S(1)}, u32[]{:S(2)}, u32[]{:S(2)}) collective-permute-start(bf16[144,2304]{1,0:T(8,128)(2,1)S(1)} %get-tuple-element.234), channel_id=1, source_target_pairs={{0,8},{4,12},{8,0},{12,4},{16,24},{20,28},{24,16},{28,20},{1,9},{5... | collective-permute-start | bytes 1990664 | tf_op jit(solution)/shard_map/ppermute | solution.py:30
  76.4 1.2 %collective-permute-start.33 = (bf16[144,1152]{1,0:T(8,128)(2,1)S(1)}, bf16[144,1152]{1,0:T(8,128)(2,1)S(1)}, u32[]{:S(2)}, u32[]{:S(2)}) collective-permute-start(bf16[144,1152]{1,0:T(8,128)(2,1)S(1)} %get-tuple-element.232), channel_id=1, source_target_pairs={{0,4},{4,0},{8,12},{12,8},{16,20},{20,16},{24,28},{28,24},{1,5},{5... | collective-permute-start | bytes 995336 | tf_op jit(solution)/shard_map/ppermute | solution.py:30
  77.6 2.5 %collective-permute-done.32.refs_1_ = bf16[144,1152]{1,0:T(8,128)(2,1)S(1)} collective-permute-done((bf16[144,1152]{1,0:T(8,128)(2,1)S(1)}, bf16[144,1152]{1,0:T(8,128)(2,1)S(1)}, u32[]{:S(2)}, u32[]{:S(2)}) %collective-permute-start.32) | collective-permute-done | bytes 331808 | tf_op jit(solution)/shard_map/ppermute | solution.py:30
  80.3 2.1 %copy-done.4 = bf16[1152,1728]{0,1:T(8,128)(2,1)S(1)} copy-done((bf16[1152,1728]{0,1:T(8,128)(2,1)S(1)}, bf16[1152,1728]{0,1:T(8,128)(2,1)}, u32[]{:S(2)}) %copy-start.4) | copy-done | bytes 3981336
  82.4 1.6 %gathered.1 = (f32[144,1728]{1,0:T(8,128)}, f32[1728]{0:T(1024)}, f32[576]{0:T(1024)}, f32[1152]{0:T(1024)}, f32[1152]{0:T(1024)}, /*index=5*/f32[1152]{0:T(1024...) custom-call(bf16[1728,1152]{1,0:T(8,128)(2,1)S(1)} %bitcast.13, ...), custom_call_target="tpu_custom_call" | custom-call | flops 5500000256 | bytes 1024 | tf_op jit(solution)/shard_map/gathered/pallas_call | solution.py:49
  84.1 1.1 %join.1 = (bf16[256,1152]{1,0:T(8,128)(2,1)}, bf16[256,1152]{1,0:T(8,128)(2,1)}, f32[8,128]{1,0:T(8,128)S(1)}) custom-call(bf16[128,2304]{1,0:T(8,128)(2,1)S(1)} %get-tuple-element.220.refs_0_, bf16[128,2304]{1,0:T(8,128)(2,1)S(1)} %collective-permute-done.30.refs_1_, f32[8,128]{1,0:T(8,128)S(1)} %get-tuple-element.228.refs_2_), custom_call_target="tpu_custom_call" | custom-call | flops 22000000 | bytes 1024 | tf_op jit(solution)/shard_map/join/pallas_call | solution.py:49
  85.3 1.1 %collective-permute-start.37 = (f32[8,288]{1,0:T(8,128)S(1)}, f32[8,288]{1,0:T(8,128)S(1)}, u32[]{:S(2)}, u32[]{:S(2)}) collective-permute-start(f32[8,288]{1,0:T(8,128)S(1)} %get-tuple-element.239), channel_id=1, source_target_pairs={{0,2},{1,3},{2,0},{3,1},{4,6},{5,7},{6,4},{7,5},{8,10},{9,11},{10,... | collective-permute-start | bytes 27656 | tf_op jit(solution)/shard_map/ppermute | solution.py:30
  86.3 2.6 %collective-permute-done.37.refs_1_ = f32[8,288]{1,0:T(8,128)S(1)} collective-permute-done((f32[8,288]{1,0:T(8,128)S(1)}, f32[8,288]{1,0:T(8,128)S(1)}, u32[]{:S(2)}, u32[]{:S(2)}) %collective-permute-start.37) | collective-permute-done | bytes 9248 | tf_op jit(solution)/shard_map/ppermute | solution.py:30
  89.0 1.0 %table.1 = (f32[288,101]{1,0:T(8,128)}, f32[8,128]{1,0:T(8,128)S(1)}) custom-call(f32[8,288]{1,0:T(8,128)S(1)} %get-tuple-element.238.refs_0_, f32[8,288]{1,0:T(8,128)S(1)} %collective-permute-done.37.refs_1_, f32[8,288]{1,0:T(8,128)S(1)} %get-tuple-element.240.refs_2_, f32[8,128]{1,0:T(8,128)S(1)} %get-tuple-element.241.refs_3_, ...), custom_call_target="tpu_custom_call" | custom-call | flops 22000000 | bytes 1024 | tf_op jit(solution)/shard_map/table/pallas_call | solution.py:49
  90.0 7.6 %collective-permute-done.34.refs_2_ = bf16[144,1152]{1,0:T(8,128)(2,1)S(1)} collective-permute-done((bf16[144,1152]{1,0:T(8,128)(2,1)S(1)}, bf16[144,1152]{1,0:T(8,128)(2,1)S(1)}, u32[]{:S(2)}, u32[]{:S(2)}) %collective-permute-start.34) | collective-permute-done | bytes 331808 | tf_op jit(solution)/shard_map/ppermute | solution.py:30
  97.6 1.1 %collective-permute-done.35.refs_4_ = bf16[144,2304]{1,0:T(8,128)(2,1)S(1)} collective-permute-done((bf16[144,2304]{1,0:T(8,128)(2,1)S(1)}, bf16[144,2304]{1,0:T(8,128)(2,1)S(1)}, u32[]{:S(2)}, u32[]{:S(2)}) %collective-permute-start.35) | collective-permute-done | bytes 663584 | tf_op jit(solution)/shard_map/ppermute | solution.py:30
  98.7 1.5 %last_add.1 = (f32[144,864]{1,0:T(8,128)}, f32[144,288]{1,0:T(8,128)}, f32[144,1152]{1,0:T(8,128)}, f32[144,1152]{1,0:T(8,128)}, f32[8,128]{1,0:T(8,128)}) custom-call(f32[144,1152]{1,0:T(8,128)S(1)} %get-tuple-element.231.refs_0_, bf16[144,1152]{1,0:T(8,128)(2,1)S(1)} %collective-permute-done.33.refs_1_, ...), custom_call_target="tpu_custom_call" | custom-call | flops 22000000 | bytes 1024 | tf_op jit(solution)/shard_map/last_add/pallas_call | solution.py:49
  (63 shorter events, 1.4 us)
Async XLA Ops:
  0.6 0.9 copy-start
  1.7 4.6 %collective-permute-start.1 = (bf16[1,288]{1,0:T(2,128)(2,1)S(1)}, bf16[1,288]{1,0:T(2,128)(2,1)S(1)}, u32[]{:S(2)}, u32[]{:S(2)}) collective-permute-start(bf16[1,288]{1,0:T(2,128)(2,1)S(1)} %copy.31.refs_0_), channel_id=1, source_target_pairs={{0,2},{1,3},{2,0},{3,1},{4,6},{5,7},{6,4},{7,5},{8,10},{9,11},{10,... | collective-permute-start | bytes 1736 | tf_op jit(solution)/shard_map/ppermute | solution.py:30
  4.7 2.2 %collective-permute-start = (bf16[1,288]{1,0:T(2,128)(2,1)S(1)}, bf16[1,288]{1,0:T(2,128)(2,1)S(1)}, u32[]{:S(2)}, u32[]{:S(2)}) collective-permute-start(bf16[1,288]{1,0:T(2,128)(2,1)S(1)} %copy.31.refs_0_), channel_id=1, source_target_pairs={{0,1},{1,0},{2,3},{3,2},{4,5},{5,4},{6,7},{7,6},{8,9},{9,8},{10,11... | collective-permute-start | bytes 1736 | tf_op jit(solution)/shard_map/ppermute | solution.py:30
  6.2 1.6 %copy-start.5 = (bf16[1152,864]{0,1:T(8,128)(2,1)S(1)}, bf16[1152,864]{0,1:T(8,128)(2,1)}, u32[]{:S(2)}) copy-start(bf16[1152,864]{0,1:T(8,128)(2,1)} %param.24) | copy-start | bytes 5971972
  6.2 2.1 %copy-start.6 = (bf16[1152,288]{0,1:T(8,128)(2,1)S(1)}, bf16[1152,288]{0,1:T(8,128)(2,1)}, u32[]{:S(2)}) copy-start(bf16[1152,288]{0,1:T(8,128)(2,1)} %param.26) | copy-start | bytes 1990660
  6.2 2.9 %copy-start.3 = (bf16[1152,1728]{0,1:T(8,128)(2,1)S(1)}, bf16[1152,1728]{0,1:T(8,128)(2,1)}, u32[]{:S(2)}) copy-start(bf16[1152,1728]{0,1:T(8,128)(2,1)} %param.22) | copy-start | bytes 11943940
  6.3 1.4 %collective-permute-start.2 = (bf16[1,288]{1,0:T(2,128)(2,1)S(1)}, bf16[1,288]{1,0:T(2,128)(2,1)S(1)}, u32[]{:S(2)}, u32[]{:S(2)}) collective-permute-start(bf16[1,288]{1,0:T(2,128)(2,1)S(1)} %collective-permute-done.1.refs_2_), channel_id=1, source_target_pairs={{0,1},{1,0},{2,3},{3,2},{4,5},{5,4},{6,7},{7,6},{8,9},{9,8},{10,11... | collective-permute-start | bytes 1736 | tf_op jit(solution)/shard_map/ppermute | solution.py:30
  7.7 6.3 %collective-permute-start.6 = (bf16[864,1152]{1,0:T(8,128)(2,1)S(1)}, bf16[864,1152]{1,0:T(8,128)(2,1)S(1)}, u32[]{:S(2)}, u32[]{:S(2)}) collective-permute-start(bf16[864,1152]{1,0:T(8,128)(2,1)S(1)} %bitcast.14), channel_id=1, source_target_pairs={{0,1},{1,0},{2,3},{3,2},{4,5},{5,4},{6,7},{7,6},{8,9},{9,8},{10,11... | collective-permute-start | bytes 5971976 | tf_op jit(solution)/shard_map/ppermute | solution.py:30
  8.2 5.8 %collective-permute-start.7 = (bf16[288,1152]{1,0:T(8,128)(2,1)S(1)}, bf16[288,1152]{1,0:T(8,128)(2,1)S(1)}, u32[]{:S(2)}, u32[]{:S(2)}) collective-permute-start(bf16[288,1152]{1,0:T(8,128)(2,1)S(1)} %bitcast.17), channel_id=1, source_target_pairs={{0,1},{1,0},{2,3},{3,2},{4,5},{5,4},{6,7},{7,6},{8,9},{9,8},{10,11... | collective-permute-start | bytes 1990664 | tf_op jit(solution)/shard_map/ppermute | solution.py:30
  8.4 5.7 %collective-permute-start.5 = (f32[1,6528]{1,0:T(1,128)S(1)}, f32[1,6528]{1,0:T(1,128)S(1)}, u32[]{:S(2)}, u32[]{:S(2)}) collective-permute-start(f32[1,6528]{1,0:T(1,128)S(1)} %reshape.43.refs_1_.refs_6_.refs_9_.refs_4_.refs_3_), channel_id=1, source_target_pairs={{0,1},{1,0},{2,3},{3,2},{4,5},{5,4},{6,7},{7,6},{8,9},{9,8},{10,11... | collective-permute-start | bytes 78344 | tf_op jit(solution)/shard_map/ppermute | solution.py:30
  9.1 2.4 %copy-start.7 = (bf16[1,16,16,1152]{3,2,1,0:T(8,128)(2,1)S(1)}, bf16[1,16,16,1152]{3,2,1,0:T(8,128)(2,1)}, u32[]{:S(2)}) copy-start(bf16[1,16,16,1152]{3,2,1,0:T(8,128)(2,1)} %param.17) | copy-start | bytes 1769476
  9.1 2.4 %copy-start.8 = (bf16[1,16,16,1152]{3,2,1,0:T(8,128)(2,1)S(1)}, bf16[1,16,16,1152]{3,2,1,0:T(8,128)(2,1)}, u32[]{:S(2)}) copy-start(bf16[1,16,16,1152]{3,2,1,0:T(8,128)(2,1)} %param.32) | copy-start | bytes 1769476
  9.1 6.3 %copy-start.2 = (bf16[1152,1152]{1,0:T(8,128)(2,1)S(1)}, bf16[1152,1152]{1,0:T(8,128)(2,1)}, u32[]{:S(2)}) copy-start(bf16[1152,1152]{1,0:T(8,128)(2,1)} %refs_1_.11) | copy-start | bytes 7962628
  10.3 3.7 %collective-permute-start.4 = (f32[1,1728]{1,0:T(1,128)S(1)}, f32[1,1728]{1,0:T(1,128)S(1)}, u32[]{:S(2)}, u32[]{:S(2)}) collective-permute-start(f32[1,1728]{1,0:T(1,128)S(1)} %get-tuple-element.141.refs_3_), channel_id=1, source_target_pairs={{0,2},{1,3},{2,0},{3,1},{4,6},{5,7},{6,4},{7,5},{8,10},{9,11},{10,... | collective-permute-start | bytes 20744 | tf_op jit(solution)/shard_map/ppermute | solution.py:30
  11.4 2.7 %collective-permute-start.3 = (f32[1,1728]{1,0:T(1,128)S(1)}, f32[1,1728]{1,0:T(1,128)S(1)}, u32[]{:S(2)}, u32[]{:S(2)}) collective-permute-start(f32[1,1728]{1,0:T(1,128)S(1)} %get-tuple-element.141.refs_3_), channel_id=1, source_target_pairs={{0,1},{1,0},{2,3},{3,2},{4,5},{5,4},{6,7},{7,6},{8,9},{9,8},{10,11... | collective-permute-start | bytes 20744 | tf_op jit(solution)/shard_map/ppermute | solution.py:30
  11.5 3.8 %copy-start.1 = (bf16[1152,1152]{1,0:T(8,128)(2,1)S(1)}, bf16[1152,1152]{1,0:T(8,128)(2,1)}, u32[]{:S(2)}) copy-start(bf16[1152,1152]{1,0:T(8,128)(2,1)} %refs_2_.7) | copy-start | bytes 7962628
  14.0 1.2 %collective-permute-start.8 = (f32[1,1728]{1,0:T(1,128)S(1)}, f32[1,1728]{1,0:T(1,128)S(1)}, u32[]{:S(2)}, u32[]{:S(2)}) collective-permute-start(f32[1,1728]{1,0:T(1,128)S(1)} %collective-permute-done.4.refs_5_), channel_id=1, source_target_pairs={{0,1},{1,0},{2,3},{3,2},{4,5},{5,4},{6,7},{7,6},{8,9},{9,8},{10,11... | collective-permute-start | bytes 20744 | tf_op jit(solution)/shard_map/ppermute | solution.py:30
  15.3 9.0 %collective-permute-start.11 = (bf16[1152,1152]{1,0:T(8,128)(2,1)S(1)}, bf16[1152,1152]{1,0:T(8,128)(2,1)S(1)}, u32[]{:S(2)}, u32[]{:S(2)}) collective-permute-start(bf16[1152,1152]{1,0:T(8,128)(2,1)S(1)} %copy-done.1), channel_id=1, source_target_pairs={{0,1},{1,0},{2,3},{3,2},{4,5},{5,4},{6,7},{7,6},{8,9},{9,8},{10,11... | collective-permute-start | bytes 7962632 | tf_op jit(solution)/shard_map/ppermute | solution.py:30
  15.4 12.8 %collective-permute-start.10 = (bf16[1152,1152]{1,0:T(8,128)(2,1)S(1)}, bf16[1152,1152]{1,0:T(8,128)(2,1)S(1)}, u32[]{:S(2)}, u32[]{:S(2)}) collective-permute-start(bf16[1152,1152]{1,0:T(8,128)(2,1)S(1)} %copy-done.2), channel_id=1, source_target_pairs={{0,1},{1,0},{2,3},{3,2},{4,5},{5,4},{6,7},{7,6},{8,9},{9,8},{10,11... | collective-permute-start | bytes 7962632 | tf_op jit(solution)/shard_map/ppermute | solution.py:30
  19.1 9.2 %collective-permute-start.9 = (bf16[128,1152]{1,0:T(8,128)(2,1)S(1)}, bf16[128,1152]{1,0:T(8,128)(2,1)S(1)}, u32[]{:S(2)}, u32[]{:S(2)}) collective-permute-start(bf16[128,1152]{1,0:T(8,128)(2,1)S(1)} %get-tuple-element.146.refs_1_), channel_id=1, source_target_pairs={{0,2},{1,3},{2,0},{3,1},{4,6},{5,7},{6,4},{7,5},{8,10},{9,11},{10,... | collective-permute-start | bytes 884744 | tf_op jit(solution)/shard_map/ppermute | solution.py:30
  20.2 14.8 %collective-permute-start.17 = (bf16[128,1152]{1,0:T(8,128)(2,1)S(1)}, bf16[128,1152]{1,0:T(8,128)(2,1)S(1)}, u32[]{:S(2)}, u32[]{:S(2)}) collective-permute-start(bf16[128,1152]{1,0:T(8,128)(2,1)S(1)} %get-tuple-element.149.refs_0_.refs_2_.refs_7_), channel_id=1, source_target_pairs={{0,4},{4,0},{8,12},{12,8},{16,20},{20,16},{24,28},{28,24},{1,5},{5... | collective-permute-start | bytes 884744 | tf_op jit(solution)/shard_map/ppermute | solution.py:30
  21.7 17.7 %collective-permute-start.13 = (bf16[128,1152]{1,0:T(8,128)(2,1)S(1)}, bf16[128,1152]{1,0:T(8,128)(2,1)S(1)}, u32[]{:S(2)}, u32[]{:S(2)}) collective-permute-start(bf16[128,1152]{1,0:T(8,128)(2,1)S(1)} %get-tuple-element.149.refs_0_.refs_2_.refs_7_), channel_id=1, source_target_pairs={{0,16},{4,20},{8,24},{12,28},{16,0},{20,4},{24,8},{28,12},{1,17},{... | collective-permute-start | bytes 884744 | tf_op jit(solution)/shard_map/ppermute | solution.py:30
  25.7 16.0 %collective-permute-start.15 = (bf16[128,1280]{1,0:T(8,128)(2,1)S(1)}, bf16[128,1280]{1,0:T(8,128)(2,1)S(1)}, u32[]{:S(2)}, u32[]{:S(2)}) collective-permute-start(bf16[128,1280]{1,0:T(8,128)(2,1)S(1)} %get-tuple-element.173.refs_4_.refs_0_), channel_id=1, source_target_pairs={{0,8},{4,12},{8,0},{12,4},{16,24},{20,28},{24,16},{28,20},{1,9},{5... | collective-permute-start | bytes 983048 | tf_op jit(solution)/shard_map/ppermute | solution.py:30
  31.3 11.4 %collective-permute-start.12 = (bf16[128,1152]{1,0:T(8,128)(2,1)S(1)}, bf16[128,1152]{1,0:T(8,128)(2,1)S(1)}, u32[]{:S(2)}, u32[]{:S(2)}) collective-permute-start(bf16[128,1152]{1,0:T(8,128)(2,1)S(1)} %get-tuple-element.158.refs_1_), channel_id=1, source_target_pairs={{0,2},{1,3},{2,0},{3,1},{4,6},{5,7},{6,4},{7,5},{8,10},{9,11},{10,... | collective-permute-start | bytes 884744 | tf_op jit(solution)/shard_map/ppermute | solution.py:30
  32.4 18.5 %collective-permute-start.19 = (bf16[128,1152]{1,0:T(8,128)(2,1)S(1)}, bf16[128,1152]{1,0:T(8,128)(2,1)S(1)}, u32[]{:S(2)}, u32[]{:S(2)}) collective-permute-start(bf16[128,1152]{1,0:T(8,128)(2,1)S(1)} %get-tuple-element.176.refs_0_.refs_4_), channel_id=1, source_target_pairs={{0,16},{4,20},{8,24},{12,28},{16,0},{20,4},{24,8},{28,12},{1,17},{... | collective-permute-start | bytes 884744 | tf_op jit(solution)/shard_map/ppermute | solution.py:30
  35.0 12.3 %collective-permute-start.18 = (bf16[128,1152]{1,0:T(8,128)(2,1)S(1)}, bf16[128,1152]{1,0:T(8,128)(2,1)S(1)}, u32[]{:S(2)}, u32[]{:S(2)}) collective-permute-start(bf16[128,1152]{1,0:T(8,128)(2,1)S(1)} %get-tuple-element.176.refs_0_.refs_4_), channel_id=1, source_target_pairs={{0,4},{4,0},{8,12},{12,8},{16,20},{20,16},{24,28},{28,24},{1,5},{5... | collective-permute-start | bytes 884744 | tf_op jit(solution)/shard_map/ppermute | solution.py:30
  39.4 19.5 %collective-permute-start.21 = (bf16[128,1152]{1,0:T(8,128)(2,1)S(1)}, bf16[128,1152]{1,0:T(8,128)(2,1)S(1)}, u32[]{:S(2)}, u32[]{:S(2)}) collective-permute-start(bf16[128,1152]{1,0:T(8,128)(2,1)S(1)} %collective-permute-done.13.refs_16_.refs_9_.refs_2_), channel_id=1, source_target_pairs={{0,4},{4,0},{8,12},{12,8},{16,20},{20,16},{24,28},{28,24},{1,5},{5... | collective-permute-start | bytes 884744 | tf_op jit(solution)/shard_map/ppermute | solution.py:30
  41.7 8.9 %collective-permute-start.16 = (bf16[128,1152]{1,0:T(8,128)(2,1)S(1)}, bf16[128,1152]{1,0:T(8,128)(2,1)S(1)}, u32[]{:S(2)}, u32[]{:S(2)}) collective-permute-start(bf16[128,1152]{1,0:T(8,128)(2,1)S(1)} %get-tuple-element.174.refs_2_), channel_id=1, source_target_pairs={{0,2},{1,3},{2,0},{3,1},{4,6},{5,7},{6,4},{7,5},{8,10},{9,11},{10,... | collective-permute-start | bytes 884744 | tf_op jit(solution)/shard_map/ppermute | solution.py:30
  46.2 8.8 %collective-permute-start.14 = (bf16[128,1152]{1,0:T(8,128)(2,1)S(1)}, bf16[128,1152]{1,0:T(8,128)(2,1)S(1)}, u32[]{:S(2)}, u32[]{:S(2)}) collective-permute-start(bf16[128,1152]{1,0:T(8,128)(2,1)S(1)} %get-tuple-element.168.refs_1_), channel_id=1, source_target_pairs={{0,2},{1,3},{2,0},{3,1},{4,6},{5,7},{6,4},{7,5},{8,10},{9,11},{10,... | collective-permute-start | bytes 884744 | tf_op jit(solution)/shard_map/ppermute | solution.py:30
  47.4 8.3 %collective-permute-start.22 = (bf16[512,1152]{1,0:T(8,128)(2,1)S(1)}, bf16[512,1152]{1,0:T(8,128)(2,1)S(1)}, u32[]{:S(2)}, u32[]{:S(2)}) collective-permute-start(bf16[512,1152]{1,0:T(8,128)(2,1)S(1)} %get-tuple-element.193), channel_id=1, source_target_pairs={{0,1},{1,0},{2,3},{3,2},{4,5},{5,4},{6,7},{7,6},{8,9},{9,8},{10,11... | collective-permute-start | bytes 3538952 | tf_op jit(solution)/shard_map/ppermute | solution.py:30
  50.6 14.5 %collective-permute-start.26 = (bf16[128,2432]{1,0:T(8,128)(2,1)S(1)}, bf16[128,2432]{1,0:T(8,128)(2,1)S(1)}, u32[]{:S(2)}, u32[]{:S(2)}) collective-permute-start(bf16[128,2432]{1,0:T(8,128)(2,1)S(1)} %get-tuple-element.208.refs_1_.refs_3_), channel_id=1, source_target_pairs={{0,8},{4,12},{8,0},{12,4},{16,24},{20,28},{24,16},{28,20},{1,9},{5... | collective-permute-start | bytes 1867784 | tf_op jit(solution)/shard_map/ppermute | solution.py:30
  50.9 8.1 %collective-permute-start.20 = (bf16[128,1152]{1,0:T(8,128)(2,1)S(1)}, bf16[128,1152]{1,0:T(8,128)(2,1)S(1)}, u32[]{:S(2)}, u32[]{:S(2)}) collective-permute-start(bf16[128,1152]{1,0:T(8,128)(2,1)S(1)} %collective-permute-done.19.refs_6_.refs_0_), channel_id=1, source_target_pairs={{0,4},{4,0},{8,12},{12,8},{16,20},{20,16},{24,28},{28,24},{1,5},{5... | collective-permute-start | bytes 884744 | tf_op jit(solution)/shard_map/ppermute | solution.py:30
  55.7 3.4 %collective-permute-start.23 = (f32[16,1152]{1,0:T(8,128)S(1)}, f32[16,1152]{1,0:T(8,128)S(1)}, u32[]{:S(2)}, u32[]{:S(2)}) collective-permute-start(f32[16,1152]{1,0:T(8,128)S(1)} %get-tuple-element.198.refs_1_), channel_id=1, source_target_pairs={{0,1},{1,0},{2,3},{3,2},{4,5},{5,4},{6,7},{7,6},{8,9},{9,8},{10,11... | collective-permute-start | bytes 221192 | tf_op jit(solution)/shard_map/ppermute | solution.py:30
  59.2 6.6 %collective-permute-start.25 = (f32[1,7424]{1,0:T(1,128)S(1)}, f32[1,7424]{1,0:T(1,128)S(1)}, u32[]{:S(2)}, u32[]{:S(2)}) collective-permute-start(f32[1,7424]{1,0:T(1,128)S(1)} %get-tuple-element.207.refs_0_), channel_id=1, source_target_pairs={{0,16},{4,20},{8,24},{12,28},{16,0},{20,4},{24,8},{28,12},{1,17},{... | collective-permute-start | bytes 89096 | tf_op jit(solution)/shard_map/ppermute | solution.py:30
  62.6 8.8 %collective-permute-start.24 = (bf16[512,1152]{1,0:T(8,128)(2,1)S(1)}, bf16[512,1152]{1,0:T(8,128)(2,1)S(1)}, u32[]{:S(2)}, u32[]{:S(2)}) collective-permute-start(bf16[512,1152]{1,0:T(8,128)(2,1)S(1)} %get-tuple-element.199), channel_id=1, source_target_pairs={{0,1},{1,0},{2,3},{3,2},{4,5},{5,4},{6,7},{7,6},{8,9},{9,8},{10,11... | collective-permute-start | bytes 3538952 | tf_op jit(solution)/shard_map/ppermute | solution.py:30
  65.3 3.1 %collective-permute-start.28 = (bf16[128,3072]{1,0:T(8,128)(2,1)S(1)}, bf16[128,3072]{1,0:T(8,128)(2,1)S(1)}, u32[]{:S(2)}, u32[]{:S(2)}) collective-permute-start(bf16[128,3072]{1,0:T(8,128)(2,1)S(1)} %get-tuple-element.214), channel_id=1, source_target_pairs={{0,1},{1,0},{2,3},{3,2},{4,5},{5,4},{6,7},{7,6},{8,9},{9,8},{10,11... | collective-permute-start | bytes 2359304 | tf_op jit(solution)/shard_map/ppermute | solution.py:30
  65.7 2.7 %collective-permute-start.29 = (bf16[128,2048]{1,0:T(8,128)(2,1)S(1)}, bf16[128,2048]{1,0:T(8,128)(2,1)S(1)}, u32[]{:S(2)}, u32[]{:S(2)}) collective-permute-start(bf16[128,2048]{1,0:T(8,128)(2,1)S(1)} %get-tuple-element.215), channel_id=1, source_target_pairs={{0,1},{1,0},{2,3},{3,2},{4,5},{5,4},{6,7},{7,6},{8,9},{9,8},{10,11... | collective-permute-start | bytes 1572872 | tf_op jit(solution)/shard_map/ppermute | solution.py:30
  65.9 4.8 %collective-permute-start.27 = (f32[2,7424]{1,0:T(2,128)S(1)}, f32[2,7424]{1,0:T(2,128)S(1)}, u32[]{:S(2)}, u32[]{:S(2)}) collective-permute-start(f32[2,7424]{1,0:T(2,128)S(1)} %get-tuple-element.213.refs_0_), channel_id=1, source_target_pairs={{0,4},{4,0},{8,12},{12,8},{16,20},{20,16},{24,28},{28,24},{1,5},{5... | collective-permute-start | bytes 178184 | tf_op jit(solution)/shard_map/ppermute | solution.py:30
  69.8 10.3 %collective-permute-start.32 = (bf16[144,1152]{1,0:T(8,128)(2,1)S(1)}, bf16[144,1152]{1,0:T(8,128)(2,1)S(1)}, u32[]{:S(2)}, u32[]{:S(2)}) collective-permute-start(bf16[144,1152]{1,0:T(8,128)(2,1)S(1)} %get-tuple-element.223), channel_id=1, source_target_pairs={{0,4},{4,0},{8,12},{12,8},{16,20},{20,16},{24,28},{28,24},{1,5},{5... | collective-permute-start | bytes 995336 | tf_op jit(solution)/shard_map/ppermute | solution.py:30
  70.7 9.5 %collective-permute-start.31 = (f32[4,7424]{1,0:T(4,128)S(1)}, f32[4,7424]{1,0:T(4,128)S(1)}, u32[]{:S(2)}, u32[]{:S(2)}) collective-permute-start(f32[4,7424]{1,0:T(4,128)S(1)} %get-tuple-element.221.refs_0_), channel_id=1, source_target_pairs={{0,8},{4,12},{8,0},{12,4},{16,24},{20,28},{24,16},{28,20},{1,9},{5... | collective-permute-start | bytes 356360 | tf_op jit(solution)/shard_map/ppermute | solution.py:30
  75.0 23.7 %collective-permute-start.35 = (bf16[144,2304]{1,0:T(8,128)(2,1)S(1)}, bf16[144,2304]{1,0:T(8,128)(2,1)S(1)}, u32[]{:S(2)}, u32[]{:S(2)}) collective-permute-start(bf16[144,2304]{1,0:T(8,128)(2,1)S(1)} %get-tuple-element.234), channel_id=1, source_target_pairs={{0,8},{4,12},{8,0},{12,4},{16,24},{20,28},{24,16},{28,20},{1,9},{5... | collective-permute-start | bytes 1990664 | tf_op jit(solution)/shard_map/ppermute | solution.py:30
  76.4 7.7 %collective-permute-start.30 = (bf16[128,2304]{1,0:T(8,128)(2,1)S(1)}, bf16[128,2304]{1,0:T(8,128)(2,1)S(1)}, u32[]{:S(2)}, u32[]{:S(2)}) collective-permute-start(bf16[128,2304]{1,0:T(8,128)(2,1)S(1)} %get-tuple-element.220.refs_0_), channel_id=1, source_target_pairs={{0,1},{1,0},{2,3},{3,2},{4,5},{5,4},{6,7},{7,6},{8,9},{9,8},{10,11... | collective-permute-start | bytes 1769480 | tf_op jit(solution)/shard_map/ppermute | solution.py:30
  76.4 13.6 %collective-permute-start.33 = (bf16[144,1152]{1,0:T(8,128)(2,1)S(1)}, bf16[144,1152]{1,0:T(8,128)(2,1)S(1)}, u32[]{:S(2)}, u32[]{:S(2)}) collective-permute-start(bf16[144,1152]{1,0:T(8,128)(2,1)S(1)} %get-tuple-element.232), channel_id=1, source_target_pairs={{0,4},{4,0},{8,12},{12,8},{16,20},{20,16},{24,28},{28,24},{1,5},{5... | collective-permute-start | bytes 995336 | tf_op jit(solution)/shard_map/ppermute | solution.py:30
  80.2 17.4 %collective-permute-start.34 = (bf16[144,1152]{1,0:T(8,128)(2,1)S(1)}, bf16[144,1152]{1,0:T(8,128)(2,1)S(1)}, u32[]{:S(2)}, u32[]{:S(2)}) collective-permute-start(bf16[144,1152]{1,0:T(8,128)(2,1)S(1)} %get-tuple-element.233), channel_id=1, source_target_pairs={{0,16},{4,20},{8,24},{12,28},{16,0},{20,4},{24,8},{28,12},{1,17},{... | collective-permute-start | bytes 995336 | tf_op jit(solution)/shard_map/ppermute | solution.py:30
  80.3 2.1 %copy-start.4 = (bf16[1152,1728]{0,1:T(8,128)(2,1)S(1)}, bf16[1152,1728]{0,1:T(8,128)(2,1)}, u32[]{:S(2)}) copy-start(bf16[1152,1728]{0,1:T(8,128)(2,1)} %param.22) | copy-start | bytes 11943940
  84.1 1.2 %collective-permute-start.36 = (f32[8,768]{1,0:T(8,128)S(1)}, f32[8,768]{1,0:T(8,128)S(1)}, u32[]{:S(2)}, u32[]{:S(2)}) collective-permute-start(f32[8,768]{1,0:T(8,128)S(1)} %get-tuple-element.236), channel_id=1, source_target_pairs={{0,1},{1,0},{2,3},{3,2},{4,5},{5,4},{6,7},{7,6},{8,9},{9,8},{10,11... | collective-permute-start | bytes 73736 | tf_op jit(solution)/shard_map/ppermute | solution.py:30
  85.3 3.7 %collective-permute-start.37 = (f32[8,288]{1,0:T(8,128)S(1)}, f32[8,288]{1,0:T(8,128)S(1)}, u32[]{:S(2)}, u32[]{:S(2)}) collective-permute-start(f32[8,288]{1,0:T(8,128)S(1)} %get-tuple-element.239), channel_id=1, source_target_pairs={{0,2},{1,3},{2,0},{3,1},{4,6},{5,7},{6,4},{7,5},{8,10},{9,11},{10,... | collective-permute-start | bytes 27656 | tf_op jit(solution)/shard_map/ppermute | solution.py:30

commit v8 on v7

--- a/solution.py
+++ b/solution.py
@@ -534,11 +534,14 @@
     send[...] = (stay[...] + other[...].astype(F32)).astype(BF)
 
 
-def last_kernel(near, near_other, far_other, mlp, mlp_other, qkv, out, down, up):
+def last_mlp_kernel(mlp, mlp_other, down, up):
+    for target, start in ((down, 0), (up, down.shape[1])):
+        at = slice(start, start + target.shape[1])
+        target[...] = mlp[:, at] + mlp_other[:, at].astype(F32)
+
+
+def last_qkv_kernel(near, near_other, far_other, qkv, out):
     cols = qkv.shape[1]
-    for source, target, start in ((mlp, down, 0), (mlp, up, down.shape[1])):
-        at = slice(start, start + target.shape[1])
-        target[...] = source[:, at] + mlp_other[:, at].astype(F32)
     total = near[...] + near_other[...].astype(F32) + far_other[...].astype(F32)
     qkv[...] = total[:, :cols]
     out[...] = total[:, cols:]
@@ -955,13 +958,16 @@
         [mine, swap(send, "tensor", 2), cond_cols, labels_all],
     )
     if n_dp == 8:
-        qkv_grad, out_grad, down_grad, up_grad = call(
+        qkv_grad, out_grad = call(
             order,
-            last_kernel,
-            "last_add",
+            last_qkv_kernel,
+            "qkv_add",
             0.02,
-            [((chunk, w), F32) for w in (n_qkv, n_att, hidden, hidden)],
-            [*qkv_grad, *mlp_grad],
+            [((chunk, w), F32) for w in (n_qkv, n_att)],
+            qkv_grad,
+        )
+        down_grad, up_grad = call(
+            order, last_mlp_kernel, "mlp_add", 0.02, [((chunk, hidden), F32)] * 2, mlp_grad
         )
     else:
         grad = halve_all(qkv_grad[0].reshape(n_dp // 2, chunk, -1), [1])

time: 100 us -> 100 us (level)
  waiting for transfers between devices: 26.6 us -> 25.6 us
    ppermute x38, waiting for transfers between devices: 26.6 us -> 25.6 us  [swap(): return lax.ppermute(value, axis, [(i, i ^ flip) for i in range(size)])]
    pallas_call x29 -> x30, Pallas kernels: 34.8 us -> 35.6 us  [call(): pl.pallas_call(whole, out_shape=[jax.ShapeDtypeStruct(s, d) for s, d in [...]
  transfers between devices with their start and end apart: 38 -> 38, of which waited for: 13 -> 13; matrix products, arithmetic and copies ran while one was open for 1% -> 1% of each run, Pallas kernels for 33% -> 34%
where the time goes in v8:
time: 100 us; the launch traced here: 99.9 us
  Pallas kernels  35.6 us (36%)
  starting transfers between devices  32.1 us (32%)
  waiting for transfers between devices  25.6 us (26%)
  between operations  2.96 us (3%)
  local copies, waits for them, and re-layouts  2.95 us (3%)
    pallas_call x30, Pallas kernels, call(): pl.pallas_call(whole, out_shape=[jax.ShapeDtypeStruct(s, d) for s, d in [...  35.6 us
    ppermute x38, starting transfers between devices, swap(): return lax.ppermute(value, axis, [(i, i ^ flip) for i in range(size)])  32.1 us
    ppermute x38, waiting for transfers between devices, swap(): return lax.ppermute(value, axis, [(i, i ^ flip) for i in range(size)])  25.6 us
    unnamed x19, local copies, waits for them, and re-layouts  2.84 us
  transfers between devices with their start and end apart: 38, of which 13 were waited for; matrix products, arithmetic and copies ran while one was open for 1% of the time, Pallas kernels for 34%

profile of v8, /device:TPU:0, one launch (start us, length us, event | category | flops | bytes accessed | tf_op | source)
XLA Modules:
  0.0 99.9 jit_solution(8206471279959137763)
XLA Ops:
  1.3 0.2 copy-done
  1.7 3.0 %collective-permute-start.1 = (bf16[1,288]{1,0:T(2,128)(2,1)S(1)}, bf16[1,288]{1,0:T(2,128)(2,1)S(1)}, u32[]{:S(2)}, u32[]{:S(2)}) collective-permute-start(bf16[1,288]{1,0:T(2,128)(2,1)S(1)} %copy.31.refs_0_), channel_id=1, source_target_pairs={{0,2},{1,3},{2,0},{3,1},{4,6},{5,7},{6,4},{7,5},{8,10},{9,11},{10,... | collective-permute-start | bytes 1736 | tf_op jit(solution)/shard_map/ppermute | solution.py:30
  4.7 0.8 add_add_fusion
  6.3 0.6 collective-permute-start.2
  6.9 0.8 collective-permute-done.2.refs_3_
  7.7 0.5 collective-permute-start.6
  8.4 0.4 collective-permute-start.5
  8.7 0.4 copy-done.3
  9.1 1.2 %modulation.1 = (f32[1,1152]{1,0:T(1,128)S(1)}, f32[1,1728]{1,0:T(1,128)S(1)}, f32[8,128]{1,0:T(8,128)S(1)}) custom-call(bf16[1,288]{1,0:T(2,128)(2,1)S(1)} %copy.31.refs_0_, bf16[1,288]{1,0:T(2,128)(2,1)S(1)} %collective-permute-done.refs_1_, bf16[1,288]{1,0:T(2,128)(2,1)S(1)} %collective-permute-done.1.refs_2_, ...), custom_call_target="tpu_custom_call" | custom-call | flops 1100000000 | bytes 1024 | tf_op jit(solution)/shard_map/modulation/pallas_call | solution.py:49
  10.3 1.1 %collective-permute-start.4 = (f32[1,1728]{1,0:T(1,128)S(1)}, f32[1,1728]{1,0:T(1,128)S(1)}, u32[]{:S(2)}, u32[]{:S(2)}) collective-permute-start(f32[1,1728]{1,0:T(1,128)S(1)} %get-tuple-element.142.refs_3_), channel_id=1, source_target_pairs={{0,2},{1,3},{2,0},{3,1},{4,6},{5,7},{6,4},{7,5},{8,10},{9,11},{10,... | collective-permute-start | bytes 20744 | tf_op jit(solution)/shard_map/ppermute | solution.py:30
  11.5 0.3 start.1
  11.8 2.2 %collective-permute-done.4.refs_5_ = f32[1,1728]{1,0:T(1,128)S(1)} collective-permute-done((f32[1,1728]{1,0:T(1,128)S(1)}, f32[1,1728]{1,0:T(1,128)S(1)}, u32[]{:S(2)}, u32[]{:S(2)}) %collective-permute-start.4) | collective-permute-done | bytes 6944 | tf_op jit(solution)/shard_map/ppermute | solution.py:30
  14.1 1.1 %collective-permute-done.8.refs_6_ = f32[1,1728]{1,0:T(1,128)S(1)} collective-permute-done((f32[1,1728]{1,0:T(1,128)S(1)}, f32[1,1728]{1,0:T(1,128)S(1)}, u32[]{:S(2)}, u32[]{:S(2)}) %collective-permute-start.8) | collective-permute-done | bytes 6944 | tf_op jit(solution)/shard_map/ppermute | solution.py:30
  15.3 0.2 collective-permute-start.11
  15.4 0.3 collective-permute-start.10
  16.4 2.6 %attention.1 = (bf16[128,1152]{1,0:T(8,128)(2,1)S(1)}, f32[8,1152]{1,0:T(8,128)S(1)}, bf16[128,1152]{1,0:T(8,128)(2,1)S(1)}, bf16[128,864]{1,0:T(8,128)(2,1)S(1)...) custom-call(s32[1]{0:T(128)S(6)} %copy.32.refs_0_, ...), custom_call_target="tpu_custom_call" | custom-call | flops 4400000000 | bytes 1024 | tf_op jit(solution)/shard_map/attention/pallas_call | solution.py:49
  19.1 1.1 %collective-permute-start.9 = (bf16[128,1152]{1,0:T(8,128)(2,1)S(1)}, bf16[128,1152]{1,0:T(8,128)(2,1)S(1)}, u32[]{:S(2)}, u32[]{:S(2)}) collective-permute-start(bf16[128,1152]{1,0:T(8,128)(2,1)S(1)} %get-tuple-element.147.refs_1_), channel_id=1, source_target_pairs={{0,2},{1,3},{2,0},{3,1},{4,6},{5,7},{6,4},{7,5},{8,10},{9,11},{10,... | collective-permute-start | bytes 884744 | tf_op jit(solution)/shard_map/ppermute | solution.py:30
  20.2 1.5 %collective-permute-start.17 = (bf16[128,1152]{1,0:T(8,128)(2,1)S(1)}, bf16[128,1152]{1,0:T(8,128)(2,1)S(1)}, u32[]{:S(2)}, u32[]{:S(2)}) collective-permute-start(bf16[128,1152]{1,0:T(8,128)(2,1)S(1)} %get-tuple-element.150.refs_0_.refs_2_.refs_7_), channel_id=1, source_target_pairs={{0,4},{4,0},{8,12},{12,8},{16,20},{20,16},{24,28},{28,24},{1,5},{5... | collective-permute-start | bytes 884744 | tf_op jit(solution)/shard_map/ppermute | solution.py:30
  21.7 2.6 %collective-permute-start.13 = (bf16[128,1152]{1,0:T(8,128)(2,1)S(1)}, bf16[128,1152]{1,0:T(8,128)(2,1)S(1)}, u32[]{:S(2)}, u32[]{:S(2)}) collective-permute-start(bf16[128,1152]{1,0:T(8,128)(2,1)S(1)} %get-tuple-element.150.refs_0_.refs_2_.refs_7_), channel_id=1, source_target_pairs={{0,16},{4,20},{8,24},{12,28},{16,0},{20,4},{24,8},{28,12},{1,17},{... | collective-permute-start | bytes 884744 | tf_op jit(solution)/shard_map/ppermute | solution.py:30
  24.3 1.4 %early_back.1 = (f32[128,1152]{1,0:T(8,128)S(1)}, f32[128,1152]{1,0:T(8,128)S(1)}, bf16[128,1280]{1,0:T(8,128)(2,1)S(1)}, bf16[128,640]{1,0:T(8,128)(2,1)S(1)}, ...) custom-call(bf16[128,1152]{1,0:T(8,128)(2,1)S(1)} %get-tuple-element.150.refs_0_.refs_2_.refs_7_, ...), custom_call_target="tpu_custom_call" | custom-call | flops 2200000000 | bytes 1024 | tf_op jit(solution)/shard_map/early_back/pallas_call | solution.py:49
  25.7 1.6 %collective-permute-start.15 = (bf16[128,1280]{1,0:T(8,128)(2,1)S(1)}, bf16[128,1280]{1,0:T(8,128)(2,1)S(1)}, u32[]{:S(2)}, u32[]{:S(2)}) collective-permute-start(bf16[128,1280]{1,0:T(8,128)(2,1)S(1)} %get-tuple-element.174.refs_4_.refs_0_), channel_id=1, source_target_pairs={{0,8},{4,12},{8,0},{12,4},{16,24},{20,28},{24,16},{28,20},{1,9},{5... | collective-permute-start | bytes 983048 | tf_op jit(solution)/shard_map/ppermute | solution.py:30
  27.3 0.9 collective-permute-done.9.refs_2_
  28.2 3.1 %mlp.1 = (bf16[128,1152]{1,0:T(8,128)(2,1)S(1)}, bf16[128,2304]{1,0:T(8,128)(2,1)S(1)}, bf16[128,1152]{1,0:T(8,128)(2,1)S(1)}, bf16[128,1152]{1,0:T(8,128)(2,1)S...) custom-call(bf16[128,1152]{1,0:T(8,128)(2,1)S(1)} %get-tuple-element, ...), custom_call_target="tpu_custom_call" | custom-call | flops 3300000000 | bytes 1024 | tf_op jit(solution)/shard_map/mlp/pallas_call | solution.py:49
  31.3 1.1 %collective-permute-start.12 = (bf16[128,1152]{1,0:T(8,128)(2,1)S(1)}, bf16[128,1152]{1,0:T(8,128)(2,1)S(1)}, u32[]{:S(2)}, u32[]{:S(2)}) collective-permute-start(bf16[128,1152]{1,0:T(8,128)(2,1)S(1)} %get-tuple-element.159.refs_1_), channel_id=1, source_target_pairs={{0,2},{1,3},{2,0},{3,1},{4,6},{5,7},{6,4},{7,5},{8,10},{9,11},{10,... | collective-permute-start | bytes 884744 | tf_op jit(solution)/shard_map/ppermute | solution.py:30
  32.4 2.6 %collective-permute-start.19 = (bf16[128,1152]{1,0:T(8,128)(2,1)S(1)}, bf16[128,1152]{1,0:T(8,128)(2,1)S(1)}, u32[]{:S(2)}, u32[]{:S(2)}) collective-permute-start(bf16[128,1152]{1,0:T(8,128)(2,1)S(1)} %get-tuple-element.177.refs_0_.refs_4_), channel_id=1, source_target_pairs={{0,16},{4,20},{8,24},{12,28},{16,0},{20,4},{24,8},{28,12},{1,17},{... | collective-permute-start | bytes 884744 | tf_op jit(solution)/shard_map/ppermute | solution.py:30
  35.0 1.5 %collective-permute-start.18 = (bf16[128,1152]{1,0:T(8,128)(2,1)S(1)}, bf16[128,1152]{1,0:T(8,128)(2,1)S(1)}, u32[]{:S(2)}, u32[]{:S(2)}) collective-permute-start(bf16[128,1152]{1,0:T(8,128)(2,1)S(1)} %get-tuple-element.177.refs_0_.refs_4_), channel_id=1, source_target_pairs={{0,4},{4,0},{8,12},{12,8},{16,20},{20,16},{24,28},{28,24},{1,5},{5... | collective-permute-start | bytes 884744 | tf_op jit(solution)/shard_map/ppermute | solution.py:30
  36.5 1.7 %mlp_tail.1 = (bf16[128,1152]{1,0:T(8,128)(2,1)S(1)}, f32[8,128]{1,0:T(8,128)S(1)}) custom-call(bf16[128,2304]{1,0:T(8,128)(2,1)S(1)} %get-tuple-element.166.refs_0_.refs_10_, bf16[1152,1152]{1,0:T(8,128)(2,1)S(1)} %copy-done.1, bf16[1152,1152]{1,0:T(8,128)(2,1)S(1)} %collective-permute-done.11.refs_2_, f32[8,128]{1,0:T(8,128)S(1)} %get-tuple-element.167.refs_3_), custom_call_target="tpu_custom_call" | custom-call | flops 1100000000 | bytes 1024 | tf_op jit(solution)/shard_map/mlp_tail/pallas_call | solution.py:49
  38.2 1.2 %collective-permute-done.13.refs_16_.refs_9_.refs_2_ = bf16[128,1152]{1,0:T(8,128)(2,1)S(1)} collective-permute-done((bf16[128,1152]{1,0:T(8,128)(2,1)S(1)}, bf16[128,1152]{1,0:T(8,128)(2,1)S(1)}, u32[]{:S(2)}, u32[]{:S(2)}) %collective-permute-start.13) | collective-permute-done | bytes 294944 | tf_op jit(solution)/shard_map/ppermute | solution.py:30
  39.5 0.5 collective-permute-start.21
  40.0 1.7 %collective-permute-done.15.refs_3_.refs_2_ = bf16[128,1280]{1,0:T(8,128)(2,1)S(1)} collective-permute-done((bf16[128,1280]{1,0:T(8,128)(2,1)S(1)}, bf16[128,1280]{1,0:T(8,128)(2,1)S(1)}, u32[]{:S(2)}, u32[]{:S(2)}) %collective-permute-start.15) | collective-permute-done | bytes 327712 | tf_op jit(solution)/shard_map/ppermute | solution.py:30
  41.7 1.0 collective-permute-start.16
  42.7 3.6 %attention_back.1 = (bf16[128,1152]{1,0:T(8,128)(2,1)S(1)}, f32[128,1152]{1,0:T(8,128)S(1)}, bf16[128,1152]{1,0:T(8,128)(2,1)S(1)}, bf16[128,1792]{1,0:T(8,128)(...) custom-call(s32[1]{0:T(128)S(6)} %copy.32.refs_0_, bf16[128,1152]{1,0:T(8,128)(2,1)S(1)} %get-tuple-element.159.refs_1_, ...), custom_call_target="tpu_custom_call" | custom-call | flops 5500000256 | bytes 1024 | tf_op jit(solution)/shard_map/attention_back/pallas_call | solution.py:49
  46.3 1.1 %collective-permute-start.14 = (bf16[128,1152]{1,0:T(8,128)(2,1)S(1)}, bf16[128,1152]{1,0:T(8,128)(2,1)S(1)}, u32[]{:S(2)}, u32[]{:S(2)}) collective-permute-start(bf16[128,1152]{1,0:T(8,128)(2,1)S(1)} %get-tuple-element.169.refs_1_), channel_id=1, source_target_pairs={{0,2},{1,3},{2,0},{3,1},{4,6},{5,7},{6,4},{7,5},{8,10},{9,11},{10,... | collective-permute-start | bytes 884744 | tf_op jit(solution)/shard_map/ppermute | solution.py:30
  47.5 0.2 pack_back.1
  47.7 2.9 %collective-permute-done.16.refs_3_ = bf16[128,1152]{1,0:T(8,128)(2,1)S(1)} collective-permute-done((bf16[128,1152]{1,0:T(8,128)(2,1)S(1)}, bf16[128,1152]{1,0:T(8,128)(2,1)S(1)}, u32[]{:S(2)}, u32[]{:S(2)}) %collective-permute-start.16) | collective-permute-done | bytes 294944 | tf_op jit(solution)/shard_map/ppermute | solution.py:30
  50.6 0.3 output.1
  50.9 0.6 collective-permute-start.20
  51.5 3.6 %remake_near.1 = (f32[288,1152]{1,0:T(8,128)S(1)}, f32[288,1152]{1,0:T(8,128)S(1)}, f32[8,128]{1,0:T(8,128)S(1)}) custom-call(bf16[288,1152]{1,0:T(8,128)(2,1)S(1)} %get-tuple-element.187.refs_0_, bf16[1152,1152]{1,0:T(8,128)(2,1)S(1)} %copy-done.2, bf16[1152,1152]{1,0:T(8,128)(2,1)S(1)} %copy-done.1, ...), custom_call_target="tpu_custom_call" | custom-call | flops 1100000000 | bytes 1024 | tf_op jit(solution)/shard_map/remake_near/pallas_call | solution.py:49
  55.1 0.6 input_back.1
  55.8 3.2 %remake_core0.1 = (f32[288,1152]{1,0:T(8,128)S(1)}, f32[288,1152]{1,0:T(8,128)S(1)}, f32[8,128]{1,0:T(8,128)S(1)}) custom-call(bf16[288,1152]{1,0:T(8,128)(2,1)S(1)} %get-tuple-element.187.refs_0_, bf16[1152,1152]{1,0:T(8,128)(2,1)S(1)} %copy-done.2, bf16[1152,1152]{1,0:T(8,128)(2,1)S(1)} %copy-done.1, ...), custom_call_target="tpu_custom_call" | custom-call | flops 2200000000 | bytes 1024 | tf_op jit(solution)/shard_map/remake_core0/pallas_call | solution.py:49
  59.3 3.4 %collective-permute-start.25 = (f32[1,7424]{1,0:T(1,128)S(1)}, f32[1,7424]{1,0:T(1,128)S(1)}, u32[]{:S(2)}, u32[]{:S(2)}) collective-permute-start(f32[1,7424]{1,0:T(1,128)S(1)} %get-tuple-element.208.refs_0_), channel_id=1, source_target_pairs={{0,16},{4,20},{8,24},{12,28},{16,0},{20,4},{24,8},{28,12},{1,17},{... | collective-permute-start | bytes 89096 | tf_op jit(solution)/shard_map/ppermute | solution.py:30
  62.6 0.2 collective-permute-start.24
  62.9 2.3 %remake_yf.1 = (f32[288,1152]{1,0:T(8,128)S(1)}, f32[288,1152]{1,0:T(8,128)S(1)}, f32[8,128]{1,0:T(8,128)S(1)}) custom-call(bf16[288,1152]{1,0:T(8,128)(2,1)S(1)} %get-tuple-element.187.refs_0_, bf16[1152,1152]{1,0:T(8,128)(2,1)S(1)} %copy-done.2, bf16[1152,1152]{1,0:T(8,128)(2,1)S(1)} %copy-done.1, ...), custom_call_target="tpu_custom_call" | custom-call | flops 22000000 | bytes 1024 | tf_op jit(solution)/shard_map/remake_yf/pallas_call | solution.py:49
  65.1 0.1 forward3.1
  65.3 0.4 collective-permute-start.28
  65.7 0.2 collective-permute-start.29
  65.9 0.9 collective-permute-start.27
  66.8 1.6 %collective-permute-done.29.refs_7_ = bf16[128,2048]{1,0:T(8,128)(2,1)S(1)} collective-permute-done((bf16[128,2048]{1,0:T(8,128)(2,1)S(1)}, bf16[128,2048]{1,0:T(8,128)(2,1)S(1)}, u32[]{:S(2)}, u32[]{:S(2)}) %collective-permute-start.29) | collective-permute-done | bytes 524320 | tf_op jit(solution)/shard_map/ppermute | solution.py:30
  68.4 1.4 %qkv_grad.1 = (f32[144,1152]{1,0:T(8,128)S(1)}, bf16[144,1152]{1,0:T(8,128)(2,1)S(1)}, f32[144,1152]{1,0:T(8,128)S(1)}, bf16[144,1152]{1,0:T(8,128)(2,1)S(1)}, f32[8,128]{1,0:T(8,128)S(1)}) custom-call(bf16[128,1280]{1,0:T(8,128)(2,1)S(1)} %get-tuple-element.174.refs_4_.refs_0_, bf16[128,640]{1,0:T(8,128)(2,1)S(1)} %get-tuple-element.211.refs_5_.refs_1_, ...), custom_call_target="tpu_custom_call" | custom-call | flops 22000000 | bytes 1024 | tf_op jit(solution)/shard_map/qkv_grad/pallas_call | solution.py:49
  69.8 0.9 collective-permute-start.32
  70.7 0.7 collective-permute-start.31
  71.4 3.5 %remake_core1.1 = (f32[144,2304]{1,0:T(8,128)S(1)}, bf16[144,2304]{1,0:T(8,128)(2,1)S(1)}, f32[8,128]{1,0:T(8,128)S(1)}) custom-call(bf16[288,1152]{1,0:T(8,128)(2,1)S(1)} %get-tuple-element.187.refs_0_, bf16[1152,1152]{1,0:T(8,128)(2,1)S(1)} %copy-done.2, bf16[1152,1152]{1,0:T(8,128)(2,1)S(1)} %copy-done.1, ...), custom_call_target="tpu_custom_call" | custom-call | flops 22000000 | bytes 1024 | tf_op jit(solution)/shard_map/remake_core1/pallas_call | solution.py:49
  75.0 1.4 %collective-permute-start.37 = (bf16[144,2304]{1,0:T(8,128)(2,1)S(1)}, bf16[144,2304]{1,0:T(8,128)(2,1)S(1)}, u32[]{:S(2)}, u32[]{:S(2)}) collective-permute-start(bf16[144,2304]{1,0:T(8,128)(2,1)S(1)} %get-tuple-element.246), channel_id=1, source_target_pairs={{0,8},{4,12},{8,0},{12,4},{16,24},{20,28},{24,16},{28,20},{1,9},{5... | collective-permute-start | bytes 1990664 | tf_op jit(solution)/shard_map/ppermute | solution.py:30
  76.4 1.2 %collective-permute-start.33 = (bf16[144,1152]{1,0:T(8,128)(2,1)S(1)}, bf16[144,1152]{1,0:T(8,128)(2,1)S(1)}, u32[]{:S(2)}, u32[]{:S(2)}) collective-permute-start(bf16[144,1152]{1,0:T(8,128)(2,1)S(1)} %get-tuple-element.233), channel_id=1, source_target_pairs={{0,4},{4,0},{8,12},{12,8},{16,20},{20,16},{24,28},{28,24},{1,5},{5... | collective-permute-start | bytes 995336 | tf_op jit(solution)/shard_map/ppermute | solution.py:30
  77.6 2.5 %collective-permute-done.32.refs_1_ = bf16[144,1152]{1,0:T(8,128)(2,1)S(1)} collective-permute-done((bf16[144,1152]{1,0:T(8,128)(2,1)S(1)}, bf16[144,1152]{1,0:T(8,128)(2,1)S(1)}, u32[]{:S(2)}, u32[]{:S(2)}) %collective-permute-start.32) | collective-permute-done | bytes 331808 | tf_op jit(solution)/shard_map/ppermute | solution.py:30
  80.3 2.1 %copy-done.4 = bf16[1152,1728]{0,1:T(8,128)(2,1)S(1)} copy-done((bf16[1152,1728]{0,1:T(8,128)(2,1)S(1)}, bf16[1152,1728]{0,1:T(8,128)(2,1)}, u32[]{:S(2)}) %copy-start.4) | copy-done | bytes 3981336
  82.4 1.6 %gathered.1 = (f32[144,1728]{1,0:T(8,128)}, f32[1728]{0:T(1024)}, f32[576]{0:T(1024)}, f32[1152]{0:T(1024)}, f32[1152]{0:T(1024)}, /*index=5*/f32[1152]{0:T(1024...) custom-call(bf16[1728,1152]{1,0:T(8,128)(2,1)S(1)} %bitcast.13, ...), custom_call_target="tpu_custom_call" | custom-call | flops 5500000256 | bytes 1024 | tf_op jit(solution)/shard_map/gathered/pallas_call | solution.py:49
  84.1 1.1 %join.1 = (bf16[256,1152]{1,0:T(8,128)(2,1)}, bf16[256,1152]{1,0:T(8,128)(2,1)}, f32[8,128]{1,0:T(8,128)S(1)}) custom-call(bf16[128,2304]{1,0:T(8,128)(2,1)S(1)} %get-tuple-element.221.refs_0_, bf16[128,2304]{1,0:T(8,128)(2,1)S(1)} %collective-permute-done.30.refs_1_, f32[8,128]{1,0:T(8,128)S(1)} %get-tuple-element.229.refs_2_), custom_call_target="tpu_custom_call" | custom-call | flops 22000000 | bytes 1024 | tf_op jit(solution)/shard_map/join/pallas_call | solution.py:49
  85.3 1.0 %collective-permute-start.36 = (f32[8,288]{1,0:T(8,128)S(1)}, f32[8,288]{1,0:T(8,128)S(1)}, u32[]{:S(2)}, u32[]{:S(2)}) collective-permute-start(f32[8,288]{1,0:T(8,128)S(1)} %get-tuple-element.239), channel_id=1, source_target_pairs={{0,2},{1,3},{2,0},{3,1},{4,6},{5,7},{6,4},{7,5},{8,10},{9,11},{10,... | collective-permute-start | bytes 27656 | tf_op jit(solution)/shard_map/ppermute | solution.py:30
  86.3 2.7 %collective-permute-done.36.refs_1_ = f32[8,288]{1,0:T(8,128)S(1)} collective-permute-done((f32[8,288]{1,0:T(8,128)S(1)}, f32[8,288]{1,0:T(8,128)S(1)}, u32[]{:S(2)}, u32[]{:S(2)}) %collective-permute-start.36) | collective-permute-done | bytes 9248 | tf_op jit(solution)/shard_map/ppermute | solution.py:30
  89.0 1.0 %table.1 = (f32[288,101]{1,0:T(8,128)}, f32[8,128]{1,0:T(8,128)S(1)}) custom-call(f32[8,288]{1,0:T(8,128)S(1)} %get-tuple-element.238.refs_0_, f32[8,288]{1,0:T(8,128)S(1)} %collective-permute-done.36.refs_1_, f32[8,288]{1,0:T(8,128)S(1)} %get-tuple-element.240.refs_2_, f32[8,128]{1,0:T(8,128)S(1)} %get-tuple-element.241.refs_3_, ...), custom_call_target="tpu_custom_call" | custom-call | flops 22000000 | bytes 1024 | tf_op jit(solution)/shard_map/table/pallas_call | solution.py:49
  90.0 7.6 %collective-permute-done.34.refs_2_ = bf16[144,1152]{1,0:T(8,128)(2,1)S(1)} collective-permute-done((bf16[144,1152]{1,0:T(8,128)(2,1)S(1)}, bf16[144,1152]{1,0:T(8,128)(2,1)S(1)}, u32[]{:S(2)}, u32[]{:S(2)}) %collective-permute-start.34) | collective-permute-done | bytes 331808 | tf_op jit(solution)/shard_map/ppermute | solution.py:30
  97.6 1.0 %qkv_add.1 = (f32[144,864]{1,0:T(8,128)}, f32[144,288]{1,0:T(8,128)}, f32[8,128]{1,0:T(8,128)S(1)}) custom-call(f32[144,1152]{1,0:T(8,128)S(1)} %get-tuple-element.232.refs_0_, bf16[144,1152]{1,0:T(8,128)(2,1)S(1)} %collective-permute-done.33.refs_1_, bf16[144,1152]{1,0:T(8,128)(2,1)S(1)} %collective-permute-done.34.refs_2_, ...), custom_call_target="tpu_custom_call" | custom-call | flops 22000000 | bytes 1024 | tf_op jit(solution)/shard_map/qkv_add/pallas_call | solution.py:49
  98.7 1.2 %mlp_add.1 = (f32[144,1152]{1,0:T(8,128)}, f32[144,1152]{1,0:T(8,128)}, f32[8,128]{1,0:T(8,128)}) custom-call(f32[144,2304]{1,0:T(8,128)S(1)} %get-tuple-element.220.refs_0_, bf16[144,2304]{1,0:T(8,128)(2,1)S(1)} %collective-permute-done.37.refs_1_, f32[8,128]{1,0:T(8,128)S(1)} %get-tuple-element.247.refs_2_), custom_call_target="tpu_custom_call" | custom-call | flops 22000000 | bytes 1024 | tf_op jit(solution)/shard_map/mlp_add/pallas_call | solution.py:49
  (64 shorter events, 1.5 us)
Async XLA Ops:
  0.6 0.9 copy-start
  1.7 4.6 %collective-permute-start.1 = (bf16[1,288]{1,0:T(2,128)(2,1)S(1)}, bf16[1,288]{1,0:T(2,128)(2,1)S(1)}, u32[]{:S(2)}, u32[]{:S(2)}) collective-permute-start(bf16[1,288]{1,0:T(2,128)(2,1)S(1)} %copy.31.refs_0_), channel_id=1, source_target_pairs={{0,2},{1,3},{2,0},{3,1},{4,6},{5,7},{6,4},{7,5},{8,10},{9,11},{10,... | collective-permute-start | bytes 1736 | tf_op jit(solution)/shard_map/ppermute | solution.py:30
  4.7 2.2 %collective-permute-start = (bf16[1,288]{1,0:T(2,128)(2,1)S(1)}, bf16[1,288]{1,0:T(2,128)(2,1)S(1)}, u32[]{:S(2)}, u32[]{:S(2)}) collective-permute-start(bf16[1,288]{1,0:T(2,128)(2,1)S(1)} %copy.31.refs_0_), channel_id=1, source_target_pairs={{0,1},{1,0},{2,3},{3,2},{4,5},{5,4},{6,7},{7,6},{8,9},{9,8},{10,11... | collective-permute-start | bytes 1736 | tf_op jit(solution)/shard_map/ppermute | solution.py:30
  6.2 1.6 %copy-start.5 = (bf16[1152,864]{0,1:T(8,128)(2,1)S(1)}, bf16[1152,864]{0,1:T(8,128)(2,1)}, u32[]{:S(2)}) copy-start(bf16[1152,864]{0,1:T(8,128)(2,1)} %param.24) | copy-start | bytes 5971972
  6.2 2.1 %copy-start.6 = (bf16[1152,288]{0,1:T(8,128)(2,1)S(1)}, bf16[1152,288]{0,1:T(8,128)(2,1)}, u32[]{:S(2)}) copy-start(bf16[1152,288]{0,1:T(8,128)(2,1)} %param.26) | copy-start | bytes 1990660
  6.2 2.9 %copy-start.3 = (bf16[1152,1728]{0,1:T(8,128)(2,1)S(1)}, bf16[1152,1728]{0,1:T(8,128)(2,1)}, u32[]{:S(2)}) copy-start(bf16[1152,1728]{0,1:T(8,128)(2,1)} %param.22) | copy-start | bytes 11943940
  6.3 1.4 %collective-permute-start.2 = (bf16[1,288]{1,0:T(2,128)(2,1)S(1)}, bf16[1,288]{1,0:T(2,128)(2,1)S(1)}, u32[]{:S(2)}, u32[]{:S(2)}) collective-permute-start(bf16[1,288]{1,0:T(2,128)(2,1)S(1)} %collective-permute-done.1.refs_2_), channel_id=1, source_target_pairs={{0,1},{1,0},{2,3},{3,2},{4,5},{5,4},{6,7},{7,6},{8,9},{9,8},{10,11... | collective-permute-start | bytes 1736 | tf_op jit(solution)/shard_map/ppermute | solution.py:30
  7.7 6.3 %collective-permute-start.6 = (bf16[864,1152]{1,0:T(8,128)(2,1)S(1)}, bf16[864,1152]{1,0:T(8,128)(2,1)S(1)}, u32[]{:S(2)}, u32[]{:S(2)}) collective-permute-start(bf16[864,1152]{1,0:T(8,128)(2,1)S(1)} %bitcast.14), channel_id=1, source_target_pairs={{0,1},{1,0},{2,3},{3,2},{4,5},{5,4},{6,7},{7,6},{8,9},{9,8},{10,11... | collective-permute-start | bytes 5971976 | tf_op jit(solution)/shard_map/ppermute | solution.py:30
  8.2 5.8 %collective-permute-start.7 = (bf16[288,1152]{1,0:T(8,128)(2,1)S(1)}, bf16[288,1152]{1,0:T(8,128)(2,1)S(1)}, u32[]{:S(2)}, u32[]{:S(2)}) collective-permute-start(bf16[288,1152]{1,0:T(8,128)(2,1)S(1)} %bitcast.17), channel_id=1, source_target_pairs={{0,1},{1,0},{2,3},{3,2},{4,5},{5,4},{6,7},{7,6},{8,9},{9,8},{10,11... | collective-permute-start | bytes 1990664 | tf_op jit(solution)/shard_map/ppermute | solution.py:30
  8.4 5.7 %collective-permute-start.5 = (f32[1,6528]{1,0:T(1,128)S(1)}, f32[1,6528]{1,0:T(1,128)S(1)}, u32[]{:S(2)}, u32[]{:S(2)}) collective-permute-start(f32[1,6528]{1,0:T(1,128)S(1)} %reshape.43.refs_1_.refs_6_.refs_9_.refs_4_.refs_3_), channel_id=1, source_target_pairs={{0,1},{1,0},{2,3},{3,2},{4,5},{5,4},{6,7},{7,6},{8,9},{9,8},{10,11... | collective-permute-start | bytes 78344 | tf_op jit(solution)/shard_map/ppermute | solution.py:30
  9.1 2.4 %copy-start.7 = (bf16[1,16,16,1152]{3,2,1,0:T(8,128)(2,1)S(1)}, bf16[1,16,16,1152]{3,2,1,0:T(8,128)(2,1)}, u32[]{:S(2)}) copy-start(bf16[1,16,16,1152]{3,2,1,0:T(8,128)(2,1)} %param.17) | copy-start | bytes 1769476
  9.1 2.4 %copy-start.8 = (bf16[1,16,16,1152]{3,2,1,0:T(8,128)(2,1)S(1)}, bf16[1,16,16,1152]{3,2,1,0:T(8,128)(2,1)}, u32[]{:S(2)}) copy-start(bf16[1,16,16,1152]{3,2,1,0:T(8,128)(2,1)} %param.32) | copy-start | bytes 1769476
  9.1 6.3 %copy-start.2 = (bf16[1152,1152]{1,0:T(8,128)(2,1)S(1)}, bf16[1152,1152]{1,0:T(8,128)(2,1)}, u32[]{:S(2)}) copy-start(bf16[1152,1152]{1,0:T(8,128)(2,1)} %refs_1_.11) | copy-start | bytes 7962628
  10.3 3.7 %collective-permute-start.4 = (f32[1,1728]{1,0:T(1,128)S(1)}, f32[1,1728]{1,0:T(1,128)S(1)}, u32[]{:S(2)}, u32[]{:S(2)}) collective-permute-start(f32[1,1728]{1,0:T(1,128)S(1)} %get-tuple-element.142.refs_3_), channel_id=1, source_target_pairs={{0,2},{1,3},{2,0},{3,1},{4,6},{5,7},{6,4},{7,5},{8,10},{9,11},{10,... | collective-permute-start | bytes 20744 | tf_op jit(solution)/shard_map/ppermute | solution.py:30
  11.4 2.7 %collective-permute-start.3 = (f32[1,1728]{1,0:T(1,128)S(1)}, f32[1,1728]{1,0:T(1,128)S(1)}, u32[]{:S(2)}, u32[]{:S(2)}) collective-permute-start(f32[1,1728]{1,0:T(1,128)S(1)} %get-tuple-element.142.refs_3_), channel_id=1, source_target_pairs={{0,1},{1,0},{2,3},{3,2},{4,5},{5,4},{6,7},{7,6},{8,9},{9,8},{10,11... | collective-permute-start | bytes 20744 | tf_op jit(solution)/shard_map/ppermute | solution.py:30
  11.5 3.8 %copy-start.1 = (bf16[1152,1152]{1,0:T(8,128)(2,1)S(1)}, bf16[1152,1152]{1,0:T(8,128)(2,1)}, u32[]{:S(2)}) copy-start(bf16[1152,1152]{1,0:T(8,128)(2,1)} %refs_2_.7) | copy-start | bytes 7962628
  14.0 1.2 %collective-permute-start.8 = (f32[1,1728]{1,0:T(1,128)S(1)}, f32[1,1728]{1,0:T(1,128)S(1)}, u32[]{:S(2)}, u32[]{:S(2)}) collective-permute-start(f32[1,1728]{1,0:T(1,128)S(1)} %collective-permute-done.4.refs_5_), channel_id=1, source_target_pairs={{0,1},{1,0},{2,3},{3,2},{4,5},{5,4},{6,7},{7,6},{8,9},{9,8},{10,11... | collective-permute-start | bytes 20744 | tf_op jit(solution)/shard_map/ppermute | solution.py:30
  15.3 9.0 %collective-permute-start.11 = (bf16[1152,1152]{1,0:T(8,128)(2,1)S(1)}, bf16[1152,1152]{1,0:T(8,128)(2,1)S(1)}, u32[]{:S(2)}, u32[]{:S(2)}) collective-permute-start(bf16[1152,1152]{1,0:T(8,128)(2,1)S(1)} %copy-done.1), channel_id=1, source_target_pairs={{0,1},{1,0},{2,3},{3,2},{4,5},{5,4},{6,7},{7,6},{8,9},{9,8},{10,11... | collective-permute-start | bytes 7962632 | tf_op jit(solution)/shard_map/ppermute | solution.py:30
  15.4 12.8 %collective-permute-start.10 = (bf16[1152,1152]{1,0:T(8,128)(2,1)S(1)}, bf16[1152,1152]{1,0:T(8,128)(2,1)S(1)}, u32[]{:S(2)}, u32[]{:S(2)}) collective-permute-start(bf16[1152,1152]{1,0:T(8,128)(2,1)S(1)} %copy-done.2), channel_id=1, source_target_pairs={{0,1},{1,0},{2,3},{3,2},{4,5},{5,4},{6,7},{7,6},{8,9},{9,8},{10,11... | collective-permute-start | bytes 7962632 | tf_op jit(solution)/shard_map/ppermute | solution.py:30
  19.1 9.1 %collective-permute-start.9 = (bf16[128,1152]{1,0:T(8,128)(2,1)S(1)}, bf16[128,1152]{1,0:T(8,128)(2,1)S(1)}, u32[]{:S(2)}, u32[]{:S(2)}) collective-permute-start(bf16[128,1152]{1,0:T(8,128)(2,1)S(1)} %get-tuple-element.147.refs_1_), channel_id=1, source_target_pairs={{0,2},{1,3},{2,0},{3,1},{4,6},{5,7},{6,4},{7,5},{8,10},{9,11},{10,... | collective-permute-start | bytes 884744 | tf_op jit(solution)/shard_map/ppermute | solution.py:30
  20.2 14.8 %collective-permute-start.17 = (bf16[128,1152]{1,0:T(8,128)(2,1)S(1)}, bf16[128,1152]{1,0:T(8,128)(2,1)S(1)}, u32[]{:S(2)}, u32[]{:S(2)}) collective-permute-start(bf16[128,1152]{1,0:T(8,128)(2,1)S(1)} %get-tuple-element.150.refs_0_.refs_2_.refs_7_), channel_id=1, source_target_pairs={{0,4},{4,0},{8,12},{12,8},{16,20},{20,16},{24,28},{28,24},{1,5},{5... | collective-permute-start | bytes 884744 | tf_op jit(solution)/shard_map/ppermute | solution.py:30
  21.7 17.8 %collective-permute-start.13 = (bf16[128,1152]{1,0:T(8,128)(2,1)S(1)}, bf16[128,1152]{1,0:T(8,128)(2,1)S(1)}, u32[]{:S(2)}, u32[]{:S(2)}) collective-permute-start(bf16[128,1152]{1,0:T(8,128)(2,1)S(1)} %get-tuple-element.150.refs_0_.refs_2_.refs_7_), channel_id=1, source_target_pairs={{0,16},{4,20},{8,24},{12,28},{16,0},{20,4},{24,8},{28,12},{1,17},{... | collective-permute-start | bytes 884744 | tf_op jit(solution)/shard_map/ppermute | solution.py:30
  25.7 16.0 %collective-permute-start.15 = (bf16[128,1280]{1,0:T(8,128)(2,1)S(1)}, bf16[128,1280]{1,0:T(8,128)(2,1)S(1)}, u32[]{:S(2)}, u32[]{:S(2)}) collective-permute-start(bf16[128,1280]{1,0:T(8,128)(2,1)S(1)} %get-tuple-element.174.refs_4_.refs_0_), channel_id=1, source_target_pairs={{0,8},{4,12},{8,0},{12,4},{16,24},{20,28},{24,16},{28,20},{1,9},{5... | collective-permute-start | bytes 983048 | tf_op jit(solution)/shard_map/ppermute | solution.py:30
  31.3 11.4 %collective-permute-start.12 = (bf16[128,1152]{1,0:T(8,128)(2,1)S(1)}, bf16[128,1152]{1,0:T(8,128)(2,1)S(1)}, u32[]{:S(2)}, u32[]{:S(2)}) collective-permute-start(bf16[128,1152]{1,0:T(8,128)(2,1)S(1)} %get-tuple-element.159.refs_1_), channel_id=1, source_target_pairs={{0,2},{1,3},{2,0},{3,1},{4,6},{5,7},{6,4},{7,5},{8,10},{9,11},{10,... | collective-permute-start | bytes 884744 | tf_op jit(solution)/shard_map/ppermute | solution.py:30
  32.4 18.5 %collective-permute-start.19 = (bf16[128,1152]{1,0:T(8,128)(2,1)S(1)}, bf16[128,1152]{1,0:T(8,128)(2,1)S(1)}, u32[]{:S(2)}, u32[]{:S(2)}) collective-permute-start(bf16[128,1152]{1,0:T(8,128)(2,1)S(1)} %get-tuple-element.177.refs_0_.refs_4_), channel_id=1, source_target_pairs={{0,16},{4,20},{8,24},{12,28},{16,0},{20,4},{24,8},{28,12},{1,17},{... | collective-permute-start | bytes 884744 | tf_op jit(solution)/shard_map/ppermute | solution.py:30
  35.0 12.3 %collective-permute-start.18 = (bf16[128,1152]{1,0:T(8,128)(2,1)S(1)}, bf16[128,1152]{1,0:T(8,128)(2,1)S(1)}, u32[]{:S(2)}, u32[]{:S(2)}) collective-permute-start(bf16[128,1152]{1,0:T(8,128)(2,1)S(1)} %get-tuple-element.177.refs_0_.refs_4_), channel_id=1, source_target_pairs={{0,4},{4,0},{8,12},{12,8},{16,20},{20,16},{24,28},{28,24},{1,5},{5... | collective-permute-start | bytes 884744 | tf_op jit(solution)/shard_map/ppermute | solution.py:30
  39.5 19.6 %collective-permute-start.21 = (bf16[128,1152]{1,0:T(8,128)(2,1)S(1)}, bf16[128,1152]{1,0:T(8,128)(2,1)S(1)}, u32[]{:S(2)}, u32[]{:S(2)}) collective-permute-start(bf16[128,1152]{1,0:T(8,128)(2,1)S(1)} %collective-permute-done.13.refs_16_.refs_9_.refs_2_), channel_id=1, source_target_pairs={{0,4},{4,0},{8,12},{12,8},{16,20},{20,16},{24,28},{28,24},{1,5},{5... | collective-permute-start | bytes 884744 | tf_op jit(solution)/shard_map/ppermute | solution.py:30
  41.7 8.9 %collective-permute-start.16 = (bf16[128,1152]{1,0:T(8,128)(2,1)S(1)}, bf16[128,1152]{1,0:T(8,128)(2,1)S(1)}, u32[]{:S(2)}, u32[]{:S(2)}) collective-permute-start(bf16[128,1152]{1,0:T(8,128)(2,1)S(1)} %get-tuple-element.175.refs_2_), channel_id=1, source_target_pairs={{0,2},{1,3},{2,0},{3,1},{4,6},{5,7},{6,4},{7,5},{8,10},{9,11},{10,... | collective-permute-start | bytes 884744 | tf_op jit(solution)/shard_map/ppermute | solution.py:30
  46.3 8.9 %collective-permute-start.14 = (bf16[128,1152]{1,0:T(8,128)(2,1)S(1)}, bf16[128,1152]{1,0:T(8,128)(2,1)S(1)}, u32[]{:S(2)}, u32[]{:S(2)}) collective-permute-start(bf16[128,1152]{1,0:T(8,128)(2,1)S(1)} %get-tuple-element.169.refs_1_), channel_id=1, source_target_pairs={{0,2},{1,3},{2,0},{3,1},{4,6},{5,7},{6,4},{7,5},{8,10},{9,11},{10,... | collective-permute-start | bytes 884744 | tf_op jit(solution)/shard_map/ppermute | solution.py:30
  47.4 8.3 %collective-permute-start.22 = (bf16[512,1152]{1,0:T(8,128)(2,1)S(1)}, bf16[512,1152]{1,0:T(8,128)(2,1)S(1)}, u32[]{:S(2)}, u32[]{:S(2)}) collective-permute-start(bf16[512,1152]{1,0:T(8,128)(2,1)S(1)} %get-tuple-element.194), channel_id=1, source_target_pairs={{0,1},{1,0},{2,3},{3,2},{4,5},{5,4},{6,7},{7,6},{8,9},{9,8},{10,11... | collective-permute-start | bytes 3538952 | tf_op jit(solution)/shard_map/ppermute | solution.py:30
  50.6 14.5 %collective-permute-start.26 = (bf16[128,2432]{1,0:T(8,128)(2,1)S(1)}, bf16[128,2432]{1,0:T(8,128)(2,1)S(1)}, u32[]{:S(2)}, u32[]{:S(2)}) collective-permute-start(bf16[128,2432]{1,0:T(8,128)(2,1)S(1)} %get-tuple-element.209.refs_1_.refs_3_), channel_id=1, source_target_pairs={{0,8},{4,12},{8,0},{12,4},{16,24},{20,28},{24,16},{28,20},{1,9},{5... | collective-permute-start | bytes 1867784 | tf_op jit(solution)/shard_map/ppermute | solution.py:30
  50.9 8.1 %collective-permute-start.20 = (bf16[128,1152]{1,0:T(8,128)(2,1)S(1)}, bf16[128,1152]{1,0:T(8,128)(2,1)S(1)}, u32[]{:S(2)}, u32[]{:S(2)}) collective-permute-start(bf16[128,1152]{1,0:T(8,128)(2,1)S(1)} %collective-permute-done.19.refs_6_.refs_0_), channel_id=1, source_target_pairs={{0,4},{4,0},{8,12},{12,8},{16,20},{20,16},{24,28},{28,24},{1,5},{5... | collective-permute-start | bytes 884744 | tf_op jit(solution)/shard_map/ppermute | solution.py:30
  55.7 3.4 %collective-permute-start.23 = (f32[16,1152]{1,0:T(8,128)S(1)}, f32[16,1152]{1,0:T(8,128)S(1)}, u32[]{:S(2)}, u32[]{:S(2)}) collective-permute-start(f32[16,1152]{1,0:T(8,128)S(1)} %get-tuple-element.199.refs_1_), channel_id=1, source_target_pairs={{0,1},{1,0},{2,3},{3,2},{4,5},{5,4},{6,7},{7,6},{8,9},{9,8},{10,11... | collective-permute-start | bytes 221192 | tf_op jit(solution)/shard_map/ppermute | solution.py:30
  59.3 6.6 %collective-permute-start.25 = (f32[1,7424]{1,0:T(1,128)S(1)}, f32[1,7424]{1,0:T(1,128)S(1)}, u32[]{:S(2)}, u32[]{:S(2)}) collective-permute-start(f32[1,7424]{1,0:T(1,128)S(1)} %get-tuple-element.208.refs_0_), channel_id=1, source_target_pairs={{0,16},{4,20},{8,24},{12,28},{16,0},{20,4},{24,8},{28,12},{1,17},{... | collective-permute-start | bytes 89096 | tf_op jit(solution)/shard_map/ppermute | solution.py:30
  62.6 8.8 %collective-permute-start.24 = (bf16[512,1152]{1,0:T(8,128)(2,1)S(1)}, bf16[512,1152]{1,0:T(8,128)(2,1)S(1)}, u32[]{:S(2)}, u32[]{:S(2)}) collective-permute-start(bf16[512,1152]{1,0:T(8,128)(2,1)S(1)} %get-tuple-element.200), channel_id=1, source_target_pairs={{0,1},{1,0},{2,3},{3,2},{4,5},{5,4},{6,7},{7,6},{8,9},{9,8},{10,11... | collective-permute-start | bytes 3538952 | tf_op jit(solution)/shard_map/ppermute | solution.py:30
  65.3 3.1 %collective-permute-start.28 = (bf16[128,3072]{1,0:T(8,128)(2,1)S(1)}, bf16[128,3072]{1,0:T(8,128)(2,1)S(1)}, u32[]{:S(2)}, u32[]{:S(2)}) collective-permute-start(bf16[128,3072]{1,0:T(8,128)(2,1)S(1)} %get-tuple-element.215), channel_id=1, source_target_pairs={{0,1},{1,0},{2,3},{3,2},{4,5},{5,4},{6,7},{7,6},{8,9},{9,8},{10,11... | collective-permute-start | bytes 2359304 | tf_op jit(solution)/shard_map/ppermute | solution.py:30
  65.7 2.7 %collective-permute-start.29 = (bf16[128,2048]{1,0:T(8,128)(2,1)S(1)}, bf16[128,2048]{1,0:T(8,128)(2,1)S(1)}, u32[]{:S(2)}, u32[]{:S(2)}) collective-permute-start(bf16[128,2048]{1,0:T(8,128)(2,1)S(1)} %get-tuple-element.216), channel_id=1, source_target_pairs={{0,1},{1,0},{2,3},{3,2},{4,5},{5,4},{6,7},{7,6},{8,9},{9,8},{10,11... | collective-permute-start | bytes 1572872 | tf_op jit(solution)/shard_map/ppermute | solution.py:30
  65.9 4.8 %collective-permute-start.27 = (f32[2,7424]{1,0:T(2,128)S(1)}, f32[2,7424]{1,0:T(2,128)S(1)}, u32[]{:S(2)}, u32[]{:S(2)}) collective-permute-start(f32[2,7424]{1,0:T(2,128)S(1)} %get-tuple-element.214.refs_0_), channel_id=1, source_target_pairs={{0,4},{4,0},{8,12},{12,8},{16,20},{20,16},{24,28},{28,24},{1,5},{5... | collective-permute-start | bytes 178184 | tf_op jit(solution)/shard_map/ppermute | solution.py:30
  69.8 10.3 %collective-permute-start.32 = (bf16[144,1152]{1,0:T(8,128)(2,1)S(1)}, bf16[144,1152]{1,0:T(8,128)(2,1)S(1)}, u32[]{:S(2)}, u32[]{:S(2)}) collective-permute-start(bf16[144,1152]{1,0:T(8,128)(2,1)S(1)} %get-tuple-element.224), channel_id=1, source_target_pairs={{0,4},{4,0},{8,12},{12,8},{16,20},{20,16},{24,28},{28,24},{1,5},{5... | collective-permute-start | bytes 995336 | tf_op jit(solution)/shard_map/ppermute | solution.py:30
  70.7 9.6 %collective-permute-start.31 = (f32[4,7424]{1,0:T(4,128)S(1)}, f32[4,7424]{1,0:T(4,128)S(1)}, u32[]{:S(2)}, u32[]{:S(2)}) collective-permute-start(f32[4,7424]{1,0:T(4,128)S(1)} %get-tuple-element.222.refs_0_), channel_id=1, source_target_pairs={{0,8},{4,12},{8,0},{12,4},{16,24},{20,28},{24,16},{28,20},{1,9},{5... | collective-permute-start | bytes 356360 | tf_op jit(solution)/shard_map/ppermute | solution.py:30
  75.0 23.7 %collective-permute-start.37 = (bf16[144,2304]{1,0:T(8,128)(2,1)S(1)}, bf16[144,2304]{1,0:T(8,128)(2,1)S(1)}, u32[]{:S(2)}, u32[]{:S(2)}) collective-permute-start(bf16[144,2304]{1,0:T(8,128)(2,1)S(1)} %get-tuple-element.246), channel_id=1, source_target_pairs={{0,8},{4,12},{8,0},{12,4},{16,24},{20,28},{24,16},{28,20},{1,9},{5... | collective-permute-start | bytes 1990664 | tf_op jit(solution)/shard_map/ppermute | solution.py:30
  76.4 7.7 %collective-permute-start.30 = (bf16[128,2304]{1,0:T(8,128)(2,1)S(1)}, bf16[128,2304]{1,0:T(8,128)(2,1)S(1)}, u32[]{:S(2)}, u32[]{:S(2)}) collective-permute-start(bf16[128,2304]{1,0:T(8,128)(2,1)S(1)} %get-tuple-element.221.refs_0_), channel_id=1, source_target_pairs={{0,1},{1,0},{2,3},{3,2},{4,5},{5,4},{6,7},{7,6},{8,9},{9,8},{10,11... | collective-permute-start | bytes 1769480 | tf_op jit(solution)/shard_map/ppermute | solution.py:30
  76.4 13.6 %collective-permute-start.33 = (bf16[144,1152]{1,0:T(8,128)(2,1)S(1)}, bf16[144,1152]{1,0:T(8,128)(2,1)S(1)}, u32[]{:S(2)}, u32[]{:S(2)}) collective-permute-start(bf16[144,1152]{1,0:T(8,128)(2,1)S(1)} %get-tuple-element.233), channel_id=1, source_target_pairs={{0,4},{4,0},{8,12},{12,8},{16,20},{20,16},{24,28},{28,24},{1,5},{5... | collective-permute-start | bytes 995336 | tf_op jit(solution)/shard_map/ppermute | solution.py:30
  80.2 17.4 %collective-permute-start.34 = (bf16[144,1152]{1,0:T(8,128)(2,1)S(1)}, bf16[144,1152]{1,0:T(8,128)(2,1)S(1)}, u32[]{:S(2)}, u32[]{:S(2)}) collective-permute-start(bf16[144,1152]{1,0:T(8,128)(2,1)S(1)} %get-tuple-element.234), channel_id=1, source_target_pairs={{0,16},{4,20},{8,24},{12,28},{16,0},{20,4},{24,8},{28,12},{1,17},{... | collective-permute-start | bytes 995336 | tf_op jit(solution)/shard_map/ppermute | solution.py:30
  80.3 2.1 %copy-start.4 = (bf16[1152,1728]{0,1:T(8,128)(2,1)S(1)}, bf16[1152,1728]{0,1:T(8,128)(2,1)}, u32[]{:S(2)}) copy-start(bf16[1152,1728]{0,1:T(8,128)(2,1)} %param.22) | copy-start | bytes 11943940
  84.1 1.2 %collective-permute-start.35 = (f32[8,768]{1,0:T(8,128)S(1)}, f32[8,768]{1,0:T(8,128)S(1)}, u32[]{:S(2)}, u32[]{:S(2)}) collective-permute-start(f32[8,768]{1,0:T(8,128)S(1)} %get-tuple-element.236), channel_id=1, source_target_pairs={{0,1},{1,0},{2,3},{3,2},{4,5},{5,4},{6,7},{7,6},{8,9},{9,8},{10,11... | collective-permute-start | bytes 73736 | tf_op jit(solution)/shard_map/ppermute | solution.py:30
  85.3 3.7 %collective-permute-start.36 = (f32[8,288]{1,0:T(8,128)S(1)}, f32[8,288]{1,0:T(8,128)S(1)}, u32[]{:S(2)}, u32[]{:S(2)}) collective-permute-start(f32[8,288]{1,0:T(8,128)S(1)} %get-tuple-element.239), channel_id=1, source_target_pairs={{0,2},{1,3},{2,0},{3,1},{4,6},{5,7},{6,4},{7,5},{8,10},{9,11},{10,... | collective-permute-start | bytes 27656 | tf_op jit(solution)/shard_map/ppermute | solution.py:30
